TPU v7x, 32 devices: a whole 2x2x4 slice. The times are simulated.
32 devices in a mesh: ctx: 8 (over y, x, core), fsdp: 4 (over z).
Axes of the slice: x: 2, y: 2, z: 4, core: 2. Of those that a mesh axis runs over, the one named last changes fastest.
Arguments:
- tokens: bfloat16 [2048, 2, 1600], P(('ctx', 'fsdp')), may hold values from -6 to 6
- block_pairs: int32 [32], replicated, may hold values from 0 to 31, each once
- out_grad: bfloat16 [2048, 2, 1600], P(('ctx', 'fsdp')), may hold values from -6 to 6
- ln1_gain: bfloat16 [1600], P('fsdp'), may hold values from 0.5 to 1.5
- ln1_bias: bfloat16 [1600], P('fsdp'), may hold values from -4 to 4
- qkv_weight: bfloat16 [1600, 4800], P('fsdp'), may hold values from -0.15625 to 0.15625
- query_bias: bfloat16 [1600], P('fsdp'), may hold values from -4 to 4
- value_bias: bfloat16 [1600], P('fsdp'), may hold values from -4 to 4
- out_weight: bfloat16 [1600, 1600], P('fsdp'), may hold values from -6 to 6
- out_bias: bfloat16 [1600], P('fsdp'), may hold values from -4 to 4
- ln2_gain: bfloat16 [1600], P('fsdp'), may hold values from 0.5 to 1.5
- ln2_bias: bfloat16 [1600], P('fsdp'), may hold values from -4 to 4
- up_weight: bfloat16 [1600, 6400], P('fsdp'), may hold values from -0.15625 to 0.15625
- up_bias: bfloat16 [6400], P('fsdp'), may hold values from -4 to 4
- down_weight: bfloat16 [6400, 1600], P('fsdp'), may hold values from -0.078125 to 0.078125
- down_bias: bfloat16 [1600], P('fsdp'), may hold values from -4 to 4
Outputs:
- block_out: bfloat16 [2048, 2, 1600], P(('ctx', 'fsdp'))
- input_grad: float32 [2048, 2, 1600], P(('ctx', 'fsdp'))
- ln1_gain_grad: float32 [1600], P('fsdp')
- ln1_bias_grad: float32 [1600], P('fsdp')
- qkv_weight_grad: float32 [1600, 4800], P('fsdp')
- query_bias_grad: float32 [1600], P('fsdp')
- value_bias_grad: float32 [1600], P('fsdp')
- out_weight_grad: float32 [1600, 1600], P('fsdp')
- out_bias_grad: float32 [1600], P('fsdp')
- ln2_gain_grad: float32 [1600], P('fsdp')
- ln2_bias_grad: float32 [1600], P('fsdp')
- up_weight_grad: float32 [1600, 6400], P('fsdp')
- up_bias_grad: float32 [6400], P('fsdp')
- down_weight_grad: float32 [6400, 1600], P('fsdp')
- down_bias_grad: float32 [1600], P('fsdp')
Inputs may be any that keep to these rules, and one draw needn't show every extreme that they name: A permutation: the device with index e along ctx+fsdp holds the position blocks block_pairs[e] and 63 - block_pairs[e] of every sequence.
All inputs are finite; a program needn't handle non-finite values.
Results may differ from a plain program's by a relative error of at most 0.017.
Values may be sent and summed in bfloat16 or wider, within the bound.
A program may use at most 960 MiB of HBM per device.

v0:
```python
import math

import jax
import jax.numpy as jnp
from jax import lax
from jax.sharding import PartitionSpec as P

HD = 64


SCORE_KEYS = 512
NEG_BIG = -1e30
NORM_EPS = 1e-05


def layer_norm(values, norm_gain, norm_shift):
    average = jnp.mean(values, axis=-1, keepdims=True)
    centered = values - average
    variance = jnp.mean(centered * centered, axis=-1, keepdims=True)
    return centered * lax.rsqrt(variance + NORM_EPS) * norm_gain + norm_shift


def gelu_tanh(values):
    return jax.nn.gelu(values, approximate=True)


def group_plan(turn_index, ranges, group_size, block_count):
    lower_low, lower_top, upper_low, upper_top = ranges
    count_lower = (lower_top - lower_low + group_size) // group_size
    count_upper = (upper_top - upper_low + group_size) // group_size
    is_lower = turn_index < count_lower
    inner_turn = jnp.where(is_lower, turn_index, turn_index - count_lower)
    is_live = is_lower | (inner_turn < count_upper)
    range_low = jnp.where(is_lower, lower_low, upper_low)
    range_top = jnp.where(is_lower, lower_top, upper_top)
    start_block = range_low + inner_turn * group_size
    first_block = jnp.minimum(start_block, block_count - group_size)
    blocks = first_block + jnp.arange(group_size, dtype=jnp.int32)
    is_valid = (
        is_live
        & (blocks >= start_block)
        & (blocks <= jnp.minimum(start_block + group_size - 1, range_top))
    )
    half_index = jnp.where(is_lower, 0, 1).astype(jnp.int32)
    return (half_index, blocks, is_valid)


def block_rows(blocks, is_valid, half_rows):
    inner_rows = jnp.arange(half_rows, dtype=jnp.int32)
    row_pos = (blocks[:, None] * half_rows + inner_rows[None, :]).reshape(-1)
    row_ok = jnp.broadcast_to(is_valid[:, None], (blocks.shape[0], half_rows)).reshape(-1)
    return (row_pos, row_ok)


def fetch_blocks(view, locations):
    taken = jnp.take(view, locations, axis=0)
    return taken.reshape((taken.shape[0] * taken.shape[1],) + taken.shape[2:])


def own_half_pos(half_index, own_block, block_count, half_rows):
    chosen = jnp.where(half_index == 0, own_block, block_count - 1 - own_block)
    return chosen * half_rows + jnp.arange(half_rows, dtype=jnp.int32)


def add_at_half(stacked, addition, half_index):
    current = lax.dynamic_index_in_dim(stacked, half_index, 0, keepdims=False)
    return lax.dynamic_update_index_in_dim(stacked, current + addition, half_index, 0)


def query_group(turn_index, query_two, pair_view, layout, score_scale):
    own_block, block_count, half_rows, group_size, block_loc = layout
    ranges = (0, own_block, 0, block_count - 1 - own_block)
    half_index, blocks, is_valid = group_plan(turn_index, ranges, group_size, block_count)
    locations = jnp.take(block_loc, blocks)
    pair_rows = fetch_blocks(pair_view, locations)
    queries = lax.dynamic_index_in_dim(query_two, half_index, 0, keepdims=False)
    query_pos = own_half_pos(half_index, own_block, block_count, half_rows)
    key_pos, key_ok = block_rows(blocks, is_valid, half_rows)
    raw_scores = (
        jnp.einsum(
            "qshe,kshe->shqk", queries, pair_rows[:, :, 0], preferred_element_type=jnp.float32
        )
        * score_scale
    )
    allowed = key_ok[None, :] & (key_pos[None, :] <= query_pos[:, None])
    return (
        half_index,
        locations,
        pair_rows,
        queries,
        jnp.where(allowed, raw_scores, NEG_BIG),
        allowed,
    )


def attend_forward(query_two, pair_view, layout, score_scale):
    own_block, block_count, half_rows, group_size, block_loc = layout
    seq_count, head_count = (query_two.shape[2], query_two.shape[3])
    stat_shape = (2, seq_count, head_count, half_rows)
    turns = jnp.arange(block_count // group_size + 1, dtype=jnp.int32)

    def stat_turn(state_now, turn_index):
        run_max, run_sum = state_now
        half_index, locations, pair_rows, queries, scores, allowed = query_group(
            turn_index, query_two, pair_view, layout, score_scale
        )
        row_max = jnp.max(scores, axis=-1)
        row_sum = jnp.sum(jnp.where(allowed, jnp.exp(scores - row_max[..., None]), 0.0), axis=-1)
        old_max = lax.dynamic_index_in_dim(run_max, half_index, 0, keepdims=False)
        old_sum = lax.dynamic_index_in_dim(run_sum, half_index, 0, keepdims=False)
        new_max = jnp.maximum(old_max, row_max)
        new_sum = old_sum * jnp.exp(old_max - new_max) + row_sum * jnp.exp(row_max - new_max)
        run_max = lax.dynamic_update_index_in_dim(run_max, new_max, half_index, 0)
        run_sum = lax.dynamic_update_index_in_dim(run_sum, new_sum, half_index, 0)
        return ((run_max, run_sum), None)

    start_state = (jnp.full(stat_shape, NEG_BIG, jnp.float32), jnp.zeros(stat_shape, jnp.float32))
    (run_max, run_sum), unused = lax.scan(stat_turn, start_state, turns)
    log_two = run_max + jnp.log(run_sum)

    def out_turn(state_now, turn_index):
        coarse, refined = state_now
        half_index, locations, pair_rows, queries, scores, allowed = query_group(
            turn_index, query_two, pair_view, layout, score_scale
        )
        log_half = lax.dynamic_index_in_dim(log_two, half_index, 0, keepdims=False)
        soft_probs = jnp.where(allowed, jnp.exp(scores - log_half[..., None]), 0.0)
        soft_low = soft_probs.astype(jnp.bfloat16)
        remainder = (soft_probs - soft_low.astype(jnp.float32)).astype(jnp.bfloat16)
        value_rows = pair_rows[:, :, 1]
        coarse = add_at_half(
            coarse,
            jnp.einsum("shqk,kshe->qshe", soft_low, value_rows, preferred_element_type=jnp.float32),
            half_index,
        )
        refined = add_at_half(
            refined,
            jnp.einsum(
                "shqk,kshe->qshe", remainder, value_rows, preferred_element_type=jnp.float32
            ),
            half_index,
        )
        return ((coarse, refined), None)

    empty = jnp.zeros(query_two.shape, jnp.float32)
    (coarse, refined), unused = lax.scan(out_turn, (empty, empty), turns)
    return (log_two, coarse, coarse + refined)


def key_side_grads(
    key_two, value_two, query_view, grad_view, total_view, dot_view, layout, score_scale
):
    own_block, block_count, half_rows, group_size, block_loc = layout
    ranges = (own_block, block_count - 1, block_count - 1 - own_block, block_count - 1)
    turns = jnp.arange(block_count // group_size + 1, dtype=jnp.int32)
    seq_count, head_count, head_dim = (key_two.shape[2], key_two.shape[3], key_two.shape[4])

    def grad_turn(state_now, turn_index):
        grad_key, grad_value, terms = state_now
        half_index, blocks, is_valid = group_plan(turn_index, ranges, group_size, block_count)
        locations = jnp.take(block_loc, blocks)
        queries = fetch_blocks(query_view, locations)
        grad_rows = fetch_blocks(grad_view, locations)
        total_piece = fetch_blocks(total_view, locations)
        dot_piece = fetch_blocks(dot_view, locations)
        key_rows = lax.dynamic_index_in_dim(key_two, half_index, 0, keepdims=False)
        value_rows = lax.dynamic_index_in_dim(value_two, half_index, 0, keepdims=False)
        key_pos = own_half_pos(half_index, own_block, block_count, half_rows)
        query_pos, query_ok = block_rows(blocks, is_valid, half_rows)
        raw_scores = (
            jnp.einsum("kshe,qshe->shkq", key_rows, queries, preferred_element_type=jnp.float32)
            * score_scale
        )
        allowed = query_ok[None, :] & (key_pos[:, None] <= query_pos[None, :])
        scores = jnp.where(allowed, raw_scores, NEG_BIG)
        total_cols = jnp.transpose(total_piece, (1, 2, 0))[:, :, None, :]
        dot_cols = jnp.transpose(dot_piece, (1, 2, 0))[:, :, None, :]
        soft_probs = jnp.where(allowed, jnp.exp(scores - total_cols), 0.0)
        grad_soft = jnp.einsum(
            "kshe,qshe->shkq", value_rows, grad_rows, preferred_element_type=jnp.float32
        )
        grad_scores = (soft_probs * (grad_soft - dot_cols)).astype(jnp.bfloat16)
        key_part = score_scale * jnp.einsum(
            "shkq,qshe->kshe", grad_scores, queries, preferred_element_type=jnp.float32
        )
        value_part = jnp.einsum(
            "shkq,qshe->kshe",
            soft_probs.astype(jnp.bfloat16),
            grad_rows,
            preferred_element_type=jnp.float32,
        )
        grad_key = add_at_half(grad_key, key_part, half_index)
        grad_value = add_at_half(grad_value, value_part, half_index)
        query_part = score_scale * jnp.einsum(
            "shkq,kshe->qshe", grad_scores, key_rows, preferred_element_type=jnp.float32
        )
        terms = terms.at[locations].add(
            query_part.reshape((group_size, half_rows, seq_count, head_count, head_dim))
        )
        return ((grad_key, grad_value, terms), None)

    terms_start = jnp.zeros((block_count, half_rows, seq_count, head_count, head_dim), jnp.float32)
    empty = jnp.zeros(key_two.shape, jnp.float32)
    (grad_key, grad_value, terms), unused = lax.scan(grad_turn, (empty, empty, terms_start), turns)
    return (grad_key, grad_value, terms)


def local(
    tokens,
    block_pairs,
    out_grad,
    ln1_gain,
    ln1_bias,
    qkv_weight,
    query_bias,
    value_bias,
    out_weight,
    out_bias,
    ln2_gain,
    ln2_bias,
    up_weight,
    up_bias,
    down_weight,
    down_bias,
):
    local_rows, seq_count, model_width = tokens.shape
    head_dim = HD
    head_count = model_width // head_dim
    score_scale = head_dim ** (-0.5)
    device_count = lax.axis_size("ctx") * lax.axis_size("fsdp")
    own_index = lax.axis_index("ctx") * lax.axis_size("fsdp") + lax.axis_index("fsdp")
    half_rows = local_rows // 2
    block_count = 2 * device_count
    total_rows = device_count * local_rows
    group_size = math.gcd(block_count, max(1, SCORE_KEYS // half_rows))
    device_ids = jnp.arange(device_count, dtype=jnp.int32)
    device_of_block = jnp.sum(
        jnp.where(block_pairs[None, :] == device_ids[:, None], device_ids[None, :], 0), axis=1
    )
    block_ids = jnp.arange(block_count, dtype=jnp.int32)
    is_first = block_ids < device_count
    owner_ids = jnp.take(
        device_of_block, jnp.where(is_first, block_ids, block_count - 1 - block_ids)
    )
    block_loc = owner_ids * 2 + jnp.where(is_first, 0, 1)
    own_block = lax.dynamic_index_in_dim(block_pairs, own_index, 0, keepdims=False)
    layout = (own_block, block_count, half_rows, group_size, block_loc)
    two_shape = (2, half_rows, seq_count, head_count, head_dim)
    view_shape = (block_count, half_rows, seq_count, head_count, head_dim)
    (
        first_gain,
        first_shift,
        joint_weight,
        query_shift,
        value_shift,
        output_weight,
        output_shift,
        second_gain,
        second_shift,
        upward_weight,
        upward_shift,
        downward_weight,
        downward_shift,
    ) = (
        lax.all_gather(ln1_gain, "fsdp", axis=0, tiled=True),
        lax.all_gather(ln1_bias, "fsdp", axis=0, tiled=True),
        lax.all_gather(qkv_weight, "fsdp", axis=0, tiled=True),
        lax.all_gather(query_bias, "fsdp", axis=0, tiled=True),
        lax.all_gather(value_bias, "fsdp", axis=0, tiled=True),
        lax.all_gather(out_weight, "fsdp", axis=0, tiled=True),
        lax.all_gather(out_bias, "fsdp", axis=0, tiled=True),
        lax.all_gather(ln2_gain, "fsdp", axis=0, tiled=True),
        lax.all_gather(ln2_bias, "fsdp", axis=0, tiled=True),
        lax.all_gather(up_weight, "fsdp", axis=0, tiled=True),
        lax.all_gather(up_bias, "fsdp", axis=0, tiled=True),
        lax.all_gather(down_weight, "fsdp", axis=0, tiled=True),
        lax.all_gather(down_bias, "fsdp", axis=0, tiled=True),
    )
    inputs = tokens.astype(jnp.float32)
    first_norm, first_back = jax.vjp(
        layer_norm, inputs, first_gain.astype(jnp.float32), first_shift.astype(jnp.float32)
    )
    normed_one = first_norm.astype(jnp.bfloat16)
    joint_out = jnp.einsum(
        "rsd,de->rse", normed_one, joint_weight, preferred_element_type=jnp.float32
    )
    query_low = (joint_out[..., :model_width] + query_shift.astype(jnp.float32)).astype(
        jnp.bfloat16
    )
    key_low = joint_out[..., model_width : 2 * model_width].astype(jnp.bfloat16)
    value_low = (joint_out[..., 2 * model_width :] + value_shift.astype(jnp.float32)).astype(
        jnp.bfloat16
    )
    gathered = lax.all_gather(
        jnp.concatenate([key_low, value_low], axis=-1), ("ctx", "fsdp"), axis=0, tiled=True
    )
    pair_view = gathered.reshape((block_count, half_rows, seq_count, 2, head_count, head_dim))
    query_two = query_low.reshape(two_shape)
    key_two = key_low.reshape(two_shape)
    value_two = value_low.reshape(two_shape)
    log_two, coarse_two, exact_two = attend_forward(query_two, pair_view, layout, score_scale)
    attended_low = coarse_two.reshape(local_rows, seq_count, model_width).astype(jnp.bfloat16)
    branch = jnp.einsum(
        "rse,ed->rsd", attended_low, output_weight, preferred_element_type=jnp.float32
    )
    mixed_sum = inputs + branch + output_shift.astype(jnp.float32)
    second_norm, second_back = jax.vjp(
        layer_norm, mixed_sum, second_gain.astype(jnp.float32), second_shift.astype(jnp.float32)
    )
    normed_two = second_norm.astype(jnp.bfloat16)
    upward = jnp.einsum(
        "rsd,df->rsf", normed_two, upward_weight, preferred_element_type=jnp.float32
    ) + upward_shift.astype(jnp.float32)
    activated, gelu_back = jax.vjp(gelu_tanh, upward)
    act_low = activated.astype(jnp.bfloat16)
    block_out = (
        mixed_sum
        + jnp.einsum("rsf,fd->rsd", act_low, downward_weight, preferred_element_type=jnp.float32)
        + downward_shift.astype(jnp.float32)
    ).astype(jnp.bfloat16)
    grad_act = jnp.einsum(
        "rsd,fd->rsf", out_grad, downward_weight, preferred_element_type=jnp.float32
    )
    (grad_upward,) = gelu_back(grad_act)
    grad_up_low = grad_upward.astype(jnp.bfloat16)
    grad_norm_two = jnp.einsum(
        "rsf,df->rsd", grad_up_low, upward_weight, preferred_element_type=jnp.float32
    )
    grad_mixed_part, grad_gain_two, grad_shift_two = second_back(grad_norm_two)
    grad_mixed = out_grad.astype(jnp.float32) + grad_mixed_part
    grad_branch = grad_mixed.astype(jnp.bfloat16)
    grad_attended = jnp.einsum(
        "rsd,ed->rse", grad_branch, output_weight, preferred_element_type=jnp.float32
    ).astype(jnp.bfloat16)
    grad_two = grad_attended.reshape(two_shape)
    row_dot_two = jnp.sum(grad_two.astype(jnp.float32) * exact_two, axis=-1)
    log_total = jnp.transpose(log_two, (0, 3, 1, 2)).reshape(local_rows, seq_count, head_count)
    row_dot = row_dot_two.reshape(local_rows, seq_count, head_count)
    sent_query, sent_grad = (
        lax.all_gather(query_low, ("ctx", "fsdp"), axis=0, tiled=True),
        lax.all_gather(grad_attended, ("ctx", "fsdp"), axis=0, tiled=True),
    )
    sent_total, sent_dot = (
        lax.all_gather(log_total, ("ctx", "fsdp"), axis=0, tiled=True),
        lax.all_gather(row_dot, ("ctx", "fsdp"), axis=0, tiled=True),
    )
    grad_key_two, grad_value_two, terms = key_side_grads(
        key_two,
        value_two,
        sent_query.reshape(view_shape),
        sent_grad.reshape(view_shape),
        sent_total.reshape(view_shape[:4]),
        sent_dot.reshape(view_shape[:4]),
        layout,
        score_scale,
    )
    grad_key_flat = grad_key_two.reshape(local_rows, seq_count, model_width)
    grad_value_flat = grad_value_two.reshape(local_rows, seq_count, model_width)
    grad_query_flat = lax.psum_scatter(
        terms.reshape(total_rows, seq_count, model_width),
        ("ctx", "fsdp"),
        scatter_dimension=0,
        tiled=True,
    )
    grad_query_low = grad_query_flat.astype(jnp.bfloat16)
    grad_value_low = grad_value_flat.astype(jnp.bfloat16)
    grad_joint = jnp.concatenate(
        [grad_query_low, grad_key_flat.astype(jnp.bfloat16), grad_value_low], axis=-1
    )
    grad_norm_one = jnp.einsum(
        "rse,de->rsd", grad_joint, joint_weight, preferred_element_type=jnp.float32
    )
    grad_input_part, grad_gain_one, grad_shift_one = first_back(grad_norm_one)
    input_grad = grad_mixed + grad_input_part
    grad_joint_weight = jnp.einsum(
        "rsd,rse->de", normed_one, grad_joint, preferred_element_type=jnp.float32
    )
    grad_query_shift = jnp.sum(grad_query_low.astype(jnp.float32), axis=(0, 1))
    grad_value_shift = jnp.sum(grad_value_low.astype(jnp.float32), axis=(0, 1))
    grad_output_weight = jnp.einsum(
        "rse,rsd->ed", attended_low, grad_branch, preferred_element_type=jnp.float32
    )
    grad_output_shift = jnp.sum(grad_branch.astype(jnp.float32), axis=(0, 1))
    grad_upward_weight = jnp.einsum(
        "rsd,rsf->df", normed_two, grad_up_low, preferred_element_type=jnp.float32
    )
    grad_upward_shift = jnp.sum(grad_up_low.astype(jnp.float32), axis=(0, 1))
    grad_downward_weight = jnp.einsum(
        "rsf,rsd->fd", act_low, out_grad, preferred_element_type=jnp.float32
    )
    grad_downward_shift = jnp.sum(out_grad.astype(jnp.float32), axis=(0, 1))
    (
        owned_gain_one,
        owned_shift_one,
        owned_joint,
        owned_query,
        owned_value,
        owned_output,
        owned_oshift,
        owned_gain_two,
        owned_shift_two,
        owned_upward,
        owned_ushift,
        owned_downward,
        owned_dshift,
    ) = (
        lax.psum_scatter(
            grad_gain_one.astype(jnp.bfloat16), "fsdp", scatter_dimension=0, tiled=True
        ).astype(jnp.float32),
        lax.psum_scatter(
            grad_shift_one.astype(jnp.bfloat16), "fsdp", scatter_dimension=0, tiled=True
        ).astype(jnp.float32),
        lax.psum_scatter(
            grad_joint_weight.astype(jnp.bfloat16), "fsdp", scatter_dimension=0, tiled=True
        ).astype(jnp.float32),
        lax.psum_scatter(
            grad_query_shift.astype(jnp.bfloat16), "fsdp", scatter_dimension=0, tiled=True
        ).astype(jnp.float32),
        lax.psum_scatter(
            grad_value_shift.astype(jnp.bfloat16), "fsdp", scatter_dimension=0, tiled=True
        ).astype(jnp.float32),
        lax.psum_scatter(
            grad_output_weight.astype(jnp.bfloat16), "fsdp", scatter_dimension=0, tiled=True
        ).astype(jnp.float32),
        lax.psum_scatter(
            grad_output_shift.astype(jnp.bfloat16), "fsdp", scatter_dimension=0, tiled=True
        ).astype(jnp.float32),
        lax.psum_scatter(
            grad_gain_two.astype(jnp.bfloat16), "fsdp", scatter_dimension=0, tiled=True
        ).astype(jnp.float32),
        lax.psum_scatter(
            grad_shift_two.astype(jnp.bfloat16), "fsdp", scatter_dimension=0, tiled=True
        ).astype(jnp.float32),
        lax.psum_scatter(
            grad_upward_weight.astype(jnp.bfloat16), "fsdp", scatter_dimension=0, tiled=True
        ).astype(jnp.float32),
        lax.psum_scatter(
            grad_upward_shift.astype(jnp.bfloat16), "fsdp", scatter_dimension=0, tiled=True
        ).astype(jnp.float32),
        lax.psum_scatter(
            grad_downward_weight.astype(jnp.bfloat16), "fsdp", scatter_dimension=0, tiled=True
        ).astype(jnp.float32),
        lax.psum_scatter(
            grad_downward_shift.astype(jnp.bfloat16), "fsdp", scatter_dimension=0, tiled=True
        ).astype(jnp.float32),
    )
    totals = (
        lax.psum(owned_gain_one.astype(jnp.bfloat16), "ctx").astype(jnp.float32),
        lax.psum(owned_shift_one.astype(jnp.bfloat16), "ctx").astype(jnp.float32),
        lax.psum(owned_joint.astype(jnp.bfloat16), "ctx").astype(jnp.float32),
        lax.psum(owned_query.astype(jnp.bfloat16), "ctx").astype(jnp.float32),
        lax.psum(owned_value.astype(jnp.bfloat16), "ctx").astype(jnp.float32),
        lax.psum(owned_output.astype(jnp.bfloat16), "ctx").astype(jnp.float32),
        lax.psum(owned_oshift.astype(jnp.bfloat16), "ctx").astype(jnp.float32),
        lax.psum(owned_gain_two.astype(jnp.bfloat16), "ctx").astype(jnp.float32),
        lax.psum(owned_shift_two.astype(jnp.bfloat16), "ctx").astype(jnp.float32),
        lax.psum(owned_upward.astype(jnp.bfloat16), "ctx").astype(jnp.float32),
        lax.psum(owned_ushift.astype(jnp.bfloat16), "ctx").astype(jnp.float32),
        lax.psum(owned_downward.astype(jnp.bfloat16), "ctx").astype(jnp.float32),
        lax.psum(owned_dshift.astype(jnp.bfloat16), "ctx").astype(jnp.float32),
    )
    return (
        block_out,
        input_grad,
        totals[0],
        totals[1],
        totals[2],
        totals[3],
        totals[4],
        totals[5],
        totals[6],
        totals[7],
        totals[8],
        totals[9],
        totals[10],
        totals[11],
        totals[12],
    )


def solution(mesh):
    in_specs = (
        P(("ctx", "fsdp"), None, None),
        P(),
        P(("ctx", "fsdp"), None, None),
        P("fsdp"),
        P("fsdp"),
        P("fsdp", None),
        P("fsdp"),
        P("fsdp"),
        P("fsdp", None),
        P("fsdp"),
        P("fsdp"),
        P("fsdp"),
        P("fsdp", None),
        P("fsdp"),
        P("fsdp", None),
        P("fsdp"),
    )
    out_specs = (
        P(("ctx", "fsdp"), None, None),
        P(("ctx", "fsdp"), None, None),
        P("fsdp"),
        P("fsdp"),
        P("fsdp", None),
        P("fsdp"),
        P("fsdp"),
        P("fsdp", None),
        P("fsdp"),
        P("fsdp"),
        P("fsdp"),
        P("fsdp", None),
        P("fsdp"),
        P("fsdp", None),
        P("fsdp"),
    )
    return jax.shard_map(local, mesh=mesh, in_specs=in_specs, out_specs=out_specs, check_vma=False)
```

profile of v0, /device:TPU:0, one launch (start us, length us, event | category | flops | bytes accessed | tf_op | source)
XLA Modules:
  0.0 4363.5 jit_solution(12039820875337513844)
XLA Ops:
  12.1 21.7 all-reduce.21
  34.3 245.4 %all-gather.8.cloned.1.call-done = bf16[1600,4800]{1,0:T(8,128)(2,1)} async-done(((bf16[400,4800]{1,0:T(8,128)(2,1)}), bf16[1600,4800]{1,0:T(8,128)(2,1)}) %all-gather.8.cloned.1.call-update) | async-done | bytes 15360016 | tf_op jit(solution)/shard_map/all_gather | solution.py:267
  300.1 147.8 %all-gather.10.cloned.1.call-done = bf16[2048,2,3200]{2,0,1:T(8,128)(2,1)} async-done(((bf16[64,2,3200]{2,0,1:T(8,128)(2,1)}), bf16[2048,2,3200]{2,0,1:T(8,128)(2,1)}) %all-gather.10.cloned.1.call-update) | async-done | bytes 26214416 | tf_op jit(solution)/shard_map/all_gather | solution.py:294
  447.9 91.1 %reshape.430 = bf16[64,32,2,2,25,64]{5,4,3,1,0,2:T(8,128)(2,1)} reshape(bf16[2048,2,3200]{2,0,1:T(8,128)(2,1)} %all-gather.10.cloned.1.call-done) | data formatting | bytes 52428800 | tf_op jit(solution)/shard_map/reshape | solution.py:297
  539.0 46.7 %copy.154 = bf16[64,32,2,2,25,64]{5,4,3,2,1,0:T(8,128)(2,1)} copy(bf16[64,32,2,2,25,64]{5,4,3,1,0,2:T(8,128)(2,1)} %reshape.430) | data formatting | bytes 52428800 | tf_op jit(solution)/shard_map/while | solution.py:146
  585.7 262.2 %while.53 = (s32[]{:T(128)}, f32[2,2,25,32]{3,2,1,0:T(8,128)S(1)}, f32[2,2,25,32]{3,2,1,0:T(8,128)S(1)}, s32[5]{0:T(128)S(1)}, s32[]{:T(128)}, /*index=5*/s32[]{...) while((s32[]{:T(128)}, f32[2,2,25,32]{3,2,1,0:T(8,128)S(1)}, ...), condition=%wide.region_6.9_spmd, body=%wide.region_3.8_spmd.sunk | while | flops 114730160 | bytes 49846380 | solution.py:118
  850.8 312.4 %while.54 = (s32[]{:T(128)}, f32[2,32,2,25,64]{4,1,3,2,0:T(8,128)}, f32[2,32,2,25,64]{4,1,3,2,0:T(8,128)}, s32[5]{0:T(128)S(1)}, s32[]{:T(128)}, /*index=5*/s32[...) while((s32[]{:T(128)}, f32[2,32,2,25,64]{4,1,3,2,0:T(8,128)}, ...), condition=%wide.region_8.11_spmd, body=%wide.region_7.10_spmd.sunk | while | flops 328739744 | bytes 96786624 | solution.py:146
  1182.2 75.9 %all-gather.16.cloned.1.call-done = bf16[6400,1600]{1,0:T(8,128)(2,1)} async-done(((bf16[1600,1600]{1,0:T(8,128)(2,1)}), bf16[6400,1600]{1,0:T(8,128)(2,1)}) %all-gather.16.cloned.1.call-update) | async-done | bytes 20480016 | tf_op jit(solution)/shard_map/all_gather | solution.py:276
  1258.1 23.0 fusion.188
  1302.9 57.9 %all-gather.18.cloned.1.call-done = bf16[2048,2,1600]{2,0,1:T(8,128)(2,1)} async-done(((bf16[64,2,1600]{2,0,1:T(8,128)(2,1)}), bf16[2048,2,1600]{2,0,1:T(8,128)(2,1)}) %all-gather.18.cloned.1.call-update) | async-done | bytes 13107216 | tf_op jit(solution)/shard_map/all_gather | solution.py:340
  1360.8 41.9 reshape.432
  1402.7 22.9 copy.166
  1427.9 106.7 %all_gather.69 = f32[2048,2,25]{2,1,0:T(2,128)} all-gather(f32[64,2,25]{2,1,0:T(2,128)S(1)} %bitcast.340), channel_id=1, replica_groups=mesh['ctx'=8,'fsdp'=4] {'ctx','fsdp'}, dimensions={0}, use_global_device_ids=true | all-gather | bytes 422400 | tf_op jit(solution)/shard_map/all_gather | solution.py:344
  1543.1 85.7 %all_gather.71 = f32[2048,2,25]{2,1,0:T(2,128)S(1)} all-gather(f32[64,2,25]{2,1,0:T(2,128)S(1)} %copy.164), channel_id=1, replica_groups=mesh['ctx'=8,'fsdp'=4] {'ctx','fsdp'}, dimensions={0}, use_global_device_ids=true | all-gather | bytes 422400 | tf_op jit(solution)/shard_map/all_gather | solution.py:345
  1632.6 41.8 reshape.437
  1674.5 22.7 copy.170
  1716.9 663.6 %while.55 = (s32[]{:T(128)}, f32[2,32,2,25,64]{4,1,3,2,0:T(8,128)}, f32[2,32,2,25,64]{4,1,3,2,0:T(8,128)}, f32[64,32,2,25,64]{4,1,3,2,0:T(8,128)}, s32[5]{0:T(12...) while((s32[]{:T(128)}, f32[2,32,2,25,64]{4,1,3,2,0:T(8,128)}, ...), condition=%wide.region_16.21_spmd, body=%wide.region_14.20_spmd.sunk | while | flops 541066112 | bytes 169189264 | solution.py:204
  1820.3 29.6 scatter_fusion
  1952.8 29.8 scatter_fusion
  2085.6 29.6 scatter_fusion
  2218.1 29.7 scatter_fusion
  2350.8 29.6 scatter_fusion
  2380.5 56.4 %copy.172 = f32[64,32,2,25,64]{4,3,1,0,2:T(8,128)} copy(f32[64,32,2,25,64]{4,1,3,2,0:T(8,128)} %get-tuple-element.1187) | data formatting | bytes 52428800 | tf_op jit(solution)/shard_map/while | solution.py:204
  2436.9 51.2 %reshape.440 = f32[2048,2,1600]{2,0,1:T(8,128)} reshape(f32[64,32,2,25,64]{4,3,1,0,2:T(8,128)} %copy.172) | data formatting | bytes 52428800 | tf_op jit(solution)/shard_map/reshape | solution.py:360
  2525.4 540.4 %reduce-scatter.6.cloned.1.call-done = f32[64,2,1600]{2,0,1:T(8,128)} async-done(((f32[2048,2,1600]{2,0,1:T(8,128)}), f32[64,2,1600]{2,0,1:T(8,128)}) %reduce-scatter.6.cloned.1.call-update) | async-done | bytes 819216 | tf_op jit(solution)/shard_map/reduce_scatter | solution.py:359
  3078.0 84.9 %reduce-scatter.10.cloned.1.call-done = bf16[400,1600]{1,0:T(8,128)(2,1)} async-done(((bf16[1600,1600]{1,0:T(8,128)(2,1)}), bf16[400,1600]{1,0:T(8,128)(2,1)}) %reduce-scatter.10.cloned.1.call-update) | async-done | bytes 1280016 | tf_op jit(solution)/shard_map/reduce_scatter | solution.py:422
  3162.9 342.4 %reduce-scatter.12.cloned.1.call-done = bf16[400,6400]{1,0:T(8,128)(2,1)} async-done(((bf16[1600,6400]{1,0:T(8,128)(2,1)}), bf16[400,6400]{1,0:T(8,128)(2,1)}) %reduce-scatter.12.cloned.1.call-update) | async-done | bytes 5120016 | tf_op jit(solution)/shard_map/reduce_scatter | solution.py:434
  3505.3 356.7 %reduce-scatter.14.cloned.1.call-done = bf16[1600,1600]{1,0:T(8,128)(2,1)} async-done(((bf16[6400,1600]{1,0:T(8,128)(2,1)}), bf16[1600,1600]{1,0:T(8,128)(2,1)}) %reduce-scatter.14.cloned.1.call-update) | async-done | bytes 5120016 | tf_op jit(solution)/shard_map/reduce_scatter | solution.py:440
  3862.0 264.2 %reduce-scatter.8.cloned.1.call-done = bf16[400,4800]{1,0:T(8,128)(2,1)} async-done(((bf16[1600,4800]{1,0:T(8,128)(2,1)}), bf16[400,4800]{1,0:T(8,128)(2,1)}) %reduce-scatter.8.cloned.1.call-update) | async-done | bytes 3840016 | tf_op jit(solution)/shard_map/reduce_scatter | solution.py:413
  4139.8 19.5 all-reduce.20
  4175.9 24.5 all-reduce.18
  4205.6 133.7 %all-reduce.24.cloned.1.call-done = (bf16[400,4800]{1,0:T(8,128)(2,1)}, bf16[400,1600]{1,0:T(8,128)(2,1)}, bf16[400,6400]{1,0:T(8,128)(2,1)}, bf16[1600,1600]{1,0:T(8,128)(2,1)}) async-done(((bf16[400,4800]{1,0:T(8,128)(2,1)}, bf16[400,1600]{1,0:T(8,128)(2,1)}, bf16[400,6400]{1,0:T(8,128)(2,1)}, bf16[1600,1600]{1,0:T(8,128)(2,1)}), (bf16[400,4800]{1,0:T(8,128)(2,1)}, bf16[400,1600]{1,0:T(8,128)(2,1)}, ...) | async-done | bytes 15360016 | tf_op jit(solution)/shard_map/psum | solution.py:450
  (785 shorter events, 1239.0 us)
Async XLA Ops:
  7.3 26.6 copy-start.15
  7.3 272.4 %all-gather.8.cloned.1.call-start = ((), (), s32[]{:S(2)}) async-start(), calls=%async_computation.5 | async-start | bytes 19456000 | tf_op jit(solution)/shard_map/all_gather | solution.py:267
  8.0 439.9 %all-gather.10.cloned.1.call-start = ((), (), s32[]{:S(2)}) async-start(), calls=%async_computation.6 | async-start | bytes 27033600 | tf_op jit(solution)/shard_map/all_gather | solution.py:294
  33.8 253.8 %copy-start.43 = (f32[1600]{0:T(1024)}, f32[1600]{0:T(1024)S(1)}, u32[]{:S(2)}) copy-start(f32[1600]{0:T(1024)S(1)} %convert_element_type.240) | copy-start | bytes 19204
  33.8 253.8 %copy-start.39 = (f32[1600]{0:T(1024)}, f32[1600]{0:T(1024)S(1)}, u32[]{:S(2)}) copy-start(f32[1600]{0:T(1024)S(1)} %convert_element_type.239) | copy-start | bytes 19204
  34.0 253.6 %copy-start.49 = (f32[64,2]{0,1:T(2,128)}, f32[64,2]{0,1:T(2,128)S(1)}, u32[]{:S(2)}) copy-start(f32[64,2]{0,1:T(2,128)S(1)} %broadcast_multiply_fusion.1) | copy-start | bytes 1540
  34.3 253.4 %copy-start.61 = (f32[64,2]{0,1:T(2,128)}, f32[64,2]{0,1:T(2,128)S(1)}, u32[]{:S(2)}) copy-start(f32[64,2]{0,1:T(2,128)S(1)} %fusion.162) | copy-start | bytes 1540
  34.3 253.4 %copy-start.52 = (f32[64,2]{0,1:T(2,128)}, f32[64,2]{0,1:T(2,128)S(1)}, u32[]{:S(2)}) copy-start(f32[64,2]{0,1:T(2,128)S(1)} %fusion.174) | copy-start | bytes 1540
  289.9 876.2 %all-gather.12.cloned.1.call-start = ((), (), s32[]{:S(2)}) async-start(), calls=%async_computation.7 | async-start | bytes 6656000 | tf_op jit(solution)/shard_map/all_gather | solution.py:270
  290.6 879.6 %all-gather.14.cloned.1.call-start = ((), (), s32[]{:S(2)}) async-start(), calls=%async_computation.8 | async-start | bytes 25600000 | tf_op jit(solution)/shard_map/all_gather | solution.py:274
  291.2 966.9 %all-gather.16.cloned.1.call-start = ((), (), s32[]{:S(2)}) async-start(), calls=%async_computation.9 | async-start | bytes 26624000 | tf_op jit(solution)/shard_map/all_gather | solution.py:276
  291.8 1069.0 %all-gather.18.cloned.1.call-start = ((), (), s32[]{:S(2)}) async-start(), calls=%async_computation.10 | async-start | bytes 14057472 | tf_op jit(solution)/shard_map/all_gather | solution.py:340
  299.8 1332.8 %all-gather.20.cloned.1.call-start = ((), (), s32[]{:S(2)}) async-start(), calls=%async_computation.11 | async-start | bytes 14057472 | tf_op jit(solution)/shard_map/all_gather | solution.py:341
  1169.9 123.3 %copy-start.4 = (f32[64,2,1600]{2,0,1:T(8,128)}, f32[64,2,1600]{2,0,1:T(8,128)S(1)}, u32[]{:S(2)}) copy-start(f32[64,2,1600]{2,0,1:T(8,128)S(1)} %get-tuple-element.1561) | copy-start | bytes 2457604
  1169.9 123.2 %copy-start.45 = (f32[64,2]{0,1:T(2,128)}, f32[64,2]{0,1:T(2,128)S(1)}, u32[]{:S(2)}) copy-start(f32[64,2]{0,1:T(2,128)S(1)} %broadcast_multiply_fusion) | copy-start | bytes 1540
  1170.1 123.0 %copy-start.47 = (f32[64,2]{0,1:T(2,128)}, f32[64,2]{0,1:T(2,128)S(1)}, u32[]{:S(2)}) copy-start(f32[64,2]{0,1:T(2,128)S(1)} %fusion.175) | copy-start | bytes 1540
  1170.1 87.9 %copy-start.23 = (bf16[64,2,1600]{2,1,0:T(2,128)(2,1)S(1)}, bf16[64,2,1600]{2,1,0:T(2,128)(2,1)}, u32[]{:S(2)}) copy-start(bf16[64,2,1600]{2,1,0:T(2,128)(2,1)} %param.32) | copy-start | bytes 1228804
  1281.0 14.9 slice-start.1
  1298.6 1767.3 %reduce-scatter.6.cloned.1.call-start = ((), (), s32[]{:S(2)}) async-start(), calls=%async_computation.12 | async-start | bytes 28114944 | tf_op jit(solution)/shard_map/reduce_scatter | solution.py:359
  1402.7 22.9 copy-start.35
  1427.8 111.5 %copy-start.3 = (f32[2,32,2,25,64]{4,1,3,2,0:T(8,128)S(1)}, f32[2,32,2,25,64]{4,1,3,2,0:T(8,128)}, u32[]{:S(2)}) copy-start(f32[2,32,2,25,64]{4,1,3,2,0:T(8,128)} %get-tuple-element.1185) | copy-start | bytes 2457604
  1427.8 111.5 %copy-start.14 = (f32[2,32,2,25,64]{4,1,3,2,0:T(8,128)S(1)}, f32[2,32,2,25,64]{4,1,3,2,0:T(8,128)}, u32[]{:S(2)}) copy-start(f32[2,32,2,25,64]{4,1,3,2,0:T(8,128)} %get-tuple-element.1186) | copy-start | bytes 2457604
  2488.1 674.8 %reduce-scatter.10.cloned.1.call-start = ((), (), s32[]{:S(2)}) async-start(), calls=%async_computation.14 | async-start | bytes 6656000 | tf_op jit(solution)/shard_map/reduce_scatter | solution.py:422
  2493.2 1012.1 %reduce-scatter.12.cloned.1.call-start = ((), (), s32[]{:S(2)}) async-start(), calls=%async_computation.15 | async-start | bytes 25600000 | tf_op jit(solution)/shard_map/reduce_scatter | solution.py:434
  2504.9 1357.1 %reduce-scatter.14.cloned.1.call-start = ((), (), s32[]{:S(2)}) async-start(), calls=%async_computation.16 | async-start | bytes 26624000 | tf_op jit(solution)/shard_map/reduce_scatter | solution.py:440
  2517.7 1608.5 %reduce-scatter.8.cloned.1.call-start = ((), (), s32[]{:S(2)}) async-start(), calls=%async_computation.13 | async-start | bytes 19456000 | tf_op jit(solution)/shard_map/reduce_scatter | solution.py:413
  2523.5 546.1 %copy-start.17 = (bf16[64,2,1600]{2,1,0:T(2,128)(2,1)S(1)}, bf16[64,2,1600]{2,1,0:T(2,128)(2,1)}, u32[]{:S(2)}) copy-start(bf16[64,2,1600]{2,1,0:T(2,128)(2,1)} %param.30) | copy-start | bytes 1228804
  2523.5 546.1 %copy-start.40 = (f32[1600]{0:T(1024)S(1)}, f32[1600]{0:T(1024)}, u32[]{:S(2)}) copy-start(f32[1600]{0:T(1024)} %copy-done.39) | copy-start | bytes 19204
  2523.5 546.1 %copy-start.44 = (f32[1600]{0:T(1024)S(1)}, f32[1600]{0:T(1024)}, u32[]{:S(2)}) copy-start(f32[1600]{0:T(1024)} %copy-done.43) | copy-start | bytes 19204
  2523.5 546.1 %copy-start.50 = (f32[64,2]{0,1:T(2,128)S(1)}, f32[64,2]{0,1:T(2,128)}, u32[]{:S(2)}) copy-start(f32[64,2]{0,1:T(2,128)} %copy-done.49) | copy-start | bytes 1540
  2523.5 546.1 %copy-start.53 = (f32[64,2]{0,1:T(2,128)S(1)}, f32[64,2]{0,1:T(2,128)}, u32[]{:S(2)}) copy-start(f32[64,2]{0,1:T(2,128)} %copy-done.52) | copy-start | bytes 1540
  3077.9 1261.4 %all-reduce.24.cloned.1.call-start = ((), (), s32[]{:S(2)}) async-start(), calls=%async_computation.17 | async-start | bytes 31334400 | tf_op jit(solution)/shard_map/psum | solution.py:450
  (101 other events, 373.8 us)
Sparse Core Ops, SparseCore 0:
  9.7 269.9 all-gather.7
  290.0 157.8 all-gather.9
  449.5 97.5 all-gather.11
  548.6 347.1 all-gather.13
  897.2 360.8 all-gather.15
  1261.5 99.2 all-gather.17
  1364.4 110.6 all-gather.19
  2488.2 577.5 reduce-scatter.5
  3068.7 94.0 reduce-scatter.9
  3165.1 340.1 reduce-scatter.11
  3507.8 354.1 reduce-scatter.13
  3864.4 261.8 reduce-scatter.7
  4130.2 209.0 all-reduce.23
where the time goes:
time: 4380 us; the launch traced here: 4360 us
  waiting for transfers between devices  2250 us (51%)
  local copies, waits for them, and re-layouts  1180 us (27%)
  other arithmetic  376 us (9%)
  blocking collectives  258 us (6%)
  matrix products  227 us (5%)
  loops' own time  51.2 us (1%)
    reduce_scatter x1, waiting for transfers between devices, local(): lax.psum_scatter(terms.reshape(total_rows, seq_count, model_width), ('ctx...  540 us
    reduce_scatter x1, waiting for transfers between devices, local(): lax.psum_scatter(grad_downward_weight.astype(jnp.bfloat16), 'fsdp', scatt...  357 us
    reduce_scatter x1, waiting for transfers between devices, local(): lax.psum_scatter(grad_upward_weight.astype(jnp.bfloat16), 'fsdp', scatter...  342 us
    reduce_scatter x1, waiting for transfers between devices, local(): lax.psum_scatter(grad_joint_weight.astype(jnp.bfloat16), 'fsdp', scatter_...  264 us
    all_gather x1, waiting for transfers between devices, local(): lax.all_gather(qkv_weight, 'fsdp', axis=0, tiled=True)  245 us
    gather x30, local copies, waits for them, and re-layouts, fetch_blocks(): taken = jnp.take(view, locations, axis=0)  215 us
    select_n x20, other arithmetic, fetch_blocks(): taken = jnp.take(view, locations, axis=0)  184 us
    while x115, local copies, waits for them, and re-layouts  173 us
  transfers between devices with their start and end apart: 13, of which 10 were waited for; matrix products, arithmetic and copies ran while one was open for 21% of the time, Pallas kernels for 0%

commit v1 on v0

v1 whole, which is shorter than its diff:
```python
import functools

import jax
import jax.numpy as jnp
from jax import lax
from jax.experimental import pallas as pl
from jax.experimental.pallas import tpu as pltpu
from jax.sharding import PartitionSpec as P

HD = 64
LANES = 128
NORM_EPS = 1e-05
NEG_BIG = -1e30
MESH = pl.DeviceIdType.MESH
F32 = jnp.float32
BF16 = jnp.bfloat16
ANY = pl.BlockSpec(memory_space=pl.ANY)
VMEM = pl.BlockSpec(memory_space=pltpu.VMEM)
DMA = pltpu.SemaphoreType.DMA
VMEM_LIMIT = 56 * 1024 * 1024


def params(cid=None):
    if cid is None:
        return pltpu.CompilerParams(vmem_limit_bytes=VMEM_LIMIT)
    return pltpu.CompilerParams(
        collective_id=cid, has_side_effects=True, vmem_limit_bytes=VMEM_LIMIT
    )


def plane_peers(chips):
    me = lax.axis_index("ctx")
    core = lax.rem(me, 2)
    chip = me // 2
    sibling = chip * 2 + 1 - core
    to = [lax.rem(chip + k, chips) * 2 + core for k in range(1, chips)]
    come = [lax.rem(chip + chips - k, chips) * 2 + core for k in range(1, chips)]
    return me, core, chip, sibling, to, come


def greet(axis, peers):
    barrier = pltpu.get_barrier_semaphore()
    for peer in peers:
        pl.semaphore_signal(barrier, inc=1, device_id={axis: peer}, device_id_type=MESH)
    pl.semaphore_wait(barrier, len(peers))


def send(src, dst, send_sem, recv_sem, axis, peer):
    copy = pltpu.make_async_remote_copy(
        src_ref=src,
        dst_ref=dst,
        send_sem=send_sem,
        recv_sem=recv_sem,
        device_id={axis: peer},
        device_id_type=MESH,
    )
    copy.start()
    return copy


def plane_gather(own_ref, all_ref, sems, chips):
    far_send, far_recv, near_send, near_recv, local_sem = sems
    me, core, chip, sibling, to, come = plane_peers(chips)
    far = [
        send(own_ref, all_ref.at[me], far_send.at[k], far_recv.at[k], "ctx", to[k])
        for k in range(chips - 1)
    ]
    near = [send(own_ref, all_ref.at[me], near_send.at[chips - 1], near_recv.at[chips - 1], "ctx", sibling)]
    local = pltpu.make_async_copy(own_ref, all_ref.at[me], local_sem)
    local.start()
    for k in range(chips - 1):
        far[k].wait_recv()
        block = all_ref.at[come[k]]
        near.append(send(block, block, near_send.at[k], near_recv.at[k], "ctx", sibling))
    for copy in far:
        copy.wait_send()
    for copy in near:
        copy.wait()
    local.wait()


def plane_scatter(part_ref, mine, paired, stage, arrived, sems, chips):
    far_send, far_recv, near_send, near_recv, local_sem = sems
    me, core, chip, sibling, to, come = plane_peers(chips)
    near, local = [None] * chips, [None] * chips
    order = list(range(1, chips)) + [0]
    for k in order:
        base = lax.rem(chip + k, chips) * 2
        near[k] = send(
            part_ref.at[base + 1 - core], paired.at[k], near_send.at[k], near_recv.at[k], "ctx", sibling
        )
        local[k] = pltpu.make_async_copy(part_ref.at[base + core], mine.at[k], local_sem.at[k])
        local[k].start()
    far = []
    for k in range(1, chips):
        local[k].wait()
        near[k].wait_recv()
        stage[k - 1] = (mine[k].astype(F32) + paired[k].astype(F32)).astype(BF16)
        far.append(
            send(stage.at[k - 1], arrived.at[k - 1], far_send.at[k - 1], far_recv.at[k - 1], "ctx", to[k - 1])
        )
    local[0].wait()
    near[0].wait_recv()
    total = mine[0].astype(F32) + paired[0].astype(F32)
    for k in range(chips - 1):
        far[k].wait_recv()
        total = total + arrived[k].astype(F32)
    for copy in far + near:
        copy.wait_send()
    return total


def gather_sems(chips):
    return [DMA((chips - 1,)), DMA((chips - 1,)), DMA((chips,)), DMA((chips,)), DMA]


def scatter_scratch(chips, rows, width):
    return [
        pltpu.VMEM((chips, rows, width), BF16),
        pltpu.VMEM((chips, rows, width), BF16),
        pltpu.VMEM((chips - 1, rows, width), BF16),
        pltpu.VMEM((chips - 1, rows, width), BF16),
        DMA((chips - 1,)),
        DMA((chips - 1,)),
        DMA((chips,)),
        DMA((chips,)),
        DMA((chips,)),
    ]


def normalize(values):
    average = jnp.mean(values, axis=-1, keepdims=True)
    centered = values - average
    variance = jnp.mean(centered * centered, axis=-1, keepdims=True)
    inverse = lax.rsqrt(variance + NORM_EPS)
    return centered * inverse, inverse


def norm_backward(grad, gain, unit, inverse):
    scaled = grad * gain
    first = jnp.mean(scaled, axis=-1, keepdims=True)
    second = jnp.mean(scaled * unit, axis=-1, keepdims=True)
    return (scaled - first - unit * second) * inverse


def first_kernel(chips, tok_ref, vec_ref, all_ref, own, *sems):
    me, core, chip, sibling, to, come = plane_peers(chips)
    unit, inverse = normalize(tok_ref[...].astype(F32))
    own[...] = (unit * vec_ref[0:1, :] + vec_ref[1:2, :]).astype(BF16)
    greet("ctx", to + [sibling])
    plane_gather(own, all_ref, sems, chips)


def first_norm_gather(tok, vecs, n_ctx):
    rows, width = tok.shape
    chips = n_ctx // 2
    return pl.pallas_call(
        functools.partial(first_kernel, chips),
        out_shape=jax.ShapeDtypeStruct((n_ctx, rows, width), BF16),
        in_specs=[VMEM, VMEM],
        out_specs=ANY,
        scratch_shapes=[pltpu.VMEM((rows, width), BF16)] + gather_sems(chips),
        compiler_params=params(0),
        name="norm_gather",
    )(tok, vecs)


def second_kernel(chips, part_ref, tok_ref, vec_ref, mixed_ref, all_ref, own, *scratch):
    me, core, chip, sibling, to, come = plane_peers(chips)
    greet("ctx", to + [sibling])
    total = plane_scatter(part_ref, *scratch[:4], scratch[4:9], chips)
    mixed = tok_ref[...].astype(F32) + total + vec_ref[2:3, :]
    mixed_ref[...] = mixed
    unit, inverse = normalize(mixed)
    own[...] = (unit * vec_ref[0:1, :] + vec_ref[1:2, :]).astype(BF16)
    plane_gather(own, all_ref, scratch[9:], chips)


def second_norm_gather(part, tok, vecs):
    n_ctx, rows, width = part.shape
    chips = n_ctx // 2
    return pl.pallas_call(
        functools.partial(second_kernel, chips),
        out_shape=(
            jax.ShapeDtypeStruct((rows, width), F32),
            jax.ShapeDtypeStruct((n_ctx, rows, width), BF16),
        ),
        in_specs=[ANY, VMEM, VMEM],
        out_specs=(VMEM, ANY),
        scratch_shapes=[pltpu.VMEM((rows, width), BF16)]
        + scatter_scratch(chips, rows, width)
        + gather_sems(chips),
        compiler_params=params(1),
        name="scatter_norm_gather",
    )(part, tok, vecs)


def third_kernel(chips, part_ref, mixed_ref, og_ref, vec_ref, dmixed_ref, sums_ref, all_ref, own, *scratch):
    me, core, chip, sibling, to, come = plane_peers(chips)
    greet("ctx", to + [sibling])
    unit, inverse = normalize(mixed_ref[...])
    grad = plane_scatter(part_ref, *scratch[:4], scratch[4:9], chips)
    out_grad = og_ref[...].astype(F32)
    dmixed = out_grad + norm_backward(grad, vec_ref[0:1, :], unit, inverse)
    dmixed_ref[...] = dmixed
    low = dmixed.astype(BF16)
    own[...] = low
    sums_ref[0:1, :] = jnp.sum(grad * unit, axis=0, keepdims=True)
    sums_ref[1:2, :] = jnp.sum(grad, axis=0, keepdims=True)
    sums_ref[2:3, :] = jnp.sum(low.astype(F32), axis=0, keepdims=True)
    sums_ref[3:4, :] = jnp.sum(out_grad, axis=0, keepdims=True)
    plane_gather(own, all_ref, scratch[9:], chips)


def second_norm_back(part, mixed, og, vecs):
    n_ctx, rows, width = part.shape
    chips = n_ctx // 2
    return pl.pallas_call(
        functools.partial(third_kernel, chips),
        out_shape=(
            jax.ShapeDtypeStruct((rows, width), F32),
            jax.ShapeDtypeStruct((4, width), F32),
            jax.ShapeDtypeStruct((n_ctx, rows, width), BF16),
        ),
        in_specs=[ANY, VMEM, VMEM, VMEM],
        out_specs=(VMEM, VMEM, ANY),
        scratch_shapes=[pltpu.VMEM((rows, width), BF16)]
        + scatter_scratch(chips, rows, width)
        + gather_sems(chips),
        compiler_params=params(2),
        name="scatter_back_gather",
    )(part, mixed, og, vecs)


def fourth_kernel(chips, part_ref, tok_ref, dmixed_ref, vec_ref, grad_ref, sums_ref, *scratch):
    me, core, chip, sibling, to, come = plane_peers(chips)
    greet("ctx", to + [sibling])
    unit, inverse = normalize(tok_ref[...].astype(F32))
    grad = plane_scatter(part_ref, *scratch[:4], scratch[4:9], chips)
    grad_ref[...] = dmixed_ref[...] + norm_backward(grad, vec_ref[0:1, :], unit, inverse)
    sums_ref[0:1, :] = jnp.sum(grad * unit, axis=0, keepdims=True)
    sums_ref[1:2, :] = jnp.sum(grad, axis=0, keepdims=True)


def first_norm_back(part, tok, dmixed, vecs):
    n_ctx, rows, width = part.shape
    chips = n_ctx // 2
    return pl.pallas_call(
        functools.partial(fourth_kernel, chips),
        out_shape=(
            jax.ShapeDtypeStruct((rows, width), F32),
            jax.ShapeDtypeStruct((2, width), F32),
        ),
        in_specs=[ANY, VMEM, VMEM, VMEM],
        out_specs=(VMEM, VMEM),
        scratch_shapes=scatter_scratch(chips, rows, width),
        compiler_params=params(3),
        name="scatter_back",
    )(part, tok, dmixed, vecs)


def out_kernel(chips, part_ref, mixed_ref, vec_ref, out_ref, *scratch):
    me, core, chip, sibling, to, come = plane_peers(chips)
    greet("ctx", to + [sibling])
    total = plane_scatter(part_ref, *scratch[:4], scratch[4:9], chips)
    out_ref[...] = (mixed_ref[...] + total + vec_ref[0:1, :]).astype(BF16)


def block_result(part, mixed, vecs):
    n_ctx, rows, width = part.shape
    chips = n_ctx // 2
    return pl.pallas_call(
        functools.partial(out_kernel, chips),
        out_shape=jax.ShapeDtypeStruct((rows, width), BF16),
        in_specs=[ANY, VMEM, VMEM],
        out_specs=VMEM,
        scratch_shapes=scatter_scratch(chips, rows, width),
        compiler_params=params(4),
        name="scatter_out",
    )(part, mixed, vecs)


def to_heads_kernel(kinds, planes, seqs, tok_ref, head_ref, send_sems, recv_sems, local_sems):
    me = lax.axis_index("fsdp")
    pairs = planes // seqs
    greet("fsdp", [lax.rem(me + k, planes) for k in range(1, planes)])
    width = tok_ref.shape[3] // kinds

    def source(kind, unit):
        start = pl.multiple_of(kind * width + lax.rem(unit, pairs) * LANES, LANES)
        return tok_ref.at[:, unit // pairs, :, pl.ds(start, LANES)]

    copies = []
    for k in range(1, planes):
        unit = lax.rem(me + k, planes)
        for kind in range(kinds):
            copies.append(
                send(
                    source(kind, unit),
                    head_ref.at[kind, :, me],
                    send_sems.at[kind, k - 1],
                    recv_sems.at[kind, k - 1],
                    "fsdp",
                    unit,
                )
            )
    local = []
    for kind in range(kinds):
        copy = pltpu.make_async_copy(source(kind, me), head_ref.at[kind, :, me], local_sems.at[kind])
        copy.start()
        local.append(copy)
    for copy in copies + local:
        copy.wait()


def to_heads(tok, kinds, planes, cid):
    n_ctx, seqs, rows, width = tok.shape
    return pl.pallas_call(
        functools.partial(to_heads_kernel, kinds, planes, seqs),
        out_shape=jax.ShapeDtypeStruct((kinds, n_ctx, planes, rows, LANES), tok.dtype),
        in_specs=[ANY],
        out_specs=ANY,
        scratch_shapes=[DMA((kinds, planes - 1)), DMA((kinds, planes - 1)), DMA((kinds,))],
        compiler_params=params(cid),
        name="to_heads",
    )(tok)


def to_tokens_kernel(kinds, planes, seqs, head_ref, tok_ref, send_sems, recv_sems, local_sems):
    me = lax.axis_index("fsdp")
    pairs = planes // seqs
    greet("fsdp", [lax.rem(me + k, planes) for k in range(1, planes)])
    width = tok_ref.shape[3] // kinds

    def target(kind):
        start = pl.multiple_of(kind * width + lax.rem(me, pairs) * LANES, LANES)
        return tok_ref.at[:, me // pairs, :, pl.ds(start, LANES)]

    copies = []
    for k in range(1, planes):
        peer = lax.rem(me + k, planes)
        for kind in range(kinds):
            copies.append(
                send(
                    head_ref.at[kind, :, peer],
                    target(kind),
                    send_sems.at[kind, k - 1],
                    recv_sems.at[kind, k - 1],
                    "fsdp",
                    peer,
                )
            )
    local = []
    for kind in range(kinds):
        copy = pltpu.make_async_copy(head_ref.at[kind, :, me], target(kind), local_sems.at[kind])
        copy.start()
        local.append(copy)
    for copy in copies + local:
        copy.wait()


def to_tokens(heads, seqs, cid):
    kinds, n_ctx, planes, rows, lanes = heads.shape
    width = kinds * (planes // seqs) * LANES
    return pl.pallas_call(
        functools.partial(to_tokens_kernel, kinds, planes, seqs),
        out_shape=jax.ShapeDtypeStruct((n_ctx, seqs, rows, width), heads.dtype),
        in_specs=[ANY],
        out_specs=ANY,
        scratch_shapes=[DMA((kinds, planes - 1)), DMA((kinds, planes - 1)), DMA((kinds,))],
        compiler_params=params(cid),
        name="to_tokens",
    )(heads)


def nt(left, right):
    return lax.dot_general(left, right, (((1,), (1,)), ((), ())), preferred_element_type=F32)


def nn(left, right):
    return lax.dot_general(left, right, (((1,), (0,)), ((), ())), preferred_element_type=F32)


def sort_blocks(order_ref, source_refs, sorted_refs, blocks, half):
    def body(block, carry):
        place = order_ref[block]
        start = pl.multiple_of(block * half, half)
        for source, target in zip(source_refs, sorted_refs):
            target[pl.ds(start, half), :] = source[place]
        return carry

    lax.fori_loop(0, blocks, body, 0)


def lane_mask(rows, head):
    lane = lax.broadcasted_iota(jnp.int32, (rows, LANES), 1)
    return (lane < HD) if head == 0 else (lane >= HD)


def forward_kernel(tile, order_ref, qkv_ref, out_ref, att_ref, lse_ref, q_s, k_s, v_s, vt_s, o_s):
    blocks, half = out_ref.shape[0], out_ref.shape[1]
    length = blocks * half
    tiles = length // tile
    sort_blocks(order_ref, [qkv_ref.at[0], qkv_ref.at[1], qkv_ref.at[2]], [q_s, k_s, v_s], blocks, half)
    for t in range(tiles):
        span = slice(t * tile, (t + 1) * tile)
        vt_s[:, span] = v_s[span, :].T
    scale = HD ** (-0.5)
    rows_iota = lax.broadcasted_iota(jnp.int32, (tile, tile), 0)
    cols_iota = lax.broadcasted_iota(jnp.int32, (tile, tile), 1)
    allowed = rows_iota <= cols_iota
    masks = [lane_mask(tile, head) for head in range(2)]

    for qt in range(tiles):
        q_span = slice(qt * tile, (qt + 1) * tile)
        query = q_s[q_span, :] * jnp.asarray(scale, BF16)
        queries = [jnp.where(masks[head], query, jnp.zeros_like(query)) for head in range(2)]

        def step(kt, state, masked, queries=queries):
            start = pl.multiple_of(kt * tile, tile)
            keys = k_s[pl.ds(start, tile), :]
            new = []
            for head in range(2):
                top, total, acc = state[head]
                scores = nt(keys, queries[head])
                if masked:
                    scores = jnp.where(allowed, scores, NEG_BIG)
                new_top = jnp.maximum(top, jnp.max(scores, axis=0, keepdims=True))
                soft = jnp.exp(scores - new_top)
                factor = jnp.exp(top - new_top)
                total = total * factor + jnp.sum(soft, axis=0, keepdims=True)
                values = vt_s[head * HD : (head + 1) * HD, pl.ds(start, tile)]
                acc = acc * factor + nn(values, soft.astype(BF16))
                new.append((new_top, total, acc))
            return tuple(new)

        state = tuple(
            (jnp.full((1, tile), NEG_BIG, F32), jnp.zeros((1, tile), F32), jnp.zeros((HD, tile), F32))
            for head in range(2)
        )
        state = step(qt, state, True)
        if qt > 0:
            state = lax.fori_loop(0, qt, lambda kt, s, step=step: step(kt, s, False), state)
        for head in range(2):
            top, total, acc = state[head]
            att_ref[head * HD : (head + 1) * HD, q_span] = acc / total
            lse_ref[head : head + 1, q_span] = top + jnp.log(total)
        o_s[q_span, :] = att_ref[:, q_span].T.astype(BF16)

    def body(block, carry):
        start = pl.multiple_of(block * half, half)
        out_ref[order_ref[block]] = o_s[pl.ds(start, half), :]
        return carry

    lax.fori_loop(0, blocks, body, 0)


SMEM = pl.BlockSpec(memory_space=pltpu.SMEM)


def attend_forward(order, qkv, tile):
    kinds, blocks, half, lanes = qkv.shape
    length = blocks * half
    return pl.pallas_call(
        functools.partial(forward_kernel, tile),
        out_shape=(
            jax.ShapeDtypeStruct((blocks, half, LANES), BF16),
            jax.ShapeDtypeStruct((LANES, length), F32),
            jax.ShapeDtypeStruct((2, length), F32),
        ),
        in_specs=[SMEM, VMEM],
        out_specs=(VMEM, VMEM, VMEM),
        scratch_shapes=[
            pltpu.VMEM((length, LANES), BF16),
            pltpu.VMEM((length, LANES), BF16),
            pltpu.VMEM((length, LANES), BF16),
            pltpu.VMEM((LANES, length), BF16),
            pltpu.VMEM((length, LANES), BF16),
        ],
        compiler_params=params(),
        name="attend_forward",
    )(order, qkv)


def backward_kernel(
    tile, order_ref, qkv_ref, grad_ref, att_ref, lse_ref, out_ref, q_s, k_s, v_s, g_s, kt_s, dq_s, dk_s, dv_s
):
    blocks, half = grad_ref.shape[0], grad_ref.shape[1]
    length = blocks * half
    tiles = length // tile
    sort_blocks(
        order_ref,
        [qkv_ref.at[0], qkv_ref.at[1], qkv_ref.at[2], grad_ref],
        [q_s, k_s, v_s, g_s],
        blocks,
        half,
    )
    for t in range(tiles):
        span = slice(t * tile, (t + 1) * tile)
        kt_s[:, span] = k_s[span, :].T
    scale = HD ** (-0.5)
    rows_iota = lax.broadcasted_iota(jnp.int32, (tile, tile), 0)
    cols_iota = lax.broadcasted_iota(jnp.int32, (tile, tile), 1)
    allowed = rows_iota <= cols_iota
    masks = [lane_mask(tile, head) for head in range(2)]
    dk_s[...] = jnp.zeros_like(dk_s)
    dv_s[...] = jnp.zeros_like(dv_s)

    for qt in range(tiles):
        q_span = slice(qt * tile, (qt + 1) * tile)
        query = q_s[q_span, :] * jnp.asarray(scale, BF16)
        grad = g_s[q_span, :]
        queries = [jnp.where(masks[head], query, jnp.zeros_like(query)) for head in range(2)]
        grads = [jnp.where(masks[head], grad, jnp.zeros_like(grad)) for head in range(2)]
        product = grad.astype(F32).T * att_ref[:, q_span]
        dots = [jnp.sum(product[head * HD : (head + 1) * HD], axis=0, keepdims=True) for head in range(2)]
        totals = [lse_ref[head : head + 1, q_span] for head in range(2)]

        def step(kt, state, masked, queries=queries, grads=grads, dots=dots, totals=totals):
            start = pl.multiple_of(kt * tile, tile)
            rows = pl.ds(start, tile)
            keys = k_s[rows, :]
            values = v_s[rows, :]
            dk = dk_s[rows, :]
            dv = dv_s[rows, :]
            new = []
            for head in range(2):
                scores = nt(keys, queries[head])
                if masked:
                    scores = jnp.where(allowed, scores, NEG_BIG)
                soft = jnp.exp(scores - totals[head])
                dsoft = nt(values, grads[head])
                dscore = (soft * (dsoft - dots[head])).astype(BF16)
                dv = dv + nn(soft.astype(BF16), grads[head])
                dk = dk + nn(dscore, queries[head])
                new.append(state[head] + nn(kt_s[head * HD : (head + 1) * HD, rows], dscore))
            dk_s[rows, :] = dk
            dv_s[rows, :] = dv
            return tuple(new)

        state = (jnp.zeros((HD, tile), F32), jnp.zeros((HD, tile), F32))
        state = step(qt, state, True)
        if qt > 0:
            state = lax.fori_loop(0, qt, lambda kt, s, step=step: step(kt, s, False), state)
        dq = jnp.concatenate(state, axis=0) * scale
        dq_s[q_span, :] = dq.T.astype(BF16)

    def body(block, carry):
        start = pl.multiple_of(block * half, half)
        place = order_ref[block]
        out_ref[0, place] = dq_s[pl.ds(start, half), :]
        out_ref[1, place] = dk_s[pl.ds(start, half), :].astype(BF16)
        out_ref[2, place] = dv_s[pl.ds(start, half), :].astype(BF16)
        return carry

    lax.fori_loop(0, blocks, body, 0)


def attend_backward(order, qkv, grad, att, lse, tile):
    kinds, blocks, half, lanes = qkv.shape
    length = blocks * half
    return pl.pallas_call(
        functools.partial(backward_kernel, tile),
        out_shape=jax.ShapeDtypeStruct((3, blocks, half, LANES), BF16),
        in_specs=[SMEM, VMEM, VMEM, VMEM, VMEM],
        out_specs=VMEM,
        scratch_shapes=[pltpu.VMEM((length, LANES), BF16)] * 4
        + [pltpu.VMEM((LANES, length), BF16), pltpu.VMEM((length, LANES), BF16)]
        + [pltpu.VMEM((length, LANES), F32)] * 2,
        compiler_params=params(),
        name="attend_backward",
    )(order, qkv, grad, att, lse)


def mm(left, right):
    return jnp.matmul(left, right, preferred_element_type=F32)


def mm_nt(left, right):
    return lax.dot_general(left, right, (((1,), (1,)), ((), ())), preferred_element_type=F32)


def mm_tn(left, right):
    return lax.dot_general(left, right, (((0,), (0,)), ((), ())), preferred_element_type=F32)


def gelu_tanh(values):
    return jax.nn.gelu(values, approximate=True)


def local(
    tokens,
    block_pairs,
    out_grad,
    ln1_gain,
    ln1_bias,
    qkv_weight,
    query_bias,
    value_bias,
    out_weight,
    out_bias,
    ln2_gain,
    ln2_bias,
    up_weight,
    up_bias,
    down_weight,
    down_bias,
):
    n_ctx, planes = lax.axis_size("ctx"), lax.axis_size("fsdp")
    c, f = lax.axis_index("ctx"), lax.axis_index("fsdp")
    local_rows, seqs, width = tokens.shape
    half = local_rows // 2
    devices = n_ctx * planes
    blocks = 2 * devices
    length = devices * local_rows
    heads = width // HD
    slots = planes * (-(-heads // devices))
    assert slots == planes and planes % seqs == 0
    span = slots * HD
    rows = local_rows * seqs
    plane_rows = n_ctx * rows
    quarter = width // planes
    ff = up_weight.shape[1]
    ff_quarter = ff // planes
    ff_piece = ff_quarter // n_ctx
    ff_span = ff_piece * planes
    tile = 256

    device_ids = jnp.arange(devices, dtype=jnp.int32)
    device_of_block = jnp.sum(
        jnp.where(block_pairs[None, :] == device_ids[:, None], device_ids[None, :], 0), axis=1
    )
    order = jnp.concatenate([device_of_block * 2, device_of_block[::-1] * 2 + 1]).astype(jnp.int32)

    qkv_padded = jnp.pad(qkv_weight, ((0, 0), (0, n_ctx * span - width)))
    qkv_own = jnp.concatenate(
        [lax.dynamic_slice(qkv_padded, (0, k * width + c * span), (quarter, span)) for k in range(3)], axis=1
    )
    qkv_slice = lax.all_gather(qkv_own, "fsdp", axis=0, tiled=True)
    out_padded = jnp.pad(out_weight, ((span, span), (0, 0)))
    out_start = jnp.clip(c * span - f * quarter + span, 0, quarter + span)
    out_slice = lax.psum(lax.dynamic_slice(out_padded, (out_start, 0), (span, width)), "fsdp")
    up_own = jnp.concatenate(
        [
            lax.dynamic_slice(up_weight, (0, k * ff_quarter + c * ff_piece), (quarter, ff_piece))
            for k in range(planes)
        ],
        axis=1,
    )
    up_slice = lax.all_gather(up_own, "fsdp", axis=0, tiled=True)
    down_own = lax.dynamic_slice(down_weight, (c * ff_piece, 0), (ff_piece, width))
    down_slice = lax.all_gather(down_own, "fsdp", axis=0, tiled=True)

    packed = jnp.concatenate(
        [
            jnp.stack([ln1_gain, ln1_bias, ln2_gain, ln2_bias, query_bias, value_bias, out_bias, down_bias]),
            up_bias.reshape(ff // width, quarter),
        ]
    )
    vectors = lax.all_gather(packed, "fsdp", axis=0).astype(F32)
    gain1, bias1, gain2, bias2, bias_q, bias_v, bias_o, bias_d = [
        vectors[:, k].reshape(width) for k in range(8)
    ]
    bias_up = lax.dynamic_slice(
        vectors[:, 8:].reshape(planes, ff_quarter), (0, c * ff_piece), (planes, ff_piece)
    ).reshape(ff_span)

    def head_part(vector):
        return lax.dynamic_slice(jnp.pad(vector, (0, n_ctx * span - width)), (c * span,), (span,))

    qkv_shift = jnp.concatenate([head_part(bias_q), jnp.zeros((span,), F32), head_part(bias_v)])

    tok = jnp.swapaxes(tokens, 0, 1).reshape(rows, width)
    og = jnp.swapaxes(out_grad, 0, 1).reshape(rows, width)
    og_all = lax.all_gather(og, "ctx", axis=0, tiled=True)

    h1 = first_norm_gather(tok, jnp.stack([gain1, bias1]), n_ctx).reshape(plane_rows, width)
    qkv = (mm(h1, qkv_slice) + qkv_shift).astype(BF16)
    qkv_heads = to_heads(qkv.reshape(n_ctx, seqs, local_rows, 3 * span), 3, planes, 5)
    qkv_heads = qkv_heads.reshape(3, blocks, half, LANES)
    att_heads, att_exact, lse = attend_forward(order, qkv_heads, tile)
    att = to_tokens(att_heads.reshape(1, n_ctx, planes, local_rows, LANES), seqs, 6).reshape(plane_rows, span)
    branch = mm(att, out_slice).astype(BF16).reshape(n_ctx, rows, width)
    mixed, h2 = second_norm_gather(branch, tok, jnp.stack([gain2, bias2, bias_o]))
    h2 = h2.reshape(plane_rows, width)
    up = mm(h2, up_slice) + bias_up
    activated, gelu_back = jax.vjp(gelu_tanh, up)
    act = activated.astype(BF16)
    out_part = mm(act, down_slice).astype(BF16).reshape(n_ctx, rows, width)

    (d_up,) = gelu_back(mm_nt(og_all, down_slice))
    d_up_low = d_up.astype(BF16)
    d_h2 = mm_nt(d_up_low, up_slice).astype(BF16).reshape(n_ctx, rows, width)
    d_mixed, sums2, d_branch = second_norm_back(d_h2, mixed, og, gain2[None, :])
    d_branch = d_branch.reshape(plane_rows, width)
    d_att = mm_nt(d_branch, out_slice).astype(BF16)
    d_att_heads = to_heads(d_att.reshape(n_ctx, seqs, local_rows, span), 1, planes, 7)
    d_heads = attend_backward(order, qkv_heads, d_att_heads.reshape(blocks, half, LANES), att_exact, lse, tile)
    d_qkv = to_tokens(d_heads.reshape(3, n_ctx, planes, local_rows, LANES), seqs, 8)
    d_qkv = d_qkv.reshape(plane_rows, 3 * span)
    d_h1 = mm_nt(d_qkv, qkv_slice).astype(BF16).reshape(n_ctx, rows, width)
    block_out = block_result(out_part, mixed, bias_d[None, :])
    grad_tok, sums1 = first_norm_back(d_h1, tok, d_mixed, gain1[None, :])

    def reduce_own(part):
        return lax.psum_scatter(part.astype(BF16), "fsdp", scatter_dimension=0, tiled=True)

    down_grad = lax.all_gather(reduce_own(mm_tn(act, og_all)), "ctx", axis=0, tiled=True).astype(F32)
    up_parts = lax.all_gather(reduce_own(mm_tn(h2, d_up_low)), "ctx", axis=0)
    up_grad = (
        up_parts.reshape(n_ctx, quarter, planes, ff_piece).transpose(1, 2, 0, 3).reshape(quarter, ff).astype(F32)
    )
    out_parts = lax.all_gather(reduce_own(mm_tn(att, d_branch)), ("ctx", "fsdp"), axis=0, tiled=True)
    out_grad_own = lax.dynamic_slice(out_parts, (f * quarter, 0), (quarter, width)).astype(F32)
    qkv_parts = lax.all_gather(reduce_own(mm_tn(h1, d_qkv)), "ctx", axis=0)
    qkv_grad = jnp.concatenate(
        [
            qkv_parts[:, :, k * span : (k + 1) * span].transpose(1, 0, 2).reshape(quarter, n_ctx * span)[:, :width]
            for k in range(3)
        ],
        axis=1,
    ).astype(F32)

    def spread(values, count):
        return lax.dynamic_update_slice(jnp.zeros((n_ctx * count,), F32), values, (c * count,))

    d_qkv_sum = jnp.sum(d_qkv.astype(F32), axis=0)
    d_up_sum = jnp.sum(d_up_low.astype(F32), axis=0).reshape(planes, ff_piece)
    up_spread = lax.dynamic_update_slice(jnp.zeros((planes, ff_quarter), F32), d_up_sum, (0, c * ff_piece))
    wide = jnp.concatenate([sums1, sums2])
    total_wide, total_q, total_v, total_up = lax.psum(
        (wide, spread(d_qkv_sum[:span], span), spread(d_qkv_sum[2 * span :], span), up_spread), ("ctx", "fsdp")
    )

    def own(vector):
        return lax.dynamic_slice(vector, (f * quarter,), (quarter,))

    up_bias_grad = lax.dynamic_slice(total_up, (f, 0), (1, ff_quarter)).reshape(ff_quarter)

    def back(values):
        return jnp.swapaxes(values.reshape(seqs, local_rows, width), 0, 1)

    return (
        back(block_out),
        back(grad_tok),
        own(total_wide[0]),
        own(total_wide[1]),
        qkv_grad,
        own(total_q),
        own(total_v),
        out_grad_own,
        own(total_wide[4]),
        own(total_wide[2]),
        own(total_wide[3]),
        up_grad,
        up_bias_grad,
        down_grad,
        own(total_wide[5]),
    )


def solution(mesh):
    both, row, vec, mat = P(("ctx", "fsdp"), None, None), P(), P("fsdp"), P("fsdp", None)
    in_specs = (both, row, both, vec, vec, mat, vec, vec, mat, vec, vec, vec, mat, vec, mat, vec)
    out_specs = (both, both, vec, vec, mat, vec, vec, mat, vec, vec, vec, mat, vec, mat, vec)
    return jax.shard_map(local, mesh=mesh, in_specs=in_specs, out_specs=out_specs, check_vma=False)
```

time: 4380 us -> 1000 us (0.23)
  waiting for transfers between devices: 2250 us -> 412 us
  local copies, waits for them, and re-layouts: 1180 us -> 111 us
  other arithmetic: 376 us -> 21.9 us
  Pallas kernels: 0 us -> 349 us
  blocking collectives: 258 us -> 15.5 us
  matrix products: 227 us -> 70.3 us
  loops' own time: 51.2 us -> 0 us
    reduce_scatter x5 -> x3, waiting for transfers between devices: 1590 us -> 81.1 us  [reduce_own(): lax.psum_scatter(part.astype(BF16), 'fsdp', scatter_dimension=0, tiled=True)]
    reshape x34 -> x8, local copies, waits for them, and re-layouts: 400 us -> 4.64 us  [the longest x2 3.76 us: back(): return jnp.swapaxes(values.reshape(seqs, local_rows, width), 0, 1)]
    pallas_call x0 -> x11, Pallas kernels: none -> 349 us  [the longest x2 59.6 us: to_tokens(): pl.pallas_call(functools.partial(to_tokens_kernel, kinds, planes, seqs),...]
    all_gather x7 -> x8, waiting for transfers between devices: 527 us -> 185 us  [the longest x1 52.8 us: local(): lax.all_gather(reduce_own(mm_tn(att, d_branch)), ('ctx', 'fsdp'), axis=0,...]
    while x124 -> x0, local copies, waits for them, and re-layouts: 334 us -> none
    gather x46 -> x0, local copies, waits for them, and re-layouts: 226 us -> none  [the longest x30 215 us: fetch_blocks(): taken = jnp.take(view, locations, axis=0)]
    select_n x36 -> x0, other arithmetic: 184 us -> none  [the longest x20 184 us: fetch_blocks(): taken = jnp.take(view, locations, axis=0)]
    all_gather x2 -> x1, blocking collectives: 192 us -> 15.5 us  [local(): vectors = lax.all_gather(packed, 'fsdp', axis=0).astype(F32)]
  transfers between devices with their start and end apart: 13 -> 14, of which waited for: 10 -> 10; matrix products, arithmetic and copies ran while one was open for 21% -> 17% of each run, Pallas kernels for 0% -> 23%
where the time goes in v1:
time: 1000 us; the launch traced here: 996 us
  waiting for transfers between devices  412 us (41%)
  Pallas kernels  349 us (35%)
  local copies, waits for them, and re-layouts  111 us (11%)
  matrix products  70.3 us (7%)
  other arithmetic  21.9 us (2%)
  blocking collectives  15.5 us (2%)
  between operations  14.9 us (1%)
    psum x1, waiting for transfers between devices, local(): lax.psum((wide, spread(d_qkv_sum[:span], span), spread(d_qkv_sum[2 * span...  89.9 us
    reduce_scatter x3, waiting for transfers between devices, reduce_own(): lax.psum_scatter(part.astype(BF16), 'fsdp', scatter_dimension=0, tiled=True)  81.1 us
    pallas_call x2, Pallas kernels, to_tokens(): pl.pallas_call(functools.partial(to_tokens_kernel, kinds, planes, seqs),...  59.6 us
    pallas_call x2, Pallas kernels, to_heads(): pl.pallas_call(functools.partial(to_heads_kernel, kinds, planes, seqs), o...  56.3 us
    unnamed x15, waiting for transfers between devices  56.1 us
    all_gather x1, waiting for transfers between devices, local(): lax.all_gather(reduce_own(mm_tn(att, d_branch)), ('ctx', 'fsdp'), axis=0,...  52.8 us
    pallas_call x1, Pallas kernels, second_norm_back(): pl.pallas_call(functools.partial(third_kernel, chips), out_shape=(jax.Sha...  50.8 us
    pallas_call x1, Pallas kernels, second_norm_gather(): pl.pallas_call(functools.partial(second_kernel, chips), out_shape=(jax.Sh...  50.2 us
  transfers between devices with their start and end apart: 14, of which 10 were waited for; matrix products, arithmetic and copies ran while one was open for 17% of the time, Pallas kernels for 23%

profile of v1, /device:TPU:0, one launch (start us, length us, event | category | flops | bytes accessed | tf_op | source)
XLA Modules:
  0.0 995.9 jit_solution(3105555034040479233)
XLA Ops:
  17.5 15.5 %all-gather.3 = bf16[4,12,400]{2,1,0:T(8,128)(2,1)S(1)} all-gather(bf16[1,12,400]{2,1,0:T(8,128)(2,1)S(1)} %bitcast.122), channel_id=2, replica_groups=mesh['ctx'=8,'fsdp'=4] {'fsdp'}, dimensions={0}, use_global_device_ids=true | all-gather | bytes 48000 | tf_op jit(solution)/shard_map/all_gather | solution.py:660
  35.8 25.1 %norm_gather.1 = bf16[8,128,1600]{2,1,0:T(8,128)(2,1)} custom-call(bf16[128,1600]{1,0:T(8,128)(2,1)} %bitcast.96, f32[2,1600]{1,0:T(2,128)} %pad_maximum_fusion.4.vec_ref), custom_call_target="tpu_custom_call" | custom-call | tf_op jit(solution)/shard_map/norm_gather/pallas_call | solution.py:157
  65.8 6.9 add_convert_fusion
  72.7 42.6 %to_heads.2 = bf16[3,8,4,64,128]{4,3,2,1,0:T(8,128)(2,1)} custom-call(bf16[8,2,64,768]{3,2,1,0:T(8,128)(2,1)} %bitcast.114), custom_call_target="tpu_custom_call" | custom-call | tf_op jit(solution)/shard_map/to_heads/pallas_call | solution.py:318
  115.3 28.4 %attend_forward.1 = (bf16[64,32,128]{2,1,0:T(8,128)(2,1)}, f32[128,2048]{1,0:T(8,128)}, f32[2,2048]{1,0:T(2,128)}) custom-call(s32[64]{0:T(128)} %pad_add_fusion.order_ref, bf16[3,64,32,128]{3,2,1,0:T(8,128)(2,1)} %bitcast.90), custom_call_target="tpu_custom_call" | custom-call | tf_op jit(solution)/shard_map/attend_forward/pallas_call | solution.py:464
  143.8 27.4 %to_tokens.2 = bf16[8,2,64,256]{3,2,1,0:T(8,128)(2,1)} custom-call(bf16[1,8,4,64,128]{4,3,2,1,0:T(8,128)(2,1)} %bitcast.117), custom_call_target="tpu_custom_call" | custom-call | tf_op jit(solution)/shard_map/to_tokens/pallas_call | solution.py:365
  177.3 50.2 %scatter_norm_gather.1 = (f32[128,1600]{1,0:T(8,128)}, bf16[8,128,1600]{2,1,0:T(8,128)(2,1)}) custom-call(bf16[8,128,1600]{2,1,0:T(8,128)(2,1)} %bitcast.92, bf16[128,1600]{1,0:T(8,128)(2,1)} %bitcast.97, f32[3,1600]{1,0:T(4,128)} %pad_maximum_fusion.3.vec_ref), custom_call_target="tpu_custom_call" | custom-call | tf_op jit(solution)/shard_map/scatter_norm_gather/pallas_call | solution.py:182
  233.5 33.8 %all-gather.17.cloned.1.call-done = bf16[800,1600]{1,0:T(8,128)(2,1)} async-done(((bf16[200,1600]{1,0:T(8,128)(2,1)}), bf16[800,1600]{1,0:T(8,128)(2,1)}) %all-gather.17.cloned.1.call-update) | async-done | bytes 2560016 | tf_op jit(solution)/shard_map/all_gather | solution.py:652
  267.4 34.1 %all-gather.19.cloned.1.call-done = bf16[1024,1600]{1,0:T(8,128)(2,1)} async-done(((bf16[128,1600]{1,0:T(8,128)(2,1)}), bf16[1024,1600]{1,0:T(8,128)(2,1)}) %all-gather.19.cloned.1.call-update) | async-done | bytes 3276816 | tf_op jit(solution)/shard_map/all_gather | solution.py:675
  301.5 7.2 convert_reduce_fusion
  319.4 50.8 %scatter_back_gather.1 = (f32[128,1600]{1,0:T(8,128)}, f32[4,1600]{1,0:T(4,128)}, bf16[8,128,1600]{2,1,0:T(8,128)(2,1)}) custom-call(bf16[8,128,1600]{2,1,0:T(8,128)(2,1)} %bitcast.94, f32[128,1600]{1,0:T(8,128)} %get-tuple-element.27.mixed_ref, bf16[128,1600]{1,0:T(8,128)(2,1)} %bitcast.107, f32[1,1600]{1,0:T(1,128)} %copy-done.9), custom_call_target="tpu_custom_call" | custom-call | tf_op jit(solution)/shard_map/scatter_back_gather/pallas_call | solution.py:218
  374.0 13.7 %to_heads.3 = bf16[1,8,4,64,128]{4,3,2,1,0:T(8,128)(2,1)} custom-call(bf16[8,2,64,256]{3,2,1,0:T(8,128)(2,1)} %bitcast.118), custom_call_target="tpu_custom_call" | custom-call | tf_op jit(solution)/shard_map/to_heads/pallas_call | solution.py:318
  387.8 26.5 %attend_backward.1 = bf16[3,64,32,128]{3,2,1,0:T(8,128)(2,1)} custom-call(s32[64]{0:T(128)} %pad_add_fusion.order_ref, bf16[3,64,32,128]{3,2,1,0:T(8,128)(2,1)} %bitcast.91, bf16[64,32,128]{2,1,0:T(8,128)(2,1)} %bitcast.112, f32[128,2048]{1,0:T(8,128)} %get-tuple-element.29.att_ref, f32[2,2048]{1,0:T(2,128)} %get-tuple-element.30.lse_ref), custom_call_target="tpu_custom_call" | custom-call | tf_op jit(solution)/shard_map/attend_backward/pallas_call | solution.py:562
  414.3 32.3 %to_tokens.3 = bf16[8,2,64,768]{3,2,1,0:T(8,128)(2,1)} custom-call(bf16[3,8,4,64,128]{4,3,2,1,0:T(8,128)(2,1)} %bitcast.101), custom_call_target="tpu_custom_call" | custom-call | tf_op jit(solution)/shard_map/to_tokens/pallas_call | solution.py:365
  452.4 7.0 convolution_convert_fusion.4
  459.5 8.4 convolution_convert_fusion.5
  483.8 26.3 %scatter_back.1 = (f32[128,1600]{1,0:T(8,128)}, f32[2,1600]{1,0:T(2,128)}) custom-call(bf16[8,128,1600]{2,1,0:T(8,128)(2,1)} %bitcast.93, bf16[128,1600]{1,0:T(8,128)(2,1)} %bitcast.98, f32[128,1600]{1,0:T(8,128)} %get-tuple-element.31.dmixed_ref, f32[1,1600]{1,0:T(1,128)} %copy-done.10), custom_call_target="tpu_custom_call" | custom-call | tf_op jit(solution)/shard_map/scatter_back/pallas_call | solution.py:248
  513.0 53.7 %reduce-scatter.13.cloned.1.call-done = bf16[400,800]{1,0:T(8,128)(2,1)} async-done(((bf16[1600,800]{1,0:T(8,128)(2,1)}), bf16[400,800]{1,0:T(8,128)(2,1)}) %reduce-scatter.13.cloned.1.call-update) | async-done | bytes 640016 | tf_op jit(solution)/shard_map/reduce_scatter | solution.py:706
  566.8 55.2 %reduce-scatter.15.cloned.1.call-done = bf16[200,1600]{1,0:T(8,128)(2,1)} async-done(((bf16[800,1600]{1,0:T(8,128)(2,1)}), bf16[200,1600]{1,0:T(8,128)(2,1)}) %reduce-scatter.15.cloned.1.call-update) | async-done | bytes 640016
  622.1 27.4 %reduce-scatter.11.cloned.1.call-done = bf16[64,1600]{1,0:T(8,128)(2,1)} async-done(((bf16[256,1600]{1,0:T(8,128)(2,1)}), bf16[64,1600]{1,0:T(8,128)(2,1)}) %reduce-scatter.11.cloned.1.call-update) | async-done | bytes 204816 | tf_op jit(solution)/shard_map/reduce_scatter | solution.py:706
  650.2 7.0 convolution_convert_fusion.2
  660.9 26.3 %scatter_out.1 = bf16[128,1600]{1,0:T(8,128)(2,1)} custom-call(bf16[8,128,1600]{2,1,0:T(8,128)(2,1)} %bitcast.95, f32[128,1600]{1,0:T(8,128)} %get-tuple-element.27.mixed_ref, f32[1,1600]{1,0:T(1,128)} %broadcast_in_dim_reshape_squeeze.2.vec_ref), custom_call_target="tpu_custom_call" | custom-call | tf_op jit(solution)/shard_map/scatter_out/pallas_call | solution.py:272
  691.0 89.9 %all-reduce.11.cloned.1.call-done = (f32[6,1600]{1,0:T(8,128)}, f32[2048]{0:T(1024)}, f32[2048]{0:T(1024)}, f32[4,1600]{1,0:T(4,128)}) async-done(((f32[6,1600]{1,0:T(8,128)}, f32[2048]{0:T(1024)}, f32[2048]{0:T(1024)}, f32[4,1600]{1,0:T(4,128)}), (f32[6,1600]{1,0:T(8,128)}, f32[2048]{0:T(1024)}, f32[2048]{0:T(1024)}, f32[4,1600]{1,0:T(4,128)})) %all-reduce.11.cloned.1.call-update) | async-done | bytes 80400 | tf_op jit(solution)/shard_map/psum | solution.py:731
  790.0 33.5 %all-gather.25.cloned.1.call-done = bf16[3200,768]{1,0:T(8,128)(2,1)} async-done(((bf16[400,768]{1,0:T(8,128)(2,1)}), bf16[3200,768]{1,0:T(8,128)(2,1)}) %all-gather.25.cloned.1.call-update) | async-done | bytes 4915216 | tf_op jit(solution)/shard_map/all_gather | solution.py:715
  828.3 7.0 concatenate.27
  841.0 27.3 %all-gather.27.cloned.1.call-done = bf16[3200,800]{1,0:T(8,128)(2,1)} async-done(((bf16[400,800]{1,0:T(8,128)(2,1)}), bf16[3200,800]{1,0:T(8,128)(2,1)}) %all-gather.27.cloned.1.call-update) | async-done | bytes 5120016 | tf_op jit(solution)/shard_map/all_gather | solution.py:709
  868.4 8.5 copy.120
  876.9 17.2 %reshape.150 = f32[8,400,4,200]{1,0,3,2:T(8,128)} reshape(bf16[3200,800]{0,1:T(8,128)(2,1)} %copy.120) | data formatting | bytes 15360000 | tf_op jit(solution)/shard_map/convert_element_type | solution.py:711
  894.1 17.8 %copy.121 = f32[400,4,8,200]{3,2,1,0:T(8,128)} copy(f32[400,4,8,200]{0,2,3,1:T(8,128)} %bitcast.89) | data formatting | bytes 20480000 | tf_op jit(solution)/shard_map/convert_element_type | solution.py:711
  912.0 14.1 %reshape.149 = f32[400,6400]{1,0:T(8,128)} reshape(f32[400,4,8,200]{3,2,1,0:T(8,128)} %copy.121) | data formatting | bytes 20480000 | tf_op jit(solution)/shard_map/convert_element_type | solution.py:711
  926.0 7.3 convert_element_type.95
  933.3 52.8 %all-gather.21.cloned.1.call-done = bf16[2048,1600]{1,0:T(8,128)(2,1)} async-done(((bf16[64,1600]{1,0:T(8,128)(2,1)}), bf16[2048,1600]{1,0:T(8,128)(2,1)}) %all-gather.21.cloned.1.call-update) | async-done | bytes 6553616 | tf_op jit(solution)/shard_map/all_gather | solution.py:713
  (169 shorter events, 99.9 us)
Async XLA Ops:
  7.2 58.7 %all-gather.13.cloned.1.call-start = ((), (), s32[]{:S(2)}) async-start(), calls=%async_computation.4 | async-start | bytes 3072000 | tf_op jit(solution)/shard_map/all_gather | solution.py:639
  9.6 161.6 %all-reduce.9.cloned.1.call-start = ((), (), s32[]{:S(2)}) async-start(), calls=%async_computation.5 | async-start | bytes 1703936 | tf_op jit(solution)/shard_map/psum | solution.py:642
  10.9 216.5 %all-gather.15.cloned.1.call-start = ((), (), s32[]{:S(2)}) async-start(), calls=%async_computation.6 | async-start | bytes 3584000 | tf_op jit(solution)/shard_map/all_gather | solution.py:650
  11.0 6.1 copy-start.16
  11.0 6.2 copy-start.17
  11.0 6.2 copy-start.18
  11.1 6.2 copy-start.19
  11.1 6.2 copy-start.20
  11.1 6.2 copy-start.21
  11.1 6.2 copy-start.22
  11.1 6.2 copy-start.14
  12.8 20.2 %copy-start.23 = (s32[32]{0:T(128)S(1)}, s32[32]{0:T(128)}, u32[]{:S(2)}) copy-start(s32[32]{0:T(128)} %param.17) | copy-start | bytes 388
  12.8 20.4 %copy-start.7 = (bf16[64,2,1600]{2,1,0:T(2,128)(2,1)S(1)}, bf16[64,2,1600]{2,1,0:T(2,128)(2,1)}, u32[]{:S(2)}) copy-start(bf16[64,2,1600]{2,1,0:T(2,128)(2,1)} %param.16) | copy-start | bytes 1228804
  14.1 253.3 %all-gather.17.cloned.1.call-start = ((), (), s32[]{:S(2)}) async-start(), calls=%async_computation.7 | async-start | bytes 3328000 | tf_op jit(solution)/shard_map/all_gather | solution.py:652
  16.2 285.3 %all-gather.19.cloned.1.call-start = ((), (), s32[]{:S(2)}) async-start(), calls=%async_computation.8 | async-start | bytes 3833856 | tf_op jit(solution)/shard_map/all_gather | solution.py:675
  17.1 495.2 %reduce-scatter.9.cloned.1.call-start = ((), (), s32[]{:S(2)}) async-start(), calls=%async_computation.9 | async-start | bytes 3072000 | tf_op jit(solution)/shard_map/reduce_scatter | solution.py:706
  34.4 38.3 %copy-start.10 = (f32[1,1600]{1,0:T(1,128)}, f32[1,1600]{1,0:T(1,128)S(1)}, u32[]{:S(2)}) copy-start(f32[1,1600]{1,0:T(1,128)S(1)} %stack_reshape_squeeze.15.vec_ref) | copy-start | bytes 19204
  34.9 37.9 %copy-start.9 = (f32[1,1600]{1,0:T(1,128)}, f32[1,1600]{1,0:T(1,128)S(1)}, u32[]{:S(2)}) copy-start(f32[1,1600]{1,0:T(1,128)S(1)} %stack_reshape_squeeze.17.vec_ref) | copy-start | bytes 19204
  233.5 75.1 %copy-start.24 = (f32[1024,800]{0,1:T(8,128)}, f32[1024,800]{0,1:T(8,128)S(1)}, u32[]{:S(2)}) copy-start(f32[1024,800]{0,1:T(8,128)S(1)} %fusion.11) | copy-start | bytes 9830404
  319.3 50.8 %copy-start.4 = (bf16[256,1600]{1,0:T(8,128)(2,1)S(1)}, bf16[256,1600]{1,0:T(8,128)(2,1)}, u32[]{:S(2)}) copy-start(bf16[256,1600]{1,0:T(8,128)(2,1)} %all-reduce.9.cloned.1.call-done) | copy-start | bytes 2457604
  387.8 58.8 %copy-start.1 = (bf16[8,128,1600]{2,1,0:T(8,128)(2,1)S(1)}, bf16[8,128,1600]{2,1,0:T(8,128)(2,1)}, u32[]{:S(2)}) copy-start(bf16[8,128,1600]{2,1,0:T(8,128)(2,1)} %norm_gather.1) | copy-start | bytes 9830404
  452.4 114.4 %reduce-scatter.13.cloned.1.call-start = ((), (), s32[]{:S(2)}) async-start(), calls=%async_computation.15 | async-start | bytes 3584000 | tf_op jit(solution)/shard_map/reduce_scatter | solution.py:706
  459.5 8.6 copy-start.2
  459.5 162.5 %reduce-scatter.15.cloned.1.call-start = ((), (), s32[]{:S(2)}) async-start(), calls=%async_computation.16 | async-start | bytes 3328000
  468.0 181.5 %reduce-scatter.11.cloned.1.call-start = ((), (), s32[]{:S(2)}) async-start(), calls=%async_computation.10 | async-start | bytes 1064960 | tf_op jit(solution)/shard_map/reduce_scatter | solution.py:706
  472.2 308.7 %all-reduce.11.cloned.1.call-start = ((), (), s32[]{:S(2)}) async-start(), calls=%async_computation.17 | async-start | bytes 192512 | tf_op jit(solution)/shard_map/psum | solution.py:731
  483.7 27.2 %copy-start.13 = (f32[4,1600]{1,0:T(4,128)S(1)}, f32[4,1600]{1,0:T(4,128)}, u32[]{:S(2)}) copy-start(f32[4,1600]{1,0:T(4,128)} %get-tuple-element.34) | copy-start | bytes 76804
  512.3 311.2 %all-gather.25.cloned.1.call-start = ((), (), s32[]{:S(2)}) async-start(), calls=%async_computation.13 | async-start | bytes 5529600 | tf_op jit(solution)/shard_map/all_gather | solution.py:715
  513.0 355.4 %all-gather.27.cloned.1.call-start = ((), (), s32[]{:S(2)}) async-start(), calls=%async_computation.14 | async-start | bytes 6451200 | tf_op jit(solution)/shard_map/all_gather | solution.py:709
  566.8 359.2 %all-gather.23.cloned.1.call-start = ((), (), s32[]{:S(2)}) async-start(), calls=%async_computation.12 | async-start | bytes 5990400 | tf_op jit(solution)/shard_map/all_gather | solution.py:708
  622.0 364.1 %all-gather.21.cloned.1.call-start = ((), (), s32[]{:S(2)}) async-start(), calls=%async_computation.11 | async-start | bytes 7028736 | tf_op jit(solution)/shard_map/all_gather | solution.py:713
  660.9 28.5 %copy-start.5 = (f32[128,1600]{1,0:T(8,128)S(1)}, f32[128,1600]{1,0:T(8,128)}, u32[]{:S(2)}) copy-start(f32[128,1600]{1,0:T(8,128)} %get-tuple-element.32) | copy-start | bytes 2457604
  (9 other events, 29.9 us)
Sparse Core Ops, SparseCore 0:
  10.2 55.6 all-gather.12
  68.8 71.3 all-reduce.8
  142.4 69.1 all-gather.14
  213.1 54.1 all-gather.16
  269.2 32.1 all-gather.18
  452.5 56.1 reduce-scatter.8
  511.0 55.6 reduce-scatter.12
  569.7 52.2 reduce-scatter.14
  625.0 24.4 reduce-scatter.10
  655.9 124.9 all-reduce.10
  782.8 40.5 all-gather.24
  825.2 43.1 all-gather.26
  870.3 41.4 all-gather.22
  914.4 71.6 all-gather.20

commit v2 on v1

--- a/solution.py
+++ b/solution.py
@@ -58,25 +58,44 @@
     return copy
 
 
-def plane_gather(own_ref, all_ref, sems, chips):
+def plane_gather_start(owns, alls, sems, chips):
     far_send, far_recv, near_send, near_recv, local_sem = sems
     me, core, chip, sibling, to, come = plane_peers(chips)
-    far = [
-        send(own_ref, all_ref.at[me], far_send.at[k], far_recv.at[k], "ctx", to[k])
-        for k in range(chips - 1)
-    ]
-    near = [send(own_ref, all_ref.at[me], near_send.at[chips - 1], near_recv.at[chips - 1], "ctx", sibling)]
-    local = pltpu.make_async_copy(own_ref, all_ref.at[me], local_sem)
-    local.start()
-    for k in range(chips - 1):
-        far[k].wait_recv()
-        block = all_ref.at[come[k]]
-        near.append(send(block, block, near_send.at[k], near_recv.at[k], "ctx", sibling))
-    for copy in far:
-        copy.wait_send()
-    for copy in near:
+    far, near, local = [], [], []
+    for i, (own_ref, all_ref) in enumerate(zip(owns, alls)):
+        far.append(
+            [
+                send(own_ref, all_ref.at[me], far_send.at[i, k], far_recv.at[i, k], "ctx", to[k])
+                for k in range(chips - 1)
+            ]
+        )
+        last = chips - 1
+        near.append(send(own_ref, all_ref.at[me], near_send.at[i, last], near_recv.at[i, last], "ctx", sibling))
+        copy = pltpu.make_async_copy(own_ref, all_ref.at[me], local_sem.at[i])
+        copy.start()
+        local.append(copy)
+    return far, near, local
+
+
+def plane_gather_finish(started, alls, sems, chips):
+    far_send, far_recv, near_send, near_recv, local_sem = sems
+    me, core, chip, sibling, to, come = plane_peers(chips)
+    far, near, local = started
+    near = list(near)
+    for i, all_ref in enumerate(alls):
+        for k in range(chips - 1):
+            far[i][k].wait_recv()
+            block = all_ref.at[come[k]]
+            near.append(send(block, block, near_send.at[i, k], near_recv.at[i, k], "ctx", sibling))
+    for group in far:
+        for copy in group:
+            copy.wait_send()
+    for copy in near + local:
         copy.wait()
-    local.wait()
+
+
+def plane_gather(owns, alls, sems, chips):
+    plane_gather_finish(plane_gather_start(owns, alls, sems, chips), alls, sems, chips)
 
 
 def plane_scatter(part_ref, mine, paired, stage, arrived, sems, chips):
@@ -110,8 +129,8 @@
     return total
 
 
-def gather_sems(chips):
-    return [DMA((chips - 1,)), DMA((chips - 1,)), DMA((chips,)), DMA((chips,)), DMA]
+def gather_sems(chips, count=1):
+    return [DMA((count, chips - 1))] * 2 + [DMA((count, chips))] * 2 + [DMA((count,))]
 
 
 def scatter_scratch(chips, rows, width):
@@ -143,26 +162,53 @@
     return (scaled - first - unit * second) * inverse
 
 
-def first_kernel(chips, tok_ref, vec_ref, all_ref, own, *sems):
+def first_kernel(
+    chips, planes, quarter, tok_ref, og_ref, vec_ref, vecs_ref, h1_ref, ogs_ref, own, v_send, v_recv, v_local, *sems
+):
     me, core, chip, sibling, to, come = plane_peers(chips)
+    plane = lax.axis_index("fsdp")
+    barrier = pltpu.get_barrier_semaphore()
+    for peer in to + [sibling]:
+        pl.semaphore_signal(barrier, inc=1, device_id={"ctx": peer}, device_id_type=MESH)
+    for k in range(1, planes):
+        peer = lax.rem(plane + k, planes)
+        pl.semaphore_signal(barrier, inc=1, device_id={"fsdp": peer}, device_id_type=MESH)
+    pl.semaphore_wait(barrier, chips + planes - 1)
+    copies = []
+    for k in range(1, planes):
+        peer = lax.rem(plane + k, planes)
+        copies.append(send(vec_ref, vecs_ref.at[plane], v_send.at[k - 1], v_recv.at[k - 1], "fsdp", peer))
+    local = pltpu.make_async_copy(vec_ref, vecs_ref.at[plane], v_local)
+    local.start()
+    og_sems, h1_sems = sems[:5], sems[5:]
+    og_started = plane_gather_start([og_ref], [ogs_ref], og_sems, chips)
     unit, inverse = normalize(tok_ref[...].astype(F32))
-    own[...] = (unit * vec_ref[0:1, :] + vec_ref[1:2, :]).astype(BF16)
-    greet("ctx", to + [sibling])
-    plane_gather(own, all_ref, sems, chips)
-
-
-def first_norm_gather(tok, vecs, n_ctx):
+    for copy in copies + [local]:
+        copy.wait()
+    gain, shift = [
+        jnp.concatenate([vecs_ref[j, k : k + 1, :quarter].astype(F32) for j in range(planes)], axis=1) for k in range(2)
+    ]
+    own[...] = (unit * gain + shift).astype(BF16)
+    h1_started = plane_gather_start([own], [h1_ref], h1_sems, chips)
+    plane_gather_finish(og_started, [ogs_ref], og_sems, chips)
+    plane_gather_finish(h1_started, [h1_ref], h1_sems, chips)
+
+
+def first_norm_gather(tok, og, vec, n_ctx, planes):
     rows, width = tok.shape
     chips = n_ctx // 2
-    return pl.pallas_call(
-        functools.partial(first_kernel, chips),
-        out_shape=jax.ShapeDtypeStruct((n_ctx, rows, width), BF16),
-        in_specs=[VMEM, VMEM],
-        out_specs=ANY,
-        scratch_shapes=[pltpu.VMEM((rows, width), BF16)] + gather_sems(chips),
+    whole = jax.ShapeDtypeStruct((n_ctx, rows, width), BF16)
+    return pl.pallas_call(
+        functools.partial(first_kernel, chips, planes, width // planes),
+        out_shape=(jax.ShapeDtypeStruct((planes,) + vec.shape, BF16), whole, whole),
+        in_specs=[VMEM, ANY, VMEM],
+        out_specs=(VMEM, ANY, ANY),
+        scratch_shapes=[pltpu.VMEM((rows, width), BF16), DMA((planes - 1,)), DMA((planes - 1,)), DMA]
+        + gather_sems(chips)
+        + gather_sems(chips),
         compiler_params=params(0),
         name="norm_gather",
-    )(tok, vecs)
+    )(tok, og, vec)
 
 
 def second_kernel(chips, part_ref, tok_ref, vec_ref, mixed_ref, all_ref, own, *scratch):
@@ -173,7 +219,7 @@
     mixed_ref[...] = mixed
     unit, inverse = normalize(mixed)
     own[...] = (unit * vec_ref[0:1, :] + vec_ref[1:2, :]).astype(BF16)
-    plane_gather(own, all_ref, scratch[9:], chips)
+    plane_gather([own], [all_ref], scratch[9:], chips)
 
 
 def second_norm_gather(part, tok, vecs):
@@ -209,7 +255,7 @@
     sums_ref[1:2, :] = jnp.sum(grad, axis=0, keepdims=True)
     sums_ref[2:3, :] = jnp.sum(low.astype(F32), axis=0, keepdims=True)
     sums_ref[3:4, :] = jnp.sum(out_grad, axis=0, keepdims=True)
-    plane_gather(own, all_ref, scratch[9:], chips)
+    plane_gather([own], [all_ref], scratch[9:], chips)
 
 
 def second_norm_back(part, mixed, og, vecs):
@@ -232,7 +278,9 @@
     )(part, mixed, og, vecs)
 
 
-def fourth_kernel(chips, part_ref, tok_ref, dmixed_ref, vec_ref, grad_ref, sums_ref, *scratch):
+def fourth_kernel(
+    chips, part_ref, out_part_ref, tok_ref, dmixed_ref, mixed_ref, vec_ref, grad_ref, out_ref, sums_ref, *scratch
+):
     me, core, chip, sibling, to, come = plane_peers(chips)
     greet("ctx", to + [sibling])
     unit, inverse = normalize(tok_ref[...].astype(F32))
@@ -240,44 +288,95 @@
     grad_ref[...] = dmixed_ref[...] + norm_backward(grad, vec_ref[0:1, :], unit, inverse)
     sums_ref[0:1, :] = jnp.sum(grad * unit, axis=0, keepdims=True)
     sums_ref[1:2, :] = jnp.sum(grad, axis=0, keepdims=True)
-
-
-def first_norm_back(part, tok, dmixed, vecs):
+    total = plane_scatter(out_part_ref, *scratch[9:13], scratch[13:], chips)
+    out_ref[...] = (mixed_ref[...] + total + vec_ref[1:2, :]).astype(BF16)
+
+
+def first_norm_back(part, out_part, tok, dmixed, mixed, vecs):
     n_ctx, rows, width = part.shape
     chips = n_ctx // 2
     return pl.pallas_call(
         functools.partial(fourth_kernel, chips),
         out_shape=(
             jax.ShapeDtypeStruct((rows, width), F32),
+            jax.ShapeDtypeStruct((rows, width), BF16),
             jax.ShapeDtypeStruct((2, width), F32),
         ),
-        in_specs=[ANY, VMEM, VMEM, VMEM],
-        out_specs=(VMEM, VMEM),
-        scratch_shapes=scatter_scratch(chips, rows, width),
+        in_specs=[ANY, ANY, VMEM, VMEM, VMEM, VMEM],
+        out_specs=(VMEM, VMEM, VMEM),
+        scratch_shapes=scatter_scratch(chips, rows, width) * 2,
         compiler_params=params(3),
         name="scatter_back",
-    )(part, tok, dmixed, vecs)
-
-
-def out_kernel(chips, part_ref, mixed_ref, vec_ref, out_ref, *scratch):
+    )(part, out_part, tok, dmixed, mixed, vecs)
+
+
+def gather_kernel(chips, count, *refs):
     me, core, chip, sibling, to, come = plane_peers(chips)
     greet("ctx", to + [sibling])
-    total = plane_scatter(part_ref, *scratch[:4], scratch[4:9], chips)
-    out_ref[...] = (mixed_ref[...] + total + vec_ref[0:1, :]).astype(BF16)
-
-
-def block_result(part, mixed, vecs):
-    n_ctx, rows, width = part.shape
-    chips = n_ctx // 2
-    return pl.pallas_call(
-        functools.partial(out_kernel, chips),
-        out_shape=jax.ShapeDtypeStruct((rows, width), BF16),
-        in_specs=[ANY, VMEM, VMEM],
+    plane_gather(refs[:count], refs[count : 2 * count], refs[2 * count :], chips)
+
+
+def gather_plane(arrays, n_ctx, cid):
+    chips, count = n_ctx // 2, len(arrays)
+    return pl.pallas_call(
+        functools.partial(gather_kernel, chips, count),
+        out_shape=tuple(jax.ShapeDtypeStruct((n_ctx,) + a.shape, a.dtype) for a in arrays),
+        in_specs=[ANY] * count,
+        out_specs=(ANY,) * count,
+        scratch_shapes=gather_sems(chips, count),
+        compiler_params=params(cid),
+        name="gather_plane",
+    )(*arrays)
+
+
+def total_kernel(n_ctx, planes, part_ref, out_ref, arrived, own, others, z_send, z_recv, c_send, c_recv):
+    me, plane = lax.axis_index("ctx"), lax.axis_index("fsdp")
+    barrier = pltpu.get_barrier_semaphore()
+    for k in range(1, planes):
+        peer = lax.rem(plane + k, planes)
+        pl.semaphore_signal(barrier, inc=1, device_id={"fsdp": peer}, device_id_type=MESH)
+    for k in range(1, n_ctx):
+        peer = lax.rem(me + k, n_ctx)
+        pl.semaphore_signal(barrier, inc=1, device_id={"ctx": peer}, device_id_type=MESH)
+    pl.semaphore_wait(barrier, planes + n_ctx - 2)
+    far = []
+    for k in range(1, planes):
+        peer = lax.rem(plane + k, planes)
+        far.append(send(part_ref.at[peer], arrived.at[k - 1], z_send.at[k - 1], z_recv.at[k - 1], "fsdp", peer))
+    total = part_ref[plane]
+    for k in range(1, planes):
+        far[k - 1].wait()
+        total = total + arrived[k - 1]
+    own[...] = total
+    near = []
+    for k in range(1, n_ctx):
+        peer = lax.rem(me + k, n_ctx)
+        near.append(send(own, others.at[k - 1], c_send.at[k - 1], c_recv.at[k - 1], "ctx", peer))
+    for k in range(1, n_ctx):
+        near[k - 1].wait()
+        total = total + others[k - 1]
+    out_ref[...] = total
+
+
+def total_vectors(part, n_ctx, cid):
+    planes, size = part.shape[0], part.shape[1:]
+    return pl.pallas_call(
+        functools.partial(total_kernel, n_ctx, planes),
+        out_shape=jax.ShapeDtypeStruct(size, F32),
+        in_specs=[VMEM],
         out_specs=VMEM,
-        scratch_shapes=scatter_scratch(chips, rows, width),
-        compiler_params=params(4),
-        name="scatter_out",
-    )(part, mixed, vecs)
+        scratch_shapes=[
+            pltpu.VMEM((planes - 1,) + size, F32),
+            pltpu.VMEM(size, F32),
+            pltpu.VMEM((n_ctx - 1,) + size, F32),
+            DMA((planes - 1,)),
+            DMA((planes - 1,)),
+            DMA((n_ctx - 1,)),
+            DMA((n_ctx - 1,)),
+        ],
+        compiler_params=params(cid),
+        name="total_vectors",
+    )(part)
 
 
 def to_heads_kernel(kinds, planes, seqs, tok_ref, head_ref, send_sems, recv_sems, local_sems):
@@ -326,10 +425,22 @@
     )(tok)
 
 
-def to_tokens_kernel(kinds, planes, seqs, head_ref, tok_ref, send_sems, recv_sems, local_sems):
+def to_tokens_kernel(kinds, planes, seqs, chips, beside, *refs):
+    head_ref, owns = refs[0], refs[1 : 1 + beside]
+    tok_ref, alls = refs[1 + beside], refs[2 + beside : 2 + 2 * beside]
+    send_sems, recv_sems, local_sems = refs[2 + 2 * beside : 5 + 2 * beside]
+    sems = refs[5 + 2 * beside :]
+    plane_me, core, chip, sibling, to, come = plane_peers(chips)
     me = lax.axis_index("fsdp")
     pairs = planes // seqs
-    greet("fsdp", [lax.rem(me + k, planes) for k in range(1, planes)])
+    barrier = pltpu.get_barrier_semaphore()
+    for k in range(1, planes):
+        peer = lax.rem(me + k, planes)
+        pl.semaphore_signal(barrier, inc=1, device_id={"fsdp": peer}, device_id_type=MESH)
+    if beside:
+        for peer in to + [sibling]:
+            pl.semaphore_signal(barrier, inc=1, device_id={"ctx": peer}, device_id_type=MESH)
+    pl.semaphore_wait(barrier, planes - 1 + (chips if beside else 0))
     width = tok_ref.shape[3] // kinds
 
     def target(kind):
@@ -355,22 +466,27 @@
         copy = pltpu.make_async_copy(head_ref.at[kind, :, me], target(kind), local_sems.at[kind])
         copy.start()
         local.append(copy)
+    if beside:
+        plane_gather(owns, alls, sems, chips)
     for copy in copies + local:
         copy.wait()
 
 
-def to_tokens(heads, seqs, cid):
+def to_tokens(heads, seqs, cid, beside=()):
     kinds, n_ctx, planes, rows, lanes = heads.shape
     width = kinds * (planes // seqs) * LANES
-    return pl.pallas_call(
-        functools.partial(to_tokens_kernel, kinds, planes, seqs),
-        out_shape=jax.ShapeDtypeStruct((n_ctx, seqs, rows, width), heads.dtype),
-        in_specs=[ANY],
-        out_specs=ANY,
-        scratch_shapes=[DMA((kinds, planes - 1)), DMA((kinds, planes - 1)), DMA((kinds,))],
+    count = len(beside)
+    return pl.pallas_call(
+        functools.partial(to_tokens_kernel, kinds, planes, seqs, n_ctx // 2, count),
+        out_shape=(jax.ShapeDtypeStruct((n_ctx, seqs, rows, width), heads.dtype),)
+        + tuple(jax.ShapeDtypeStruct((n_ctx,) + a.shape, a.dtype) for a in beside),
+        in_specs=[ANY] * (1 + count),
+        out_specs=(ANY,) * (1 + count),
+        scratch_shapes=[DMA((kinds, planes - 1)), DMA((kinds, planes - 1)), DMA((kinds,))]
+        + (gather_sems(n_ctx // 2, count) if count else []),
         compiler_params=params(cid),
         name="to_tokens",
-    )(heads)
+    )(heads, *beside)
 
 
 def nt(left, right):
@@ -570,6 +686,24 @@
         compiler_params=params(),
         name="attend_backward",
     )(order, qkv, grad, att, lse)
+
+
+def assemble_kernel(pieces, part_ref, out_ref):
+    for start, source, first, size in pieces:
+        out_ref[:, start : start + size] = part_ref[source, :, first : first + size].astype(F32)
+
+
+def assemble(parts, pieces, width, block):
+    n_ctx, rows, columns = parts.shape
+    return pl.pallas_call(
+        functools.partial(assemble_kernel, pieces),
+        grid=(rows // block,),
+        out_shape=jax.ShapeDtypeStruct((rows, width), F32),
+        in_specs=[pl.BlockSpec((n_ctx, block, columns), lambda i: (0, i, 0))],
+        out_specs=pl.BlockSpec((block, width), lambda i: (i, 0)),
+        compiler_params=params(),
+        name="assemble",
+    )(parts)
 
 
 def mm(left, right):
@@ -632,14 +766,28 @@
     )
     order = jnp.concatenate([device_of_block * 2, device_of_block[::-1] * 2 + 1]).astype(jnp.int32)
 
-    qkv_padded = jnp.pad(qkv_weight, ((0, 0), (0, n_ctx * span - width)))
+    first = [-(-quarter * j // HD) for j in range(planes)] + [heads]
+    counts = [first[j + 1] - first[j] for j in range(planes)]
+    assert max(counts) <= n_ctx
+    slot_head = [jnp.minimum(first[j] + c, heads - 1) for j in range(planes)]
+    first_own = jnp.asarray(first, jnp.int32)[f]
+    count_own = jnp.asarray(counts, jnp.int32)[f]
+
     qkv_own = jnp.concatenate(
-        [lax.dynamic_slice(qkv_padded, (0, k * width + c * span), (quarter, span)) for k in range(3)], axis=1
+        [
+            lax.dynamic_slice(qkv_weight, (0, k * width + slot_head[j] * HD), (quarter, HD))
+            for k in range(3)
+            for j in range(planes)
+        ],
+        axis=1,
     )
     qkv_slice = lax.all_gather(qkv_own, "fsdp", axis=0, tiled=True)
-    out_padded = jnp.pad(out_weight, ((span, span), (0, 0)))
-    out_start = jnp.clip(c * span - f * quarter + span, 0, quarter + span)
-    out_slice = lax.psum(lax.dynamic_slice(out_padded, (out_start, 0), (span, width)), "fsdp")
+    next_rows = lax.ppermute(out_weight[:HD], "fsdp", [(j + 1, j) for j in range(planes - 1)])
+    out_own = lax.dynamic_slice(
+        jnp.concatenate([out_weight, next_rows]), ((first_own + c) * HD - f * quarter, 0), (HD, width)
+    )
+    out_own = jnp.where(c < count_own, out_own, jnp.zeros_like(out_own))
+    out_slice = lax.all_gather(out_own, "fsdp", axis=0, tiled=True)
     up_own = jnp.concatenate(
         [
             lax.dynamic_slice(up_weight, (0, k * ff_quarter + c * ff_piece), (quarter, ff_piece))
@@ -651,35 +799,38 @@
     down_own = lax.dynamic_slice(down_weight, (c * ff_piece, 0), (ff_piece, width))
     down_slice = lax.all_gather(down_own, "fsdp", axis=0, tiled=True)
 
+    tok = jnp.swapaxes(tokens, 0, 1).reshape(rows, width)
+    og = jnp.swapaxes(out_grad, 0, 1).reshape(rows, width)
+
     packed = jnp.concatenate(
         [
             jnp.stack([ln1_gain, ln1_bias, ln2_gain, ln2_bias, query_bias, value_bias, out_bias, down_bias]),
             up_bias.reshape(ff // width, quarter),
         ]
     )
-    vectors = lax.all_gather(packed, "fsdp", axis=0).astype(F32)
+    packed = jnp.pad(packed, ((0, -packed.shape[0] % 16), (0, -quarter % LANES)))
+    vectors, h1, og_all = first_norm_gather(tok, og, packed, n_ctx, planes)
+    h1 = h1.reshape(plane_rows, width)
+    og_all = og_all.reshape(plane_rows, width)
+    vectors = vectors[:, :, :quarter].astype(F32)
     gain1, bias1, gain2, bias2, bias_q, bias_v, bias_o, bias_d = [
         vectors[:, k].reshape(width) for k in range(8)
     ]
     bias_up = lax.dynamic_slice(
-        vectors[:, 8:].reshape(planes, ff_quarter), (0, c * ff_piece), (planes, ff_piece)
+        vectors[:, 8 : 8 + ff // width].reshape(planes, ff_quarter), (0, c * ff_piece), (planes, ff_piece)
     ).reshape(ff_span)
 
     def head_part(vector):
-        return lax.dynamic_slice(jnp.pad(vector, (0, n_ctx * span - width)), (c * span,), (span,))
-
-    qkv_shift = jnp.concatenate([head_part(bias_q), jnp.zeros((span,), F32), head_part(bias_v)])
-
-    tok = jnp.swapaxes(tokens, 0, 1).reshape(rows, width)
-    og = jnp.swapaxes(out_grad, 0, 1).reshape(rows, width)
-    og_all = lax.all_gather(og, "ctx", axis=0, tiled=True)
-
-    h1 = first_norm_gather(tok, jnp.stack([gain1, bias1]), n_ctx).reshape(plane_rows, width)
+        return [lax.dynamic_slice(vector, (slot_head[j] * HD,), (HD,)) for j in range(planes)]
+
+    qkv_shift = jnp.concatenate(head_part(bias_q) + [jnp.zeros((span,), F32)] + head_part(bias_v))
+
     qkv = (mm(h1, qkv_slice) + qkv_shift).astype(BF16)
     qkv_heads = to_heads(qkv.reshape(n_ctx, seqs, local_rows, 3 * span), 3, planes, 5)
     qkv_heads = qkv_heads.reshape(3, blocks, half, LANES)
     att_heads, att_exact, lse = attend_forward(order, qkv_heads, tile)
-    att = to_tokens(att_heads.reshape(1, n_ctx, planes, local_rows, LANES), seqs, 6).reshape(plane_rows, span)
+    (att,) = to_tokens(att_heads.reshape(1, n_ctx, planes, local_rows, LANES), seqs, 6)
+    att = att.reshape(plane_rows, span)
     branch = mm(att, out_slice).astype(BF16).reshape(n_ctx, rows, width)
     mixed, h2 = second_norm_gather(branch, tok, jnp.stack([gain2, bias2, bias_o]))
     h2 = h2.reshape(plane_rows, width)
@@ -688,54 +839,82 @@
     act = activated.astype(BF16)
     out_part = mm(act, down_slice).astype(BF16).reshape(n_ctx, rows, width)
 
+    def reduce_own(part):
+        return lax.psum_scatter(part, "fsdp", scatter_dimension=0, tiled=True)
+
     (d_up,) = gelu_back(mm_nt(og_all, down_slice))
     d_up_low = d_up.astype(BF16)
+    down_part = mm_tn(act, og_all).astype(BF16)
     d_h2 = mm_nt(d_up_low, up_slice).astype(BF16).reshape(n_ctx, rows, width)
+    up_part = mm_tn(h2, d_up_low).astype(BF16)
+    d_h2, down_part, up_part = lax.optimization_barrier((d_h2, down_part, up_part))
+    down_own_grad, up_own_grad = reduce_own(down_part), reduce_own(up_part)
     d_mixed, sums2, d_branch = second_norm_back(d_h2, mixed, og, gain2[None, :])
     d_branch = d_branch.reshape(plane_rows, width)
     d_att = mm_nt(d_branch, out_slice).astype(BF16)
     d_att_heads = to_heads(d_att.reshape(n_ctx, seqs, local_rows, span), 1, planes, 7)
+    out_w_part = mm_tn(att, d_branch).astype(BF16)
+    d_att_heads, out_w_part = lax.optimization_barrier((d_att_heads, out_w_part))
+    out_own_grad = reduce_own(out_w_part)
     d_heads = attend_backward(order, qkv_heads, d_att_heads.reshape(blocks, half, LANES), att_exact, lse, tile)
-    d_qkv = to_tokens(d_heads.reshape(3, n_ctx, planes, local_rows, LANES), seqs, 8)
+    d_qkv, down_parts = to_tokens(
+        d_heads.reshape(3, n_ctx, planes, local_rows, LANES), seqs, 8, (down_own_grad,)
+    )
     d_qkv = d_qkv.reshape(plane_rows, 3 * span)
+    qkv_part = mm_tn(h1, d_qkv).astype(BF16)
     d_h1 = mm_nt(d_qkv, qkv_slice).astype(BF16).reshape(n_ctx, rows, width)
-    block_out = block_result(out_part, mixed, bias_d[None, :])
-    grad_tok, sums1 = first_norm_back(d_h1, tok, d_mixed, gain1[None, :])
-
-    def reduce_own(part):
-        return lax.psum_scatter(part.astype(BF16), "fsdp", scatter_dimension=0, tiled=True)
-
-    down_grad = lax.all_gather(reduce_own(mm_tn(act, og_all)), "ctx", axis=0, tiled=True).astype(F32)
-    up_parts = lax.all_gather(reduce_own(mm_tn(h2, d_up_low)), "ctx", axis=0)
-    up_grad = (
-        up_parts.reshape(n_ctx, quarter, planes, ff_piece).transpose(1, 2, 0, 3).reshape(quarter, ff).astype(F32)
-    )
-    out_parts = lax.all_gather(reduce_own(mm_tn(att, d_branch)), ("ctx", "fsdp"), axis=0, tiled=True)
-    out_grad_own = lax.dynamic_slice(out_parts, (f * quarter, 0), (quarter, width)).astype(F32)
-    qkv_parts = lax.all_gather(reduce_own(mm_tn(h1, d_qkv)), "ctx", axis=0)
-    qkv_grad = jnp.concatenate(
-        [
-            qkv_parts[:, :, k * span : (k + 1) * span].transpose(1, 0, 2).reshape(quarter, n_ctx * span)[:, :width]
-            for k in range(3)
-        ],
-        axis=1,
-    ).astype(F32)
-
-    def spread(values, count):
-        return lax.dynamic_update_slice(jnp.zeros((n_ctx * count,), F32), values, (c * count,))
+    d_h1, qkv_part = lax.optimization_barrier((d_h1, qkv_part))
+    qkv_own_grad = reduce_own(qkv_part)
+    grad_tok, block_out, sums1 = first_norm_back(
+        d_h1, out_part, tok, d_mixed, mixed, jnp.stack([gain1, bias_d])
+    )
 
     d_qkv_sum = jnp.sum(d_qkv.astype(F32), axis=0)
     d_up_sum = jnp.sum(d_up_low.astype(F32), axis=0).reshape(planes, ff_piece)
     up_spread = lax.dynamic_update_slice(jnp.zeros((planes, ff_quarter), F32), d_up_sum, (0, c * ff_piece))
-    wide = jnp.concatenate([sums1, sums2])
-    total_wide, total_q, total_v, total_up = lax.psum(
-        (wide, spread(d_qkv_sum[:span], span), spread(d_qkv_sum[2 * span :], span), up_spread), ("ctx", "fsdp")
-    )
-
-    def own(vector):
-        return lax.dynamic_slice(vector, (f * quarter,), (quarter,))
-
-    up_bias_grad = lax.dynamic_slice(total_up, (f, 0), (1, ff_quarter)).reshape(ff_quarter)
+
+    def spread(values):
+        full = jnp.zeros((width + HD,), F32)
+        for j in range(planes):
+            place = jnp.where(c < counts[j], (first[j] + c) * HD, width)
+            full = lax.dynamic_update_slice(full, values[j * HD : (j + 1) * HD], (place,))
+        return full[None, :width]
+
+    wide = jnp.concatenate([sums1, sums2, spread(d_qkv_sum[:span]), spread(d_qkv_sum[2 * span :])])
+    wide = wide.reshape(8, planes, quarter).transpose(1, 0, 2).reshape(planes, 8 * quarter)
+    flat = jnp.concatenate([wide, up_spread], axis=1)
+    size = flat.shape[1]
+    flat = jnp.pad(flat, ((0, 0), (0, -size % (8 * LANES))))
+    totals = total_vectors(flat.reshape(planes, -1, LANES), n_ctx, 9).reshape(-1)
+    sums = totals[: 8 * quarter].reshape(8, quarter)
+    up_bias_grad = totals[8 * quarter : size]
+
+    up_parts, out_parts = gather_plane([up_own_grad, out_own_grad], n_ctx, 10)
+    (qkv_parts,) = gather_plane([qkv_own_grad], n_ctx, 11)
+    down_grad = down_parts.reshape(ff_quarter, width).astype(F32)
+    block = quarter // 5
+    up_pieces = [
+        (j * ff_quarter + d * ff_piece, d, j * ff_piece, ff_piece) for j in range(planes) for d in range(n_ctx)
+    ]
+    up_grad = assemble(up_parts, up_pieces, ff, block)
+    qkv_pieces = [
+        (k * width + (first[j] + d) * HD, d, k * span + j * HD, HD)
+        for k in range(3)
+        for j in range(planes)
+        for d in range(counts[j])
+    ]
+    qkv_grad = assemble(qkv_parts, qkv_pieces, 3 * width, block)
+    out_rows = out_parts.reshape(n_ctx * HD, width)
+    tail = (f + 1) * quarter - first_own * HD
+    tail_rows = lax.dynamic_slice(out_rows, (tail, 0), (HD, width))
+    tail_rows = lax.ppermute(tail_rows, "fsdp", [(j, j + 1) for j in range(planes - 1)])
+    lead = first_own * HD - f * quarter
+    shifted = lax.dynamic_slice(
+        jnp.concatenate([jnp.zeros((HD, width), BF16), out_rows]), (HD - lead, 0), (quarter, width)
+    )
+    from_tail = jnp.concatenate([tail_rows, jnp.zeros((quarter - HD, width), BF16)])
+    row_ids = lax.broadcasted_iota(jnp.int32, (quarter, width), 0)
+    out_grad_own = jnp.where(row_ids < lead, from_tail, shifted).astype(F32)
 
     def back(values):
         return jnp.swapaxes(values.reshape(seqs, local_rows, width), 0, 1)
@@ -743,19 +922,19 @@
     return (
         back(block_out),
         back(grad_tok),
-        own(total_wide[0]),
-        own(total_wide[1]),
+        sums[0],
+        sums[1],
         qkv_grad,
-        own(total_q),
-        own(total_v),
+        sums[6],
+        sums[7],
         out_grad_own,
-        own(total_wide[4]),
-        own(total_wide[2]),
-        own(total_wide[3]),
+        sums[4],
+        sums[2],
+        sums[3],
         up_grad,
         up_bias_grad,
         down_grad,
-        own(total_wide[5]),
+        sums[5],
     )
 
 

time: 1000 us -> 714 us (0.71)
  waiting for transfers between devices: 412 us -> 0.69 us
  Pallas kernels: 349 us -> 539 us
  local copies, waits for them, and re-layouts: 111 us -> 38.5 us
  blocking collectives: 15.5 us -> 32 us
  other arithmetic: 21.9 us -> 11.5 us
    pallas_call x4 -> x8, Pallas kernels: 111 us -> 264 us  [the longest x2 85.2 us: to_tokens(): pl.pallas_call(functools.partial(to_tokens_kernel, kinds, planes, seqs, n...]
    all_gather x5 -> x0, waiting for transfers between devices: 148 us -> none  [the longest x1 52.8 us: local(): lax.all_gather(reduce_own(mm_tn(att, d_branch)), ('ctx', 'fsdp'), axis=0,...]
    psum x2 -> x0, waiting for transfers between devices: 89.9 us -> none  [the longest x1 89.9 us: local(): lax.psum((wide, spread(d_qkv_sum[:span], span), spread(d_qkv_sum[2 * span...]
    reduce_scatter x3, waiting for transfers between devices: 81.1 us -> 0.04 us  [reduce_own(): return lax.psum_scatter(part, 'fsdp', scatter_dimension=0, tiled=True)]
    unnamed x15 -> x8, waiting for transfers between devices: 56.1 us -> 0.62 us
    convert_element_type x3 -> x0, local copies, waits for them, and re-layouts: 49.1 us -> none  [local(): up_parts.reshape(n_ctx, quarter, planes, ff_piece).transpose(1, 2, 0, 3)]
    all_gather x1, waiting for transfers between devices: 33.8 us -> 0.01 us  [local(): down_slice = lax.all_gather(down_own, 'fsdp', axis=0, tiled=True)]
    pallas_call x1, Pallas kernels: 26.3 us -> 50 us  [first_norm_back(): pl.pallas_call(functools.partial(fourth_kernel, chips), out_shape=(jax.Sh...]
  transfers between devices with their start and end apart: 14 -> 9, of which waited for: 10 -> 0; matrix products, arithmetic and copies ran while one was open for 17% -> 12% of each run, Pallas kernels for 23% -> 71%
where the time goes in v2:
time: 714 us; the launch traced here: 708 us
  Pallas kernels  539 us (75%)
  matrix products  63.9 us (9%)
  local copies, waits for them, and re-layouts  38.5 us (5%)
  blocking collectives  32 us (4%)
  between operations  17.3 us (2%)
  other arithmetic  11.5 us (2%)
    pallas_call x2, Pallas kernels, to_tokens(): pl.pallas_call(functools.partial(to_tokens_kernel, kinds, planes, seqs, n...  85.2 us
    pallas_call x2, Pallas kernels, gather_plane(): pl.pallas_call(functools.partial(gather_kernel, chips, count), out_shape=...  78.9 us
    pallas_call x2, Pallas kernels, to_heads(): pl.pallas_call(functools.partial(to_heads_kernel, kinds, planes, seqs), o...  71 us
    pallas_call x1, Pallas kernels, second_norm_back(): pl.pallas_call(functools.partial(third_kernel, chips), out_shape=(jax.Sha...  50.7 us
    pallas_call x1, Pallas kernels, first_norm_back(): pl.pallas_call(functools.partial(fourth_kernel, chips), out_shape=(jax.Sh...  50 us
    pallas_call x1, Pallas kernels, first_norm_gather(): pl.pallas_call(functools.partial(first_kernel, chips, planes, width // pl...  49 us
    pallas_call x1, Pallas kernels, second_norm_gather(): pl.pallas_call(functools.partial(second_kernel, chips), out_shape=(jax.Sh...  48.7 us
    pallas_call x1, Pallas kernels, total_vectors(): pl.pallas_call(functools.partial(total_kernel, n_ctx, planes), out_shape=...  34.5 us
  transfers between devices with their start and end apart: 9, of which 0 were waited for; matrix products, arithmetic and copies ran while one was open for 12% of the time, Pallas kernels for 71%

profile of v2, /device:TPU:0, one launch (start us, length us, event | category | flops | bytes accessed | tf_op | source)
XLA Modules:
  0.0 707.8 jit_solution(12445879862483221001)
XLA Ops:
  19.5 49.0 %norm_gather.1 = (bf16[4,16,512]{2,1,0:T(8,128)(2,1)}, bf16[8,128,1600]{2,1,0:T(8,128)(2,1)}, bf16[8,128,1600]{2,1,0:T(8,128)(2,1)}) custom-call(bf16[128,1600]{1,0:T(8,128)(2,1)} %bitcast.81, bf16[128,1600]{1,0:T(8,128)(2,1)} %bitcast.87, bf16[16,512]{1,0:T(8,128)(2,1)} %pad.10.vec_ref), custom_call_target="tpu_custom_call" | custom-call | tf_op jit(solution)/shard_map/norm_gather/pallas_call | solution.py:201
  74.5 32.0 %all_gather.14 = bf16[256,1600]{1,0:T(8,128)(2,1)} all-gather(bf16[64,1600]{1,0:T(8,128)(2,1)S(1)} %fusion.10), channel_id=1, replica_groups=mesh['ctx'=8,'fsdp'=4] {'fsdp'}, dimensions={0}, use_global_device_ids=true | all-gather | bytes 1024000 | tf_op jit(solution)/shard_map/all_gather | solution.py:790
  106.5 6.9 add_convert_fusion
  113.5 48.9 %to_heads.2 = bf16[3,8,4,64,128]{4,3,2,1,0:T(8,128)(2,1)} custom-call(bf16[8,2,64,768]{3,2,1,0:T(8,128)(2,1)} %bitcast.96), custom_call_target="tpu_custom_call" | custom-call | tf_op jit(solution)/shard_map/to_heads/pallas_call | solution.py:417
  162.3 28.7 %attend_forward.1 = (bf16[64,32,128]{2,1,0:T(8,128)(2,1)}, f32[128,2048]{1,0:T(8,128)}, f32[2,2048]{1,0:T(2,128)}) custom-call(s32[64]{0:T(128)} %pad_add_fusion.order_ref, bf16[3,64,32,128]{3,2,1,0:T(8,128)(2,1)} %bitcast.75), custom_call_target="tpu_custom_call" | custom-call | tf_op jit(solution)/shard_map/attend_forward/pallas_call | solution.py:580
  191.0 29.8 %to_tokens.2 = bf16[8,2,64,256]{3,2,1,0:T(8,128)(2,1)} custom-call(bf16[1,8,4,64,128]{4,3,2,1,0:T(8,128)(2,1)} %bitcast.99), custom_call_target="tpu_custom_call" | custom-call | tf_op jit(solution)/shard_map/to_tokens/pallas_call | solution.py:479
  222.9 3.5 copy.57
  226.4 48.7 %scatter_norm_gather.1 = (f32[128,1600]{1,0:T(8,128)}, bf16[8,128,1600]{2,1,0:T(8,128)(2,1)}) custom-call(bf16[8,128,1600]{2,1,0:T(8,128)(2,1)} %bitcast.79, bf16[128,1600]{1,0:T(8,128)(2,1)} %bitcast.82, f32[3,1600]{1,0:T(4,128)} %pad_maximum_fusion.1.vec_ref), custom_call_target="tpu_custom_call" | custom-call | tf_op jit(solution)/shard_map/scatter_norm_gather/pallas_call | solution.py:228
  275.1 6.2 fusion.16
  281.3 5.9 convolution_convert_fusion.5
  287.2 7.3 %convert_reduce_fusion = (f32[800]{0:T(1024)S(1)}, bf16[1024,800]{0,1:T(8,128)(2,1)S(1)}) fusion(f32[1024,800]{0,1:T(8,128)S(1)} %fusion.16, f32[800]{0:T(1024)S(1)} %add.252, bf16[1024,1600]{1,0:T(8,128)(2,1)} %bitcast.119, bf16[800,1600]{1,0:T(8,128)(2,1)} %all-gather.6.cloned.1.call-done), kind=kOutput, calls=%fused_computation.17 | convolution fusion | flops 2640280832 | bytes 10758400 | tf_op jit(solution)/shard_map/dot_general | solution.py:714
  295.7 5.0 convolution_convert_fusion.4
  300.6 5.9 convolution_convert_fusion
  306.5 3.5 copy.58
  310.3 50.7 %scatter_back_gather.1 = (f32[128,1600]{1,0:T(8,128)}, f32[4,1600]{1,0:T(4,128)}, bf16[8,128,1600]{2,1,0:T(8,128)(2,1)}) custom-call(bf16[8,128,1600]{2,1,0:T(8,128)(2,1)} %bitcast.80, f32[128,1600]{1,0:T(8,128)} %get-tuple-element.46.mixed_ref, bf16[128,1600]{1,0:T(8,128)(2,1)} %bitcast.88, f32[1,1600]{1,0:T(1,128)} %copy-done.8), custom_call_target="tpu_custom_call" | custom-call | tf_op jit(solution)/shard_map/scatter_back_gather/pallas_call | solution.py:264
  361.0 4.1 convolution_convert_fusion.8
  365.1 22.1 %to_heads.3 = bf16[1,8,4,64,128]{4,3,2,1,0:T(8,128)(2,1)} custom-call(bf16[8,2,64,256]{3,2,1,0:T(8,128)(2,1)} %bitcast.100), custom_call_target="tpu_custom_call" | custom-call | tf_op jit(solution)/shard_map/to_heads/pallas_call | solution.py:417
  391.4 26.4 %attend_backward.1 = bf16[3,64,32,128]{3,2,1,0:T(8,128)(2,1)} custom-call(s32[64]{0:T(128)} %pad_add_fusion.order_ref, bf16[3,64,32,128]{3,2,1,0:T(8,128)(2,1)} %bitcast.76, bf16[64,32,128]{2,1,0:T(8,128)(2,1)} %bitcast.93, f32[128,2048]{1,0:T(8,128)} %get-tuple-element.49.att_ref, f32[2,2048]{1,0:T(2,128)} %get-tuple-element.50.lse_ref), custom_call_target="tpu_custom_call" | custom-call | tf_op jit(solution)/shard_map/attend_backward/pallas_call | solution.py:678
  417.8 55.4 %to_tokens.3 = (bf16[8,2,64,768]{3,2,1,0:T(8,128)(2,1)}, bf16[8,200,1600]{2,1,0:T(8,128)(2,1)}) custom-call(bf16[3,8,4,64,128]{4,3,2,1,0:T(8,128)(2,1)} %bitcast.84, bf16[200,1600]{1,0:T(8,128)(2,1)} %reduce-scatter.13.cloned.1.call-done.refs_1_), custom_call_target="tpu_custom_call" | custom-call | tf_op jit(solution)/shard_map/to_tokens/pallas_call | solution.py:479
  473.2 4.9 convolution_convert_fusion.2
  478.1 3.7 copy.61
  481.8 6.7 convolution_convert_fusion.6
  488.5 7.0 convolution_convert_fusion.1
  495.5 3.5 copy.62
  499.5 50.0 %scatter_back.1 = (f32[128,1600]{1,0:T(8,128)}, bf16[128,1600]{1,0:T(8,128)(2,1)}, f32[2,1600]{1,0:T(2,128)}) custom-call(bf16[8,128,1600]{2,1,0:T(8,128)(2,1)} %bitcast.77, bf16[8,128,1600]{2,1,0:T(8,128)(2,1)} %bitcast.78, bf16[128,1600]{1,0:T(8,128)(2,1)} %bitcast.83, f32[128,1600]{1,0:T(8,128)} %get-tuple-element.54.dmixed_ref, ...), custom_call_target="tpu_custom_call" | custom-call | tf_op jit(solution)/shard_map/scatter_back/pallas_call | solution.py:298
  551.8 2.7 copy.72
  557.1 34.5 %total_vectors.1 = f32[40,128]{1,0:T(8,128)} custom-call(f32[4,40,128]{2,1,0:T(8,128)} %bitcast.105), custom_call_target="tpu_custom_call" | custom-call | tf_op jit(solution)/shard_map/total_vectors/pallas_call | solution.py:363
  592.4 45.9 %gather_plane.3 = (bf16[8,400,800]{2,1,0:T(8,128)(2,1)}, bf16[8,64,1600]{2,1,0:T(8,128)(2,1)}) custom-call(bf16[400,800]{1,0:T(8,128)(2,1)} %reduce-scatter.9.cloned.1.call-done.refs_0_, bf16[64,1600]{1,0:T(8,128)(2,1)} %reduce-scatter.11.cloned.1.call-done.refs_1_), custom_call_target="tpu_custom_call" | custom-call | tf_op jit(solution)/shard_map/gather_plane/pallas_call | solution.py:321
  642.0 9.4 %assemble.3 = f32[400,6400]{1,0:T(8,128)} custom-call(bf16[8,400,800]{2,1,0:T(8,128)(2,1)} %get-tuple-element.63.part_ref), custom_call_target="tpu_custom_call" | custom-call | tf_op jit(solution)/shard_map/assemble/pallas_call | solution.py:698
  652.7 5.2 bitcast_convert_fusion
  660.3 33.0 %gather_plane.2.part_ref = bf16[8,400,768]{2,1,0:T(8,128)(2,1)} custom-call(bf16[400,768]{1,0:T(8,128)(2,1)} %reduce-scatter.7.cloned.1.call-done.refs_0_), custom_call_target="tpu_custom_call" | custom-call | tf_op jit(solution)/shard_map/gather_plane/pallas_call | solution.py:321
  693.3 7.2 %assemble.2 = f32[400,4800]{1,0:T(8,128)} custom-call(bf16[8,400,768]{2,1,0:T(8,128)(2,1)} %gather_plane.2.part_ref), custom_call_target="tpu_custom_call" | custom-call | tf_op jit(solution)/shard_map/assemble/pallas_call | solution.py:698
  (160 shorter events, 37.1 us)
Async XLA Ops:
  7.2 99.3 %all-gather.4.cloned.1.call-start = ((), (), s32[]{:S(2)}) async-start(), calls=%async_computation.4 | async-start | bytes 3072000 | tf_op jit(solution)/shard_map/all_gather | solution.py:784
  10.3 6.6 copy-start.6
  10.4 264.7 %all-gather.8.cloned.1.call-start = ((), (), s32[]{:S(2)}) async-start(), calls=%async_computation.6 | async-start | bytes 3584000 | tf_op jit(solution)/shard_map/all_gather | solution.py:798
  10.4 7.3 %copy-start.7 = (bf16[64,2,1600]{2,1,0:T(2,128)(2,1)S(1)}, bf16[64,2,1600]{2,1,0:T(2,128)(2,1)}, u32[]{:S(2)}) copy-start(bf16[64,2,1600]{2,1,0:T(2,128)(2,1)} %param.20) | copy-start | bytes 1228804
  12.1 6.5 copy-start.12
  12.1 6.5 copy-start.13
  12.1 6.5 copy-start.14
  12.1 6.5 copy-start.15
  12.1 6.5 copy-start.16
  12.2 6.5 copy-start.17
  12.2 6.5 copy-start.18
  12.2 6.5 copy-start.19
  12.2 6.5 copy-start.11
  13.5 56.1 %copy-start.23 = (s32[32]{0:T(128)S(1)}, s32[32]{0:T(128)}, u32[]{:S(2)}) copy-start(s32[32]{0:T(128)} %param.19) | copy-start | bytes 388
  13.5 56.5 %copy-start.25 = (s32[5]{0:T(128)S(1)}, s32[5]{0:T(128)}, u32[]{:S(2)}) copy-start(s32[5]{0:T(128)} %constant.93.clone) | copy-start | bytes 64
  13.5 57.7 %copy-start.24 = (s32[4]{0:T(128)S(1)}, s32[4]{0:T(128)}, u32[]{:S(2)}) copy-start(s32[4]{0:T(128)} %constant.94.clone) | copy-start | bytes 52
  13.5 273.7 %all-gather.6.cloned.1.call-start = ((), (), s32[]{:S(2)}) async-start(), calls=%async_computation.5 | async-start | bytes 3328000 | tf_op jit(solution)/shard_map/all_gather | solution.py:800
  13.6 60.8 %collective-permute-start = (bf16[64,1600]{1,0:T(8,128)(2,1)S(1)}, bf16[64,1600]{1,0:T(8,128)(2,1)S(1)}, u32[]{:S(2)}, u32[]{:S(2)}) collective-permute-start(bf16[64,1600]{1,0:T(8,128)(2,1)S(1)} %slice.104), channel_id=1, source_target_pairs={{1,0},{2,1},{3,2},{5,4},{6,5},{7,6},{9,8},{10,9},{11,10},{13,12},{... | collective-permute-start | bytes 614408 | tf_op jit(solution)/shard_map/ppermute | solution.py:785
  16.9 400.9 %reduce-scatter.13.cloned.1.call-start = ((), (), s32[]{:S(2)}) async-start(), calls=%async_computation.10 | async-start | bytes 3328000
  72.7 40.7 %copy-start.8 = (f32[1,1600]{1,0:T(1,128)}, f32[1,1600]{1,0:T(1,128)S(1)}, u32[]{:S(2)}) copy-start(f32[1,1600]{1,0:T(1,128)S(1)} %stack_reshape_squeeze.15.vec_ref) | copy-start | bytes 19204
  113.5 107.3 %copy-start = (bf16[256,1600]{1,0:T(8,128)(2,1)S(1)}, bf16[256,1600]{1,0:T(8,128)(2,1)}, u32[]{:S(2)}) copy-start(bf16[256,1600]{1,0:T(8,128)(2,1)} %all_gather.14) | copy-start | bytes 2457604
  287.2 8.5 %copy-start.21 = (bf16[8,128,1600]{2,1,0:T(8,128)(2,1)S(1)}, bf16[8,128,1600]{2,1,0:T(8,128)(2,1)}, u32[]{:S(2)}) copy-start(bf16[8,128,1600]{2,1,0:T(8,128)(2,1)} %get-tuple-element.44) | copy-start | bytes 9830404
  310.0 51.0 %copy-start.1 = (bf16[256,1600]{1,0:T(8,128)(2,1)S(1)}, bf16[256,1600]{1,0:T(8,128)(2,1)}, u32[]{:S(2)}) copy-start(bf16[256,1600]{1,0:T(8,128)(2,1)} %all_gather.14) | copy-start | bytes 2457604
  310.0 282.3 %reduce-scatter.11.cloned.1.call-start = ((), (), s32[]{:S(2)}) async-start(), calls=%async_computation.9 | async-start | bytes 1064960 | tf_op jit(solution)/shard_map/reduce_scatter | solution.py:843
  361.0 26.2 %copy-start.2 = (bf16[8,2,64,256]{3,2,1,0:T(8,128)(2,1)S(1)}, bf16[8,2,64,256]{3,2,1,0:T(8,128)(2,1)}, u32[]{:S(2)}) copy-start(bf16[8,2,64,256]{3,2,1,0:T(8,128)(2,1)} %to_tokens.2) | copy-start | bytes 1572868
  361.0 26.2 %copy-start.22 = (bf16[8,128,1600]{2,1,0:T(8,128)(2,1)S(1)}, bf16[8,128,1600]{2,1,0:T(8,128)(2,1)}, u32[]{:S(2)}) copy-start(bf16[8,128,1600]{2,1,0:T(8,128)(2,1)} %get-tuple-element.47) | copy-start | bytes 9830404
  389.3 203.1 %reduce-scatter.9.cloned.1.call-start = ((), (), s32[]{:S(2)}) async-start(), calls=%async_computation.8 | async-start | bytes 3584000 | tf_op jit(solution)/shard_map/reduce_scatter | solution.py:843
  389.9 270.4 %reduce-scatter.7.cloned.1.call-start = ((), (), s32[]{:S(2)}) async-start(), calls=%async_computation.7 | async-start | bytes 3072000 | tf_op jit(solution)/shard_map/reduce_scatter | solution.py:843
  549.5 6.7 copy-start.10
  639.3 19.2 %collective-permute-start.1 = (bf16[64,1600]{1,0:T(8,128)(2,1)S(1)}, bf16[64,1600]{1,0:T(8,128)(2,1)S(1)}, u32[]{:S(2)}, u32[]{:S(2)}) collective-permute-start(bf16[64,1600]{1,0:T(8,128)(2,1)S(1)} %constant_dynamic-slice_fusion), channel_id=1, source_target_pairs={{0,1},{1,2},{2,3},{4,5},{5,6},{6,7},{8,9},{9,10},{10,11},{12,13},{... | collective-permute-start | bytes 614408 | tf_op jit(solution)/shard_map/ppermute | solution.py:910
  642.0 10.7 %slice-start = ((s8[5324800]{0:T(1024)(128)(4,1)}), s8[4194304]{0:T(1024)(128)(4,1)S(1)}, s32[]{:S(2)}) async-start(s8[5324800]{0:T(1024)(128)(4,1)} %bitcast.85), calls=%async_computation.11 | async-start | bytes 8388608
  642.0 10.7 %slice-start.1 = ((s8[5324800]{0:T(1024)(128)(4,1)}), s8[1130496]{0:T(1024)(128)(4,1)S(1)}, s32[]{:S(2)}) async-start(s8[5324800]{0:T(1024)(128)(4,1)} %bitcast.85), calls=%async_computation.12 | async-start | bytes 2260992
  (7 other events, 32.2 us)
Sparse Core Ops, SparseCore 0:
  10.5 56.1 all-gather.3
  68.8 96.0 all-gather.7
  167.1 65.8 all-gather.5
  310.2 60.0 reduce-scatter.12
  389.4 25.4 reduce-scatter.10
  417.7 81.7 reduce-scatter.8
  501.9 58.5 reduce-scatter.6

commit v3 on v2

--- a/solution.py
+++ b/solution.py
@@ -18,6 +18,7 @@
 VMEM = pl.BlockSpec(memory_space=pltpu.VMEM)
 DMA = pltpu.SemaphoreType.DMA
 VMEM_LIMIT = 56 * 1024 * 1024
+SMALL = pl.CostEstimate(flops=1, bytes_accessed=1, transcendentals=0)
 
 
 def params(cid=None):
@@ -33,16 +34,31 @@
     core = lax.rem(me, 2)
     chip = me // 2
     sibling = chip * 2 + 1 - core
-    to = [lax.rem(chip + k, chips) * 2 + core for k in range(1, chips)]
-    come = [lax.rem(chip + chips - k, chips) * 2 + core for k in range(1, chips)]
+    if chips == 4:
+        across_x = chip + 1 - 2 * lax.rem(chip, 2)
+        across_y = lax.rem(chip + 2, 4)
+        corner = lax.rem(across_x + 2, 4)
+        first = across_x * (1 - core) + across_y * core
+        second = across_y * (1 - core) + across_x * core
+        to = come = [first * 2 + core, second * 2 + core, corner * 2 + core]
+    else:
+        to = [lax.rem(chip + k, chips) * 2 + core for k in range(1, chips)]
+        come = [lax.rem(chip + chips - k, chips) * 2 + core for k in range(1, chips)]
     return me, core, chip, sibling, to, come
 
 
-def greet(axis, peers):
+def greet(plane=(), across=()):
     barrier = pltpu.get_barrier_semaphore()
-    for peer in peers:
-        pl.semaphore_signal(barrier, inc=1, device_id={axis: peer}, device_id_type=MESH)
-    pl.semaphore_wait(barrier, len(peers))
+    for peer in plane:
+        pl.semaphore_signal(barrier, inc=1, device_id={"ctx": peer}, device_id_type=MESH)
+    for peer in across:
+        pl.semaphore_signal(barrier, inc=1, device_id={"fsdp": peer}, device_id_type=MESH)
+    pl.semaphore_wait(barrier, len(plane) + len(across))
+
+
+def other_planes(planes):
+    me = lax.axis_index("fsdp")
+    return me, [lax.rem(me + k, planes) for k in range(1, planes)]
 
 
 def send(src, dst, send_sem, recv_sem, axis, peer):
@@ -61,15 +77,16 @@
 def plane_gather_start(owns, alls, sems, chips):
     far_send, far_recv, near_send, near_recv, local_sem = sems
     me, core, chip, sibling, to, come = plane_peers(chips)
+    direct = 2 if chips == 4 else chips - 1
+    last = chips - 1
     far, near, local = [], [], []
     for i, (own_ref, all_ref) in enumerate(zip(owns, alls)):
         far.append(
             [
                 send(own_ref, all_ref.at[me], far_send.at[i, k], far_recv.at[i, k], "ctx", to[k])
-                for k in range(chips - 1)
+                for k in range(direct)
             ]
         )
-        last = chips - 1
         near.append(send(own_ref, all_ref.at[me], near_send.at[i, last], near_recv.at[i, last], "ctx", sibling))
         copy = pltpu.make_async_copy(own_ref, all_ref.at[me], local_sem.at[i])
         copy.start()
@@ -82,11 +99,21 @@
     me, core, chip, sibling, to, come = plane_peers(chips)
     far, near, local = started
     near = list(near)
+
+    def pass_on(i, all_ref, k):
+        far[i][k].wait_recv()
+        block = all_ref.at[come[k]]
+        if chips == 4 and k == 0:
+            far[i].append(send(block, block, far_send.at[i, 2], far_recv.at[i, 2], "ctx", to[1]))
+        near.append(send(block, block, near_send.at[i, k], near_recv.at[i, k], "ctx", sibling))
+
+    direct = 2 if chips == 4 else chips - 1
     for i, all_ref in enumerate(alls):
-        for k in range(chips - 1):
-            far[i][k].wait_recv()
-            block = all_ref.at[come[k]]
-            near.append(send(block, block, near_send.at[i, k], near_recv.at[i, k], "ctx", sibling))
+        for k in range(direct):
+            pass_on(i, all_ref, k)
+    for i, all_ref in enumerate(alls):
+        for k in range(direct, chips - 1):
+            pass_on(i, all_ref, k)
     for group in far:
         for copy in group:
             copy.wait_send()
@@ -101,27 +128,43 @@
 def plane_scatter(part_ref, mine, paired, stage, arrived, sems, chips):
     far_send, far_recv, near_send, near_recv, local_sem = sems
     me, core, chip, sibling, to, come = plane_peers(chips)
+    targets = to + [me]
+    order = [2, 1, 0, 3] if chips == 4 else list(range(chips))
     near, local = [None] * chips, [None] * chips
-    order = list(range(1, chips)) + [0]
+    crossed = [1, 0, 2, 3] if chips == 4 else list(range(chips))
     for k in order:
-        base = lax.rem(chip + k, chips) * 2
-        near[k] = send(
-            part_ref.at[base + 1 - core], paired.at[k], near_send.at[k], near_recv.at[k], "ctx", sibling
-        )
-        local[k] = pltpu.make_async_copy(part_ref.at[base + core], mine.at[k], local_sem.at[k])
+        other = targets[crossed[k]] + 1 - 2 * core
+        near[k] = send(part_ref.at[other], paired.at[k], near_send.at[k], near_recv.at[k], "ctx", sibling)
+        local[k] = pltpu.make_async_copy(part_ref.at[targets[k]], mine.at[k], local_sem.at[k])
         local[k].start()
-    far = []
-    for k in range(1, chips):
+
+    def both(k):
         local[k].wait()
         near[k].wait_recv()
-        stage[k - 1] = (mine[k].astype(F32) + paired[k].astype(F32)).astype(BF16)
-        far.append(
-            send(stage.at[k - 1], arrived.at[k - 1], far_send.at[k - 1], far_recv.at[k - 1], "ctx", to[k - 1])
-        )
-    local[0].wait()
-    near[0].wait_recv()
-    total = mine[0].astype(F32) + paired[0].astype(F32)
-    for k in range(chips - 1):
+        return mine[k].astype(F32) + paired[k].astype(F32)
+
+    def dispatch(k, target):
+        return send(stage.at[k], arrived.at[k], far_send.at[k], far_recv.at[k], "ctx", target)
+
+    far = [None] * (chips - 1)
+    if chips == 4:
+        stage[2] = both(2).astype(BF16)
+        far[2] = dispatch(2, to[0])
+        stage[0] = both(0).astype(BF16)
+        far[0] = dispatch(0, to[0])
+        partial = both(1)
+        far[2].wait_recv()
+        stage[1] = (partial + arrived[2].astype(F32)).astype(BF16)
+        far[1] = dispatch(1, to[1])
+        total = both(3)
+        arriving = [0, 1]
+    else:
+        for k in range(chips - 1):
+            stage[k] = both(k).astype(BF16)
+            far[k] = dispatch(k, to[k])
+        total = both(chips - 1)
+        arriving = range(chips - 1)
+    for k in arriving:
         far[k].wait_recv()
         total = total + arrived[k].astype(F32)
     for copy in far + near:
@@ -166,18 +209,11 @@
     chips, planes, quarter, tok_ref, og_ref, vec_ref, vecs_ref, h1_ref, ogs_ref, own, v_send, v_recv, v_local, *sems
 ):
     me, core, chip, sibling, to, come = plane_peers(chips)
-    plane = lax.axis_index("fsdp")
-    barrier = pltpu.get_barrier_semaphore()
-    for peer in to + [sibling]:
-        pl.semaphore_signal(barrier, inc=1, device_id={"ctx": peer}, device_id_type=MESH)
-    for k in range(1, planes):
-        peer = lax.rem(plane + k, planes)
-        pl.semaphore_signal(barrier, inc=1, device_id={"fsdp": peer}, device_id_type=MESH)
-    pl.semaphore_wait(barrier, chips + planes - 1)
-    copies = []
-    for k in range(1, planes):
-        peer = lax.rem(plane + k, planes)
-        copies.append(send(vec_ref, vecs_ref.at[plane], v_send.at[k - 1], v_recv.at[k - 1], "fsdp", peer))
+    plane, others = other_planes(planes)
+    greet(to + [sibling], others)
+    copies = [
+        send(vec_ref, vecs_ref.at[plane], v_send.at[k], v_recv.at[k], "fsdp", peer) for k, peer in enumerate(others)
+    ]
     local = pltpu.make_async_copy(vec_ref, vecs_ref.at[plane], v_local)
     local.start()
     og_sems, h1_sems = sems[:5], sems[5:]
@@ -213,7 +249,7 @@
 
 def second_kernel(chips, part_ref, tok_ref, vec_ref, mixed_ref, all_ref, own, *scratch):
     me, core, chip, sibling, to, come = plane_peers(chips)
-    greet("ctx", to + [sibling])
+    greet(to + [sibling])
     total = plane_scatter(part_ref, *scratch[:4], scratch[4:9], chips)
     mixed = tok_ref[...].astype(F32) + total + vec_ref[2:3, :]
     mixed_ref[...] = mixed
@@ -237,13 +273,14 @@
         + scatter_scratch(chips, rows, width)
         + gather_sems(chips),
         compiler_params=params(1),
+        cost_estimate=SMALL,
         name="scatter_norm_gather",
     )(part, tok, vecs)
 
 
 def third_kernel(chips, part_ref, mixed_ref, og_ref, vec_ref, dmixed_ref, sums_ref, all_ref, own, *scratch):
     me, core, chip, sibling, to, come = plane_peers(chips)
-    greet("ctx", to + [sibling])
+    greet(to + [sibling])
     unit, inverse = normalize(mixed_ref[...])
     grad = plane_scatter(part_ref, *scratch[:4], scratch[4:9], chips)
     out_grad = og_ref[...].astype(F32)
@@ -274,45 +311,125 @@
         + scatter_scratch(chips, rows, width)
         + gather_sems(chips),
         compiler_params=params(2),
+        cost_estimate=SMALL,
         name="scatter_back_gather",
     )(part, mixed, og, vecs)
 
 
 def fourth_kernel(
-    chips, part_ref, out_part_ref, tok_ref, dmixed_ref, mixed_ref, vec_ref, grad_ref, out_ref, sums_ref, *scratch
+    chips,
+    planes,
+    part_ref,
+    outw_ref,
+    flat_ref,
+    tok_ref,
+    dmixed_ref,
+    vec_ref,
+    grad_ref,
+    outw_all,
+    sums_ref,
+    flat_out,
+    small,
+    small_own,
+    small_z,
+    small_c,
+    flat_own,
+    flat_z,
+    flat_c,
+    z_send,
+    z_recv,
+    c_send,
+    c_recv,
+    *scratch,
 ):
+    n_ctx = 2 * chips
     me, core, chip, sibling, to, come = plane_peers(chips)
-    greet("ctx", to + [sibling])
+    plane, others = other_planes(planes)
+    around = [lax.rem(me + k, n_ctx) for k in range(1, n_ctx)]
+    greet(around, others)
+    scatter, outw_sems = scratch[:9], scratch[9:]
+    flat_sent = [
+        send(flat_ref.at[peer], flat_z.at[k], z_send.at[0, k], z_recv.at[0, k], "fsdp", peer)
+        for k, peer in enumerate(others)
+    ]
     unit, inverse = normalize(tok_ref[...].astype(F32))
-    grad = plane_scatter(part_ref, *scratch[:4], scratch[4:9], chips)
+    grad = plane_scatter(part_ref, *scatter[:4], scatter[4:9], chips)
+    outw_started = plane_gather_start([outw_ref], [outw_all], outw_sems, chips)
+    sums = jnp.concatenate(
+        [jnp.sum(grad * unit, axis=0, keepdims=True), jnp.sum(grad, axis=0, keepdims=True)], axis=0
+    )
+    quarter = sums.shape[1] // planes
+    small[...] = jnp.zeros_like(small)
+    for j in range(planes):
+        small[j, 0:2, 0:quarter] = sums[:, j * quarter : (j + 1) * quarter]
+    small_sent = [
+        send(small.at[peer], small_z.at[k], z_send.at[1, k], z_recv.at[1, k], "fsdp", peer)
+        for k, peer in enumerate(others)
+    ]
     grad_ref[...] = dmixed_ref[...] + norm_backward(grad, vec_ref[0:1, :], unit, inverse)
-    sums_ref[0:1, :] = jnp.sum(grad * unit, axis=0, keepdims=True)
-    sums_ref[1:2, :] = jnp.sum(grad, axis=0, keepdims=True)
-    total = plane_scatter(out_part_ref, *scratch[9:13], scratch[13:], chips)
-    out_ref[...] = (mixed_ref[...] + total + vec_ref[1:2, :]).astype(BF16)
-
-
-def first_norm_back(part, out_part, tok, dmixed, mixed, vecs):
+    small_total = small[plane]
+    flat_total = flat_ref[plane]
+    for k in range(planes - 1):
+        flat_sent[k].wait()
+        small_sent[k].wait()
+        small_total = small_total + small_z[k]
+        flat_total = flat_total + flat_z[k]
+    small_own[...] = small_total
+    flat_own[...] = flat_total
+    sent = []
+    for k, peer in enumerate(around):
+        sent.append(send(small_own, small_c.at[k], c_send.at[0, k], c_recv.at[0, k], "ctx", peer))
+        sent.append(send(flat_own, flat_c.at[k], c_send.at[1, k], c_recv.at[1, k], "ctx", peer))
+    plane_gather_finish(outw_started, [outw_all], outw_sems, chips)
+    for copy in sent:
+        copy.wait()
+    for k in range(n_ctx - 1):
+        small_total = small_total + small_c[k]
+        flat_total = flat_total + flat_c[k]
+    sums_ref[...] = small_total
+    flat_out[...] = flat_total
+
+
+def first_norm_back(part, outw_own, flat, tok, dmixed, vecs):
     n_ctx, rows, width = part.shape
+    planes = flat.shape[0]
+    quarter = width // planes
     chips = n_ctx // 2
+    size = (8, quarter + -quarter % LANES)
     return pl.pallas_call(
-        functools.partial(fourth_kernel, chips),
+        functools.partial(fourth_kernel, chips, planes),
         out_shape=(
             jax.ShapeDtypeStruct((rows, width), F32),
-            jax.ShapeDtypeStruct((rows, width), BF16),
-            jax.ShapeDtypeStruct((2, width), F32),
+            jax.ShapeDtypeStruct((n_ctx,) + outw_own.shape, BF16),
+            jax.ShapeDtypeStruct(size, F32),
+            jax.ShapeDtypeStruct(flat.shape[1:], F32),
         ),
         in_specs=[ANY, ANY, VMEM, VMEM, VMEM, VMEM],
-        out_specs=(VMEM, VMEM, VMEM),
-        scratch_shapes=scatter_scratch(chips, rows, width) * 2,
+        out_specs=(VMEM, ANY, VMEM, VMEM),
+        scratch_shapes=[
+            pltpu.VMEM((planes,) + size, F32),
+            pltpu.VMEM(size, F32),
+            pltpu.VMEM((planes - 1,) + size, F32),
+            pltpu.VMEM((n_ctx - 1,) + size, F32),
+            pltpu.VMEM(flat.shape[1:], F32),
+            pltpu.VMEM((planes - 1,) + flat.shape[1:], F32),
+            pltpu.VMEM((n_ctx - 1,) + flat.shape[1:], F32),
+            DMA((2, planes - 1)),
+            DMA((2, planes - 1)),
+            DMA((2, n_ctx - 1)),
+            DMA((2, n_ctx - 1)),
+        ]
+        + scatter_scratch(chips, rows, width)
+        + gather_sems(chips),
         compiler_params=params(3),
+        cost_estimate=SMALL,
         name="scatter_back",
-    )(part, out_part, tok, dmixed, mixed, vecs)
+    )(part, outw_own, flat, tok, dmixed, vecs)
 
 
 def gather_kernel(chips, count, *refs):
     me, core, chip, sibling, to, come = plane_peers(chips)
-    greet("ctx", to + [sibling])
+    greet(to + [sibling])
     plane_gather(refs[:count], refs[count : 2 * count], refs[2 * count :], chips)
 
 
@@ -325,64 +442,21 @@
         out_specs=(ANY,) * count,
         scratch_shapes=gather_sems(chips, count),
         compiler_params=params(cid),
+        cost_estimate=SMALL,
         name="gather_plane",
     )(*arrays)
 
 
-def total_kernel(n_ctx, planes, part_ref, out_ref, arrived, own, others, z_send, z_recv, c_send, c_recv):
-    me, plane = lax.axis_index("ctx"), lax.axis_index("fsdp")
-    barrier = pltpu.get_barrier_semaphore()
-    for k in range(1, planes):
-        peer = lax.rem(plane + k, planes)
-        pl.semaphore_signal(barrier, inc=1, device_id={"fsdp": peer}, device_id_type=MESH)
-    for k in range(1, n_ctx):
-        peer = lax.rem(me + k, n_ctx)
-        pl.semaphore_signal(barrier, inc=1, device_id={"ctx": peer}, device_id_type=MESH)
-    pl.semaphore_wait(barrier, planes + n_ctx - 2)
-    far = []
-    for k in range(1, planes):
-        peer = lax.rem(plane + k, planes)
-        far.append(send(part_ref.at[peer], arrived.at[k - 1], z_send.at[k - 1], z_recv.at[k - 1], "fsdp", peer))
-    total = part_ref[plane]
-    for k in range(1, planes):
-        far[k - 1].wait()
-        total = total + arrived[k - 1]
-    own[...] = total
-    near = []
-    for k in range(1, n_ctx):
-        peer = lax.rem(me + k, n_ctx)
-        near.append(send(own, others.at[k - 1], c_send.at[k - 1], c_recv.at[k - 1], "ctx", peer))
-    for k in range(1, n_ctx):
-        near[k - 1].wait()
-        total = total + others[k - 1]
-    out_ref[...] = total
-
-
-def total_vectors(part, n_ctx, cid):
-    planes, size = part.shape[0], part.shape[1:]
-    return pl.pallas_call(
-        functools.partial(total_kernel, n_ctx, planes),
-        out_shape=jax.ShapeDtypeStruct(size, F32),
-        in_specs=[VMEM],
-        out_specs=VMEM,
-        scratch_shapes=[
-            pltpu.VMEM((planes - 1,) + size, F32),
-            pltpu.VMEM(size, F32),
-            pltpu.VMEM((n_ctx - 1,) + size, F32),
-            DMA((planes - 1,)),
-            DMA((planes - 1,)),
-            DMA((n_ctx - 1,)),
-            DMA((n_ctx - 1,)),
-        ],
-        compiler_params=params(cid),
-        name="total_vectors",
-    )(part)
-
-
-def to_heads_kernel(kinds, planes, seqs, tok_ref, head_ref, send_sems, recv_sems, local_sems):
-    me = lax.axis_index("fsdp")
+def to_heads_kernel(kinds, planes, seqs, chips, beside, *refs):
+    inputs = 4 if beside else 1
+    outputs = 2 if beside else 1
+    tok_ref, head_ref = refs[0], refs[inputs]
+    send_sems, recv_sems, local_sems = refs[inputs + outputs : inputs + outputs + 3]
+    scratch = refs[inputs + outputs + 3 :]
+    plane_me, core, chip, sibling, to, come = plane_peers(chips)
+    me, others = other_planes(planes)
     pairs = planes // seqs
-    greet("fsdp", [lax.rem(me + k, planes) for k in range(1, planes)])
+    greet(to + [sibling] if beside else [], others)
     width = tok_ref.shape[3] // kinds
 
     def source(kind, unit):
@@ -390,39 +464,51 @@
         return tok_ref.at[:, unit // pairs, :, pl.ds(start, LANES)]
 
     copies = []
-    for k in range(1, planes):
-        unit = lax.rem(me + k, planes)
+    for k, unit in enumerate(others):
         for kind in range(kinds):
             copies.append(
                 send(
                     source(kind, unit),
                     head_ref.at[kind, :, me],
-                    send_sems.at[kind, k - 1],
-                    recv_sems.at[kind, k - 1],
+                    send_sems.at[kind, k],
+                    recv_sems.at[kind, k],
                     "fsdp",
                     unit,
                 )
             )
-    local = []
     for kind in range(kinds):
         copy = pltpu.make_async_copy(source(kind, me), head_ref.at[kind, :, me], local_sems.at[kind])
         copy.start()
-        local.append(copy)
-    for copy in copies + local:
+        copies.append(copy)
+    if beside:
+        part_ref, mixed_ref, vec_ref, out_ref = refs[1], refs[2], refs[3], refs[inputs + 1]
+        total = plane_scatter(part_ref, *scratch[:4], scratch[4:], chips)
+        out_ref[...] = (mixed_ref[...] + total + vec_ref[...]).astype(BF16)
+    for copy in copies:
         copy.wait()
 
 
-def to_heads(tok, kinds, planes, cid):
-    n_ctx, seqs, rows, width = tok.shape
+def to_heads(tok, kinds, planes, cid, beside=()):
+    n_ctx, seqs, local_rows, width = tok.shape
+    chips = n_ctx // 2
+    out_shape = (jax.ShapeDtypeStruct((kinds, n_ctx, planes, local_rows, LANES), tok.dtype),)
+    in_specs, out_specs = [ANY], (ANY,)
+    scratch = [DMA((kinds, planes - 1)), DMA((kinds, planes - 1)), DMA((kinds,))]
+    if beside:
+        rows, model = beside[1].shape
+        out_shape += (jax.ShapeDtypeStruct((rows, model), BF16),)
+        in_specs, out_specs = [ANY, ANY, VMEM, VMEM], (ANY, VMEM)
+        scratch += scatter_scratch(chips, rows, model)
     return pl.pallas_call(
-        functools.partial(to_heads_kernel, kinds, planes, seqs),
-        out_shape=jax.ShapeDtypeStruct((kinds, n_ctx, planes, rows, LANES), tok.dtype),
-        in_specs=[ANY],
-        out_specs=ANY,
-        scratch_shapes=[DMA((kinds, planes - 1)), DMA((kinds, planes - 1)), DMA((kinds,))],
+        functools.partial(to_heads_kernel, kinds, planes, seqs, chips, bool(beside)),
+        out_shape=out_shape,
+        in_specs=in_specs,
+        out_specs=out_specs,
+        scratch_shapes=scratch,
         compiler_params=params(cid),
+        cost_estimate=SMALL,
         name="to_heads",
-    )(tok)
+    )(tok, *beside)
 
 
 def to_tokens_kernel(kinds, planes, seqs, chips, beside, *refs):
@@ -431,16 +517,9 @@
     send_sems, recv_sems, local_sems = refs[2 + 2 * beside : 5 + 2 * beside]
     sems = refs[5 + 2 * beside :]
     plane_me, core, chip, sibling, to, come = plane_peers(chips)
-    me = lax.axis_index("fsdp")
+    me, others = other_planes(planes)
     pairs = planes // seqs
-    barrier = pltpu.get_barrier_semaphore()
-    for k in range(1, planes):
-        peer = lax.rem(me + k, planes)
-        pl.semaphore_signal(barrier, inc=1, device_id={"fsdp": peer}, device_id_type=MESH)
-    if beside:
-        for peer in to + [sibling]:
-            pl.semaphore_signal(barrier, inc=1, device_id={"ctx": peer}, device_id_type=MESH)
-    pl.semaphore_wait(barrier, planes - 1 + (chips if beside else 0))
+    greet(to + [sibling] if beside else [], others)
     width = tok_ref.shape[3] // kinds
 
     def target(kind):
@@ -485,6 +564,7 @@
         scratch_shapes=[DMA((kinds, planes - 1)), DMA((kinds, planes - 1)), DMA((kinds,))]
         + (gather_sems(n_ctx // 2, count) if count else []),
         compiler_params=params(cid),
+        cost_estimate=SMALL,
         name="to_tokens",
     )(heads, *beside)
 
@@ -594,6 +674,7 @@
             pltpu.VMEM((length, LANES), BF16),
         ],
         compiler_params=params(),
+        cost_estimate=SMALL,
         name="attend_forward",
     )(order, qkv)
 
@@ -684,6 +765,7 @@
         + [pltpu.VMEM((LANES, length), BF16), pltpu.VMEM((length, LANES), BF16)]
         + [pltpu.VMEM((length, LANES), F32)] * 2,
         compiler_params=params(),
+        cost_estimate=SMALL,
         name="attend_backward",
     )(order, qkv, grad, att, lse)
 
@@ -787,7 +869,19 @@
         jnp.concatenate([out_weight, next_rows]), ((first_own + c) * HD - f * quarter, 0), (HD, width)
     )
     out_own = jnp.where(c < count_own, out_own, jnp.zeros_like(out_own))
-    out_slice = lax.all_gather(out_own, "fsdp", axis=0, tiled=True)
+    down_own = lax.dynamic_slice(down_weight, (c * ff_piece, 0), (ff_piece, width))
+
+    tok = jnp.swapaxes(tokens, 0, 1).reshape(rows, width)
+    og = jnp.swapaxes(out_grad, 0, 1).reshape(rows, width)
+
+    packed = jnp.concatenate(
+        [
+            jnp.stack([ln1_gain, ln1_bias, ln2_gain, ln2_bias, query_bias, value_bias, out_bias, down_bias]),
+            up_bias.reshape(ff // width, quarter),
+        ]
+    )
+    packed = jnp.pad(packed, ((0, -packed.shape[0] % 16), (0, -quarter % LANES)))
+    vectors, h1, og_all = first_norm_gather(tok, og, packed, n_ctx, planes)
     up_own = jnp.concatenate(
         [
             lax.dynamic_slice(up_weight, (0, k * ff_quarter + c * ff_piece), (quarter, ff_piece))
@@ -795,21 +889,7 @@
         ],
         axis=1,
     )
-    up_slice = lax.all_gather(up_own, "fsdp", axis=0, tiled=True)
-    down_own = lax.dynamic_slice(down_weight, (c * ff_piece, 0), (ff_piece, width))
-    down_slice = lax.all_gather(down_own, "fsdp", axis=0, tiled=True)
-
-    tok = jnp.swapaxes(tokens, 0, 1).reshape(rows, width)
-    og = jnp.swapaxes(out_grad, 0, 1).reshape(rows, width)
-
-    packed = jnp.concatenate(
-        [
-            jnp.stack([ln1_gain, ln1_bias, ln2_gain, ln2_bias, query_bias, value_bias, out_bias, down_bias]),
-            up_bias.reshape(ff // width, quarter),
-        ]
-    )
-    packed = jnp.pad(packed, ((0, -packed.shape[0] % 16), (0, -quarter % LANES)))
-    vectors, h1, og_all = first_norm_gather(tok, og, packed, n_ctx, planes)
+    rows_own = jnp.concatenate([out_own, down_own])
     h1 = h1.reshape(plane_rows, width)
     og_all = og_all.reshape(plane_rows, width)
     vectors = vectors[:, :, :quarter].astype(F32)
@@ -826,9 +906,15 @@
     qkv_shift = jnp.concatenate(head_part(bias_q) + [jnp.zeros((span,), F32)] + head_part(bias_v))
 
     qkv = (mm(h1, qkv_slice) + qkv_shift).astype(BF16)
-    qkv_heads = to_heads(qkv.reshape(n_ctx, seqs, local_rows, 3 * span), 3, planes, 5)
+    (qkv_heads,) = to_heads(qkv.reshape(n_ctx, seqs, local_rows, 3 * span), 3, planes, 5)
+    qkv_heads, rows_own = lax.optimization_barrier((qkv_heads, rows_own))
+    mixed_rows = lax.all_gather(rows_own, "fsdp", axis=0)
+    out_slice = mixed_rows[:, :HD].reshape(span, width)
+    down_slice = mixed_rows[:, HD:].reshape(ff_span, width)
     qkv_heads = qkv_heads.reshape(3, blocks, half, LANES)
     att_heads, att_exact, lse = attend_forward(order, qkv_heads, tile)
+    att_heads, up_own = lax.optimization_barrier((att_heads, up_own))
+    up_slice = lax.all_gather(up_own, "fsdp", axis=0, tiled=True)
     (att,) = to_tokens(att_heads.reshape(1, n_ctx, planes, local_rows, LANES), seqs, 6)
     att = att.reshape(plane_rows, span)
     branch = mm(att, out_slice).astype(BF16).reshape(n_ctx, rows, width)
@@ -842,32 +928,32 @@
     def reduce_own(part):
         return lax.psum_scatter(part, "fsdp", scatter_dimension=0, tiled=True)
 
+    down_part = mm_tn(act, og_all).astype(BF16)
+    og_all, unused = lax.optimization_barrier((og_all, down_part))
     (d_up,) = gelu_back(mm_nt(og_all, down_slice))
     d_up_low = d_up.astype(BF16)
-    down_part = mm_tn(act, og_all).astype(BF16)
     d_h2 = mm_nt(d_up_low, up_slice).astype(BF16).reshape(n_ctx, rows, width)
     up_part = mm_tn(h2, d_up_low).astype(BF16)
-    d_h2, down_part, up_part = lax.optimization_barrier((d_h2, down_part, up_part))
+    d_h2, unused = lax.optimization_barrier((d_h2, up_part))
     down_own_grad, up_own_grad = reduce_own(down_part), reduce_own(up_part)
     d_mixed, sums2, d_branch = second_norm_back(d_h2, mixed, og, gain2[None, :])
     d_branch = d_branch.reshape(plane_rows, width)
     d_att = mm_nt(d_branch, out_slice).astype(BF16)
-    d_att_heads = to_heads(d_att.reshape(n_ctx, seqs, local_rows, span), 1, planes, 7)
     out_w_part = mm_tn(att, d_branch).astype(BF16)
-    d_att_heads, out_w_part = lax.optimization_barrier((d_att_heads, out_w_part))
+    d_att, unused = lax.optimization_barrier((d_att, out_w_part))
     out_own_grad = reduce_own(out_w_part)
+    d_att_heads, block_out = to_heads(
+        d_att.reshape(n_ctx, seqs, local_rows, span), 1, planes, 7, (out_part, mixed, bias_d[None, :])
+    )
     d_heads = attend_backward(order, qkv_heads, d_att_heads.reshape(blocks, half, LANES), att_exact, lse, tile)
-    d_qkv, down_parts = to_tokens(
-        d_heads.reshape(3, n_ctx, planes, local_rows, LANES), seqs, 8, (down_own_grad,)
+    d_qkv, down_parts, up_parts = to_tokens(
+        d_heads.reshape(3, n_ctx, planes, local_rows, LANES), seqs, 8, (down_own_grad, up_own_grad)
     )
     d_qkv = d_qkv.reshape(plane_rows, 3 * span)
     qkv_part = mm_tn(h1, d_qkv).astype(BF16)
+    qkv_part, d_qkv = lax.optimization_barrier((qkv_part, d_qkv))
+    qkv_own_grad = reduce_own(qkv_part)
     d_h1 = mm_nt(d_qkv, qkv_slice).astype(BF16).reshape(n_ctx, rows, width)
-    d_h1, qkv_part = lax.optimization_barrier((d_h1, qkv_part))
-    qkv_own_grad = reduce_own(qkv_part)
-    grad_tok, block_out, sums1 = first_norm_back(
-        d_h1, out_part, tok, d_mixed, mixed, jnp.stack([gain1, bias_d])
-    )
 
     d_qkv_sum = jnp.sum(d_qkv.astype(F32), axis=0)
     d_up_sum = jnp.sum(d_up_low.astype(F32), axis=0).reshape(planes, ff_piece)
@@ -880,23 +966,28 @@
             full = lax.dynamic_update_slice(full, values[j * HD : (j + 1) * HD], (place,))
         return full[None, :width]
 
-    wide = jnp.concatenate([sums1, sums2, spread(d_qkv_sum[:span]), spread(d_qkv_sum[2 * span :])])
-    wide = wide.reshape(8, planes, quarter).transpose(1, 0, 2).reshape(planes, 8 * quarter)
+    wide = jnp.concatenate([sums2, spread(d_qkv_sum[:span]), spread(d_qkv_sum[2 * span :])])
+    wide = wide.reshape(6, planes, quarter).transpose(1, 0, 2).reshape(planes, 6 * quarter)
     flat = jnp.concatenate([wide, up_spread], axis=1)
     size = flat.shape[1]
-    flat = jnp.pad(flat, ((0, 0), (0, -size % (8 * LANES))))
-    totals = total_vectors(flat.reshape(planes, -1, LANES), n_ctx, 9).reshape(-1)
-    sums = totals[: 8 * quarter].reshape(8, quarter)
-    up_bias_grad = totals[8 * quarter : size]
-
-    up_parts, out_parts = gather_plane([up_own_grad, out_own_grad], n_ctx, 10)
-    (qkv_parts,) = gather_plane([qkv_own_grad], n_ctx, 11)
+    flat = jnp.pad(flat, ((0, 0), (0, -size % (8 * LANES)))).reshape(planes, -1, LANES)
+
+    grad_tok, out_parts, sums1, totals = first_norm_back(
+        d_h1, out_own_grad, flat, tok, d_mixed, gain1[None, :]
+    )
+    sums1 = sums1[:2, :quarter]
+    totals = totals.reshape(-1)
+    sums = totals[: 6 * quarter].reshape(6, quarter)
+    up_bias_grad = totals[6 * quarter : size]
+
     down_grad = down_parts.reshape(ff_quarter, width).astype(F32)
     block = quarter // 5
     up_pieces = [
         (j * ff_quarter + d * ff_piece, d, j * ff_piece, ff_piece) for j in range(planes) for d in range(n_ctx)
     ]
     up_grad = assemble(up_parts, up_pieces, ff, block)
+    out_parts, up_grad, qkv_own_grad = lax.optimization_barrier((out_parts, up_grad, qkv_own_grad))
+    (qkv_parts,) = gather_plane([qkv_own_grad], n_ctx, 9)
     qkv_pieces = [
         (k * width + (first[j] + d) * HD, d, k * span + j * HD, HD)
         for k in range(3)
@@ -922,19 +1013,19 @@
     return (
         back(block_out),
         back(grad_tok),
+        sums1[0],
+        sums1[1],
+        qkv_grad,
+        sums[4],
+        sums[5],
+        out_grad_own,
+        sums[2],
         sums[0],
         sums[1],
-        qkv_grad,
-        sums[6],
-        sums[7],
-        out_grad_own,
-        sums[4],
-        sums[2],
-        sums[3],
         up_grad,
         up_bias_grad,
         down_grad,
-        sums[5],
+        sums[3],
     )
 
 

time: 714 us -> 606 us (0.85)
  Pallas kernels: 539 us -> 414 us
  waiting for transfers between devices: 0.69 us -> 38.2 us
  blocking collectives: 32 us -> 0 us
    pallas_call x4 -> x3, Pallas kernels: 155 us -> 90.6 us  [the longest x2 53.2 us: to_heads(): pl.pallas_call(functools.partial(to_heads_kernel, kinds, planes, seqs, ch...]
    pallas_call x2 -> x1, Pallas kernels: 78.9 us -> 28.2 us  [gather_plane(): pl.pallas_call(functools.partial(gather_kernel, chips, count), out_shape=...]
    all_gather x1 -> x0, blocking collectives: 32 us -> none  [local(): out_slice = lax.all_gather(out_own, 'fsdp', axis=0, tiled=True)]
    all_gather x1, waiting for transfers between devices: 0.01 us -> 26.7 us  [local(): mixed_rows = lax.all_gather(rows_own, 'fsdp', axis=0)]
    all_gather x1, waiting for transfers between devices: 0.02 us -> 8.93 us  [local(): up_slice = lax.all_gather(up_own, 'fsdp', axis=0, tiled=True)]
    pallas_call x2, Pallas kernels: 85.2 us -> 93.3 us  [to_tokens(): pl.pallas_call(functools.partial(to_tokens_kernel, kinds, planes, seqs, n...]
    pallas_call x1, Pallas kernels: 50.7 us -> 43.5 us  [second_norm_back(): pl.pallas_call(functools.partial(third_kernel, chips), out_shape=(jax.Sha...]
  transfers between devices with their start and end apart: 9 -> 9, of which waited for: 0 -> 3; matrix products, arithmetic and copies ran while one was open for 12% -> 14% of each run, Pallas kernels for 71% -> 64%
where the time goes in v3:
time: 606 us; the launch traced here: 597 us
  Pallas kernels  414 us (68%)
  matrix products  67 us (11%)
  local copies, waits for them, and re-layouts  43.2 us (7%)
  waiting for transfers between devices  38.2 us (6%)
  between operations  17.1 us (3%)
  other arithmetic  11.9 us (2%)
    pallas_call x2, Pallas kernels, to_tokens(): pl.pallas_call(functools.partial(to_tokens_kernel, kinds, planes, seqs, n...  93.3 us
    pallas_call x2, Pallas kernels, to_heads(): pl.pallas_call(functools.partial(to_heads_kernel, kinds, planes, seqs, ch...  53.2 us
    pallas_call x1, Pallas kernels, first_norm_gather(): pl.pallas_call(functools.partial(first_kernel, chips, planes, width // pl...  44.3 us
    pallas_call x1, Pallas kernels, second_norm_back(): pl.pallas_call(functools.partial(third_kernel, chips), out_shape=(jax.Sha...  43.5 us
    pallas_call x1, Pallas kernels, second_norm_gather(): pl.pallas_call(functools.partial(second_kernel, chips), out_shape=(jax.Sh...  42.7 us
    pallas_call x1, Pallas kernels, first_norm_back(): pl.pallas_call(functools.partial(fourth_kernel, chips, planes), out_shape...  37.4 us
    pallas_call x1, Pallas kernels, attend_forward(): pl.pallas_call(functools.partial(forward_kernel, tile), out_shape=(jax.Sh...  28.4 us
    pallas_call x1, Pallas kernels, gather_plane(): pl.pallas_call(functools.partial(gather_kernel, chips, count), out_shape=...  28.2 us
  transfers between devices with their start and end apart: 9, of which 3 were waited for; matrix products, arithmetic and copies ran while one was open for 14% of the time, Pallas kernels for 64%

profile of v3, /device:TPU:0, one launch (start us, length us, event | category | flops | bytes accessed | tf_op | source)
XLA Modules:
  0.0 596.5 jit_solution(17813765510621794011)
XLA Ops:
  17.0 44.3 %norm_gather.1 = (bf16[4,16,512]{2,1,0:T(8,128)(2,1)}, bf16[8,128,1600]{2,1,0:T(8,128)(2,1)}, bf16[8,128,1600]{2,1,0:T(8,128)(2,1)}) custom-call(bf16[128,1600]{1,0:T(8,128)(2,1)} %bitcast.78, bf16[128,1600]{1,0:T(8,128)(2,1)} %bitcast.84, bf16[16,512]{1,0:T(8,128)(2,1)} %pad.10.vec_ref), custom_call_target="tpu_custom_call" | custom-call | tf_op jit(solution)/shard_map/norm_gather/pallas_call | solution.py:237
  66.9 6.9 %add_convert_fusion = bf16[1024,768]{1,0:T(8,128)(2,1)} fusion(bf16[1024,1600]{1,0:T(8,128)(2,1)} %bitcast.116, bf16[1600,768]{1,0:T(8,128)(2,1)} %all-gather.5.cloned.1.call-done, f32[768]{0:T(1024)S(1)} %concatenate.43), kind=kOutput, calls=%fused_computation.20 | convolution fusion | flops 2518155264 | bytes 7310336 | tf_op jit(solution)/shard_map/dot_general | solution.py:792
  73.8 30.1 %to_heads.2 = bf16[3,8,4,64,128]{4,3,2,1,0:T(8,128)(2,1)} custom-call(bf16[8,2,64,768]{3,2,1,0:T(8,128)(2,1)} %bitcast.99), custom_call_target="tpu_custom_call" | custom-call | flops 1 | bytes 1 | tf_op jit(solution)/shard_map/to_heads/pallas_call | solution.py:502
  107.7 28.4 %attend_forward.1 = (bf16[64,32,128]{2,1,0:T(8,128)(2,1)}, f32[128,2048]{1,0:T(8,128)}, f32[2,2048]{1,0:T(2,128)}) custom-call(s32[64]{0:T(128)} %pad_add_fusion.order_ref, bf16[3,64,32,128]{3,2,1,0:T(8,128)(2,1)} %bitcast.72), custom_call_target="tpu_custom_call" | custom-call | flops 1 | bytes 1 | tf_op jit(solution)/shard_map/attend_forward/pallas_call | solution.py:660
  137.9 26.4 %to_tokens.2 = bf16[8,2,64,256]{3,2,1,0:T(8,128)(2,1)} custom-call(bf16[1,8,4,64,128]{4,3,2,1,0:T(8,128)(2,1)} %bitcast.103), custom_call_target="tpu_custom_call" | custom-call | flops 1 | bytes 1 | tf_op jit(solution)/shard_map/to_tokens/pallas_call | solution.py:558
  164.3 26.7 %all-gather.9.cloned.1.call-done = bf16[1056,1600]{1,0:T(8,128)(2,1)} async-done(((bf16[264,1600]{1,0:T(8,128)(2,1)}), bf16[1056,1600]{1,0:T(8,128)(2,1)}) %all-gather.9.cloned.1.call-update) | async-done | bytes 3379216 | tf_op jit(solution)/shard_map/all_gather | solution.py:911
  195.3 3.5 copy.68
  198.8 42.7 %scatter_norm_gather.1 = (f32[128,1600]{1,0:T(8,128)}, bf16[8,128,1600]{2,1,0:T(8,128)(2,1)}) custom-call(bf16[8,128,1600]{2,1,0:T(8,128)(2,1)} %bitcast.74, bf16[128,1600]{1,0:T(8,128)(2,1)} %bitcast.79, f32[3,1600]{1,0:T(4,128)} %pad_maximum_fusion.2.vec_ref), custom_call_target="tpu_custom_call" | custom-call | flops 1 | bytes 1 | tf_op jit(solution)/shard_map/scatter_norm_gather/pallas_call | solution.py:264
  241.7 8.9 %all-gather.7.cloned.1.call-done = bf16[1600,800]{1,0:T(8,128)(2,1)} async-done(((bf16[400,800]{1,0:T(8,128)(2,1)}), bf16[1600,800]{1,0:T(8,128)(2,1)}) %all-gather.7.cloned.1.call-update) | async-done | bytes 2560016 | tf_op jit(solution)/shard_map/all_gather | solution.py:917
  250.7 6.2 %fusion.17 = f32[1024,800]{0,1:T(8,128)S(1)} fusion(bf16[1024,1600]{1,0:T(8,128)(2,1)} %bitcast.122, bf16[1600,800]{1,0:T(8,128)(2,1)} %all-gather.7.cloned.1.call-done), kind=kOutput, calls=%fused_computation.85 | convolution fusion | flops 2621440000 | bytes 9113600 | tf_op jit(solution)/shard_map/dot_general | solution.py:792
  258.6 5.4 convolution_convert_fusion.5
  264.0 7.5 %convert_reduce_fusion = (f32[800]{0:T(1024)S(1)}, bf16[1024,800]{0,1:T(8,128)(2,1)S(1)}) fusion(f32[1024,800]{0,1:T(8,128)} %copy-done.29, f32[800]{0:T(1024)S(1)} %add.252, bf16[1024,1600]{1,0:T(8,128)(2,1)} %bitcast.118, bf16[800,1600]{1,0:T(8,128)(2,1)S(1)} %bitcast.92), kind=kOutput, calls=%fused_computation.17 | convolution fusion | flops 2640280832 | bytes 10758400 | tf_op jit(solution)/shard_map/dot_general | solution.py:796
  272.7 5.2 convolution_convert_fusion.4
  279.3 5.9 convolution_convert_fusion
  285.2 3.5 copy.69
  288.7 43.5 %scatter_back_gather.1 = (f32[128,1600]{1,0:T(8,128)}, f32[4,1600]{1,0:T(4,128)}, bf16[8,128,1600]{2,1,0:T(8,128)(2,1)}) custom-call(bf16[8,128,1600]{2,1,0:T(8,128)(2,1)} %bitcast.77, f32[128,1600]{1,0:T(8,128)} %get-tuple-element.58.mixed_ref.refs_2_, bf16[128,1600]{1,0:T(8,128)(2,1)} %bitcast.85, f32[1,1600]{1,0:T(1,128)} %copy-done.12), custom_call_target="tpu_custom_call" | custom-call | flops 1 | bytes 1 | tf_op jit(solution)/shard_map/scatter_back_gather/pallas_call | solution.py:301
  332.2 4.2 convolution_convert_fusion.7
  336.5 7.9 %convolution_convert_fusion.2 = bf16[1024,1600]{0,1:T(8,128)(2,1)} fusion(bf16[800,1600]{1,0:T(8,128)(2,1)S(1)} %bitcast.93, f32[1024,800]{0,1:T(8,128)} %copy-done.29, f32[800]{0:T(1024)S(1)} %add.252), kind=kOutput, calls=%fused_computation.5 | convolution fusion | flops 2631270400 | bytes 9116800 | tf_op jit(solution)/shard_map/dot_general | solution.py:792
  344.4 5.7 copy.72
  350.0 3.9 convolution_convert_fusion.8
  354.0 23.1 %to_heads.3 = (bf16[1,8,4,64,128]{4,3,2,1,0:T(8,128)(2,1)}, bf16[128,1600]{1,0:T(8,128)(2,1)}) custom-call(bf16[8,2,64,256]{3,2,1,0:T(8,128)(2,1)} %bitcast.104, bf16[8,128,1600]{2,1,0:T(8,128)(2,1)} %bitcast.76, f32[128,1600]{1,0:T(8,128)} %get-tuple-element.58.mixed_ref.refs_2_, f32[1,1600]{1,0:T(1,128)} %broadcast_in_dim_reshape_squeeze.7.refs_3_), custom_call_target="tpu_custom_call" | custom-call | flops 1 | bytes 1 | tf_op jit(solution)/shard_map/to_heads/pallas_call | solution.py:502
  377.0 26.4 %attend_backward.1 = bf16[3,64,32,128]{3,2,1,0:T(8,128)(2,1)} custom-call(s32[64]{0:T(128)} %pad_add_fusion.order_ref, bf16[3,64,32,128]{3,2,1,0:T(8,128)(2,1)} %bitcast.73, bf16[64,32,128]{2,1,0:T(8,128)(2,1)} %bitcast.102, f32[128,2048]{1,0:T(8,128)} %get-tuple-element.63.att_ref, f32[2,2048]{1,0:T(2,128)} %get-tuple-element.64.lse_ref), custom_call_target="tpu_custom_call" | custom-call | flops 1 | bytes 1 | tf_op jit(solution)/shard_map/attend_backward/pallas_call | solution.py:759
  403.4 66.9 %to_tokens.3 = (bf16[8,2,64,768]{3,2,1,0:T(8,128)(2,1)}, bf16[8,200,1600]{2,1,0:T(8,128)(2,1)}, bf16[8,400,800]{2,1,0:T(8,128)(2,1)}) custom-call(bf16[3,8,4,64,128]{4,3,2,1,0:T(8,128)(2,1)} %bitcast.81, bf16[200,1600]{1,0:T(8,128)(2,1)} %reduce-scatter.13.cloned.1.call-done.refs_1_, bf16[400,800]{1,0:T(8,128)(2,1)} %reduce-scatter.7.cloned.1.call-done.refs_2_), custom_call_target="tpu_custom_call" | custom-call | flops 1 | bytes 1 | tf_op jit(solution)/shard_map/to_tokens/pallas_call | solution.py:558
  470.3 6.7 %convolution_convert_fusion.6 = bf16[1600,768]{1,0:T(8,128)(2,1)} fusion(bf16[1024,1600]{1,0:T(8,128)(2,1)} %bitcast.117, bf16[1024,768]{1,0:T(8,128)(2,1)} %bitcast.96), kind=kOutput, calls=%fused_computation.9 | convolution fusion | flops 2517811200 | bytes 7307264 | tf_op jit(solution)/shard_map/dot_general | solution.py:800
  482.4 5.0 convolution_convert_fusion.1
  487.4 3.7 copy.74
  491.1 37.4 %scatter_back.1 = (f32[128,1600]{1,0:T(8,128)}, bf16[8,64,1600]{2,1,0:T(8,128)(2,1)}, f32[8,512]{1,0:T(8,128)}, f32[32,128]{1,0:T(8,128)}) custom-call(bf16[8,128,1600]{2,1,0:T(8,128)(2,1)} %bitcast.75, bf16[64,1600]{1,0:T(8,128)(2,1)} %reduce-scatter.9.cloned.1.call-done.outw_ref, f32[4,32,128]{2,1,0:T(8,128)} %bitcast.109, bf16[128,1600]{1,0:T(8,128)(2,1)} %bitcast.80, ...), custom_call_target="tpu_custom_call" | custom-call | flops 1 | bytes 1 | tf_op jit(solution)/shard_map/scatter_back/pallas_call | solution.py:399
  532.6 9.4 %assemble.2 = f32[400,6400]{1,0:T(8,128)} custom-call(bf16[8,400,800]{2,1,0:T(8,128)(2,1)} %get-tuple-element.72.part_ref), custom_call_target="tpu_custom_call" | custom-call | tf_op jit(solution)/shard_map/assemble/pallas_call | solution.py:780
  543.4 5.2 bitcast_convert_fusion
  548.7 3.0 collective-permute-start.1
  552.3 28.2 %gather_plane.1.part_ref = bf16[8,400,768]{2,1,0:T(8,128)(2,1)} custom-call(bf16[400,768]{1,0:T(8,128)(2,1)} %reduce-scatter.11.cloned.1.call-done.refs_0_), custom_call_target="tpu_custom_call" | custom-call | flops 1 | bytes 1 | tf_op jit(solution)/shard_map/gather_plane/pallas_call | solution.py:438
  580.6 7.2 %assemble.3 = f32[400,4800]{1,0:T(8,128)} custom-call(bf16[8,400,768]{2,1,0:T(8,128)(2,1)} %gather_plane.1.part_ref), custom_call_target="tpu_custom_call" | custom-call | tf_op jit(solution)/shard_map/assemble/pallas_call | solution.py:780
  (163 shorter events, 40.3 us)
Async XLA Ops:
  7.2 6.0 %copy-start.27 = (s32[5]{0:T(128)S(1)}, s32[5]{0:T(128)}, u32[]{:S(2)}) copy-start(s32[5]{0:T(128)} %constant.93.clone) | copy-start | bytes 64
  7.2 7.3 %copy-start.16 = (bf16[400]{0:T(512)(128)(2,1)S(1)}, bf16[400]{0:T(512)(128)(2,1)}, u32[]{:S(2)}) copy-start(bf16[400]{0:T(512)(128)(2,1)} %param.21) | copy-start | bytes 2404
  7.2 7.3 %copy-start.17 = (bf16[400]{0:T(512)(128)(2,1)S(1)}, bf16[400]{0:T(512)(128)(2,1)}, u32[]{:S(2)}) copy-start(bf16[400]{0:T(512)(128)(2,1)} %param.22) | copy-start | bytes 2404
  7.2 7.3 %copy-start.18 = (bf16[400]{0:T(512)(128)(2,1)S(1)}, bf16[400]{0:T(512)(128)(2,1)}, u32[]{:S(2)}) copy-start(bf16[400]{0:T(512)(128)(2,1)} %param.24) | copy-start | bytes 2404
  7.2 7.3 %copy-start.19 = (bf16[400]{0:T(512)(128)(2,1)S(1)}, bf16[400]{0:T(512)(128)(2,1)}, u32[]{:S(2)}) copy-start(bf16[400]{0:T(512)(128)(2,1)} %param.25) | copy-start | bytes 2404
  7.3 7.3 %copy-start.20 = (bf16[400]{0:T(512)(128)(2,1)S(1)}, bf16[400]{0:T(512)(128)(2,1)}, u32[]{:S(2)}) copy-start(bf16[400]{0:T(512)(128)(2,1)} %param.27) | copy-start | bytes 2404
  7.3 7.3 %copy-start.21 = (bf16[400]{0:T(512)(128)(2,1)S(1)}, bf16[400]{0:T(512)(128)(2,1)}, u32[]{:S(2)}) copy-start(bf16[400]{0:T(512)(128)(2,1)} %param.28) | copy-start | bytes 2404
  7.3 7.3 %copy-start.22 = (bf16[400]{0:T(512)(128)(2,1)S(1)}, bf16[400]{0:T(512)(128)(2,1)}, u32[]{:S(2)}) copy-start(bf16[400]{0:T(512)(128)(2,1)} %param.29) | copy-start | bytes 2404
  7.3 7.4 %copy-start.23 = (bf16[400]{0:T(512)(128)(2,1)S(1)}, bf16[400]{0:T(512)(128)(2,1)}, u32[]{:S(2)}) copy-start(bf16[400]{0:T(512)(128)(2,1)} %param.33) | copy-start | bytes 2404
  7.3 7.4 %copy-start.15 = (bf16[1600]{0:T(1024)(128)(2,1)S(1)}, bf16[1600]{0:T(1024)(128)(2,1)}, u32[]{:S(2)}) copy-start(bf16[1600]{0:T(1024)(128)(2,1)} %param.31) | copy-start | bytes 9604
  7.3 7.5 %copy-start.9 = (bf16[64,2,1600]{2,1,0:T(2,128)(2,1)S(1)}, bf16[64,2,1600]{2,1,0:T(2,128)(2,1)}, u32[]{:S(2)}) copy-start(bf16[64,2,1600]{2,1,0:T(2,128)(2,1)} %param.18) | copy-start | bytes 1228804
  7.3 8.3 %copy-start.10 = (bf16[64,2,1600]{2,1,0:T(2,128)(2,1)S(1)}, bf16[64,2,1600]{2,1,0:T(2,128)(2,1)}, u32[]{:S(2)}) copy-start(bf16[64,2,1600]{2,1,0:T(2,128)(2,1)} %param.20) | copy-start | bytes 1228804
  7.3 59.6 %all-gather.5.cloned.1.call-start = ((), (), s32[]{:S(2)}) async-start(), calls=%async_computation.4 | async-start | bytes 3072000 | tf_op jit(solution)/shard_map/all_gather | solution.py:866
  10.6 180.4 %all-gather.9.cloned.1.call-start = ((), (), s32[]{:S(2)}) async-start(), calls=%async_computation.9 | async-start | bytes 4392960 | tf_op jit(solution)/shard_map/all_gather | solution.py:911
  10.7 53.2 %collective-permute-start = (bf16[64,1600]{1,0:T(8,128)(2,1)S(1)}, bf16[64,1600]{1,0:T(8,128)(2,1)S(1)}, u32[]{:S(2)}, u32[]{:S(2)}) collective-permute-start(bf16[64,1600]{1,0:T(8,128)(2,1)S(1)} %slice.122), channel_id=1, source_target_pairs={{1,0},{2,1},{3,2},{5,4},{6,5},{7,6},{9,8},{10,9},{11,10},{13,12},{... | collective-permute-start | bytes 614408 | tf_op jit(solution)/shard_map/ppermute | solution.py:867
  73.8 30.2 %copy-start.26 = (s32[32]{0:T(128)S(1)}, s32[32]{0:T(128)}, u32[]{:S(2)}) copy-start(s32[32]{0:T(128)} %param.19) | copy-start | bytes 388
  104.0 146.7 %all-gather.7.cloned.1.call-start = ((), (), s32[]{:S(2)}) async-start(), calls=%async_computation.5 | async-start | bytes 3584000 | tf_op jit(solution)/shard_map/all_gather | solution.py:917
  136.2 267.3 %reduce-scatter.7.cloned.1.call-start = ((), (), s32[]{:S(2)}) async-start(), calls=%async_computation.6 | async-start | bytes 3584000 | tf_op jit(solution)/shard_map/reduce_scatter | solution.py:929
  137.0 58.2 %copy-start.12 = (f32[1,1600]{1,0:T(1,128)}, f32[1,1600]{1,0:T(1,128)S(1)}, u32[]{:S(2)}) copy-start(f32[1,1600]{1,0:T(1,128)S(1)} %stack_reshape_squeeze.9.vec_ref) | copy-start | bytes 19204
  198.8 42.7 %copy-start = (bf16[1056,1600]{1,0:T(8,128)(2,1)S(1)}, bf16[1056,1600]{1,0:T(8,128)(2,1)}, u32[]{:S(2)}) copy-start(bf16[1056,1600]{1,0:T(8,128)(2,1)} %all-gather.9.cloned.1.call-done) | copy-start | bytes 10137604
  241.7 22.3 %copy-start.4 = (bf16[4,200,1600]{2,1,0:T(8,128)(2,1)}, bf16[4,200,1600]{2,1,0:T(8,128)(2,1)S(1)}, u32[]{:S(2)}) copy-start(bf16[4,200,1600]{2,1,0:T(8,128)(2,1)S(1)} %slice.157) | copy-start | bytes 7680004
  250.7 8.0 %copy-start.24 = (bf16[8,128,1600]{2,1,0:T(8,128)(2,1)S(1)}, bf16[8,128,1600]{2,1,0:T(8,128)(2,1)}, u32[]{:S(2)}) copy-start(bf16[8,128,1600]{2,1,0:T(8,128)(2,1)} %get-tuple-element.47) | copy-start | bytes 9830404
  264.0 8.7 %copy-start.25 = (bf16[8,128,1600]{2,1,0:T(8,128)(2,1)S(1)}, bf16[8,128,1600]{2,1,0:T(8,128)(2,1)}, u32[]{:S(2)}) copy-start(bf16[8,128,1600]{2,1,0:T(8,128)(2,1)} %get-tuple-element.54) | copy-start | bytes 9830404
  278.0 125.5 %reduce-scatter.13.cloned.1.call-start = ((), (), s32[]{:S(2)}) async-start(), calls=%async_computation.10 | async-start | bytes 3328000
  278.6 212.6 %reduce-scatter.9.cloned.1.call-start = ((), (), s32[]{:S(2)}) async-start(), calls=%async_computation.7 | async-start | bytes 1064960 | tf_op jit(solution)/shard_map/reduce_scatter | solution.py:929
  288.7 43.5 %copy-start.3 = (bf16[8,2,64,256]{3,2,1,0:T(8,128)(2,1)S(1)}, bf16[8,2,64,256]{3,2,1,0:T(8,128)(2,1)}, u32[]{:S(2)}) copy-start(bf16[8,2,64,256]{3,2,1,0:T(8,128)(2,1)} %to_tokens.2) | copy-start | bytes 1572868
  336.4 212.2 %reduce-scatter.11.cloned.1.call-start = ((), (), s32[]{:S(2)}) async-start(), calls=%async_computation.8 | async-start | bytes 3072000 | tf_op jit(solution)/shard_map/reduce_scatter | solution.py:929
  470.3 8.3 %copy-start.11 = (bf16[128,1600]{1,0:T(8,128)(2,1)S(1)}, bf16[128,1600]{1,0:T(8,128)(2,1)}, u32[]{:S(2)}) copy-start(bf16[128,1600]{1,0:T(8,128)(2,1)} %get-tuple-element.61) | copy-start | bytes 1228804
  532.6 10.8 %slice-start = ((s8[5324800]{0:T(1024)(128)(4,1)}), s8[4194304]{0:T(1024)(128)(4,1)S(1)}, s32[]{:S(2)}) async-start(s8[5324800]{0:T(1024)(128)(4,1)} %bitcast.82), calls=%async_computation.11 | async-start | bytes 8388608
  532.6 10.8 %slice-start.1 = ((s8[5324800]{0:T(1024)(128)(4,1)}), s8[1130496]{0:T(1024)(128)(4,1)S(1)}, s32[]{:S(2)}) async-start(s8[5324800]{0:T(1024)(128)(4,1)} %bitcast.82), calls=%async_computation.12 | async-start | bytes 2260992
  543.4 8.2 %copy-start.14 = (f32[32,128]{1,0:T(8,128)S(1)}, f32[32,128]{1,0:T(8,128)}, u32[]{:S(2)}) copy-start(f32[32,128]{1,0:T(8,128)} %get-tuple-element.75) | copy-start | bytes 49156
  548.7 39.1 %collective-permute-start.1 = (bf16[64,1600]{1,0:T(8,128)(2,1)S(1)}, bf16[64,1600]{1,0:T(8,128)(2,1)S(1)}, u32[]{:S(2)}, u32[]{:S(2)}) collective-permute-start(bf16[64,1600]{1,0:T(8,128)(2,1)S(1)} %constant_dynamic-slice_fusion), channel_id=1, source_target_pairs={{0,1},{1,2},{2,3},{4,5},{5,6},{6,7},{8,9},{9,10},{10,11},{12,13},{... | collective-permute-start | bytes 614408 | tf_op jit(solution)/shard_map/ppermute | solution.py:1001
  (10 other events, 33.2 us)
Sparse Core Ops, SparseCore 0:
  10.7 56.1 all-gather.4
  104.1 86.8 all-gather.8
  193.2 57.4 all-gather.6
  278.1 54.7 reduce-scatter.6
  335.1 62.5 reduce-scatter.12
  399.8 34.8 reduce-scatter.8
  477.2 51.0 reduce-scatter.10

commit v4 on v3

v4 whole, which is shorter than its diff:
```python
import functools
import math

import jax
import jax.numpy as jnp
from jax import lax
from jax.experimental import pallas as pl
from jax.experimental.pallas import tpu as pltpu
from jax.sharding import PartitionSpec as P

HD = 64
LANES = 128
NORM_EPS = 1e-05
NEG_BIG = -1e30
MESH = pl.DeviceIdType.MESH
F32 = jnp.float32
BF16 = jnp.bfloat16
ANY = pl.BlockSpec(memory_space=pl.ANY)
VMEM = pl.BlockSpec(memory_space=pltpu.VMEM)
DMA = pltpu.SemaphoreType.DMA
VMEM_LIMIT = 56 * 1024 * 1024
SMALL = pl.CostEstimate(flops=1, bytes_accessed=1, transcendentals=0)


def params(cid=None):
    if cid is None:
        return pltpu.CompilerParams(vmem_limit_bytes=VMEM_LIMIT)
    return pltpu.CompilerParams(
        collective_id=cid, has_side_effects=True, vmem_limit_bytes=VMEM_LIMIT
    )


def plane_peers(chips):
    me = lax.axis_index("ctx")
    core = lax.rem(me, 2)
    chip = me // 2
    sibling = chip * 2 + 1 - core
    if chips == 4:
        across_x = chip + 1 - 2 * lax.rem(chip, 2)
        across_y = lax.rem(chip + 2, 4)
        corner = lax.rem(across_x + 2, 4)
        first = across_x * (1 - core) + across_y * core
        second = across_y * (1 - core) + across_x * core
        to = come = [first * 2 + core, second * 2 + core, corner * 2 + core]
    else:
        to = [lax.rem(chip + k, chips) * 2 + core for k in range(1, chips)]
        come = [lax.rem(chip + chips - k, chips) * 2 + core for k in range(1, chips)]
    return me, core, chip, sibling, to, come


def greet(plane=(), across=()):
    barrier = pltpu.get_barrier_semaphore()
    for peer in plane:
        pl.semaphore_signal(barrier, inc=1, device_id={"ctx": peer}, device_id_type=MESH)
    for peer in across:
        pl.semaphore_signal(barrier, inc=1, device_id={"fsdp": peer}, device_id_type=MESH)
    pl.semaphore_wait(barrier, len(plane) + len(across))


def other_planes(planes):
    me = lax.axis_index("fsdp")
    return me, [lax.rem(me + k, planes) for k in range(1, planes)]


def send(src, dst, send_sem, recv_sem, axis, peer):
    copy = pltpu.make_async_remote_copy(
        src_ref=src,
        dst_ref=dst,
        send_sem=send_sem,
        recv_sem=recv_sem,
        device_id={axis: peer},
        device_id_type=MESH,
    )
    copy.start()
    return copy


def plane_gather_start(owns, alls, sems, chips):
    far_send, far_recv, near_send, near_recv, local_sem = sems
    me, core, chip, sibling, to, come = plane_peers(chips)
    direct = 2 if chips == 4 else chips - 1
    last = chips - 1
    far, near, local = [], [], []
    for i, (own_ref, all_ref) in enumerate(zip(owns, alls)):
        far.append(
            [
                send(own_ref, all_ref.at[me], far_send.at[i, k], far_recv.at[i, k], "ctx", to[k])
                for k in range(direct)
            ]
        )
        near.append(send(own_ref, all_ref.at[me], near_send.at[i, last], near_recv.at[i, last], "ctx", sibling))
        copy = pltpu.make_async_copy(own_ref, all_ref.at[me], local_sem.at[i])
        copy.start()
        local.append(copy)
    return far, near, local


def plane_gather_finish(started, alls, sems, chips):
    far_send, far_recv, near_send, near_recv, local_sem = sems
    me, core, chip, sibling, to, come = plane_peers(chips)
    far, near, local = started
    near = list(near)

    def pass_on(i, all_ref, k):
        far[i][k].wait_recv()
        block = all_ref.at[come[k]]
        if chips == 4 and k == 0:
            far[i].append(send(block, block, far_send.at[i, 2], far_recv.at[i, 2], "ctx", to[1]))
        near.append(send(block, block, near_send.at[i, k], near_recv.at[i, k], "ctx", sibling))

    direct = 2 if chips == 4 else chips - 1
    for i, all_ref in enumerate(alls):
        for k in range(direct):
            pass_on(i, all_ref, k)
    for i, all_ref in enumerate(alls):
        for k in range(direct, chips - 1):
            pass_on(i, all_ref, k)
    for group in far:
        for copy in group:
            copy.wait_send()
    for copy in near + local:
        copy.wait()


def plane_gather(owns, alls, sems, chips):
    plane_gather_finish(plane_gather_start(owns, alls, sems, chips), alls, sems, chips)


def plane_scatter(block_of, mine, paired, arrived, sems, chips):
    far_send, far_recv, near_send, near_recv, local_sem = sems
    me, core, chip, sibling, to, come = plane_peers(chips)
    targets = to + [me]
    order = [2, 1, 0, 3] if chips == 4 else list(range(chips))
    near, local = [None] * chips, [None] * chips
    crossed = [1, 0, 2, 3] if chips == 4 else list(range(chips))
    for k in order:
        other = targets[crossed[k]] + 1 - 2 * core
        near[k] = send(block_of(other), paired.at[k], near_send.at[k], near_recv.at[k], "ctx", sibling)
        local[k] = pltpu.make_async_copy(block_of(targets[k]), mine.at[k], local_sem.at[k])
        local[k].start()

    def both(k):
        local[k].wait()
        near[k].wait_recv()
        return mine[k].astype(F32) + paired[k].astype(F32)

    def dispatch(k, target):
        return send(mine.at[k], arrived.at[k], far_send.at[k], far_recv.at[k], "ctx", target)

    far = [None] * (chips - 1)
    if chips == 4:
        mine[2] = both(2).astype(BF16)
        far[2] = dispatch(2, to[0])
        mine[0] = both(0).astype(BF16)
        far[0] = dispatch(0, to[0])
        partial = both(1)
        far[2].wait_recv()
        mine[1] = (partial + arrived[2].astype(F32)).astype(BF16)
        far[1] = dispatch(1, to[1])
        total = both(3)
        arriving = [0, 1]
    else:
        for k in range(chips - 1):
            mine[k] = both(k).astype(BF16)
            far[k] = dispatch(k, to[k])
        total = both(chips - 1)
        arriving = range(chips - 1)
    for k in arriving:
        far[k].wait_recv()
        total = total + arrived[k].astype(F32)
    for copy in far + near:
        copy.wait_send()
    return total


def gather_sems(chips, count=1):
    return [DMA((count, chips - 1))] * 2 + [DMA((count, chips))] * 2 + [DMA((count,))]


def scatter_scratch(chips, *block):
    return [
        pltpu.VMEM((chips,) + block, BF16),
        pltpu.VMEM((chips,) + block, BF16),
        pltpu.VMEM((chips - 1,) + block, BF16),
        DMA((chips - 1,)),
        DMA((chips - 1,)),
        DMA((chips,)),
        DMA((chips,)),
        DMA((chips,)),
    ]


def normalize(values):
    average = jnp.mean(values, axis=-1, keepdims=True)
    centered = values - average
    variance = jnp.mean(centered * centered, axis=-1, keepdims=True)
    inverse = lax.rsqrt(variance + NORM_EPS)
    return centered * inverse, inverse


def norm_backward(grad, gain, unit, inverse):
    scaled = grad * gain
    first = jnp.mean(scaled, axis=-1, keepdims=True)
    second = jnp.mean(scaled * unit, axis=-1, keepdims=True)
    return (scaled - first - unit * second) * inverse


def first_kernel(
    chips,
    planes,
    seqs,
    quarter,
    tok_ref,
    og_ref,
    vec_ref,
    weight_ref,
    vecs_ref,
    ogs_ref,
    h1_ref,
    weights_ref,
    own,
    column,
    v_send,
    v_recv,
    v_local,
    h_send,
    h_recv,
    w_send,
    w_recv,
    w_local,
    *sems,
):
    me, core, chip, sibling, to, come = plane_peers(chips)
    plane, others = other_planes(planes)
    pairs = planes // seqs
    rows = own.shape[0] // seqs
    greet(to + [sibling], others)
    og_sems, h1_sems = sems[:5], [sems[5 + 5 * k : 10 + 5 * k] for k in range(planes)]
    copies = [
        send(vec_ref, vecs_ref.at[plane], v_send.at[k], v_recv.at[k], "fsdp", peer) for k, peer in enumerate(others)
    ]
    local = pltpu.make_async_copy(vec_ref, vecs_ref.at[plane], v_local)
    local.start()
    og_started = plane_gather_start([og_ref], [ogs_ref], og_sems, chips)
    unit, inverse = normalize(tok_ref[...].astype(F32))
    for copy in copies + [local]:
        copy.wait()
    lines = quarter // LANES + 1

    def vector(k):
        pieces = []
        for j in range(planes):
            for line in range(lines):
                size = min(LANES, quarter - line * LANES)
                if size:
                    row = k * lines + line
                    pieces.append(vecs_ref[j, row : row + 1, :size].astype(F32))
        return jnp.concatenate(pieces, axis=1)

    own[...] = (unit * vector(0) + vector(1)).astype(BF16)

    def half_of(peer):
        return own.at[pl.ds(pl.multiple_of(peer // pairs * rows, rows), rows)]

    halves = [
        send(half_of(peer), column.at[k], h_send.at[k], h_recv.at[k], "fsdp", peer) for k, peer in enumerate(others)
    ]
    weights = [
        send(weight_ref.at[lax.rem(peer, pairs)], weights_ref.at[plane], w_send.at[k], w_recv.at[k], "fsdp", peer)
        for k, peer in enumerate(others)
    ]
    weights.append(pltpu.make_async_copy(weight_ref.at[lax.rem(plane, pairs)], weights_ref.at[plane], w_local))
    weights[-1].start()
    sources = [plane] + [lax.rem(plane + planes - k, planes) for k in range(1, planes)]
    blocks = [half_of(plane)] + [column.at[k] for k in range(planes - 1)]
    started = [plane_gather_start([blocks[0]], [h1_ref.at[sources[0]]], h1_sems[0], chips)]
    plane_gather_finish(og_started, [ogs_ref], og_sems, chips)
    for k in range(1, planes):
        halves[k - 1].wait_recv()
        started.append(plane_gather_start([blocks[k]], [h1_ref.at[sources[k]]], h1_sems[k], chips))
    for k in range(planes):
        plane_gather_finish(started[k], [h1_ref.at[sources[k]]], h1_sems[k], chips)
    for copy in halves:
        copy.wait_send()
    for copy in weights:
        copy.wait()


def first_norm_gather(tok, og, vec, weight, n_ctx, planes, seqs):
    rows, width = tok.shape
    chips, half = n_ctx // 2, rows // seqs
    return pl.pallas_call(
        functools.partial(first_kernel, chips, planes, seqs, width // planes),
        out_shape=(
            jax.ShapeDtypeStruct((planes,) + vec.shape, BF16),
            jax.ShapeDtypeStruct((n_ctx, rows, width), BF16),
            jax.ShapeDtypeStruct((planes, n_ctx, half, width), BF16),
            jax.ShapeDtypeStruct((planes,) + weight.shape[1:], BF16),
        ),
        in_specs=[VMEM, ANY, VMEM, ANY],
        out_specs=(VMEM, ANY, ANY, ANY),
        scratch_shapes=[
            pltpu.VMEM((rows, width), BF16),
            pltpu.VMEM((planes - 1, half, width), BF16),
            DMA((planes - 1,)),
            DMA((planes - 1,)),
            DMA,
            DMA((planes - 1,)),
            DMA((planes - 1,)),
            DMA((planes - 1,)),
            DMA((planes - 1,)),
            DMA,
        ]
        + gather_sems(chips)
        + gather_sems(chips) * planes,
        compiler_params=params(0),
        cost_estimate=SMALL,
        name="norm_gather",
    )(tok, og, vec, weight)


def second_kernel(chips, part_ref, tok_ref, vec_ref, mixed_ref, all_ref, own, *scratch):
    me, core, chip, sibling, to, come = plane_peers(chips)
    greet(to + [sibling])
    total = plane_scatter(lambda c: part_ref.at[c], *scratch[:3], scratch[3:8], chips)
    mixed = tok_ref[...].astype(F32) + total + vec_ref[2:3, :]
    mixed_ref[...] = mixed
    unit, inverse = normalize(mixed)
    own[...] = (unit * vec_ref[0:1, :] + vec_ref[1:2, :]).astype(BF16)
    plane_gather([own], [all_ref], scratch[8:], chips)


def second_norm_gather(part, tok, vecs):
    n_ctx, rows, width = part.shape
    chips = n_ctx // 2
    return pl.pallas_call(
        functools.partial(second_kernel, chips),
        out_shape=(
            jax.ShapeDtypeStruct((rows, width), F32),
            jax.ShapeDtypeStruct((n_ctx, rows, width), BF16),
        ),
        in_specs=[ANY, VMEM, VMEM],
        out_specs=(VMEM, ANY),
        scratch_shapes=[pltpu.VMEM((rows, width), BF16)]
        + scatter_scratch(chips, rows, width)
        + gather_sems(chips),
        compiler_params=params(1),
        cost_estimate=SMALL,
        name="scatter_norm_gather",
    )(part, tok, vecs)


def third_kernel(chips, part_ref, mixed_ref, og_ref, vec_ref, dmixed_ref, sums_ref, all_ref, own, *scratch):
    me, core, chip, sibling, to, come = plane_peers(chips)
    greet(to + [sibling])
    unit, inverse = normalize(mixed_ref[...])
    grad = plane_scatter(lambda c: part_ref.at[c], *scratch[:3], scratch[3:8], chips)
    out_grad = og_ref[...].astype(F32)
    dmixed = out_grad + norm_backward(grad, vec_ref[0:1, :], unit, inverse)
    dmixed_ref[...] = dmixed
    low = dmixed.astype(BF16)
    own[...] = low
    sums_ref[0:1, :] = jnp.sum(grad * unit, axis=0, keepdims=True)
    sums_ref[1:2, :] = jnp.sum(grad, axis=0, keepdims=True)
    sums_ref[2:3, :] = jnp.sum(low.astype(F32), axis=0, keepdims=True)
    sums_ref[3:4, :] = jnp.sum(out_grad, axis=0, keepdims=True)
    plane_gather([own], [all_ref], scratch[8:], chips)


def second_norm_back(part, mixed, og, vecs):
    n_ctx, rows, width = part.shape
    chips = n_ctx // 2
    return pl.pallas_call(
        functools.partial(third_kernel, chips),
        out_shape=(
            jax.ShapeDtypeStruct((rows, width), F32),
            jax.ShapeDtypeStruct((4, width), F32),
            jax.ShapeDtypeStruct((n_ctx, rows, width), BF16),
        ),
        in_specs=[ANY, VMEM, VMEM, VMEM],
        out_specs=(VMEM, VMEM, ANY),
        scratch_shapes=[pltpu.VMEM((rows, width), BF16)]
        + scatter_scratch(chips, rows, width)
        + gather_sems(chips),
        compiler_params=params(2),
        cost_estimate=SMALL,
        name="scatter_back_gather",
    )(part, mixed, og, vecs)


def fourth_kernel(
    chips,
    planes,
    seqs,
    part_ref,
    qkv_ref,
    outw_ref,
    flat_ref,
    tok_ref,
    dmixed_ref,
    vec_ref,
    grad_ref,
    qkv_all,
    outw_all,
    sums_ref,
    flat_out,
    q_arrived,
    q_own,
    q_send,
    q_recv,
    q_local,
    rows_own,
    rows_arrived,
    r_send,
    r_recv,
    small,
    small_own,
    small_z,
    small_c,
    flat_own,
    flat_z,
    flat_c,
    z_send,
    z_recv,
    c_send,
    c_recv,
    *scratch,
):
    n_ctx = 2 * chips
    pairs = planes // seqs
    me, core, chip, sibling, to, come = plane_peers(chips)
    plane, others = other_planes(planes)
    around = [lax.rem(me + k, n_ctx) for k in range(1, n_ctx)]
    greet(around, others)
    scatter, rest_sems, qkv_sems = scratch[:8], scratch[8:13], scratch[13:]

    pushed = [
        send(qkv_ref.at[peer], q_arrived.at[plane], q_send.at[k], q_recv.at[k], "fsdp", peer)
        for k, peer in enumerate(others)
    ]
    held = pltpu.make_async_copy(qkv_ref.at[plane], q_arrived.at[plane], q_local)
    held.start()
    flat_sent = [
        send(flat_ref.at[peer], flat_z.at[k], z_send.at[0, k], z_recv.at[0, k], "fsdp", peer)
        for k, peer in enumerate(others)
    ]
    unit, inverse = normalize(tok_ref[...].astype(F32))
    total = plane_scatter(lambda c: part_ref.at[:, c], *scatter[:3], scatter[3:], chips)
    rows_own[...] = total.astype(BF16)
    rows_sent = [
        send(rows_own.at[peer], rows_arrived.at[plane], r_send.at[k], r_recv.at[k], "fsdp", peer)
        for k, peer in enumerate(others)
    ]
    rows_arrived[plane] = rows_own[plane]
    rest_started = plane_gather_start([outw_ref], [outw_all], rest_sems, chips)
    for copy in pushed + [held]:
        copy.wait()
    for pair in range(pairs):
        terms = [q_arrived[seq * pairs + pair].astype(F32) for seq in range(seqs)]
        q_own[pair] = sum(terms[1:], terms[0]).astype(BF16)
    qkv_started = plane_gather_start([q_own], [qkv_all], qkv_sems, chips)
    plane_gather_finish(rest_started, [outw_all], rest_sems, chips)

    for copy in rows_sent:
        copy.wait()
    halves = []
    for seq in range(seqs):
        terms = [rows_arrived[seq * pairs + pair].astype(F32) for pair in range(pairs)]
        halves.append(sum(terms[1:], terms[0]))
    grad = jnp.concatenate(halves, axis=0)
    sums = jnp.concatenate(
        [jnp.sum(grad * unit, axis=0, keepdims=True), jnp.sum(grad, axis=0, keepdims=True)], axis=0
    )
    quarter = sums.shape[1] // planes
    small[...] = jnp.zeros_like(small)
    for j in range(planes):
        small[j, 0:2, 0:quarter] = sums[:, j * quarter : (j + 1) * quarter]
    small_sent = [
        send(small.at[peer], small_z.at[k], z_send.at[1, k], z_recv.at[1, k], "fsdp", peer)
        for k, peer in enumerate(others)
    ]
    grad_ref[...] = dmixed_ref[...] + norm_backward(grad, vec_ref[0:1, :], unit, inverse)
    small_total = small[plane]
    flat_total = flat_ref[plane]
    for k in range(planes - 1):
        flat_sent[k].wait()
        small_sent[k].wait()
        small_total = small_total + small_z[k]
        flat_total = flat_total + flat_z[k]
    small_own[...] = small_total
    flat_own[...] = flat_total
    sent = []
    for k, peer in enumerate(around):
        sent.append(send(small_own, small_c.at[k], c_send.at[0, k], c_recv.at[0, k], "ctx", peer))
        sent.append(send(flat_own, flat_c.at[k], c_send.at[1, k], c_recv.at[1, k], "ctx", peer))
    plane_gather_finish(qkv_started, [qkv_all], qkv_sems, chips)
    for copy in sent:
        copy.wait()
    for k in range(n_ctx - 1):
        small_total = small_total + small_c[k]
        flat_total = flat_total + flat_c[k]
    sums_ref[...] = small_total
    flat_out[...] = flat_total


def first_norm_back(part, qkv_part, outw_own, flat, tok, dmixed, vecs):
    planes, n_ctx, half, width = part.shape
    rows = tok.shape[0]
    seqs = rows // half
    quarter, columns = qkv_part.shape[1:]
    chips, pairs = n_ctx // 2, planes // seqs
    size = (8, quarter + -quarter % LANES)
    return pl.pallas_call(
        functools.partial(fourth_kernel, chips, planes, seqs),
        out_shape=(
            jax.ShapeDtypeStruct((rows, width), F32),
            jax.ShapeDtypeStruct((n_ctx, pairs, quarter, columns), BF16),
            jax.ShapeDtypeStruct((n_ctx,) + outw_own.shape, BF16),
            jax.ShapeDtypeStruct(size, F32),
            jax.ShapeDtypeStruct(flat.shape[1:], F32),
        ),
        in_specs=[ANY, ANY, ANY, VMEM, VMEM, VMEM, VMEM],
        out_specs=(VMEM, ANY, ANY, VMEM, VMEM),
        scratch_shapes=[
            pltpu.VMEM((planes, quarter, columns), BF16),
            pltpu.VMEM((pairs, quarter, columns), BF16),
            DMA((planes - 1,)),
            DMA((planes - 1,)),
            DMA,
            pltpu.VMEM((planes, half, width), BF16),
            pltpu.VMEM((planes, half, width), BF16),
            DMA((planes - 1,)),
            DMA((planes - 1,)),
            pltpu.VMEM((planes,) + size, F32),
            pltpu.VMEM(size, F32),
            pltpu.VMEM((planes - 1,) + size, F32),
            pltpu.VMEM((n_ctx - 1,) + size, F32),
            pltpu.VMEM(flat.shape[1:], F32),
            pltpu.VMEM((planes - 1,) + flat.shape[1:], F32),
            pltpu.VMEM((n_ctx - 1,) + flat.shape[1:], F32),
            DMA((2, planes - 1)),
            DMA((2, planes - 1)),
            DMA((2, n_ctx - 1)),
            DMA((2, n_ctx - 1)),
        ]
        + scatter_scratch(chips, planes, half, width)
        + gather_sems(chips)
        + gather_sems(chips),
        compiler_params=params(3),
        cost_estimate=SMALL,
        name="scatter_back",
    )(part, qkv_part, outw_own, flat, tok, dmixed, vecs)


def to_heads_kernel(
    planes,
    seqs,
    chips,
    tok_ref,
    part_ref,
    mixed_ref,
    vec_ref,
    down_ref,
    head_ref,
    out_ref,
    down_all,
    send_sems,
    recv_sems,
    local_sem,
    *scratch,
):
    ctx_me, core, chip, sibling, to, come = plane_peers(chips)
    me, others = other_planes(planes)
    pairs = planes // seqs
    greet(to + [sibling], others)

    def source(unit):
        start = pl.multiple_of(lax.rem(unit, pairs) * LANES, LANES)
        return tok_ref.at[:, unit // pairs, :, pl.ds(start, LANES)]

    copies = [
        send(source(unit), head_ref.at[me], send_sems.at[k], recv_sems.at[k], "fsdp", unit)
        for k, unit in enumerate(others)
    ]
    copies.append(pltpu.make_async_copy(source(me), head_ref.at[me], local_sem))
    copies[-1].start()
    total = plane_scatter(lambda c: part_ref.at[c], *scratch[:3], scratch[3:8], chips)
    gathered = plane_gather_start([down_ref], [down_all], scratch[8:], chips)
    out_ref[...] = (mixed_ref[...] + total + vec_ref[...]).astype(BF16)
    plane_gather_finish(gathered, [down_all], scratch[8:], chips)
    for copy in copies:
        copy.wait()


def to_heads(tok, planes, cid, part, mixed, vec, down_own):
    n_ctx, seqs, local_rows, width = tok.shape
    chips = n_ctx // 2
    rows, model = mixed.shape
    return pl.pallas_call(
        functools.partial(to_heads_kernel, planes, seqs, chips),
        out_shape=(
            jax.ShapeDtypeStruct((planes, n_ctx, local_rows, LANES), BF16),
            jax.ShapeDtypeStruct((rows, model), BF16),
            jax.ShapeDtypeStruct((n_ctx,) + down_own.shape, BF16),
        ),
        in_specs=[ANY, ANY, VMEM, VMEM, ANY],
        out_specs=(ANY, VMEM, ANY),
        scratch_shapes=[DMA((planes - 1,)), DMA((planes - 1,)), DMA]
        + scatter_scratch(chips, rows, model)
        + gather_sems(chips),
        compiler_params=params(cid),
        cost_estimate=SMALL,
        name="to_heads",
    )(tok, part, mixed, vec, down_own)


def to_tokens_kernel(
    planes, seqs, head_ref, weight_ref, tok_ref, weights_ref, send_sems, recv_sems, local_sem, w_send, w_recv, w_local
):
    me, others = other_planes(planes)
    pairs = planes // seqs
    greet((), others)
    start = pl.multiple_of(lax.rem(me, pairs) * LANES, LANES)
    target = tok_ref.at[:, me // pairs, :, pl.ds(start, LANES)]
    copies = [
        send(head_ref.at[peer], target, send_sems.at[k], recv_sems.at[k], "fsdp", peer) for k, peer in enumerate(others)
    ]
    copies += [
        send(weight_ref, weights_ref.at[me], w_send.at[k], w_recv.at[k], "fsdp", peer) for k, peer in enumerate(others)
    ]
    for copy in (
        pltpu.make_async_copy(head_ref.at[me], target, local_sem),
        pltpu.make_async_copy(weight_ref, weights_ref.at[me], w_local),
    ):
        copy.start()
        copies.append(copy)
    for copy in copies:
        copy.wait()


def to_tokens(heads, seqs, cid, weight):
    planes, n_ctx, rows, lanes = heads.shape
    width = (planes // seqs) * LANES
    return pl.pallas_call(
        functools.partial(to_tokens_kernel, planes, seqs),
        out_shape=(
            jax.ShapeDtypeStruct((n_ctx, seqs, rows, width), heads.dtype),
            jax.ShapeDtypeStruct((planes,) + weight.shape, BF16),
        ),
        in_specs=[ANY] * 2,
        out_specs=(ANY,) * 2,
        scratch_shapes=[DMA((planes - 1,)), DMA((planes - 1,)), DMA] * 2,
        compiler_params=params(cid),
        cost_estimate=SMALL,
        name="to_tokens",
    )(heads, weight)


def nt(left, right):
    return lax.dot_general(left, right, (((1,), (1,)), ((), ())), preferred_element_type=F32)


def nn(left, right):
    return lax.dot_general(left, right, (((1,), (0,)), ((), ())), preferred_element_type=F32)


def sort_blocks(order_ref, qkv_ref, targets, blocks, half):
    def body(block, carry):
        row = qkv_ref[order_ref[block]]
        start = pl.multiple_of(block * half, half)
        for k, target in enumerate(targets):
            target[pl.ds(start, half), :] = row[:, k * LANES : (k + 1) * LANES]
        return carry

    lax.fori_loop(0, blocks, body, 0)


def lane_mask(rows, head):
    lane = lax.broadcasted_iota(jnp.int32, (rows, LANES), 1)
    return (lane < HD) if head == 0 else (lane >= HD)


def unsort_blocks(order_ref, sorted_refs, target_ref, blocks, half):
    def body(block, carry):
        start = pl.multiple_of(block * half, half)
        place = order_ref[block]
        for k, source in enumerate(sorted_refs):
            target_ref[place, :, k * LANES : (k + 1) * LANES] = source[pl.ds(start, half), :].astype(BF16)
        return carry

    lax.fori_loop(0, blocks, body, 0)


def long_forward_kernel(tile, order_ref, qkv_ref, out_ref, att_ref, lse_ref, q_s, k_s, v_s, vt_s, o_s):
    blocks, half = out_ref.shape[0], out_ref.shape[1]
    length = blocks * half
    tiles = length // tile
    sort_blocks(order_ref, qkv_ref, [q_s, k_s, v_s], blocks, half)
    for t in range(tiles):
        span = slice(t * tile, (t + 1) * tile)
        vt_s[:, span] = v_s[span, :].T
    scale = HD ** (-0.5)
    rows_iota = lax.broadcasted_iota(jnp.int32, (tile, tile), 0)
    cols_iota = lax.broadcasted_iota(jnp.int32, (tile, tile), 1)
    allowed = rows_iota <= cols_iota
    masks = [lane_mask(tile, head) for head in range(2)]

    for qt in range(tiles):
        q_span = slice(qt * tile, (qt + 1) * tile)
        query = q_s[q_span, :] * jnp.asarray(scale, BF16)
        queries = [jnp.where(masks[head], query, jnp.zeros_like(query)) for head in range(2)]

        def step(kt, state, masked, queries=queries):
            start = pl.multiple_of(kt * tile, tile)
            keys = k_s[pl.ds(start, tile), :]
            new = []
            for head in range(2):
                top, total, acc = state[head]
                scores = nt(keys, queries[head])
                if masked:
                    scores = jnp.where(allowed, scores, NEG_BIG)
                new_top = jnp.maximum(top, jnp.max(scores, axis=0, keepdims=True))
                soft = jnp.exp(scores - new_top)
                factor = jnp.exp(top - new_top)
                total = total * factor + jnp.sum(soft, axis=0, keepdims=True)
                values = vt_s[head * HD : (head + 1) * HD, pl.ds(start, tile)]
                acc = acc * factor + nn(values, soft.astype(BF16))
                new.append((new_top, total, acc))
            return tuple(new)

        state = tuple(
            (jnp.full((1, tile), NEG_BIG, F32), jnp.zeros((1, tile), F32), jnp.zeros((HD, tile), F32))
            for head in range(2)
        )
        state = step(qt, state, True)
        if qt > 0:
            state = lax.fori_loop(0, qt, lambda kt, s, step=step: step(kt, s, False), state)
        parts = []
        for head in range(2):
            top, total, acc = state[head]
            parts.append(acc / total)
            lse_ref[head : head + 1, q_span] = top + jnp.log(total)
        att = jnp.concatenate(parts, axis=0).T
        att_ref[q_span, :] = att
        o_s[q_span, :] = att.astype(BF16)

    unsort_blocks(order_ref, [o_s], out_ref, blocks, half)


def forward_kernel(tile, order_ref, qkv_ref, out_ref, att_ref, lse_ref, q_s, k_s, v_s, o_s, s_s, p_s):
    blocks, half = out_ref.shape[0], out_ref.shape[1]
    length = blocks * half
    tiles = length // tile
    sort_blocks(order_ref, qkv_ref, [q_s, k_s, v_s], blocks, half)
    scale = HD ** (-0.5)
    rows_iota = lax.broadcasted_iota(jnp.int32, (tile, tile), 0)
    cols_iota = lax.broadcasted_iota(jnp.int32, (tile, tile), 1)
    allowed = cols_iota <= rows_iota
    masks = [lane_mask(tile, head) for head in range(2)]

    for qt in range(tiles):
        q_span = slice(qt * tile, (qt + 1) * tile)
        query = q_s[q_span, :] * jnp.asarray(scale, BF16)
        parts = []
        for head in range(2):
            one = jnp.where(masks[head], query, jnp.zeros_like(query))
            top = jnp.full((tile, LANES), NEG_BIG, F32)
            for kt in range(qt + 1):
                k_span = slice(kt * tile, (kt + 1) * tile)
                scores = nt(one, k_s[k_span, :])
                if kt == qt:
                    scores = jnp.where(allowed, scores, NEG_BIG)
                s_s[head, :, k_span] = scores
                for lane in range(0, tile, LANES):
                    top = jnp.maximum(top, scores[:, lane : lane + LANES])
            top = jnp.max(top, axis=1, keepdims=True)
            total = jnp.zeros((tile, LANES), F32)
            for kt in range(qt + 1):
                k_span = slice(kt * tile, (kt + 1) * tile)
                soft = jnp.exp(s_s[head, :, k_span] - top)
                for lane in range(0, tile, LANES):
                    total = total + soft[:, lane : lane + LANES]
                p_s[head, :, k_span] = soft.astype(BF16)
            total = jnp.sum(total, axis=1, keepdims=True)
            span = slice(0, (qt + 1) * tile)
            parts.append(nn(p_s[head, :, span], v_s[span, :]) / total)
            lse = jnp.broadcast_to(top + jnp.log(total), (tile, LANES))
            lse_ref[head : head + 1, q_span] = lse.T[0:1, :]
        att = jnp.where(masks[0], parts[0], parts[1])
        att_ref[q_span, :] = att
        o_s[q_span, :] = att.astype(BF16)
    unsort_blocks(order_ref, [o_s], out_ref, blocks, half)


SMEM = pl.BlockSpec(memory_space=pltpu.SMEM)
SHORT = 2048


def attend_forward(order, qkv, tile):
    blocks, half, lanes = qkv.shape
    length = blocks * half
    rows, short = pltpu.VMEM((length, LANES), BF16), length <= SHORT
    return pl.pallas_call(
        functools.partial(forward_kernel if short else long_forward_kernel, tile),
        out_shape=(
            jax.ShapeDtypeStruct((blocks, half, LANES), BF16),
            jax.ShapeDtypeStruct((length, LANES), F32),
            jax.ShapeDtypeStruct((2, length), F32),
        ),
        in_specs=[SMEM, VMEM],
        out_specs=(VMEM, VMEM, VMEM),
        scratch_shapes=[rows, rows, rows, rows, pltpu.VMEM((2, tile, length), F32), pltpu.VMEM((2, tile, length), BF16)]
        if short
        else [rows, rows, rows, pltpu.VMEM((LANES, length), BF16), rows],
        compiler_params=params(),
        cost_estimate=SMALL,
        name="attend_forward",
    )(order, qkv)


def long_backward_kernel(
    tile, order_ref, qkv_ref, grad_ref, att_ref, lse_ref, out_ref, q_s, k_s, v_s, g_s, kt_s, dq_s, dk_s, dv_s
):
    blocks, half = grad_ref.shape[0], grad_ref.shape[1]
    length = blocks * half
    tiles = length // tile
    sort_blocks(order_ref, qkv_ref, [q_s, k_s, v_s], blocks, half)
    sort_blocks(order_ref, grad_ref, [g_s], blocks, half)
    for t in range(tiles):
        span = slice(t * tile, (t + 1) * tile)
        kt_s[:, span] = k_s[span, :].T
    scale = HD ** (-0.5)
    rows_iota = lax.broadcasted_iota(jnp.int32, (tile, tile), 0)
    cols_iota = lax.broadcasted_iota(jnp.int32, (tile, tile), 1)
    allowed = rows_iota <= cols_iota
    masks = [lane_mask(tile, head) for head in range(2)]
    dk_s[...] = jnp.zeros_like(dk_s)
    dv_s[...] = jnp.zeros_like(dv_s)

    for qt in range(tiles):
        q_span = slice(qt * tile, (qt + 1) * tile)
        query = q_s[q_span, :] * jnp.asarray(scale, BF16)
        grad = g_s[q_span, :]
        queries = [jnp.where(masks[head], query, jnp.zeros_like(query)) for head in range(2)]
        grads = [jnp.where(masks[head], grad, jnp.zeros_like(grad)) for head in range(2)]
        product = (grad.astype(F32) * att_ref[q_span, :]).T
        dots = [jnp.sum(product[head * HD : (head + 1) * HD], axis=0, keepdims=True) for head in range(2)]
        totals = [lse_ref[head : head + 1, q_span] for head in range(2)]

        def step(kt, state, masked, queries=queries, grads=grads, dots=dots, totals=totals):
            start = pl.multiple_of(kt * tile, tile)
            rows = pl.ds(start, tile)
            keys = k_s[rows, :]
            values = v_s[rows, :]
            dk = dk_s[rows, :]
            dv = dv_s[rows, :]
            new = []
            for head in range(2):
                scores = nt(keys, queries[head])
                if masked:
                    scores = jnp.where(allowed, scores, NEG_BIG)
                soft = jnp.exp(scores - totals[head])
                dsoft = nt(values, grads[head])
                dscore = (soft * (dsoft - dots[head])).astype(BF16)
                dv = dv + nn(soft.astype(BF16), grads[head])
                dk = dk + nn(dscore, queries[head])
                new.append(state[head] + nn(kt_s[head * HD : (head + 1) * HD, rows], dscore))
            dk_s[rows, :] = dk
            dv_s[rows, :] = dv
            return tuple(new)

        state = (jnp.zeros((HD, tile), F32), jnp.zeros((HD, tile), F32))
        state = step(qt, state, True)
        if qt > 0:
            state = lax.fori_loop(0, qt, lambda kt, s, step=step: step(kt, s, False), state)
        dq = jnp.concatenate(state, axis=0) * scale
        dq_s[q_span, :] = dq.T.astype(BF16)

    unsort_blocks(order_ref, [dq_s, dk_s, dv_s], out_ref, blocks, half)


def backward_kernel(
    tile, order_ref, qkv_ref, grad_ref, att_ref, lse_ref, out_ref, q_s, k_s, v_s, g_s, kt_s, dq_s, dk_s, dv_s, qh_s, gh_s, dot_s, p_s, ds_s
):
    blocks, half = grad_ref.shape[0], grad_ref.shape[1]
    length = blocks * half
    tiles = length // tile
    sort_blocks(order_ref, qkv_ref, [q_s, k_s, v_s], blocks, half)
    sort_blocks(order_ref, grad_ref, [g_s], blocks, half)
    scale = HD ** (-0.5)
    rows_iota = lax.broadcasted_iota(jnp.int32, (tile, tile), 0)
    cols_iota = lax.broadcasted_iota(jnp.int32, (tile, tile), 1)
    allowed = rows_iota <= cols_iota
    masks = [lane_mask(tile, head) for head in range(2)]
    for t in range(tiles):
        span = slice(t * tile, (t + 1) * tile)
        kt_s[:, span] = k_s[span, :].T
        query = q_s[span, :] * jnp.asarray(scale, BF16)
        grad = g_s[span, :]
        product = (grad.astype(F32) * att_ref[span, :]).T
        for head in range(2):
            qh_s[head, span, :] = jnp.where(masks[head], query, jnp.zeros_like(query))
            gh_s[head, span, :] = jnp.where(masks[head], grad, jnp.zeros_like(grad))
            dot_s[head : head + 1, span] = jnp.sum(product[head * HD : (head + 1) * HD], axis=0, keepdims=True)

    for kt in range(tiles):
        k_span = slice(kt * tile, (kt + 1) * tile)
        rest = slice(kt * tile, length)
        keys, values = k_s[k_span, :], v_s[k_span, :]
        dk, dv = None, None
        for head in range(2):
            for qt in range(kt, tiles):
                span = slice(qt * tile, (qt + 1) * tile)
                scores = nt(keys, qh_s[head, span, :])
                if kt == qt:
                    scores = jnp.where(allowed, scores, NEG_BIG)
                soft = jnp.exp(scores - lse_ref[head : head + 1, span])
                p_s[head, :, span] = soft.astype(BF16)
                dsoft = nt(values, gh_s[head, span, :])
                ds_s[head, k_span, span] = (soft * (dsoft - dot_s[head : head + 1, span])).astype(BF16)
            dv_one = nn(p_s[head, :, rest], gh_s[head, rest, :])
            dk_one = nn(ds_s[head, k_span, rest], qh_s[head, rest, :])
            dv = dv_one if dv is None else dv + dv_one
            dk = dk_one if dk is None else dk + dk_one
        dk_s[k_span, :] = dk.astype(BF16)
        dv_s[k_span, :] = dv.astype(BF16)
    for qt in range(tiles):
        span = slice(qt * tile, (qt + 1) * tile)
        upto = slice(0, (qt + 1) * tile)
        dq = [nn(kt_s[head * HD : (head + 1) * HD, upto], ds_s[head, upto, span]) for head in range(2)]
        dq_s[span, :] = (jnp.concatenate(dq, axis=0) * scale).T.astype(BF16)
    unsort_blocks(order_ref, [dq_s, dk_s, dv_s], out_ref, blocks, half)


def attend_backward(order, qkv, grad, att, lse, tile):
    blocks, half, lanes = qkv.shape
    length = blocks * half
    rows, short = pltpu.VMEM((length, LANES), BF16), length <= SHORT
    flipped = pltpu.VMEM((LANES, length), BF16)
    return pl.pallas_call(
        functools.partial(backward_kernel if short else long_backward_kernel, tile),
        out_shape=jax.ShapeDtypeStruct((blocks, half, 3 * LANES), BF16),
        in_specs=[SMEM, VMEM, VMEM, VMEM, VMEM],
        out_specs=VMEM,
        scratch_shapes=[rows, rows, rows, rows, flipped, rows, rows, rows]
        + [pltpu.VMEM((2, length, LANES), BF16)] * 2
        + [pltpu.VMEM((2, length), F32), pltpu.VMEM((2, tile, length), BF16), pltpu.VMEM((2, length, length), BF16)]
        if short
        else [rows, rows, rows, rows, flipped, rows] + [pltpu.VMEM((length, LANES), F32)] * 2,
        compiler_params=params(),
        cost_estimate=SMALL,
        name="attend_backward",
    )(order, qkv, grad, att, lse)


def assemble_kernel(pieces, part_ref, out_ref):
    for start, source, first, size in pieces:
        out_ref[:, start : start + size] = part_ref[source, :, first : first + size].astype(F32)


def assemble(parts, pieces, width, block):
    n_ctx, rows, columns = parts.shape
    return pl.pallas_call(
        functools.partial(assemble_kernel, pieces),
        grid=(rows // block,),
        out_shape=jax.ShapeDtypeStruct((rows, width), F32),
        in_specs=[pl.BlockSpec((n_ctx, block, columns), lambda i: (0, i, 0))],
        out_specs=pl.BlockSpec((block, width), lambda i: (i, 0)),
        compiler_params=params(),
        name="assemble",
    )(parts)


def tn(left, right):
    return nn(left.T, right)


def rows_block(rows, most):
    return math.gcd(rows, most)


def whole_block(shape):
    return pl.BlockSpec(shape, lambda i: (0,) * len(shape), pipeline_mode=pl.Buffered(1))


def row_spec(block, width):
    return pl.BlockSpec((block, width), lambda i: (i, 0))


def product_kernel(left_ref, right_ref, shift_ref, out_ref):
    out_ref[...] = (nn(left_ref[...], right_ref[...]) + shift_ref[...]).astype(BF16)


def product(left, right, shift=None):
    rows, depth = left.shape
    width = right.shape[1]
    block = rows_block(rows, 512)
    if shift is None:
        shift = jnp.zeros((width,), F32)
    return pl.pallas_call(
        product_kernel,
        grid=(rows // block,),
        out_shape=jax.ShapeDtypeStruct((rows, width), BF16),
        in_specs=[row_spec(block, depth), whole_block((depth, width)), whole_block((1, width))],
        out_specs=row_spec(block, width),
        compiler_params=params(),
        cost_estimate=SMALL,
        name="product",
    )(left, right, shift[None, :])


def back_kernel(left_ref, grad_ref, weight_ref, grad_left_ref, grad_weight_ref, sum_ref, total):
    step = pl.program_id(0)
    grad = grad_ref[...]
    grad_left_ref[...] = nt(grad, weight_ref[...]).astype(BF16)
    term = tn(grad, left_ref[...])
    sums = jnp.sum(grad.astype(F32), axis=0, keepdims=True)

    @pl.when(step == 0)
    def _():
        total[...] = term
        sum_ref[...] = sums

    @pl.when(step > 0)
    def _():
        total[...] += term
        sum_ref[...] += sums

    @pl.when(step == pl.num_programs(0) - 1)
    def _():
        grad_weight_ref[...] = total[...].T.astype(BF16)


def product_back(left, grad, weight):
    rows, depth = left.shape
    width = grad.shape[1]
    block = rows_block(rows, 512)
    return pl.pallas_call(
        back_kernel,
        grid=(rows // block,),
        out_shape=(
            jax.ShapeDtypeStruct((rows, depth), BF16),
            jax.ShapeDtypeStruct((depth, width), BF16),
            jax.ShapeDtypeStruct((1, width), F32),
        ),
        in_specs=[row_spec(block, depth), row_spec(block, width), whole_block((depth, width))],
        out_specs=(
            row_spec(block, depth),
            pl.BlockSpec((depth, width), lambda i: (0, 0)),
            pl.BlockSpec((1, width), lambda i: (0, 0)),
        ),
        scratch_shapes=[pltpu.VMEM((width, depth), F32)],
        compiler_params=params(),
        cost_estimate=SMALL,
        name="product_back",
    )(left, grad, weight)


def out_back_kernel(att_ref, grad_ref, weight_ref, grad_att_ref, grad_weight_ref, total):
    step = pl.program_id(0)
    grad = grad_ref[...]
    grad_att_ref[...] = nt(grad, weight_ref[...]).astype(BF16)
    term = tn(att_ref[...], grad)

    @pl.when(step == 0)
    def _():
        total[...] = term

    @pl.when(step > 0)
    def _():
        total[...] += term

    @pl.when(step == pl.num_programs(0) - 1)
    def _():
        grad_weight_ref[...] = total[...].astype(BF16)


def out_back(att, grad, weight):
    rows, depth = att.shape
    width = grad.shape[1]
    block = rows_block(rows, 512)
    return pl.pallas_call(
        out_back_kernel,
        grid=(rows // block,),
        out_shape=(jax.ShapeDtypeStruct((rows, depth), BF16), jax.ShapeDtypeStruct((depth, width), BF16)),
        in_specs=[row_spec(block, depth), row_spec(block, width), whole_block((depth, width))],
        out_specs=(row_spec(block, depth), pl.BlockSpec((depth, width), lambda i: (0, 0))),
        scratch_shapes=[pltpu.VMEM((depth, width), F32)],
        compiler_params=params(),
        cost_estimate=SMALL,
        name="out_back",
    )(att, grad, weight)


GELU_A = math.sqrt(2.0 / math.pi)
GELU_B = 0.044715


def up_kernel(h_ref, og_ref, weight_ref, shift_ref, act_ref, slope_ref, grad_ref, total):
    step = pl.program_id(0)
    up = nn(h_ref[...], weight_ref[...]) + shift_ref[...]
    square = up * up
    soft = jnp.tanh(GELU_A * up * (1.0 + GELU_B * square))
    half = 0.5 * (1.0 + soft)
    act = (up * half).astype(BF16)
    act_ref[...] = act
    slope_ref[...] = half + 0.5 * up * (1.0 - soft * soft) * (GELU_A * (1.0 + 3.0 * GELU_B * square))
    term = tn(act, og_ref[...])

    @pl.when(step == 0)
    def _():
        total[...] = term

    @pl.when(step > 0)
    def _():
        total[...] += term

    @pl.when(step == pl.num_programs(0) - 1)
    def _():
        grad_ref[...] = total[...].astype(BF16)


def feed_up(values, out_grad, weight, shift):
    rows, width = values.shape
    hidden = weight.shape[1]
    block = rows_block(rows, 512)
    return pl.pallas_call(
        up_kernel,
        grid=(rows // block,),
        out_shape=(
            jax.ShapeDtypeStruct((rows, hidden), BF16),
            jax.ShapeDtypeStruct((rows, hidden), F32),
            jax.ShapeDtypeStruct((hidden, width), BF16),
        ),
        in_specs=[
            row_spec(block, width),
            row_spec(block, width),
            whole_block((width, hidden)),
            whole_block((1, hidden)),
        ],
        out_specs=(
            row_spec(block, hidden),
            row_spec(block, hidden),
            pl.BlockSpec((hidden, width), lambda i: (0, 0)),
        ),
        scratch_shapes=[pltpu.VMEM((hidden, width), F32)],
        compiler_params=params(),
        cost_estimate=SMALL,
        name="feed_up",
    )(values, out_grad, weight, shift[None, :])


def down_kernel(
    h_ref, og_ref, act_ref, slope_ref, up_w_ref, down_w_ref, out_ref, d_h_ref, grad_ref, sum_ref, total
):
    step = pl.program_id(0)
    d_up = (nt(og_ref[...], down_w_ref[...]) * slope_ref[...]).astype(BF16)
    d_h_ref[...] = nt(d_up, up_w_ref[...]).astype(BF16)
    sums = jnp.sum(d_up.astype(F32), axis=0, keepdims=True)
    term = tn(d_up, h_ref[...])
    out_ref[...] = nn(act_ref[...], down_w_ref[...]).astype(BF16)

    @pl.when(step == 0)
    def _():
        total[...] = term
        sum_ref[...] = sums

    @pl.when(step > 0)
    def _():
        total[...] += term
        sum_ref[...] += sums

    @pl.when(step == pl.num_programs(0) - 1)
    def _():
        grad_ref[...] = total[...].T.astype(BF16)


def feed_down(values, out_grad, act, slope, up_weight, down_weight):
    rows, width = values.shape
    hidden = up_weight.shape[1]
    block = rows_block(rows, 512)
    return pl.pallas_call(
        down_kernel,
        grid=(rows // block,),
        out_shape=(
            jax.ShapeDtypeStruct((rows, width), BF16),
            jax.ShapeDtypeStruct((rows, width), BF16),
            jax.ShapeDtypeStruct((width, hidden), BF16),
            jax.ShapeDtypeStruct((1, hidden), F32),
        ),
        in_specs=[
            row_spec(block, width),
            row_spec(block, width),
            row_spec(block, hidden),
            row_spec(block, hidden),
            whole_block((width, hidden)),
            whole_block((hidden, width)),
        ],
        out_specs=(
            row_spec(block, width),
            row_spec(block, width),
            pl.BlockSpec((width, hidden), lambda i: (0, 0)),
            pl.BlockSpec((1, hidden), lambda i: (0, 0)),
        ),
        scratch_shapes=[pltpu.VMEM((hidden, width), F32)],
        compiler_params=params(),
        cost_estimate=SMALL,
        name="feed_down",
    )(values, out_grad, act, slope, up_weight, down_weight)


def local(
    tokens,
    block_pairs,
    out_grad,
    ln1_gain,
    ln1_bias,
    qkv_weight,
    query_bias,
    value_bias,
    out_weight,
    out_bias,
    ln2_gain,
    ln2_bias,
    up_weight,
    up_bias,
    down_weight,
    down_bias,
):
    n_ctx, planes = lax.axis_size("ctx"), lax.axis_size("fsdp")
    c, f = lax.axis_index("ctx"), lax.axis_index("fsdp")
    local_rows, seqs, width = tokens.shape
    half = local_rows // 2
    devices = n_ctx * planes
    blocks = 2 * devices
    length = devices * local_rows
    heads = width // HD
    slots = planes * (-(-heads // devices))
    assert slots == planes and planes % seqs == 0
    span = slots * HD
    rows = local_rows * seqs
    plane_rows = n_ctx * rows
    quarter = width // planes
    ff = up_weight.shape[1]
    ff_quarter = ff // planes
    ff_piece = ff_quarter // n_ctx
    ff_span = ff_piece * planes
    tile = 256

    device_ids = jnp.arange(devices, dtype=jnp.int32)
    device_of_block = jnp.sum(
        jnp.where(block_pairs[None, :] == device_ids[:, None], device_ids[None, :], 0), axis=1
    )
    place_of_block = lax.rem(device_of_block, planes) * n_ctx + device_of_block // planes
    order = jnp.concatenate([place_of_block * 2, place_of_block[::-1] * 2 + 1]).astype(jnp.int32)

    first = [-(-quarter * j // HD) for j in range(planes)] + [heads]
    counts = [first[j + 1] - first[j] for j in range(planes)]
    assert max(counts) <= n_ctx
    slot_head = [jnp.minimum(first[j] + c, heads - 1) for j in range(planes)]
    first_own = jnp.asarray(first, jnp.int32)[f]
    count_own = jnp.asarray(counts, jnp.int32)[f]

    pairs = planes // seqs
    pair, pair_span = lax.rem(f, pairs), 2 * HD
    qkv_own = jnp.stack(
        [
            jnp.concatenate(
                [
                    lax.dynamic_slice(qkv_weight, (0, k * width + slot_head[j] * HD), (quarter, HD))
                    for k in range(3)
                    for j in (2 * p, 2 * p + 1)
                ],
                axis=1,
            )
            for p in range(pairs)
        ]
    )
    next_rows = lax.ppermute(out_weight[:HD], "fsdp", [(j + 1, j) for j in range(planes - 1)])
    out_own = lax.dynamic_slice(
        jnp.concatenate([out_weight, next_rows]), ((first_own + c) * HD - f * quarter, 0), (HD, width)
    )
    out_own = jnp.where(c < count_own, out_own, jnp.zeros_like(out_own))
    down_own = lax.dynamic_slice(down_weight, (c * ff_piece, 0), (ff_piece, width))


    tok = jnp.swapaxes(tokens, 0, 1).reshape(rows, width)
    og = jnp.swapaxes(out_grad, 0, 1).reshape(rows, width)

    short = -quarter % LANES
    vector_list = [ln1_gain, ln1_bias, ln2_gain, ln2_bias, query_bias, value_bias, out_bias, down_bias]
    vector_list += [up_bias[k * quarter : (k + 1) * quarter] for k in range(ff // width)]
    packed = jnp.concatenate([jnp.pad(v, (0, short)) for v in vector_list])
    packed = jnp.pad(packed, (0, -packed.size % (16 * LANES))).reshape(-1, LANES)
    vectors, og_all, h1, qkv_slice = first_norm_gather(tok, og, packed, qkv_own, n_ctx, planes, seqs)
    h1 = h1.reshape(length, width)
    qkv_slice = qkv_slice.reshape(width, 3 * pair_span)
    h1, up_weight, down_own = lax.optimization_barrier((h1, up_weight, down_own))
    down_slice = lax.all_gather(down_own, "fsdp", axis=0, tiled=True)
    up_own = jnp.concatenate(
        [
            lax.dynamic_slice(up_weight, (0, k * ff_quarter + c * ff_piece), (quarter, ff_piece))
            for k in range(planes)
        ],
        axis=1,
    )
    up_slice = lax.all_gather(up_own, "fsdp", axis=0, tiled=True)
    og_all = og_all.reshape(plane_rows, width)
    vectors = vectors.reshape(planes, -1)[:, : len(vector_list) * (quarter + short)]
    vectors = vectors.reshape(planes, len(vector_list), quarter + short)[:, :, :quarter].astype(F32)
    gain1, bias1, gain2, bias2, bias_q, bias_v, bias_o, bias_d = [
        vectors[:, k].reshape(width) for k in range(8)
    ]
    bias_up = lax.dynamic_slice(
        vectors[:, 8 : 8 + ff // width].reshape(planes, ff_quarter), (0, c * ff_piece), (planes, ff_piece)
    ).reshape(ff_span)

    pair_heads = [jnp.minimum(jnp.asarray(first, jnp.int32)[2 * pair + i] + c, heads - 1) for i in range(2)]

    def head_part(vector):
        return [lax.dynamic_slice(vector, (head * HD,), (HD,)) for head in pair_heads]

    qkv_shift = jnp.concatenate(head_part(bias_q) + [jnp.zeros((pair_span,), F32)] + head_part(bias_v))

    qkv = product(h1, qkv_slice, qkv_shift).reshape(blocks, half, 3 * pair_span)
    att_heads, att_exact, lse = attend_forward(order, qkv, tile)
    att, out_slice = to_tokens(att_heads.reshape(planes, n_ctx, local_rows, LANES), seqs, 6, out_own)
    out_slice = out_slice.reshape(span, width)
    att = att.reshape(plane_rows, span)
    branch = product(att, out_slice).reshape(n_ctx, rows, width)
    mixed, h2 = second_norm_gather(branch, tok, jnp.stack([gain2, bias2, bias_o]))
    h2 = h2.reshape(plane_rows, width)
    def reduce_own(part):
        return lax.psum_scatter(part, "fsdp", scatter_dimension=0, tiled=True)

    act, slope, down_part = feed_up(h2, og_all, up_slice, bias_up)
    down_own_grad = reduce_own(down_part)
    out_part, d_h2, up_part, d_up_sum = feed_down(h2, og_all, act, slope, up_slice, down_slice)
    up_own_grad = reduce_own(up_part)
    out_part, d_h2 = [part.reshape(n_ctx, rows, width) for part in (out_part, d_h2)]
    d_mixed, sums2, d_branch = second_norm_back(d_h2, mixed, og, gain2[None, :])
    d_branch = d_branch.reshape(plane_rows, width)
    d_att, out_w_part = out_back(att, d_branch, out_slice)
    d_att_heads, block_out, down_parts = to_heads(
        d_att.reshape(n_ctx, seqs, local_rows, span), planes, 7, out_part, mixed, bias_d[None, :], down_own_grad
    )
    d_att_heads, out_w_part = lax.optimization_barrier((d_att_heads, out_w_part))
    out_own_grad = reduce_own(out_w_part)
    up_parts = lax.all_gather(up_own_grad, "ctx", axis=0)
    d_qkv = attend_backward(order, qkv, d_att_heads.reshape(blocks, half, LANES), att_exact, lse, tile)
    d_qkv = d_qkv.reshape(length, 3 * pair_span)
    d_h1, qkv_part, d_qkv_sum = product_back(h1, d_qkv, qkv_slice)
    qkv_part = qkv_part.reshape(planes, quarter, 3 * pair_span)
    d_h1 = d_h1.reshape(planes, n_ctx, local_rows, width)
    d_qkv_sum = d_qkv_sum[0]

    d_up_sum = d_up_sum.reshape(planes, ff_piece)
    up_spread = lax.dynamic_update_slice(jnp.zeros((planes, ff_quarter), F32), d_up_sum, (0, c * ff_piece))

    def spread(values):
        full = jnp.zeros((width + HD,), F32)
        for i in range(2):
            slot = 2 * pair + i
            real = c < jnp.asarray(counts, jnp.int32)[slot]
            place = jnp.where(real, pair_heads[i] * HD, width)
            full = lax.dynamic_update_slice(full, values[i * HD : (i + 1) * HD], (place,))
        return full[None, :width]

    wide = jnp.concatenate([sums2, spread(d_qkv_sum[:pair_span]), spread(d_qkv_sum[2 * pair_span :])])
    wide = wide.reshape(6, planes, quarter).transpose(1, 0, 2).reshape(planes, 6 * quarter)
    flat = jnp.concatenate([wide, up_spread], axis=1)
    size = flat.shape[1]
    flat = jnp.pad(flat, ((0, 0), (0, -size % (8 * LANES)))).reshape(planes, -1, LANES)

    grad_tok, qkv_parts, out_parts, sums1, totals = first_norm_back(
        d_h1, qkv_part, out_own_grad, flat, tok, d_mixed, gain1[None, :]
    )
    sums1 = sums1[:2, :quarter]
    totals = totals.reshape(-1)
    sums = totals[: 6 * quarter].reshape(6, quarter)
    up_bias_grad = totals[6 * quarter : size]

    down_grad = down_parts.reshape(ff_quarter, width).astype(F32)
    block = quarter // 5
    up_pieces = [
        (j * ff_quarter + d * ff_piece, d, j * ff_piece, ff_piece) for j in range(planes) for d in range(n_ctx)
    ]
    up_grad = assemble(up_parts, up_pieces, ff, block)
    qkv_pieces = [
        (k * width + (first[j] + d) * HD, d * pairs + j // 2, k * pair_span + j % 2 * HD, HD)
        for k in range(3)
        for j in range(planes)
        for d in range(counts[j])
    ]
    qkv_grad = assemble(qkv_parts.reshape(n_ctx * pairs, quarter, 3 * pair_span), qkv_pieces, 3 * width, block)
    out_rows = out_parts.reshape(n_ctx * HD, width)
    tail = (f + 1) * quarter - first_own * HD
    tail_rows = lax.dynamic_slice(out_rows, (tail, 0), (HD, width))
    tail_rows = lax.ppermute(tail_rows, "fsdp", [(j, j + 1) for j in range(planes - 1)])
    lead = first_own * HD - f * quarter
    shifted = lax.dynamic_slice(
        jnp.concatenate([jnp.zeros((HD, width), BF16), out_rows]), (HD - lead, 0), (quarter, width)
    )
    from_tail = jnp.concatenate([tail_rows, jnp.zeros((quarter - HD, width), BF16)])
    row_ids = lax.broadcasted_iota(jnp.int32, (quarter, width), 0)
    out_grad_own = jnp.where(row_ids < lead, from_tail, shifted).astype(F32)

    def back(values):
        return jnp.swapaxes(values.reshape(seqs, local_rows, width), 0, 1)

    return (
        back(block_out),
        back(grad_tok),
        sums1[0],
        sums1[1],
        qkv_grad,
        sums[4],
        sums[5],
        out_grad_own,
        sums[2],
        sums[0],
        sums[1],
        up_grad,
        up_bias_grad,
        down_grad,
        sums[3],
    )


def solution(mesh):
    both, row, vec, mat = P(("ctx", "fsdp"), None, None), P(), P("fsdp"), P("fsdp", None)
    in_specs = (both, row, both, vec, vec, mat, vec, vec, mat, vec, vec, vec, mat, vec, mat, vec)
    out_specs = (both, both, vec, vec, mat, vec, vec, mat, vec, vec, vec, mat, vec, mat, vec)
    return jax.shard_map(local, mesh=mesh, in_specs=in_specs, out_specs=out_specs, check_vma=False)
```

time: 606 us -> 545 us (0.90)
  matrix products: 67 us -> 0 us
  Pallas kernels: 414 us -> 471 us
  waiting for transfers between devices: 38.2 us -> 1.33 us
  local copies, waits for them, and re-layouts: 43.2 us -> 30 us
    dot_general x12 -> x0, matrix products: 67 us -> none  [the longest x4 23.1 us: mm(): return jnp.matmul(left, right, preferred_element_type=F32)]
    pallas_call x9 -> x12, Pallas kernels: 311 us -> 369 us  [the longest x1 92.3 us: first_norm_back(): pl.pallas_call(functools.partial(fourth_kernel, chips, planes, seqs), out...]
    all_gather x2, waiting for transfers between devices: 28.6 us -> 0.02 us  [the longest x1 0.02 us: local(): down_slice = lax.all_gather(down_own, 'fsdp', axis=0, tiled=True)]
    convert_element_type x4 -> x0, local copies, waits for them, and re-layouts: 16.3 us -> none  [the longest x1 5.65 us: local(): out_part = mm(act, down_slice).astype(BF16).reshape(n_ctx, rows, width)]
    all_gather x1, waiting for transfers between devices: 8.93 us -> 0.02 us  [local(): up_slice = lax.all_gather(up_own, 'fsdp', axis=0, tiled=True)]
  transfers between devices with their start and end apart: 9 -> 8, of which waited for: 3 -> 0; matrix products, arithmetic and copies ran while one was open for 14% -> 5% of each run, Pallas kernels for 64% -> 73%
where the time goes in v4:
time: 545 us; the launch traced here: 540 us
  Pallas kernels  471 us (86%)
  local copies, waits for them, and re-layouts  30 us (6%)
  between operations  19.4 us (4%)
  other arithmetic  14.2 us (3%)
    pallas_call x1, Pallas kernels, first_norm_back(): pl.pallas_call(functools.partial(fourth_kernel, chips, planes, seqs), out...  92.3 us
    pallas_call x1, Pallas kernels, first_norm_gather(): pl.pallas_call(functools.partial(first_kernel, chips, planes, seqs, width...  69.3 us
    pallas_call x1, Pallas kernels, to_heads(): pl.pallas_call(functools.partial(to_heads_kernel, planes, seqs, chips), o...  55.5 us
    pallas_call x1, Pallas kernels, to_tokens(): pl.pallas_call(functools.partial(to_tokens_kernel, planes, seqs), out_sha...  54 us
    pallas_call x1, Pallas kernels, second_norm_back(): pl.pallas_call(functools.partial(third_kernel, chips), out_shape=(jax.Sha...  43.2 us
    pallas_call x1, Pallas kernels, second_norm_gather(): pl.pallas_call(functools.partial(second_kernel, chips), out_shape=(jax.Sh...  42.8 us
    pallas_call x1, Pallas kernels, feed_down(): pl.pallas_call(down_kernel, grid=(rows // block,), out_shape=(jax.ShapeDt...  24 us
    pallas_call x1, Pallas kernels, attend_backward(): pl.pallas_call(functools.partial(backward_kernel if short else long_backw...  17 us
  transfers between devices with their start and end apart: 8, of which 0 were waited for; matrix products, arithmetic and copies ran while one was open for 5% of the time, Pallas kernels for 73%

profile of v4, /device:TPU:0, one launch (start us, length us, event | category | flops | bytes accessed | tf_op | source)
XLA Modules:
  0.0 540.0 jit_solution(8122563741112289171)
XLA Ops:
  8.1 1.8 copy.55
  9.9 1.8 copy.56
  11.8 1.9 constant_dynamic-slice_fusion.13
  14.1 0.9 pad_maximum_fusion.1.weight_ref
  15.8 2.0 constant_dynamic-slice_fusion.6
  17.8 3.6 concatenate.75.vec_ref
  21.4 69.3 %norm_gather.1 = (bf16[4,48,128]{2,1,0:T(8,128)(2,1)}, bf16[8,128,1600]{2,1,0:T(8,128)(2,1)}, bf16[4,8,64,1600]{3,2,1,0:T(8,128)(2,1)}, bf16[4,400,384]{2,1,0:T(8,128)(2,1)}) custom-call(bf16[128,1600]{1,0:T(8,128)(2,1)} %bitcast.98, bf16[128,1600]{1,0:T(8,128)(2,1)} %bitcast.106, bf16[48,128]{1,0:T(8,128)(2,1)} %concatenate.75.vec_ref, ...), custom_call_target="tpu_custom_call" | custom-call | flops 1 | bytes 1 | tf_op jit(solution)/shard_map/norm_gather/pallas_call | solution.py:292
  90.7 1.7 constant_dynamic-slice_fusion.5
  92.5 1.2 pad_maximum_fusion
  94.6 1.3 collective-permute-start
  99.0 7.7 %product.2 = bf16[2048,384]{1,0:T(8,128)(2,1)} custom-call(bf16[2048,1600]{1,0:T(8,128)(2,1)} %bitcast.88, bf16[1600,384]{1,0:T(8,128)(2,1)} %bitcast.104, f32[1,384]{1,0:T(1,128)} %broadcast_in_dim.30.shift_ref), custom_call_target="tpu_custom_call" | custom-call | flops 1 | bytes 1 | tf_op jit(solution)/shard_map/product/pallas_call | solution.py:1000
  107.6 12.4 %attend_forward.1 = (bf16[64,32,128]{2,1,0:T(8,128)(2,1)}, f32[2048,128]{1,0:T(8,128)}, f32[2,2048]{1,0:T(2,128)}) custom-call(s32[64]{0:T(128)} %pad_add_fusion.order_ref, bf16[64,32,384]{2,1,0:T(8,128)(2,1)} %bitcast.90), custom_call_target="tpu_custom_call" | custom-call | flops 1 | bytes 1 | tf_op jit(solution)/shard_map/attend_forward/pallas_call | solution.py:803
  124.5 54.0 %to_tokens.1 = (bf16[8,2,64,256]{3,2,1,0:T(8,128)(2,1)}, bf16[4,64,1600]{2,1,0:T(8,128)(2,1)}) custom-call(bf16[4,8,64,128]{3,2,1,0:T(8,128)(2,1)} %bitcast.123, bf16[64,1600]{1,0:T(8,128)(2,1)} %fusion.3.weight_ref), custom_call_target="tpu_custom_call" | custom-call | flops 1 | bytes 1 | tf_op jit(solution)/shard_map/to_tokens/pallas_call | solution.py:644
  179.2 3.7 product.3
  182.9 42.8 %scatter_norm_gather.1 = (f32[128,1600]{1,0:T(8,128)}, bf16[8,128,1600]{2,1,0:T(8,128)(2,1)}) custom-call(bf16[8,128,1600]{2,1,0:T(8,128)(2,1)} %bitcast.96, bf16[128,1600]{1,0:T(8,128)(2,1)} %bitcast.99, f32[3,1600]{1,0:T(4,128)} %pad_maximum_fusion.2.vec_ref), custom_call_target="tpu_custom_call" | custom-call | flops 1 | bytes 1 | tf_op jit(solution)/shard_map/scatter_norm_gather/pallas_call | solution.py:336
  225.8 15.3 %feed_up.1 = (bf16[1024,800]{1,0:T(8,128)(2,1)}, f32[1024,800]{1,0:T(8,128)}, bf16[800,1600]{1,0:T(8,128)(2,1)}) custom-call(bf16[1024,1600]{1,0:T(8,128)(2,1)} %bitcast.94, bf16[1024,1600]{1,0:T(8,128)(2,1)} %bitcast.92, bf16[1600,800]{1,0:T(8,128)(2,1)} %all-gather.5.cloned.1.call-done.weight_ref.up_w_ref, f32[1,800]{1,0:T(1,128)} %broadcast_in_dim_reshape.3.shift_ref), custom_call_target="tpu_custom_call" | custom-call | flops 1 | bytes 1 | tf_op jit(solution)/shard_map/feed_up/pallas_call | solution.py:1127
  241.2 24.0 %feed_down.1 = (bf16[1024,1600]{1,0:T(8,128)(2,1)}, bf16[1024,1600]{1,0:T(8,128)(2,1)}, bf16[1600,800]{1,0:T(8,128)(2,1)}, f32[1,800]{1,0:T(1,128)}) custom-call(bf16[1024,1600]{1,0:T(8,128)(2,1)} %bitcast.95, bf16[1024,1600]{1,0:T(8,128)(2,1)} %bitcast.93, bf16[1024,800]{1,0:T(8,128)(2,1)} %get-tuple-element.64.act_ref, ...), custom_call_target="tpu_custom_call" | custom-call | flops 1 | bytes 1 | tf_op jit(solution)/shard_map/feed_down/pallas_call | solution.py:1182
  265.9 43.2 %scatter_back_gather.1 = (f32[128,1600]{1,0:T(8,128)}, f32[4,1600]{1,0:T(4,128)}, bf16[8,128,1600]{2,1,0:T(8,128)(2,1)}) custom-call(bf16[8,128,1600]{2,1,0:T(8,128)(2,1)} %bitcast.112, f32[128,1600]{1,0:T(8,128)} %get-tuple-element.68.mixed_ref, bf16[128,1600]{1,0:T(8,128)(2,1)} %bitcast.107, f32[1,1600]{1,0:T(1,128)} %copy-done.4), custom_call_target="tpu_custom_call" | custom-call | flops 1 | bytes 1 | tf_op jit(solution)/shard_map/scatter_back_gather/pallas_call | solution.py:373
  309.1 5.4 %out_back.1 = (bf16[1024,256]{1,0:T(8,128)(2,1)}, bf16[256,1600]{1,0:T(8,128)(2,1)}) custom-call(bf16[1024,256]{1,0:T(8,128)(2,1)} %bitcast.116, bf16[1024,1600]{1,0:T(8,128)(2,1)} %bitcast.110, bf16[256,1600]{1,0:T(8,128)(2,1)} %bitcast.109), custom_call_target="tpu_custom_call" | custom-call | flops 1 | bytes 1 | tf_op jit(solution)/shard_map/out_back/pallas_call | solution.py:1082
  314.6 55.5 %to_heads.1 = (bf16[4,8,64,128]{3,2,1,0:T(8,128)(2,1)}, bf16[128,1600]{1,0:T(8,128)(2,1)}, bf16[8,200,1600]{2,1,0:T(8,128)(2,1)}) custom-call(bf16[8,2,64,256]{3,2,1,0:T(8,128)(2,1)} %bitcast.124, bf16[8,128,1600]{2,1,0:T(8,128)(2,1)} %bitcast.111, f32[128,1600]{1,0:T(8,128)} %get-tuple-element.68.mixed_ref, ...), custom_call_target="tpu_custom_call" | custom-call | flops 1 | bytes 1 | tf_op jit(solution)/shard_map/to_heads/pallas_call | solution.py:599
  373.9 17.0 %attend_backward.1 = bf16[64,32,384]{2,1,0:T(8,128)(2,1)} custom-call(s32[64]{0:T(128)} %pad_add_fusion.order_ref, bf16[64,32,384]{2,1,0:T(8,128)(2,1)} %bitcast.91, bf16[64,32,128]{2,1,0:T(8,128)(2,1)} %bitcast.122, f32[2048,128]{1,0:T(8,128)} %get-tuple-element.77.att_ref, f32[2,2048]{1,0:T(2,128)} %get-tuple-element.78.lse_ref), custom_call_target="tpu_custom_call" | custom-call | flops 1 | bytes 1 | tf_op jit(solution)/shard_map/attend_backward/pallas_call | solution.py:940
  390.9 12.4 %product_back.1 = (bf16[2048,1600]{1,0:T(8,128)(2,1)}, bf16[1600,384]{1,0:T(8,128)(2,1)}, f32[1,384]{1,0:T(1,128)}) custom-call(bf16[2048,1600]{1,0:T(8,128)(2,1)} %bitcast.89, bf16[2048,384]{1,0:T(8,128)(2,1)} %bitcast.101, bf16[1600,384]{1,0:T(8,128)(2,1)} %bitcast.105), custom_call_target="tpu_custom_call" | custom-call | flops 1 | bytes 1 | tf_op jit(solution)/shard_map/product_back/pallas_call | solution.py:1038
  406.8 1.2 copy.65
  408.0 7.3 %bitcast_convert_fusion = f32[1600,1600]{1,0:T(8,128)} fusion(bf16[8,200,1600]{2,1,0:T(8,128)(2,1)} %get-tuple-element.92), kind=kLoop, calls=%fused_computation | loop fusion | flops 2560000 | bytes 15360000 | tf_op jit(solution)/shard_map/convert_element_type | solution.py:1383
  415.3 92.3 %scatter_back.1 = (f32[128,1600]{1,0:T(8,128)}, bf16[8,2,400,384]{3,2,1,0:T(8,128)(2,1)}, bf16[8,64,1600]{2,1,0:T(8,128)(2,1)}, f32[8,512]{1,0:T(8,128)}, f32[32,128]{1,0:T(8,128)}) custom-call(bf16[4,8,64,1600]{3,2,1,0:T(8,128)(2,1)} %bitcast.97, bf16[4,400,384]{2,1,0:T(8,128)(2,1)} %bitcast.119, ...), custom_call_target="tpu_custom_call" | custom-call | flops 1 | bytes 1 | tf_op jit(solution)/shard_map/scatter_back/pallas_call | solution.py:513
  507.6 1.0 constant_dynamic-slice_fusion
  508.6 2.7 collective-permute-start.1
  511.3 7.2 %assemble.2 = f32[400,4800]{1,0:T(8,128)} custom-call(bf16[16,400,384]{2,1,0:T(8,128)(2,1)} %bitcast.103), custom_call_target="tpu_custom_call" | custom-call | tf_op jit(solution)/shard_map/assemble/pallas_call | solution.py:963
  518.5 1.6 copy.64
  520.8 1.4 fusion.6
  522.8 1.8 fusion.1
  524.6 8.3 %assemble.3 = f32[400,6400]{1,0:T(8,128)} custom-call(bf16[8,400,800]{2,1,0:T(8,128)(2,1)} %bitcast.102), custom_call_target="tpu_custom_call" | custom-call | tf_op jit(solution)/shard_map/assemble/pallas_call | solution.py:963
  (121 shorter events, 16.7 us)
Async XLA Ops:
  7.2 218.6 %all-gather.5.cloned.1.call-start = ((), (), s32[]{:S(2)}) async-start(), calls=%async_computation.3 | async-start | bytes 3584000 | tf_op jit(solution)/shard_map/all_gather | solution.py:1307
  11.7 3.3 copy-start.19
  11.7 4.0 copy-start.11
  11.7 4.0 copy-start.12
  11.7 4.0 copy-start.13
  11.7 4.0 copy-start.14
  11.7 4.1 copy-start.15
  11.7 4.1 copy-start.16
  11.7 4.1 copy-start.17
  11.7 4.1 copy-start.18
  90.7 3.8 copy-start.1
  90.7 5.2 copy-start.9
  90.7 7.1 %copy-start.5 = (bf16[4,48,128]{2,1,0:T(8,128)(2,1)S(1)}, bf16[4,48,128]{2,1,0:T(8,128)(2,1)}, u32[]{:S(2)}) copy-start(bf16[4,48,128]{2,1,0:T(8,128)(2,1)} %get-tuple-element.57) | copy-start | bytes 147460
  93.7 147.5 %all-gather.7.cloned.1.call-start = ((), (), s32[]{:S(2)}) async-start(), calls=%async_computation.4 | async-start | bytes 3328000 | tf_op jit(solution)/shard_map/all_gather | solution.py:1299
  94.5 220.1 %reduce-scatter.10.cloned.1.call-start = ((), (), s32[]{:S(2)}) async-start(), calls=%async_computation.8 | async-start | bytes 3328000
  94.6 29.2 %collective-permute-start = (bf16[64,1600]{1,0:T(8,128)(2,1)S(1)}, bf16[64,1600]{1,0:T(8,128)(2,1)S(1)}, u32[]{:S(2)}, u32[]{:S(2)}) collective-permute-start(bf16[64,1600]{1,0:T(8,128)(2,1)S(1)} %slice.131), channel_id=1, source_target_pairs={{1,0},{2,1},{3,2},{5,4},{6,5},{7,6},{9,8},{10,9},{11,10},{13,12},{... | collective-permute-start | bytes 614408 | tf_op jit(solution)/shard_map/ppermute | solution.py:1279
  99.0 7.7 %copy-start.20 = (s32[32]{0:T(128)S(1)}, s32[32]{0:T(128)}, u32[]{:S(2)}) copy-start(s32[32]{0:T(128)} %param.25) | copy-start | bytes 388
  99.0 21.9 %copy-start.8 = (s32[4]{0:T(128)S(1)}, s32[4]{0:T(128)}, u32[]{:S(2)}) copy-start(s32[4]{0:T(128)} %constant.105.clone) | copy-start | bytes 52
  120.3 62.6 %copy-start.4 = (f32[1,1600]{1,0:T(1,128)}, f32[1,1600]{1,0:T(1,128)S(1)}, u32[]{:S(2)}) copy-start(f32[1,1600]{1,0:T(1,128)S(1)} %stack_reshape_squeeze.9.vec_ref) | copy-start | bytes 19204
  241.1 129.1 %reduce-scatter.8.cloned.1.call-start = ((), (), s32[]{:S(2)}) async-start(), calls=%async_computation.6 | async-start | bytes 3584000 | tf_op jit(solution)/shard_map/reduce_scatter | solution.py:1334
  265.2 150.1 %reduce-scatter.6.cloned.1.call-start = ((), (), s32[]{:S(2)}) async-start(), calls=%async_computation.5 | async-start | bytes 1064960 | tf_op jit(solution)/shard_map/reduce_scatter | solution.py:1334
  314.6 58.8 %copy-start.6 = (f32[4,1600]{1,0:T(4,128)S(1)}, f32[4,1600]{1,0:T(4,128)}, u32[]{:S(2)}) copy-start(f32[4,1600]{1,0:T(4,128)} %get-tuple-element.82) | copy-start | bytes 76804
  314.6 58.9 %copy-start.10 = (f32[1,800]{1,0:T(1,128)S(1)}, f32[1,800]{1,0:T(1,128)}, u32[]{:S(2)}) copy-start(f32[1,800]{1,0:T(1,128)} %get-tuple-element.84) | copy-start | bytes 9604
  370.1 154.5 %all-gather.9.cloned.1.call-start = ((), (), s32[]{:S(2)}) async-start(), calls=%async_computation.7 | async-start | bytes 6451200 | tf_op jit(solution)/shard_map/all_gather | solution.py:1349
  390.9 15.9 %copy-start.3 = (bf16[128,1600]{1,0:T(8,128)(2,1)S(1)}, bf16[128,1600]{1,0:T(8,128)(2,1)}, u32[]{:S(2)}) copy-start(bf16[128,1600]{1,0:T(8,128)(2,1)} %get-tuple-element.73) | copy-start | bytes 1228804
  508.6 14.2 %collective-permute-start.1 = (bf16[64,1600]{1,0:T(8,128)(2,1)S(1)}, bf16[64,1600]{1,0:T(8,128)(2,1)S(1)}, u32[]{:S(2)}, u32[]{:S(2)}) collective-permute-start(bf16[64,1600]{1,0:T(8,128)(2,1)S(1)} %constant_dynamic-slice_fusion), channel_id=1, source_target_pairs={{0,1},{1,2},{2,3},{4,5},{5,6},{6,7},{8,9},{9,10},{10,11},{12,13},{... | collective-permute-start | bytes 614408 | tf_op jit(solution)/shard_map/ppermute | solution.py:1399
  511.3 7.3 %copy-start.2 = (f32[128,1600]{1,0:T(8,128)S(1)}, f32[128,1600]{1,0:T(8,128)}, u32[]{:S(2)}) copy-start(f32[128,1600]{1,0:T(8,128)} %get-tuple-element.86) | copy-start | bytes 2457604
  511.3 8.8 %copy-start.7 = (f32[32,128]{1,0:T(8,128)S(1)}, f32[32,128]{1,0:T(8,128)}, u32[]{:S(2)}) copy-start(f32[32,128]{1,0:T(8,128)} %get-tuple-element.89) | copy-start | bytes 49156
  518.5 4.3 copy-start
Sparse Core Ops, SparseCore 0:
  93.8 86.7 all-gather.4
  182.8 53.3 all-gather.6
  241.3 55.1 reduce-scatter.9
  298.6 64.6 reduce-scatter.7
  370.3 23.2 reduce-scatter.5
  395.5 48.1 all-gather.8

commit v5 on v4

--- a/solution.py
+++ b/solution.py
@@ -95,26 +95,26 @@
     return far, near, local
 
 
-def plane_gather_finish(started, alls, sems, chips):
+def plane_gather_pass(started, alls, sems, chips, turns):
     far_send, far_recv, near_send, near_recv, local_sem = sems
     me, core, chip, sibling, to, come = plane_peers(chips)
     far, near, local = started
-    near = list(near)
-
-    def pass_on(i, all_ref, k):
-        far[i][k].wait_recv()
-        block = all_ref.at[come[k]]
-        if chips == 4 and k == 0:
-            far[i].append(send(block, block, far_send.at[i, 2], far_recv.at[i, 2], "ctx", to[1]))
-        near.append(send(block, block, near_send.at[i, k], near_recv.at[i, k], "ctx", sibling))
-
-    direct = 2 if chips == 4 else chips - 1
     for i, all_ref in enumerate(alls):
-        for k in range(direct):
-            pass_on(i, all_ref, k)
-    for i, all_ref in enumerate(alls):
-        for k in range(direct, chips - 1):
-            pass_on(i, all_ref, k)
+        for k in turns:
+            far[i][k].wait_recv()
+            block = all_ref.at[come[k]]
+            if chips == 4 and k == 0:
+                far[i].append(send(block, block, far_send.at[i, 2], far_recv.at[i, 2], "ctx", to[1]))
+            near.append(send(block, block, near_send.at[i, k], near_recv.at[i, k], "ctx", sibling))
+
+
+def plane_gather_middle(started, alls, sems, chips):
+    plane_gather_pass(started, alls, sems, chips, range(2 if chips == 4 else chips - 1))
+
+
+def plane_gather_end(started, alls, sems, chips):
+    plane_gather_pass(started, alls, sems, chips, range(2, chips - 1) if chips == 4 else ())
+    far, near, local = started
     for group in far:
         for copy in group:
             copy.wait_send()
@@ -122,11 +122,16 @@
         copy.wait()
 
 
+def plane_gather_finish(started, alls, sems, chips):
+    plane_gather_middle(started, alls, sems, chips)
+    plane_gather_end(started, alls, sems, chips)
+
+
 def plane_gather(owns, alls, sems, chips):
     plane_gather_finish(plane_gather_start(owns, alls, sems, chips), alls, sems, chips)
 
 
-def plane_scatter(block_of, mine, paired, arrived, sems, chips):
+def plane_scatter_stages(block_of, mine, paired, arrived, sems, chips, result):
     far_send, far_recv, near_send, near_recv, local_sem = sems
     me, core, chip, sibling, to, come = plane_peers(chips)
     targets = to + [me]
@@ -138,6 +143,7 @@
         near[k] = send(block_of(other), paired.at[k], near_send.at[k], near_recv.at[k], "ctx", sibling)
         local[k] = pltpu.make_async_copy(block_of(targets[k]), mine.at[k], local_sem.at[k])
         local[k].start()
+    yield
 
     def both(k):
         local[k].wait()
@@ -154,6 +160,7 @@
         mine[0] = both(0).astype(BF16)
         far[0] = dispatch(0, to[0])
         partial = both(1)
+        yield
         far[2].wait_recv()
         mine[1] = (partial + arrived[2].astype(F32)).astype(BF16)
         far[1] = dispatch(1, to[1])
@@ -165,6 +172,73 @@
             far[k] = dispatch(k, to[k])
         total = both(chips - 1)
         arriving = range(chips - 1)
+    yield
+    for k in arriving:
+        far[k].wait_recv()
+        total = total + arrived[k].astype(F32)
+    for copy in far + near:
+        copy.wait_send()
+    result.append(total)
+
+
+def plane_scatter(block_of, mine, paired, arrived, sems, chips):
+    result = []
+    for unused in plane_scatter_stages(block_of, mine, paired, arrived, sems, chips, result):
+        pass
+    return result[0]
+
+
+def gather_sems(chips, count=1):
+    return [DMA((count, chips - 1))] * 2 + [DMA((count, chips))] * 2 + [DMA((count,))]
+
+
+def scatter_orders(chips):
+    if chips == 4:
+        return [2, 0, 1, 3], [1, 0, 2, 3]
+    return list(range(chips)), list(range(chips))
+
+
+def plane_scatter_made(make, part, paired, arrived, sems, chips, meanwhile):
+    far_send, far_recv, near_send, near_recv = sems
+    me, core, chip, sibling, to, come = plane_peers(chips)
+    targets = to + [me]
+    order, crossed = scatter_orders(chips)
+    near, far = [None] * chips, [None] * (chips - 1)
+
+    def produce(k):
+        make(k, targets[k] // 2)
+        place = crossed[k]
+        near[place] = send(
+            part.at[k, 1 - core], paired.at[place], near_send.at[place], near_recv.at[place], "ctx", sibling
+        )
+
+    def both(k):
+        near[k].wait_recv()
+        return part[k, core].astype(F32) + paired[k].astype(F32)
+
+    def dispatch(k, values, target):
+        paired[k] = values.astype(BF16)
+        far[k] = send(paired.at[k], arrived.at[k], far_send.at[k], far_recv.at[k], "ctx", target)
+
+    if chips == 4:
+        produce(2)
+        produce(0)
+        dispatch(2, both(2), to[0])
+        produce(1)
+        dispatch(0, both(0), to[0])
+        produce(3)
+        partial = both(1)
+        far[2].wait_recv()
+        dispatch(1, partial + arrived[2].astype(F32), to[1])
+        arriving = [0, 1]
+    else:
+        for k in order:
+            produce(k)
+        for k in range(chips - 1):
+            dispatch(k, both(k), to[k])
+        arriving = range(chips - 1)
+    meanwhile()
+    total = both(chips - 1)
     for k in arriving:
         far[k].wait_recv()
         total = total + arrived[k].astype(F32)
@@ -173,8 +247,16 @@
     return total
 
 
-def gather_sems(chips, count=1):
-    return [DMA((count, chips - 1))] * 2 + [DMA((count, chips))] * 2 + [DMA((count,))]
+def made_scratch(chips, *block):
+    return [
+        pltpu.VMEM((chips, 2) + block, BF16),
+        pltpu.VMEM((chips,) + block, BF16),
+        pltpu.VMEM((chips - 1,) + block, BF16),
+        DMA((chips - 1,)),
+        DMA((chips - 1,)),
+        DMA((chips,)),
+        DMA((chips,)),
+    ]
 
 
 def scatter_scratch(chips, *block):
@@ -350,25 +432,96 @@
     )(part, tok, vecs)
 
 
-def third_kernel(chips, part_ref, mixed_ref, og_ref, vec_ref, dmixed_ref, sums_ref, all_ref, own, *scratch):
+def third_kernel(
+    chips,
+    h_hbm,
+    og_hbm,
+    act_hbm,
+    slope_hbm,
+    up_w_hbm,
+    down_w_hbm,
+    mixed_ref,
+    og_ref,
+    vec_ref,
+    dmixed_ref,
+    sums_ref,
+    all_ref,
+    out_hbm,
+    up_grad_ref,
+    up_sum_ref,
+    h_ref,
+    ogs_ref,
+    act_ref,
+    slope_ref,
+    up_w_ref,
+    down_w_ref,
+    d_up_ref,
+    out_ref,
+    load_sem,
+    out_sem,
+    own,
+    *scratch,
+):
     me, core, chip, sibling, to, come = plane_peers(chips)
+    made, gather = scratch[:7], scratch[7:]
+    loads = [
+        pltpu.make_async_copy(source, target, load_sem.at[k])
+        for k, (source, target) in enumerate(
+            [
+                (down_w_hbm, down_w_ref),
+                (og_hbm, ogs_ref),
+                (slope_hbm, slope_ref),
+                (up_w_hbm, up_w_ref),
+                (h_hbm, h_ref),
+                (act_hbm, act_ref),
+            ]
+        )
+    ]
+    for load in loads:
+        load.start()
     greet(to + [sibling])
     unit, inverse = normalize(mixed_ref[...])
-    grad = plane_scatter(lambda c: part_ref.at[c], *scratch[:3], scratch[3:8], chips)
+    rows = mixed_ref.shape[0]
+    for load in loads[:4]:
+        load.wait()
+    part = made[0]
+
+    def make(k, target):
+        span = pl.ds(pl.multiple_of(target * 2 * rows, 2 * rows), 2 * rows)
+        d_up = (nt(ogs_ref[span, :], down_w_ref[...]) * slope_ref[span, :]).astype(BF16)
+        d_up_ref[span, :] = d_up
+        d_h = nt(d_up, up_w_ref[...]).astype(BF16)
+        part[k, 0] = d_h[:rows]
+        part[k, 1] = d_h[rows:]
+
+    def meanwhile():
+        for load in loads[4:]:
+            load.wait()
+        d_up = d_up_ref[...]
+        up_sum_ref[...] = jnp.sum(d_up.astype(F32), axis=0, keepdims=True)
+        up_grad_ref[...] = tn(d_up, h_ref[...]).T.astype(BF16)
+        out_ref[...] = nn(act_ref[...], down_w_ref[...]).astype(BF16)
+        pltpu.make_async_copy(out_ref, out_hbm, out_sem).start()
+
+    grad = plane_scatter_made(make, *made[:3], made[3:], chips, meanwhile)
     out_grad = og_ref[...].astype(F32)
     dmixed = out_grad + norm_backward(grad, vec_ref[0:1, :], unit, inverse)
-    dmixed_ref[...] = dmixed
     low = dmixed.astype(BF16)
     own[...] = low
+    started = plane_gather_start([own], [all_ref], gather, chips)
+    dmixed_ref[...] = dmixed
     sums_ref[0:1, :] = jnp.sum(grad * unit, axis=0, keepdims=True)
     sums_ref[1:2, :] = jnp.sum(grad, axis=0, keepdims=True)
     sums_ref[2:3, :] = jnp.sum(low.astype(F32), axis=0, keepdims=True)
     sums_ref[3:4, :] = jnp.sum(out_grad, axis=0, keepdims=True)
-    plane_gather([own], [all_ref], scratch[8:], chips)
-
-
-def second_norm_back(part, mixed, og, vecs):
-    n_ctx, rows, width = part.shape
+    plane_gather_finish(started, [all_ref], gather, chips)
+    pltpu.make_async_copy(out_ref, out_hbm, out_sem).wait()
+
+
+def feed_back(values, out_grads, act, slope, up_weight, down_weight, mixed, og, vecs):
+    rows, width = mixed.shape
+    total_rows, hidden = act.shape
+    n_ctx = total_rows // rows
     chips = n_ctx // 2
     return pl.pallas_call(
         functools.partial(third_kernel, chips),
@@ -376,16 +529,31 @@
             jax.ShapeDtypeStruct((rows, width), F32),
             jax.ShapeDtypeStruct((4, width), F32),
             jax.ShapeDtypeStruct((n_ctx, rows, width), BF16),
+            jax.ShapeDtypeStruct((total_rows, width), BF16),
+            jax.ShapeDtypeStruct((width, hidden), BF16),
+            jax.ShapeDtypeStruct((1, hidden), F32),
         ),
-        in_specs=[ANY, VMEM, VMEM, VMEM],
-        out_specs=(VMEM, VMEM, ANY),
-        scratch_shapes=[pltpu.VMEM((rows, width), BF16)]
-        + scatter_scratch(chips, rows, width)
+        in_specs=[ANY] * 6 + [VMEM] * 3,
+        out_specs=(VMEM, VMEM, ANY, ANY, VMEM, VMEM),
+        scratch_shapes=[
+            pltpu.VMEM((total_rows, width), BF16),
+            pltpu.VMEM((total_rows, width), BF16),
+            pltpu.VMEM((total_rows, hidden), BF16),
+            pltpu.VMEM((total_rows, hidden), F32),
+            pltpu.VMEM((width, hidden), BF16),
+            pltpu.VMEM((hidden, width), BF16),
+            pltpu.VMEM((total_rows, hidden), BF16),
+            pltpu.VMEM((total_rows, width), BF16),
+            DMA((6,)),
+            DMA,
+            pltpu.VMEM((rows, width), BF16),
+        ]
+        + made_scratch(chips, rows, width)
         + gather_sems(chips),
         compiler_params=params(2),
         cost_estimate=SMALL,
-        name="scatter_back_gather",
-    )(part, mixed, og, vecs)
+        name="feed_back",
+    )(values, out_grads, act, slope, up_weight, down_weight, mixed, og, vecs)
 
 
 def fourth_kernel(
@@ -552,22 +720,242 @@
     )(part, qkv_part, outw_own, flat, tok, dmixed, vecs)
 
 
-def to_heads_kernel(
+def finish_kernel(
+    chips,
     planes,
     seqs,
-    chips,
+    h1_hbm,
+    d_hbm,
+    w_hbm,
+    out_part_ref,
+    outw_ref,
+    flat_ref,
     tok_ref,
-    part_ref,
+    dmixed_ref,
     mixed_ref,
     vec_ref,
-    down_ref,
-    head_ref,
+    grad_ref,
     out_ref,
-    down_all,
-    send_sems,
-    recv_sems,
-    local_sem,
+    qkv_all,
+    outw_all,
+    sums_ref,
+    flat_out,
+    h1_ref,
+    d_ref,
+    w_ref,
+    load_sem,
+    dw_ref,
+    q_arrived,
+    q_own,
+    q_send,
+    q_recv,
+    outw_arrived,
+    outw_own,
+    o_send,
+    o_recv,
+    rows_own,
+    rows_arrived,
+    r_send,
+    r_recv,
+    small,
+    small_own,
+    small_z,
+    small_c,
+    flat_own,
+    flat_z,
+    flat_c,
+    z_send,
+    z_recv,
+    c_send,
+    c_recv,
     *scratch,
+):
+    n_ctx = 2 * chips
+    pairs = planes // seqs
+    me, core, chip, sibling, to, come = plane_peers(chips)
+    plane, others = other_planes(planes)
+    around = [lax.rem(me + k, n_ctx) for k in range(1, n_ctx)]
+    made, out_scatter, outw_sems, qkv_sems = scratch[:7], scratch[7:15], scratch[15:20], scratch[20:]
+    loads = [
+        pltpu.make_async_copy(source, target, load_sem.at[k])
+        for k, (source, target) in enumerate([(d_hbm, d_ref), (h1_hbm, h1_ref), (w_hbm, w_ref)])
+    ]
+    for load in loads:
+        load.start()
+    greet(around, others)
+    outw_sent = [
+        send(outw_ref.at[peer], outw_arrived.at[k], o_send.at[k], o_recv.at[k], "fsdp", peer)
+        for k, peer in enumerate(others)
+    ]
+    flat_sent = [
+        send(flat_ref.at[peer], flat_z.at[k], z_send.at[0, k], z_recv.at[0, k], "fsdp", peer)
+        for k, peer in enumerate(others)
+    ]
+    unit, inverse = normalize(tok_ref[...].astype(F32))
+
+    for load in loads:
+        load.wait()
+    quarter = dw_ref.shape[1]
+    dw = tn(d_ref[...], h1_ref[...]).T.astype(BF16)
+    for j in range(planes):
+        dw_ref[j] = dw[j * quarter : (j + 1) * quarter]
+    pushed = [
+        send(dw_ref.at[peer], q_arrived.at[plane], q_send.at[k], q_recv.at[k], "fsdp", peer)
+        for k, peer in enumerate(others)
+    ]
+    q_arrived[plane] = dw_ref[plane]
+
+    part = made[0]
+    half = part.shape[3]
+
+    def make(k, target):
+        blocks = []
+        for j in range(planes):
+            start = pl.multiple_of(j * n_ctx * half + target * 2 * half, 2 * half)
+            blocks.append(d_ref[pl.ds(start, 2 * half), :])
+        d_h = nt(jnp.concatenate(blocks, axis=0), w_ref[...]).astype(BF16)
+        for j in range(planes):
+            for side in range(2):
+                start = (2 * j + side) * half
+                part[k, side, j] = d_h[start : start + half]
+
+    total = plane_scatter_made(make, *made[:3], made[3:], chips, lambda: None)
+    rows_own[...] = total.astype(BF16)
+    rows_sent = [
+        send(rows_own.at[peer], rows_arrived.at[plane], r_send.at[k], r_recv.at[k], "fsdp", peer)
+        for k, peer in enumerate(others)
+    ]
+    rows_arrived[plane] = rows_own[plane]
+
+    total = outw_ref[plane].astype(F32)
+    for k, copy in enumerate(outw_sent):
+        copy.wait()
+        total = total + outw_arrived[k].astype(F32)
+    outw_own[...] = total.astype(BF16)
+    outw_started = plane_gather_start([outw_own], [outw_all], outw_sems, chips)
+    out_total = []
+    out_stages = plane_scatter_stages(
+        lambda c: out_part_ref.at[c], *out_scatter[:3], out_scatter[3:], chips, out_total
+    )
+    next(out_stages)
+    next(out_stages)
+    for copy in pushed:
+        copy.wait()
+    for pair in range(pairs):
+        terms = [q_arrived[seq * pairs + pair].astype(F32) for seq in range(seqs)]
+        q_own[pair] = sum(terms[1:], terms[0]).astype(BF16)
+    qkv_started = plane_gather_start([q_own], [qkv_all], qkv_sems, chips)
+    plane_gather_middle(outw_started, [outw_all], outw_sems, chips)
+    next(out_stages, None)
+    plane_gather_middle(qkv_started, [qkv_all], qkv_sems, chips)
+
+    for copy in rows_sent:
+        copy.wait()
+    halves = []
+    for seq in range(seqs):
+        terms = [rows_arrived[seq * pairs + pair].astype(F32) for pair in range(pairs)]
+        halves.append(sum(terms[1:], terms[0]))
+    grad = jnp.concatenate(halves, axis=0)
+    sums = jnp.concatenate(
+        [jnp.sum(grad * unit, axis=0, keepdims=True), jnp.sum(grad, axis=0, keepdims=True)], axis=0
+    )
+    small[...] = jnp.zeros_like(small)
+    for j in range(planes):
+        small[j, 0:2, 0:quarter] = sums[:, j * quarter : (j + 1) * quarter]
+    small_sent = [
+        send(small.at[peer], small_z.at[k], z_send.at[1, k], z_recv.at[1, k], "fsdp", peer)
+        for k, peer in enumerate(others)
+    ]
+    grad_ref[...] = dmixed_ref[...] + norm_backward(grad, vec_ref[0:1, :], unit, inverse)
+    small_total = small[plane]
+    flat_total = flat_ref[plane]
+    for k in range(planes - 1):
+        flat_sent[k].wait()
+        small_sent[k].wait()
+        small_total = small_total + small_z[k]
+        flat_total = flat_total + flat_z[k]
+    small_own[...] = small_total
+    flat_own[...] = flat_total
+    sent = []
+    for k, peer in enumerate(around):
+        sent.append(send(small_own, small_c.at[k], c_send.at[0, k], c_recv.at[0, k], "ctx", peer))
+        sent.append(send(flat_own, flat_c.at[k], c_send.at[1, k], c_recv.at[1, k], "ctx", peer))
+    for unused in out_stages:
+        pass
+    out_ref[...] = (mixed_ref[...] + out_total[0] + vec_ref[1:2, :]).astype(BF16)
+    plane_gather_end(outw_started, [outw_all], outw_sems, chips)
+    plane_gather_end(qkv_started, [qkv_all], qkv_sems, chips)
+    for copy in sent:
+        copy.wait()
+    for k in range(n_ctx - 1):
+        small_total = small_total + small_c[k]
+        flat_total = flat_total + flat_c[k]
+    sums_ref[...] = small_total
+    flat_out[...] = flat_total
+
+
+def finish(h1, d_qkv, weight, out_part, outw_part, flat, tok, dmixed, mixed, vecs):
+    n_ctx, rows, width = out_part.shape
+    planes, half = outw_part.shape[0], h1.shape[0] // (outw_part.shape[0] * n_ctx)
+    seqs = rows // half
+    quarter, columns = width // planes, weight.shape[1]
+    chips, pairs = n_ctx // 2, planes // seqs
+    size = (8, quarter + -quarter % LANES)
+    piece = outw_part.shape[1:]
+    return pl.pallas_call(
+        functools.partial(finish_kernel, chips, planes, seqs),
+        out_shape=(
+            jax.ShapeDtypeStruct((rows, width), F32),
+            jax.ShapeDtypeStruct((rows, width), BF16),
+            jax.ShapeDtypeStruct((n_ctx, pairs, quarter, columns), BF16),
+            jax.ShapeDtypeStruct((n_ctx,) + piece, BF16),
+            jax.ShapeDtypeStruct(size, F32),
+            jax.ShapeDtypeStruct(flat.shape[1:], F32),
+        ),
+        in_specs=[ANY] * 4 + [VMEM] * 6,
+        out_specs=(VMEM, VMEM, ANY, ANY, VMEM, VMEM),
+        scratch_shapes=[
+            pltpu.VMEM(h1.shape, BF16),
+            pltpu.VMEM(d_qkv.shape, BF16),
+            pltpu.VMEM(weight.shape, BF16),
+            DMA((3,)),
+            pltpu.VMEM((planes, quarter, columns), BF16),
+            pltpu.VMEM((planes, quarter, columns), BF16),
+            pltpu.VMEM((pairs, quarter, columns), BF16),
+            DMA((planes - 1,)),
+            DMA((planes - 1,)),
+            pltpu.VMEM((planes - 1,) + piece, BF16),
+            pltpu.VMEM(piece, BF16),
+            DMA((planes - 1,)),
+            DMA((planes - 1,)),
+            pltpu.VMEM((planes, half, width), BF16),
+            pltpu.VMEM((planes, half, width), BF16),
+            DMA((planes - 1,)),
+            DMA((planes - 1,)),
+            pltpu.VMEM((planes,) + size, F32),
+            pltpu.VMEM(size, F32),
+            pltpu.VMEM((planes - 1,) + size, F32),
+            pltpu.VMEM((n_ctx - 1,) + size, F32),
+            pltpu.VMEM(flat.shape[1:], F32),
+            pltpu.VMEM((planes - 1,) + flat.shape[1:], F32),
+            pltpu.VMEM((n_ctx - 1,) + flat.shape[1:], F32),
+            DMA((2, planes - 1)),
+            DMA((2, planes - 1)),
+            DMA((2, n_ctx - 1)),
+            DMA((2, n_ctx - 1)),
+        ]
+        + made_scratch(chips, planes, half, width)
+        + scatter_scratch(chips, rows, width)
+        + gather_sems(chips)
+        + gather_sems(chips),
+        compiler_params=params(9),
+        cost_estimate=SMALL,
+        name="finish",
+    )(h1, d_qkv, weight, out_part, outw_part, flat, tok, dmixed, mixed, vecs)
+
+
+def to_heads_kernel(
+    planes, seqs, chips, tok_ref, down_ref, head_ref, down_all, send_sems, recv_sems, local_sem, *sems
 ):
     ctx_me, core, chip, sibling, to, come = plane_peers(chips)
     me, others = other_planes(planes)
@@ -584,34 +972,27 @@
     ]
     copies.append(pltpu.make_async_copy(source(me), head_ref.at[me], local_sem))
     copies[-1].start()
-    total = plane_scatter(lambda c: part_ref.at[c], *scratch[:3], scratch[3:8], chips)
-    gathered = plane_gather_start([down_ref], [down_all], scratch[8:], chips)
-    out_ref[...] = (mixed_ref[...] + total + vec_ref[...]).astype(BF16)
-    plane_gather_finish(gathered, [down_all], scratch[8:], chips)
+    plane_gather([down_ref], [down_all], sems, chips)
     for copy in copies:
         copy.wait()
 
 
-def to_heads(tok, planes, cid, part, mixed, vec, down_own):
+def to_heads(tok, planes, cid, down_own):
     n_ctx, seqs, local_rows, width = tok.shape
     chips = n_ctx // 2
-    rows, model = mixed.shape
     return pl.pallas_call(
         functools.partial(to_heads_kernel, planes, seqs, chips),
         out_shape=(
             jax.ShapeDtypeStruct((planes, n_ctx, local_rows, LANES), BF16),
-            jax.ShapeDtypeStruct((rows, model), BF16),
             jax.ShapeDtypeStruct((n_ctx,) + down_own.shape, BF16),
         ),
-        in_specs=[ANY, ANY, VMEM, VMEM, ANY],
-        out_specs=(ANY, VMEM, ANY),
-        scratch_shapes=[DMA((planes - 1,)), DMA((planes - 1,)), DMA]
-        + scatter_scratch(chips, rows, model)
-        + gather_sems(chips),
+        in_specs=[ANY, ANY],
+        out_specs=(ANY, ANY),
+        scratch_shapes=[DMA((planes - 1,)), DMA((planes - 1,)), DMA] + gather_sems(chips),
         compiler_params=params(cid),
         cost_estimate=SMALL,
         name="to_heads",
-    )(tok, part, mixed, vec, down_own)
+    )(tok, down_own)
 
 
 def to_tokens_kernel(
@@ -819,7 +1200,7 @@
 
 
 def long_backward_kernel(
-    tile, order_ref, qkv_ref, grad_ref, att_ref, lse_ref, out_ref, q_s, k_s, v_s, g_s, kt_s, dq_s, dk_s, dv_s
+    tile, order_ref, qkv_ref, grad_ref, att_ref, lse_ref, out_ref, sum_ref, q_s, k_s, v_s, g_s, kt_s, dq_s, dk_s, dv_s
 ):
     blocks, half = grad_ref.shape[0], grad_ref.shape[1]
     length = blocks * half
@@ -877,10 +1258,13 @@
         dq_s[q_span, :] = dq.T.astype(BF16)
 
     unsort_blocks(order_ref, [dq_s, dk_s, dv_s], out_ref, blocks, half)
+    for k, source in enumerate([dq_s, dk_s, dv_s]):
+        values = source[...].astype(BF16).astype(F32)
+        sum_ref[:, k * LANES : (k + 1) * LANES] = jnp.sum(values, axis=0, keepdims=True)
 
 
 def backward_kernel(
-    tile, order_ref, qkv_ref, grad_ref, att_ref, lse_ref, out_ref, q_s, k_s, v_s, g_s, kt_s, dq_s, dk_s, dv_s, qh_s, gh_s, dot_s, p_s, ds_s
+    tile, order_ref, qkv_ref, grad_ref, att_ref, lse_ref, out_ref, sum_ref, q_s, k_s, v_s, g_s, kt_s, dq_s, dk_s, dv_s, qh_s, gh_s, dot_s, p_s, ds_s
 ):
     blocks, half = grad_ref.shape[0], grad_ref.shape[1]
     length = blocks * half
@@ -930,6 +1314,9 @@
         dq = [nn(kt_s[head * HD : (head + 1) * HD, upto], ds_s[head, upto, span]) for head in range(2)]
         dq_s[span, :] = (jnp.concatenate(dq, axis=0) * scale).T.astype(BF16)
     unsort_blocks(order_ref, [dq_s, dk_s, dv_s], out_ref, blocks, half)
+    for k, source in enumerate([dq_s, dk_s, dv_s]):
+        values = source[...].astype(BF16).astype(F32)
+        sum_ref[:, k * LANES : (k + 1) * LANES] = jnp.sum(values, axis=0, keepdims=True)
 
 
 def attend_backward(order, qkv, grad, att, lse, tile):
@@ -939,9 +1326,12 @@
     flipped = pltpu.VMEM((LANES, length), BF16)
     return pl.pallas_call(
         functools.partial(backward_kernel if short else long_backward_kernel, tile),
-        out_shape=jax.ShapeDtypeStruct((blocks, half, 3 * LANES), BF16),
+        out_shape=(
+            jax.ShapeDtypeStruct((blocks, half, 3 * LANES), BF16),
+            jax.ShapeDtypeStruct((1, 3 * LANES), F32),
+        ),
         in_specs=[SMEM, VMEM, VMEM, VMEM, VMEM],
-        out_specs=VMEM,
+        out_specs=(VMEM, VMEM),
         scratch_shapes=[rows, rows, rows, rows, flipped, rows, rows, rows]
         + [pltpu.VMEM((2, length, LANES), BF16)] * 2
         + [pltpu.VMEM((2, length), F32), pltpu.VMEM((2, tile, length), BF16), pltpu.VMEM((2, length, length), BF16)]
@@ -1148,65 +1538,6 @@
         cost_estimate=SMALL,
         name="feed_up",
     )(values, out_grad, weight, shift[None, :])
-
-
-def down_kernel(
-    h_ref, og_ref, act_ref, slope_ref, up_w_ref, down_w_ref, out_ref, d_h_ref, grad_ref, sum_ref, total
-):
-    step = pl.program_id(0)
-    d_up = (nt(og_ref[...], down_w_ref[...]) * slope_ref[...]).astype(BF16)
-    d_h_ref[...] = nt(d_up, up_w_ref[...]).astype(BF16)
-    sums = jnp.sum(d_up.astype(F32), axis=0, keepdims=True)
-    term = tn(d_up, h_ref[...])
-    out_ref[...] = nn(act_ref[...], down_w_ref[...]).astype(BF16)
-
-    @pl.when(step == 0)
-    def _():
-        total[...] = term
-        sum_ref[...] = sums
-
-    @pl.when(step > 0)
-    def _():
-        total[...] += term
-        sum_ref[...] += sums
-
-    @pl.when(step == pl.num_programs(0) - 1)
-    def _():
-        grad_ref[...] = total[...].T.astype(BF16)
-
-
-def feed_down(values, out_grad, act, slope, up_weight, down_weight):
-    rows, width = values.shape
-    hidden = up_weight.shape[1]
-    block = rows_block(rows, 512)
-    return pl.pallas_call(
-        down_kernel,
-        grid=(rows // block,),
-        out_shape=(
-            jax.ShapeDtypeStruct((rows, width), BF16),
-            jax.ShapeDtypeStruct((rows, width), BF16),
-            jax.ShapeDtypeStruct((width, hidden), BF16),
-            jax.ShapeDtypeStruct((1, hidden), F32),
-        ),
-        in_specs=[
-            row_spec(block, width),
-            row_spec(block, width),
-            row_spec(block, hidden),
-            row_spec(block, hidden),
-            whole_block((width, hidden)),
-            whole_block((hidden, width)),
-        ],
-        out_specs=(
-            row_spec(block, width),
-            row_spec(block, width),
-            pl.BlockSpec((width, hidden), lambda i: (0, 0)),
-            pl.BlockSpec((1, hidden), lambda i: (0, 0)),
-        ),
-        scratch_shapes=[pltpu.VMEM((hidden, width), F32)],
-        compiler_params=params(),
-        cost_estimate=SMALL,
-        name="feed_down",
-    )(values, out_grad, act, slope, up_weight, down_weight)
 
 
 def local(
@@ -1335,24 +1666,20 @@
 
     act, slope, down_part = feed_up(h2, og_all, up_slice, bias_up)
     down_own_grad = reduce_own(down_part)
-    out_part, d_h2, up_part, d_up_sum = feed_down(h2, og_all, act, slope, up_slice, down_slice)
+    d_mixed, sums2, d_branch, out_part, up_part, d_up_sum = feed_back(
+        h2, og_all, act, slope, up_slice, down_slice, mixed, og, gain2[None, :]
+    )
     up_own_grad = reduce_own(up_part)
-    out_part, d_h2 = [part.reshape(n_ctx, rows, width) for part in (out_part, d_h2)]
-    d_mixed, sums2, d_branch = second_norm_back(d_h2, mixed, og, gain2[None, :])
+    out_part = out_part.reshape(n_ctx, rows, width)
     d_branch = d_branch.reshape(plane_rows, width)
     d_att, out_w_part = out_back(att, d_branch, out_slice)
-    d_att_heads, block_out, down_parts = to_heads(
-        d_att.reshape(n_ctx, seqs, local_rows, span), planes, 7, out_part, mixed, bias_d[None, :], down_own_grad
+    d_att_heads, down_parts = to_heads(d_att.reshape(n_ctx, seqs, local_rows, span), planes, 7, down_own_grad)
+    d_qkv, d_qkv_sum = attend_backward(
+        order, qkv, d_att_heads.reshape(blocks, half, LANES), att_exact, lse, tile
     )
-    d_att_heads, out_w_part = lax.optimization_barrier((d_att_heads, out_w_part))
-    out_own_grad = reduce_own(out_w_part)
-    up_parts = lax.all_gather(up_own_grad, "ctx", axis=0)
-    d_qkv = attend_backward(order, qkv, d_att_heads.reshape(blocks, half, LANES), att_exact, lse, tile)
-    d_qkv = d_qkv.reshape(length, 3 * pair_span)
-    d_h1, qkv_part, d_qkv_sum = product_back(h1, d_qkv, qkv_slice)
-    qkv_part = qkv_part.reshape(planes, quarter, 3 * pair_span)
-    d_h1 = d_h1.reshape(planes, n_ctx, local_rows, width)
-    d_qkv_sum = d_qkv_sum[0]
+    d_qkv, d_qkv_sum = d_qkv.reshape(length, 3 * pair_span), d_qkv_sum[0]
+    down_parts, unused = lax.optimization_barrier((down_parts, d_qkv))
+    down_grad = down_parts.reshape(ff_quarter, width).astype(F32)
 
     d_up_sum = d_up_sum.reshape(planes, ff_piece)
     up_spread = lax.dynamic_update_slice(jnp.zeros((planes, ff_quarter), F32), d_up_sum, (0, c * ff_piece))
@@ -1372,15 +1699,39 @@
     size = flat.shape[1]
     flat = jnp.pad(flat, ((0, 0), (0, -size % (8 * LANES)))).reshape(planes, -1, LANES)
 
-    grad_tok, qkv_parts, out_parts, sums1, totals = first_norm_back(
-        d_h1, qkv_part, out_own_grad, flat, tok, d_mixed, gain1[None, :]
-    )
+    if length <= SHORT:
+        grad_tok, block_out, qkv_parts, out_parts, sums1, totals = finish(
+            h1,
+            d_qkv,
+            qkv_slice,
+            out_part,
+            out_w_part.reshape(planes, HD, width),
+            flat,
+            tok,
+            d_mixed,
+            mixed,
+            jnp.stack([gain1, bias_d]),
+        )
+    else:
+        d_h1, qkv_part, unused = product_back(h1, d_qkv, qkv_slice)
+        grad_tok, qkv_parts, out_parts, sums1, totals = first_norm_back(
+            d_h1.reshape(planes, n_ctx, local_rows, width),
+            qkv_part.reshape(planes, quarter, 3 * pair_span),
+            reduce_own(out_w_part),
+            flat,
+            tok,
+            d_mixed,
+            gain1[None, :],
+        )
+        total = lax.psum_scatter(out_part.reshape(plane_rows, width), "ctx", scatter_dimension=0, tiled=True)
+        block_out = (mixed + total.astype(F32) + bias_d).astype(BF16)
+    qkv_parts, up_own_grad = lax.optimization_barrier((qkv_parts, up_own_grad))
+    up_parts = lax.all_gather(up_own_grad, "ctx", axis=0)
     sums1 = sums1[:2, :quarter]
     totals = totals.reshape(-1)
     sums = totals[: 6 * quarter].reshape(6, quarter)
     up_bias_grad = totals[6 * quarter : size]
 
-    down_grad = down_parts.reshape(ff_quarter, width).astype(F32)
     block = quarter // 5
     up_pieces = [
         (j * ff_quarter + d * ff_piece, d, j * ff_piece, ff_piece) for j in range(planes) for d in range(n_ctx)

time: 545 us -> 517 us (0.949)
  Pallas kernels: 471 us -> 424 us
  waiting for transfers between devices: 1.33 us -> 16.4 us
  starting transfers between devices: 4.21 us -> 10.1 us
    pallas_call x4 -> x2, Pallas kernels: 172 us -> 144 us  [the longest x1 94.7 us: finish(): pl.pallas_call(functools.partial(finish_kernel, chips, planes, seqs), out...]
    pallas_call x1, Pallas kernels: 55.5 us -> 35.4 us  [to_heads(): pl.pallas_call(functools.partial(to_heads_kernel, planes, seqs, chips), o...]
    all_gather x1, waiting for transfers between devices: 0.01 us -> 15.6 us  [local(): up_parts = lax.all_gather(up_own_grad, 'ctx', axis=0)]
    ppermute x1, starting transfers between devices: 2.67 us -> 8.63 us  [local(): lax.ppermute(tail_rows, 'fsdp', [(j, j + 1) for j in range(planes - 1)])]
  transfers between devices with their start and end apart: 8 -> 7, of which waited for: 0 -> 1; matrix products, arithmetic and copies ran while one was open for 5% -> 5% of each run, Pallas kernels for 73% -> 68%
where the time goes in v5:
time: 517 us; the launch traced here: 512 us
  Pallas kernels  424 us (82%)
  local copies, waits for them, and re-layouts  28.9 us (6%)
  between operations  19.4 us (4%)
  waiting for transfers between devices  16.4 us (3%)
  other arithmetic  13.1 us (3%)
  starting transfers between devices  10.1 us (2%)
    pallas_call x1, Pallas kernels, finish(): pl.pallas_call(functools.partial(finish_kernel, chips, planes, seqs), out...  94.7 us
    pallas_call x1, Pallas kernels, first_norm_gather(): pl.pallas_call(functools.partial(first_kernel, chips, planes, seqs, width...  69.3 us
    pallas_call x1, Pallas kernels, to_tokens(): pl.pallas_call(functools.partial(to_tokens_kernel, planes, seqs), out_sha...  54 us
    pallas_call x1, Pallas kernels, feed_back(): pl.pallas_call(functools.partial(third_kernel, chips), out_shape=(jax.Sha...  49.7 us
    pallas_call x1, Pallas kernels, second_norm_gather(): pl.pallas_call(functools.partial(second_kernel, chips), out_shape=(jax.Sh...  42.8 us
    pallas_call x1, Pallas kernels, to_heads(): pl.pallas_call(functools.partial(to_heads_kernel, planes, seqs, chips), o...  35.4 us
    pallas_call x2, Pallas kernels, assemble(): pl.pallas_call(functools.partial(assemble_kernel, pieces), grid=(rows //...  16.9 us
    pallas_call x1, Pallas kernels, attend_backward(): pl.pallas_call(functools.partial(backward_kernel if short else long_backw...  16.8 us
  transfers between devices with their start and end apart: 7, of which 1 were waited for; matrix products, arithmetic and copies ran while one was open for 5% of the time, Pallas kernels for 68%

profile of v5, /device:TPU:0, one launch (start us, length us, event | category | flops | bytes accessed | tf_op | source)
XLA Modules:
  0.0 512.1 jit_solution(11348143785159167144)
XLA Ops:
  8.1 1.8 copy.55
  9.9 1.8 copy.56
  11.8 1.9 constant_dynamic-slice_fusion.13
  14.1 0.9 pad_maximum_fusion.1.weight_ref
  15.8 2.0 constant_dynamic-slice_fusion.6
  17.9 3.6 concatenate.74.vec_ref
  21.5 69.3 %norm_gather.1 = (bf16[4,48,128]{2,1,0:T(8,128)(2,1)}, bf16[8,128,1600]{2,1,0:T(8,128)(2,1)}, bf16[4,8,64,1600]{3,2,1,0:T(8,128)(2,1)}, bf16[4,400,384]{2,1,0:T(8,128)(2,1)}) custom-call(bf16[128,1600]{1,0:T(8,128)(2,1)} %bitcast.95, bf16[128,1600]{1,0:T(8,128)(2,1)} %bitcast.104, bf16[48,128]{1,0:T(8,128)(2,1)} %concatenate.74.vec_ref, ...), custom_call_target="tpu_custom_call" | custom-call | flops 1 | bytes 1 | tf_op jit(solution)/shard_map/norm_gather/pallas_call | solution.py:374
  90.8 1.7 constant_dynamic-slice_fusion.5
  92.5 1.2 pad_maximum_fusion
  94.6 1.3 collective-permute-start
  99.1 7.8 %product.2 = bf16[2048,384]{1,0:T(8,128)(2,1)} custom-call(bf16[2048,1600]{1,0:T(8,128)(2,1)} %bitcast.86, bf16[1600,384]{1,0:T(8,128)(2,1)} %bitcast.101, f32[1,384]{1,0:T(1,128)} %broadcast_in_dim.30.shift_ref), custom_call_target="tpu_custom_call" | custom-call | flops 1 | bytes 1 | tf_op jit(solution)/shard_map/product/pallas_call | solution.py:1390
  107.7 12.4 %attend_forward.1 = (bf16[64,32,128]{2,1,0:T(8,128)(2,1)}, f32[2048,128]{1,0:T(8,128)}, f32[2,2048]{1,0:T(2,128)}) custom-call(s32[64]{0:T(128)} %pad_add_fusion.order_ref, bf16[64,32,384]{2,1,0:T(8,128)(2,1)} %bitcast.88), custom_call_target="tpu_custom_call" | custom-call | flops 1 | bytes 1 | tf_op jit(solution)/shard_map/attend_forward/pallas_call | solution.py:1184
  124.6 54.0 %to_tokens.1 = (bf16[8,2,64,256]{3,2,1,0:T(8,128)(2,1)}, bf16[4,64,1600]{2,1,0:T(8,128)(2,1)}) custom-call(bf16[4,8,64,128]{3,2,1,0:T(8,128)(2,1)} %bitcast.121, bf16[64,1600]{1,0:T(8,128)(2,1)} %fusion.3.weight_ref), custom_call_target="tpu_custom_call" | custom-call | flops 1 | bytes 1 | tf_op jit(solution)/shard_map/to_tokens/pallas_call | solution.py:1025
  179.2 3.7 product.3
  183.0 42.8 %scatter_norm_gather.1 = (f32[128,1600]{1,0:T(8,128)}, bf16[8,128,1600]{2,1,0:T(8,128)(2,1)}) custom-call(bf16[8,128,1600]{2,1,0:T(8,128)(2,1)} %bitcast.90, bf16[128,1600]{1,0:T(8,128)(2,1)} %bitcast.96, f32[3,1600]{1,0:T(4,128)} %pad_maximum_fusion.2.vec_ref), custom_call_target="tpu_custom_call" | custom-call | flops 1 | bytes 1 | tf_op jit(solution)/shard_map/scatter_norm_gather/pallas_call | solution.py:418
  225.8 15.4 %feed_up.1 = (bf16[1024,800]{1,0:T(8,128)(2,1)}, f32[1024,800]{1,0:T(8,128)}, bf16[800,1600]{1,0:T(8,128)(2,1)}) custom-call(bf16[1024,1600]{1,0:T(8,128)(2,1)} %bitcast.93, bf16[1024,1600]{1,0:T(8,128)(2,1)} %bitcast.91, bf16[1600,800]{1,0:T(8,128)(2,1)} %all-gather.5.cloned.1.call-done.weight_ref.up_w_hbm, f32[1,800]{1,0:T(1,128)} %broadcast_in_dim_reshape.3.shift_ref), custom_call_target="tpu_custom_call" | custom-call | flops 1 | bytes 1 | tf_op jit(solution)/shard_map/feed_up/pallas_call | solution.py:1517
  241.3 49.7 %feed_back.1 = (f32[128,1600]{1,0:T(8,128)}, f32[4,1600]{1,0:T(4,128)}, bf16[8,128,1600]{2,1,0:T(8,128)(2,1)}, bf16[1024,1600]{1,0:T(8,128)(2,1)}, bf16[1600,800]{1,0:T(8,128)(2,1)}, /*index=5*/f32[1,800]{1,0:T(1,128)}) custom-call(bf16[1024,1600]{1,0:T(8,128)(2,1)} %bitcast.94, bf16[1024,1600]{1,0:T(8,128)(2,1)} %bitcast.92, ...), custom_call_target="tpu_custom_call" | custom-call | flops 1 | bytes 1 | tf_op jit(solution)/shard_map/feed_back/pallas_call | solution.py:526
  293.2 5.4 %out_back.1 = (bf16[1024,256]{1,0:T(8,128)(2,1)}, bf16[256,1600]{1,0:T(8,128)(2,1)}) custom-call(bf16[1024,256]{1,0:T(8,128)(2,1)} %bitcast.113, bf16[1024,1600]{1,0:T(8,128)(2,1)} %bitcast.109, bf16[256,1600]{1,0:T(8,128)(2,1)} %bitcast.108), custom_call_target="tpu_custom_call" | custom-call | flops 1 | bytes 1 | tf_op jit(solution)/shard_map/out_back/pallas_call | solution.py:1472
  299.1 35.4 %to_heads.1 = (bf16[4,8,64,128]{3,2,1,0:T(8,128)(2,1)}, bf16[8,200,1600]{2,1,0:T(8,128)(2,1)}) custom-call(bf16[8,2,64,256]{3,2,1,0:T(8,128)(2,1)} %bitcast.120, bf16[200,1600]{1,0:T(8,128)(2,1)} %reduce-scatter.7.cloned.1.call-done.down_ref), custom_call_target="tpu_custom_call" | custom-call | flops 1 | bytes 1 | tf_op jit(solution)/shard_map/to_heads/pallas_call | solution.py:983
  334.6 16.8 %attend_backward.1 = (bf16[64,32,384]{2,1,0:T(8,128)(2,1)}, f32[1,384]{1,0:T(1,128)}) custom-call(s32[64]{0:T(128)} %pad_add_fusion.order_ref, bf16[64,32,384]{2,1,0:T(8,128)(2,1)} %bitcast.89, bf16[64,32,128]{2,1,0:T(8,128)(2,1)} %bitcast.122, f32[2048,128]{1,0:T(8,128)} %get-tuple-element.71.att_ref, f32[2,2048]{1,0:T(2,128)} %get-tuple-element.72.lse_ref), custom_call_target="tpu_custom_call" | custom-call | flops 1 | bytes 1 | tf_op jit(solution)/shard_map/attend_backward/pallas_call | solution.py:1327
  352.1 0.8 bitcast_dynamic-update-slice_fusion.2
  354.8 94.7 %finish.1 = (f32[128,1600]{1,0:T(8,128)}, bf16[128,1600]{1,0:T(8,128)(2,1)}, bf16[8,2,400,384]{3,2,1,0:T(8,128)(2,1)}, bf16[8,64,1600]{2,1,0:T(8,128)(2,1)}, f32[8,512]{1,0:T(8,128)}, /*index=5*/f32[32,128]{1,0:T(8,128)}) custom-call(bf16[2048,1600]{1,0:T(8,128)(2,1)} %bitcast.87, bf16[2048,384]{1,0:T(8,128)(2,1)} %bitcast.114, bf16[1600,384]{1,0:T(8,128)(2,1)} %bitcast.102, ...), custom_call_target="tpu_custom_call" | custom-call | flops 1 | bytes 1 | tf_op jit(solution)/shard_map/finish/pallas_call | solution.py:905
  450.2 1.0 constant_dynamic-slice_fusion
  451.2 8.6 %collective-permute-start.1 = (bf16[64,1600]{1,0:T(8,128)(2,1)S(1)}, bf16[64,1600]{1,0:T(8,128)(2,1)S(1)}, u32[]{:S(2)}, u32[]{:S(2)}) collective-permute-start(bf16[64,1600]{1,0:T(8,128)(2,1)S(1)} %constant_dynamic-slice_fusion), channel_id=1, source_target_pairs={{0,1},{1,2},{2,3},{4,5},{5,6},{6,7},{8,9},{9,10},{10,11},{12,13},{... | collective-permute-start | bytes 614408 | tf_op jit(solution)/shard_map/ppermute | solution.py:1750
  459.9 8.6 %assemble.2 = f32[400,4800]{1,0:T(8,128)} custom-call(bf16[16,400,384]{2,1,0:T(8,128)(2,1)} %bitcast.103), custom_call_target="tpu_custom_call" | custom-call | tf_op jit(solution)/shard_map/assemble/pallas_call | solution.py:1353
  468.5 1.6 copy.64
  470.1 1.2 copy.65
  471.9 1.4 fusion.6
  473.3 5.5 %bitcast_convert_fusion = f32[1600,1600]{1,0:T(8,128)} fusion(bf16[8,200,1600]{2,1,0:T(8,128)(2,1)S(1)} %bitcast.100), kind=kLoop, calls=%fused_computation | loop fusion | flops 2560000 | bytes 15360000 | tf_op jit(solution)/shard_map/convert_element_type | solution.py:1682
  479.5 1.8 fusion.1
  481.3 15.6 %all-gather.9.cloned.1.call-done = bf16[3200,800]{1,0:T(8,128)(2,1)} async-done(((bf16[400,800]{1,0:T(8,128)(2,1)}), bf16[3200,800]{1,0:T(8,128)(2,1)}) %all-gather.9.cloned.1.call-update) | async-done | bytes 5120016 | tf_op jit(solution)/shard_map/all_gather | solution.py:1729
  496.9 8.3 %assemble.3 = f32[400,6400]{1,0:T(8,128)} custom-call(bf16[8,400,800]{2,1,0:T(8,128)(2,1)} %bitcast.98), custom_call_target="tpu_custom_call" | custom-call | tf_op jit(solution)/shard_map/assemble/pallas_call | solution.py:1353
  (122 shorter events, 14.8 us)
Async XLA Ops:
  7.2 218.6 %all-gather.5.cloned.1.call-start = ((), (), s32[]{:S(2)}) async-start(), calls=%async_computation.2 | async-start | bytes 3584000 | tf_op jit(solution)/shard_map/all_gather | solution.py:1638
  11.7 3.3 copy-start.19
  11.7 4.0 copy-start.11
  11.7 4.0 copy-start.12
  11.7 4.0 copy-start.13
  11.7 4.0 copy-start.14
  11.7 4.1 copy-start.15
  11.7 4.1 copy-start.16
  11.7 4.1 copy-start.17
  11.8 4.1 copy-start.18
  90.8 3.8 copy-start.1
  90.8 5.2 %copy-start.9 = (s32[5]{0:T(128)S(1)}, s32[5]{0:T(128)}, u32[]{:S(2)}) copy-start(s32[5]{0:T(128)} %constant.104.clone) | copy-start | bytes 64
  90.8 7.1 %copy-start.5 = (bf16[4,48,128]{2,1,0:T(8,128)(2,1)S(1)}, bf16[4,48,128]{2,1,0:T(8,128)(2,1)}, u32[]{:S(2)}) copy-start(bf16[4,48,128]{2,1,0:T(8,128)(2,1)} %get-tuple-element.56) | copy-start | bytes 147460
  93.8 147.5 %all-gather.7.cloned.1.call-start = ((), (), s32[]{:S(2)}) async-start(), calls=%async_computation.3 | async-start | bytes 3328000 | tf_op jit(solution)/shard_map/all_gather | solution.py:1630
  94.5 204.6 %reduce-scatter.7.cloned.1.call-start = ((), (), s32[]{:S(2)}) async-start(), calls=%async_computation.6 | async-start | bytes 3328000
  94.6 29.2 %collective-permute-start = (bf16[64,1600]{1,0:T(8,128)(2,1)S(1)}, bf16[64,1600]{1,0:T(8,128)(2,1)S(1)}, u32[]{:S(2)}, u32[]{:S(2)}) collective-permute-start(bf16[64,1600]{1,0:T(8,128)(2,1)S(1)} %slice.131), channel_id=1, source_target_pairs={{1,0},{2,1},{3,2},{5,4},{6,5},{7,6},{9,8},{10,9},{11,10},{13,12},{... | collective-permute-start | bytes 614408 | tf_op jit(solution)/shard_map/ppermute | solution.py:1610
  99.1 7.8 %copy-start.20 = (s32[32]{0:T(128)S(1)}, s32[32]{0:T(128)}, u32[]{:S(2)}) copy-start(s32[32]{0:T(128)} %param.25) | copy-start | bytes 388
  99.1 22.0 %copy-start.8 = (s32[4]{0:T(128)S(1)}, s32[4]{0:T(128)}, u32[]{:S(2)}) copy-start(s32[4]{0:T(128)} %constant.105.clone) | copy-start | bytes 52
  120.2 62.8 %copy-start.4 = (f32[1,1600]{1,0:T(1,128)}, f32[1,1600]{1,0:T(1,128)S(1)}, u32[]{:S(2)}) copy-start(f32[1,1600]{1,0:T(1,128)S(1)} %stack_reshape_squeeze.15.vec_ref) | copy-start | bytes 19204
  241.2 208.4 %reduce-scatter.5.cloned.1.call-start = ((), (), s32[]{:S(2)}) async-start(), calls=%async_computation.4 | async-start | bytes 3584000 | tf_op jit(solution)/shard_map/reduce_scatter | solution.py:1665
  291.0 7.6 %copy-start.6 = (f32[4,1600]{1,0:T(4,128)S(1)}, f32[4,1600]{1,0:T(4,128)}, u32[]{:S(2)}) copy-start(f32[4,1600]{1,0:T(4,128)} %get-tuple-element.76) | copy-start | bytes 76804
  291.0 7.7 %copy-start.10 = (f32[1,800]{1,0:T(1,128)S(1)}, f32[1,800]{1,0:T(1,128)}, u32[]{:S(2)}) copy-start(f32[1,800]{1,0:T(1,128)} %get-tuple-element.78) | copy-start | bytes 9604
  291.0 205.9 %all-gather.9.cloned.1.call-start = ((), (), s32[]{:S(2)}) async-start(), calls=%async_computation.5 | async-start | bytes 6451200 | tf_op jit(solution)/shard_map/all_gather | solution.py:1729
  451.2 28.3 %collective-permute-start.1 = (bf16[64,1600]{1,0:T(8,128)(2,1)S(1)}, bf16[64,1600]{1,0:T(8,128)(2,1)S(1)}, u32[]{:S(2)}, u32[]{:S(2)}) collective-permute-start(bf16[64,1600]{1,0:T(8,128)(2,1)S(1)} %constant_dynamic-slice_fusion), channel_id=1, source_target_pairs={{0,1},{1,2},{2,3},{4,5},{5,6},{6,7},{8,9},{9,10},{10,11},{12,13},{... | collective-permute-start | bytes 614408 | tf_op jit(solution)/shard_map/ppermute | solution.py:1750
  459.8 13.5 %slice-start = ((s8[5324800]{0:T(1024)(128)(4,1)}), s8[4194304]{0:T(1024)(128)(4,1)S(1)}, s32[]{:S(2)}) async-start(s8[5324800]{0:T(1024)(128)(4,1)} %bitcast.99), calls=%async_computation.7 | async-start | bytes 8388608
  459.9 8.6 %copy-start.2 = (f32[128,1600]{1,0:T(8,128)S(1)}, f32[128,1600]{1,0:T(8,128)}, u32[]{:S(2)}) copy-start(f32[128,1600]{1,0:T(8,128)} %get-tuple-element.81) | copy-start | bytes 2457604
  459.9 10.2 %copy-start.3 = (bf16[128,1600]{1,0:T(8,128)(2,1)S(1)}, bf16[128,1600]{1,0:T(8,128)(2,1)}, u32[]{:S(2)}) copy-start(bf16[128,1600]{1,0:T(8,128)(2,1)} %get-tuple-element.80) | copy-start | bytes 1228804
  459.9 11.4 %copy-start.7 = (f32[32,128]{1,0:T(8,128)S(1)}, f32[32,128]{1,0:T(8,128)}, u32[]{:S(2)}) copy-start(f32[32,128]{1,0:T(8,128)} %get-tuple-element.86) | copy-start | bytes 49156
  459.9 13.4 %slice-start.1 = ((s8[5324800]{0:T(1024)(128)(4,1)}), s8[1130496]{0:T(1024)(128)(4,1)S(1)}, s32[]{:S(2)}) async-start(s8[5324800]{0:T(1024)(128)(4,1)} %bitcast.99), calls=%async_computation.8 | async-start | bytes 2260992
  473.3 6.2 %copy-start = (bf16[8,64,1600]{2,1,0:T(8,128)(2,1)S(1)}, bf16[8,64,1600]{2,1,0:T(8,128)(2,1)}, u32[]{:S(2)}) copy-start(bf16[8,64,1600]{2,1,0:T(8,128)(2,1)} %get-tuple-element.87) | copy-start | bytes 4915204
Sparse Core Ops, SparseCore 0:
  93.9 86.7 all-gather.4
  182.3 53.3 all-gather.6
  241.3 55.1 reduce-scatter.6
  298.6 64.9 reduce-scatter.4
  449.7 47.1 all-gather.8

commit v6 on v5

--- a/solution.py
+++ b/solution.py
@@ -296,10 +296,12 @@
     og_ref,
     vec_ref,
     weight_ref,
+    out_w_ref,
     vecs_ref,
     ogs_ref,
     h1_ref,
     weights_ref,
+    next_ref,
     own,
     column,
     v_send,
@@ -310,6 +312,9 @@
     w_send,
     w_recv,
     w_local,
+    n_send,
+    n_recv,
+    n_local,
     *sems,
 ):
     me, core, chip, sibling, to, come = plane_peers(chips)
@@ -323,6 +328,27 @@
     ]
     local = pltpu.make_async_copy(vec_ref, vecs_ref.at[plane], v_local)
     local.start()
+    lead = out_w_ref.at[pl.ds(0, HD)]
+    last = plane == planes - 1
+
+    def lead_copy():
+        return pltpu.make_async_remote_copy(
+            src_ref=lead,
+            dst_ref=next_ref,
+            send_sem=n_send,
+            recv_sem=n_recv,
+            device_id={"fsdp": lax.rem(plane + planes - 1, planes)},
+            device_id_type=MESH,
+        )
+
+    @pl.when(plane > 0)
+    def _():
+        lead_copy().start()
+
+    @pl.when(last)
+    def _():
+        pltpu.make_async_copy(lead, next_ref, n_local).start()
+
     og_started = plane_gather_start([og_ref], [ogs_ref], og_sems, chips)
     unit, inverse = normalize(tok_ref[...].astype(F32))
     for copy in copies + [local]:
@@ -356,19 +382,34 @@
     sources = [plane] + [lax.rem(plane + planes - k, planes) for k in range(1, planes)]
     blocks = [half_of(plane)] + [column.at[k] for k in range(planes - 1)]
     started = [plane_gather_start([blocks[0]], [h1_ref.at[sources[0]]], h1_sems[0], chips)]
-    plane_gather_finish(og_started, [ogs_ref], og_sems, chips)
+    plane_gather_middle(og_started, [ogs_ref], og_sems, chips)
     for k in range(1, planes):
         halves[k - 1].wait_recv()
         started.append(plane_gather_start([blocks[k]], [h1_ref.at[sources[k]]], h1_sems[k], chips))
+        plane_gather_middle(started[k - 1], [h1_ref.at[sources[k - 1]]], h1_sems[k - 1], chips)
+    plane_gather_middle(started[-1], [h1_ref.at[sources[-1]]], h1_sems[-1], chips)
+    plane_gather_end(og_started, [ogs_ref], og_sems, chips)
     for k in range(planes):
-        plane_gather_finish(started[k], [h1_ref.at[sources[k]]], h1_sems[k], chips)
+        plane_gather_end(started[k], [h1_ref.at[sources[k]]], h1_sems[k], chips)
+    @pl.when(plane > 0)
+    def _():
+        lead_copy().wait_send()
+
+    @pl.when(last)
+    def _():
+        pltpu.make_async_copy(lead, next_ref, n_local).wait()
+
+    @pl.when(plane < planes - 1)
+    def _():
+        lead_copy().wait_recv()
+
     for copy in halves:
         copy.wait_send()
     for copy in weights:
         copy.wait()
 
 
-def first_norm_gather(tok, og, vec, weight, n_ctx, planes, seqs):
+def first_norm_gather(tok, og, vec, weight, out_weight, n_ctx, planes, seqs):
     rows, width = tok.shape
     chips, half = n_ctx // 2, rows // seqs
     return pl.pallas_call(
@@ -378,9 +419,10 @@
             jax.ShapeDtypeStruct((n_ctx, rows, width), BF16),
             jax.ShapeDtypeStruct((planes, n_ctx, half, width), BF16),
             jax.ShapeDtypeStruct((planes,) + weight.shape[1:], BF16),
+            jax.ShapeDtypeStruct((HD, width), BF16),
         ),
-        in_specs=[VMEM, ANY, VMEM, ANY],
-        out_specs=(VMEM, ANY, ANY, ANY),
+        in_specs=[VMEM, ANY, VMEM, ANY, ANY],
+        out_specs=(VMEM, ANY, ANY, ANY, ANY),
         scratch_shapes=[
             pltpu.VMEM((rows, width), BF16),
             pltpu.VMEM((planes - 1, half, width), BF16),
@@ -392,28 +434,40 @@
             DMA((planes - 1,)),
             DMA((planes - 1,)),
             DMA,
+            DMA,
+            DMA,
+            DMA,
         ]
         + gather_sems(chips)
         + gather_sems(chips) * planes,
         compiler_params=params(0),
         cost_estimate=SMALL,
         name="norm_gather",
-    )(tok, og, vec, weight)
-
-
-def second_kernel(chips, part_ref, tok_ref, vec_ref, mixed_ref, all_ref, own, *scratch):
+    )(tok, og, vec, weight, out_weight)
+
+
+def second_kernel(chips, att_ref, weight_ref, tok_ref, vec_ref, mixed_ref, all_ref, own, *scratch):
     me, core, chip, sibling, to, come = plane_peers(chips)
     greet(to + [sibling])
-    total = plane_scatter(lambda c: part_ref.at[c], *scratch[:3], scratch[3:8], chips)
+    rows = tok_ref.shape[0]
+    part = scratch[0]
+
+    def make(k, target):
+        span = pl.ds(pl.multiple_of(target * 2 * rows, 2 * rows), 2 * rows)
+        branch = nn(att_ref[span, :], weight_ref[...]).astype(BF16)
+        part[k, 0] = branch[:rows]
+        part[k, 1] = branch[rows:]
+
+    total = plane_scatter_made(make, *scratch[:3], scratch[3:7], chips, lambda: None)
     mixed = tok_ref[...].astype(F32) + total + vec_ref[2:3, :]
     mixed_ref[...] = mixed
     unit, inverse = normalize(mixed)
     own[...] = (unit * vec_ref[0:1, :] + vec_ref[1:2, :]).astype(BF16)
-    plane_gather([own], [all_ref], scratch[8:], chips)
-
-
-def second_norm_gather(part, tok, vecs):
-    n_ctx, rows, width = part.shape
+    plane_gather([own], [all_ref], scratch[7:], chips)
+
+
+def second_norm_gather(att, weight, tok, vecs, n_ctx):
+    rows, width = tok.shape
     chips = n_ctx // 2
     return pl.pallas_call(
         functools.partial(second_kernel, chips),
@@ -421,15 +475,15 @@
             jax.ShapeDtypeStruct((rows, width), F32),
             jax.ShapeDtypeStruct((n_ctx, rows, width), BF16),
         ),
-        in_specs=[ANY, VMEM, VMEM],
+        in_specs=[VMEM] * 4,
         out_specs=(VMEM, ANY),
         scratch_shapes=[pltpu.VMEM((rows, width), BF16)]
-        + scatter_scratch(chips, rows, width)
+        + made_scratch(chips, rows, width)
         + gather_sems(chips),
         compiler_params=params(1),
         cost_estimate=SMALL,
         name="scatter_norm_gather",
-    )(part, tok, vecs)
+    )(att, weight, tok, vecs)
 
 
 def third_kernel(
@@ -727,16 +781,15 @@
     h1_hbm,
     d_hbm,
     w_hbm,
-    out_part_ref,
+    up_ref,
     outw_ref,
     flat_ref,
     tok_ref,
     dmixed_ref,
-    mixed_ref,
     vec_ref,
     grad_ref,
-    out_ref,
     qkv_all,
+    up_all,
     outw_all,
     sums_ref,
     flat_out,
@@ -775,7 +828,7 @@
     me, core, chip, sibling, to, come = plane_peers(chips)
     plane, others = other_planes(planes)
     around = [lax.rem(me + k, n_ctx) for k in range(1, n_ctx)]
-    made, out_scatter, outw_sems, qkv_sems = scratch[:7], scratch[7:15], scratch[15:20], scratch[20:]
+    made, outw_sems, qkv_sems, up_sems = scratch[:7], scratch[7:12], scratch[12:17], scratch[17:]
     loads = [
         pltpu.make_async_copy(source, target, load_sem.at[k])
         for k, (source, target) in enumerate([(d_hbm, d_ref), (h1_hbm, h1_ref), (w_hbm, w_ref)])
@@ -827,26 +880,21 @@
     ]
     rows_arrived[plane] = rows_own[plane]
 
+    up_started = plane_gather_start([up_ref], [up_all], up_sems, chips)
     total = outw_ref[plane].astype(F32)
     for k, copy in enumerate(outw_sent):
         copy.wait()
         total = total + outw_arrived[k].astype(F32)
     outw_own[...] = total.astype(BF16)
     outw_started = plane_gather_start([outw_own], [outw_all], outw_sems, chips)
-    out_total = []
-    out_stages = plane_scatter_stages(
-        lambda c: out_part_ref.at[c], *out_scatter[:3], out_scatter[3:], chips, out_total
-    )
-    next(out_stages)
-    next(out_stages)
     for copy in pushed:
         copy.wait()
     for pair in range(pairs):
         terms = [q_arrived[seq * pairs + pair].astype(F32) for seq in range(seqs)]
         q_own[pair] = sum(terms[1:], terms[0]).astype(BF16)
     qkv_started = plane_gather_start([q_own], [qkv_all], qkv_sems, chips)
+    plane_gather_middle(up_started, [up_all], up_sems, chips)
     plane_gather_middle(outw_started, [outw_all], outw_sems, chips)
-    next(out_stages, None)
     plane_gather_middle(qkv_started, [qkv_all], qkv_sems, chips)
 
     for copy in rows_sent:
@@ -880,11 +928,9 @@
     for k, peer in enumerate(around):
         sent.append(send(small_own, small_c.at[k], c_send.at[0, k], c_recv.at[0, k], "ctx", peer))
         sent.append(send(flat_own, flat_c.at[k], c_send.at[1, k], c_recv.at[1, k], "ctx", peer))
-    for unused in out_stages:
-        pass
-    out_ref[...] = (mixed_ref[...] + out_total[0] + vec_ref[1:2, :]).astype(BF16)
     plane_gather_end(outw_started, [outw_all], outw_sems, chips)
     plane_gather_end(qkv_started, [qkv_all], qkv_sems, chips)
+    plane_gather_end(up_started, [up_all], up_sems, chips)
     for copy in sent:
         copy.wait()
     for k in range(n_ctx - 1):
@@ -894,9 +940,11 @@
     flat_out[...] = flat_total
 
 
-def finish(h1, d_qkv, weight, out_part, outw_part, flat, tok, dmixed, mixed, vecs):
-    n_ctx, rows, width = out_part.shape
-    planes, half = outw_part.shape[0], h1.shape[0] // (outw_part.shape[0] * n_ctx)
+def finish(h1, d_qkv, weight, up_own, outw_part, flat, tok, dmixed, vecs):
+    rows, width = tok.shape
+    planes = outw_part.shape[0]
+    n_ctx = lax.axis_size("ctx")
+    half = h1.shape[0] // (planes * n_ctx)
     seqs = rows // half
     quarter, columns = width // planes, weight.shape[1]
     chips, pairs = n_ctx // 2, planes // seqs
@@ -906,14 +954,14 @@
         functools.partial(finish_kernel, chips, planes, seqs),
         out_shape=(
             jax.ShapeDtypeStruct((rows, width), F32),
-            jax.ShapeDtypeStruct((rows, width), BF16),
             jax.ShapeDtypeStruct((n_ctx, pairs, quarter, columns), BF16),
+            jax.ShapeDtypeStruct((n_ctx,) + up_own.shape, BF16),
             jax.ShapeDtypeStruct((n_ctx,) + piece, BF16),
             jax.ShapeDtypeStruct(size, F32),
             jax.ShapeDtypeStruct(flat.shape[1:], F32),
         ),
-        in_specs=[ANY] * 4 + [VMEM] * 6,
-        out_specs=(VMEM, VMEM, ANY, ANY, VMEM, VMEM),
+        in_specs=[ANY] * 4 + [VMEM] * 5,
+        out_specs=(VMEM, ANY, ANY, ANY, VMEM, VMEM),
         scratch_shapes=[
             pltpu.VMEM(h1.shape, BF16),
             pltpu.VMEM(d_qkv.shape, BF16),
@@ -945,13 +993,13 @@
             DMA((2, n_ctx - 1)),
         ]
         + made_scratch(chips, planes, half, width)
-        + scatter_scratch(chips, rows, width)
+        + gather_sems(chips)
         + gather_sems(chips)
         + gather_sems(chips),
         compiler_params=params(9),
         cost_estimate=SMALL,
         name="finish",
-    )(h1, d_qkv, weight, out_part, outw_part, flat, tok, dmixed, mixed, vecs)
+    )(h1, d_qkv, weight, up_own, outw_part, flat, tok, dmixed, vecs)
 
 
 def to_heads_kernel(
@@ -1128,17 +1176,103 @@
     unsort_blocks(order_ref, [o_s], out_ref, blocks, half)
 
 
-def forward_kernel(tile, order_ref, qkv_ref, out_ref, att_ref, lse_ref, q_s, k_s, v_s, o_s, s_s, p_s):
-    blocks, half = out_ref.shape[0], out_ref.shape[1]
-    length = blocks * half
-    tiles = length // tile
-    sort_blocks(order_ref, qkv_ref, [q_s, k_s, v_s], blocks, half)
+def block_places(order, n_ctx):
+    blocks = order.shape[0]
+    places = jnp.stack([order // (2 * n_ctx), lax.rem(order // 2, n_ctx), lax.rem(order, 2)]).astype(jnp.int32)
+    match = order[:, None] == jnp.arange(blocks)[None, :]
+    inverse = jnp.sum(jnp.where(match, jnp.arange(blocks)[:, None], 0), axis=0).astype(jnp.int32)
+    return places, inverse
+
+
+def sort_places(order_ref, source, targets):
+    blocks, half = order_ref.shape[1], source.shape[3]
+
+    def body(block, carry):
+        row = source[order_ref[0, block], order_ref[1, block], order_ref[2, block]]
+        start = pl.multiple_of(block * half, half)
+        for k, target in enumerate(targets):
+            target[pl.ds(start, half), :] = row[:, k * LANES : (k + 1) * LANES]
+        return carry
+
+    lax.fori_loop(0, blocks, body, 0)
+
+
+def unsort_places(place_ref, sources, target):
+    n_ctx = target.shape[1]
+
+    def body(place, carry):
+        block = place_ref[place]
+        f, c, side = place // (2 * n_ctx), lax.rem(place // 2, n_ctx), lax.rem(place, 2)
+        for k, source in enumerate(sources):
+            target[f, c, side, :, k * LANES : (k + 1) * LANES] = source[block]
+        return carry
+
+    lax.fori_loop(0, place_ref.shape[0], body, 0)
+
+
+def attend_kernel(
+    tile,
+    planes,
+    seqs,
+    order_ref,
+    place_ref,
+    h1_hbm,
+    w_hbm,
+    shift_ref,
+    out_w_ref,
+    qkv_ref,
+    att_ref,
+    lse_ref,
+    tok_ref,
+    out_ws_ref,
+    h1_ref,
+    w_ref,
+    load_sem,
+    heads,
+    a_send,
+    a_recv,
+    a_local,
+    w_send,
+    w_recv,
+    w_local,
+    q_s,
+    k_s,
+    v_s,
+    o_s,
+    s_s,
+    p_s,
+):
+    me, others = other_planes(planes)
+    pairs = planes // seqs
+    n_ctx, half = qkv_ref.shape[1], qkv_ref.shape[3]
+    length = att_ref.shape[0]
+    tiles, step = length // tile, tile // half
+    rows = length // planes
+    loads = [pltpu.make_async_copy(w_hbm, w_ref, load_sem.at[planes])]
+    for j in range(planes):
+        span = pl.ds(j * rows, rows)
+        loads.append(pltpu.make_async_copy(h1_hbm.at[span], h1_ref.at[span], load_sem.at[j]))
+    for load in loads:
+        load.start()
+    greet((), others)
+    moved = [
+        send(out_w_ref, out_ws_ref.at[me], w_send.at[k], w_recv.at[k], "fsdp", peer) for k, peer in enumerate(others)
+    ]
+    moved.append(pltpu.make_async_copy(out_w_ref, out_ws_ref.at[me], w_local))
+    moved[-1].start()
+
+    loads[0].wait()
+    for j in range(planes):
+        loads[1 + j].wait()
+        values = nn(h1_ref[j * rows : (j + 1) * rows, :], w_ref[...]) + shift_ref[...]
+        qkv_ref[j] = values.astype(BF16).reshape(n_ctx, 2, half, values.shape[1])
+
+    sort_places(order_ref, qkv_ref, [q_s, k_s, v_s])
     scale = HD ** (-0.5)
     rows_iota = lax.broadcasted_iota(jnp.int32, (tile, tile), 0)
     cols_iota = lax.broadcasted_iota(jnp.int32, (tile, tile), 1)
     allowed = cols_iota <= rows_iota
     masks = [lane_mask(tile, head) for head in range(2)]
-
     for qt in range(tiles):
         q_span = slice(qt * tile, (qt + 1) * tile)
         query = q_s[q_span, :] * jnp.asarray(scale, BF16)
@@ -1169,8 +1303,52 @@
             lse_ref[head : head + 1, q_span] = lse.T[0:1, :]
         att = jnp.where(masks[0], parts[0], parts[1])
         att_ref[q_span, :] = att
-        o_s[q_span, :] = att.astype(BF16)
-    unsort_blocks(order_ref, [o_s], out_ref, blocks, half)
+        o_s[qt * step : (qt + 1) * step] = att.astype(BF16).reshape(step, half, LANES)
+    unsort_places(place_ref, [o_s], heads)
+
+    start = pl.multiple_of(lax.rem(me, pairs) * LANES, LANES)
+    target = tok_ref.at[:, me // pairs, :, :, pl.ds(start, LANES)]
+    moved += [
+        send(heads.at[peer], target, a_send.at[k], a_recv.at[k], "fsdp", peer) for k, peer in enumerate(others)
+    ]
+    moved.append(pltpu.make_async_copy(heads.at[me], target, a_local))
+    moved[-1].start()
+    for copy in moved:
+        copy.wait()
+
+
+def attend(places, inverse, h1, weight, shift, out_own, n_ctx, planes, seqs, half, tile):
+    length = h1.shape[0]
+    lanes = weight.shape[1]
+    blocks = length // half
+    width = (planes // seqs) * LANES
+    rows_s = pltpu.VMEM((length, LANES), BF16)
+    sems = [DMA((planes - 1,)), DMA((planes - 1,)), DMA]
+    return pl.pallas_call(
+        functools.partial(attend_kernel, tile, planes, seqs),
+        out_shape=(
+            jax.ShapeDtypeStruct((planes, n_ctx, 2, half, lanes), BF16),
+            jax.ShapeDtypeStruct((length, LANES), F32),
+            jax.ShapeDtypeStruct((2, length), F32),
+            jax.ShapeDtypeStruct((n_ctx, seqs, 2, half, width), BF16),
+            jax.ShapeDtypeStruct((planes,) + out_own.shape, BF16),
+        ),
+        in_specs=[SMEM, SMEM, ANY, ANY, VMEM, ANY],
+        out_specs=(VMEM, VMEM, VMEM, ANY, ANY),
+        scratch_shapes=[
+            pltpu.VMEM(h1.shape, BF16),
+            pltpu.VMEM(weight.shape, BF16),
+            DMA((planes + 1,)),
+            pltpu.VMEM((planes, n_ctx, 2, half, LANES), BF16),
+        ]
+        + sems
+        + sems
+        + [rows_s, rows_s, rows_s, pltpu.VMEM((blocks, half, LANES), BF16)]
+        + [pltpu.VMEM((2, tile, length), F32), pltpu.VMEM((2, tile, length), BF16)],
+        compiler_params=params(5),
+        cost_estimate=SMALL,
+        name="attend",
+    )(places, inverse, h1, weight, shift, out_own)
 
 
 SMEM = pl.BlockSpec(memory_space=pltpu.SMEM)
@@ -1180,9 +1358,9 @@
 def attend_forward(order, qkv, tile):
     blocks, half, lanes = qkv.shape
     length = blocks * half
-    rows, short = pltpu.VMEM((length, LANES), BF16), length <= SHORT
+    rows = pltpu.VMEM((length, LANES), BF16)
     return pl.pallas_call(
-        functools.partial(forward_kernel if short else long_forward_kernel, tile),
+        functools.partial(long_forward_kernel, tile),
         out_shape=(
             jax.ShapeDtypeStruct((blocks, half, LANES), BF16),
             jax.ShapeDtypeStruct((length, LANES), F32),
@@ -1190,9 +1368,7 @@
         ),
         in_specs=[SMEM, VMEM],
         out_specs=(VMEM, VMEM, VMEM),
-        scratch_shapes=[rows, rows, rows, rows, pltpu.VMEM((2, tile, length), F32), pltpu.VMEM((2, tile, length), BF16)]
-        if short
-        else [rows, rows, rows, pltpu.VMEM((LANES, length), BF16), rows],
+        scratch_shapes=[rows, rows, rows, pltpu.VMEM((LANES, length), BF16), rows],
         compiler_params=params(),
         cost_estimate=SMALL,
         name="attend_forward",
@@ -1263,14 +1439,97 @@
         sum_ref[:, k * LANES : (k + 1) * LANES] = jnp.sum(values, axis=0, keepdims=True)
 
 
-def backward_kernel(
-    tile, order_ref, qkv_ref, grad_ref, att_ref, lse_ref, out_ref, sum_ref, q_s, k_s, v_s, g_s, kt_s, dq_s, dk_s, dv_s, qh_s, gh_s, dot_s, p_s, ds_s
+def branch_back_kernel(
+    tile,
+    planes,
+    seqs,
+    chips,
+    order_ref,
+    place_ref,
+    db_hbm,
+    w_hbm,
+    at_hbm,
+    qkv_hbm,
+    att_hbm,
+    down_ref,
+    out_part_ref,
+    mixed_ref,
+    vec_ref,
+    lse_ref,
+    out_ref,
+    sum_ref,
+    out_w_ref,
+    block_ref,
+    down_all,
+    db_ref,
+    w_ref,
+    at_ref,
+    qkv_ref,
+    att_ref,
+    load_sem,
+    d_att,
+    heads,
+    h_send,
+    h_recv,
+    h_local,
+    q_s,
+    k_s,
+    v_s,
+    g_s,
+    kt_s,
+    dq_s,
+    dk_s,
+    dv_s,
+    qh_s,
+    gh_s,
+    dot_s,
+    p_s,
+    ds_s,
+    *scratch,
 ):
-    blocks, half = grad_ref.shape[0], grad_ref.shape[1]
+    n_ctx = 2 * chips
+    ctx_me, core, chip, sibling, to, come = plane_peers(chips)
+    me, others = other_planes(planes)
+    pairs = planes // seqs
+    out_scatter, down_sems = scratch[:8], scratch[8:]
+    loads = [
+        pltpu.make_async_copy(source, target, load_sem.at[k])
+        for k, (source, target) in enumerate(
+            [(db_hbm, db_ref), (w_hbm, w_ref), (qkv_hbm, qkv_ref), (at_hbm, at_ref), (att_hbm, att_ref)]
+        )
+    ]
+    for load in loads:
+        load.start()
+    greet(to + [sibling], others)
+    down_started = plane_gather_start([down_ref], [down_all], down_sems, chips)
+    out_total = []
+    out_stages = plane_scatter_stages(
+        lambda c: out_part_ref.at[c], *out_scatter[:3], out_scatter[3:], chips, out_total
+    )
+    next(out_stages)
+
+    loads[0].wait()
+    loads[1].wait()
+    d_att[...] = nt(db_ref[...], w_ref[...]).astype(BF16).reshape(d_att.shape)
+
+    def source(unit):
+        start = pl.multiple_of(lax.rem(unit, pairs) * LANES, LANES)
+        return d_att.at[:, unit // pairs, :, :, pl.ds(start, LANES)]
+
+    moved = [
+        send(source(unit), heads.at[me], h_send.at[k], h_recv.at[k], "fsdp", unit) for k, unit in enumerate(others)
+    ]
+    moved.append(pltpu.make_async_copy(source(me), heads.at[me], h_local))
+    moved[-1].start()
+    for load in loads[2:]:
+        load.wait()
+    out_w_ref[...] = tn(at_ref[...], db_ref[...]).astype(BF16)
+
+    blocks, half = dq_s.shape[0], dq_s.shape[1]
     length = blocks * half
-    tiles = length // tile
-    sort_blocks(order_ref, qkv_ref, [q_s, k_s, v_s], blocks, half)
-    sort_blocks(order_ref, grad_ref, [g_s], blocks, half)
+    tiles, step = length // tile, tile // half
+
+    sort_places(order_ref, qkv_ref, [q_s, k_s, v_s])
     scale = HD ** (-0.5)
     rows_iota = lax.broadcasted_iota(jnp.int32, (tile, tile), 0)
     cols_iota = lax.broadcasted_iota(jnp.int32, (tile, tile), 1)
@@ -1280,12 +1539,23 @@
         span = slice(t * tile, (t + 1) * tile)
         kt_s[:, span] = k_s[span, :].T
         query = q_s[span, :] * jnp.asarray(scale, BF16)
+        for head in range(2):
+            qh_s[head, span, :] = jnp.where(masks[head], query, jnp.zeros_like(query))
+    next(out_stages)
+    for copy in moved:
+        copy.wait()
+    sort_places(order_ref, heads, [g_s])
+    for t in range(tiles):
+        span = slice(t * tile, (t + 1) * tile)
         grad = g_s[span, :]
         product = (grad.astype(F32) * att_ref[span, :]).T
         for head in range(2):
-            qh_s[head, span, :] = jnp.where(masks[head], query, jnp.zeros_like(query))
             gh_s[head, span, :] = jnp.where(masks[head], grad, jnp.zeros_like(grad))
             dot_s[head : head + 1, span] = jnp.sum(product[head * HD : (head + 1) * HD], axis=0, keepdims=True)
+    plane_gather_middle(down_started, [down_all], down_sems, chips)
+
+    def keep(target, index, values):
+        target[index * step : (index + 1) * step] = values.astype(BF16).reshape(step, half, LANES)
 
     for kt in range(tiles):
         k_span = slice(kt * tile, (kt + 1) * tile)
@@ -1306,37 +1576,95 @@
             dk_one = nn(ds_s[head, k_span, rest], qh_s[head, rest, :])
             dv = dv_one if dv is None else dv + dv_one
             dk = dk_one if dk is None else dk + dk_one
-        dk_s[k_span, :] = dk.astype(BF16)
-        dv_s[k_span, :] = dv.astype(BF16)
+        keep(dk_s, kt, dk)
+        keep(dv_s, kt, dv)
+        if kt == 0:
+            next(out_stages, None)
     for qt in range(tiles):
         span = slice(qt * tile, (qt + 1) * tile)
         upto = slice(0, (qt + 1) * tile)
         dq = [nn(kt_s[head * HD : (head + 1) * HD, upto], ds_s[head, upto, span]) for head in range(2)]
-        dq_s[span, :] = (jnp.concatenate(dq, axis=0) * scale).T.astype(BF16)
-    unsort_blocks(order_ref, [dq_s, dk_s, dv_s], out_ref, blocks, half)
-    for k, source in enumerate([dq_s, dk_s, dv_s]):
-        values = source[...].astype(BF16).astype(F32)
-        sum_ref[:, k * LANES : (k + 1) * LANES] = jnp.sum(values, axis=0, keepdims=True)
+        keep(dq_s, qt, (jnp.concatenate(dq, axis=0) * scale).T)
+    for unused in out_stages:
+        pass
+    block_ref[...] = (mixed_ref[...] + out_total[0] + vec_ref[...]).astype(BF16)
+
+    unsort_places(place_ref, [dq_s, dk_s, dv_s], out_ref)
+    for k, ref in enumerate([dq_s, dk_s, dv_s]):
+        values = ref[...].astype(F32)
+        sum_ref[:, k * LANES : (k + 1) * LANES] = jnp.sum(jnp.sum(values, axis=0), axis=0, keepdims=True)
+    plane_gather_end(down_started, [down_all], down_sems, chips)
+
+
+def branch_back(places, inverse, d_branch, weight, att, qkv, att_exact, lse, down_own, out_part, mixed, vec, planes, tile):
+    shape = qkv.shape
+    half, lanes = shape[3:]
+    n_ctx, rows, width = out_part.shape
+    blocks = 2 * planes * n_ctx
+    length = blocks * half
+    seqs = rows * n_ctx * planes // length
+    chips = n_ctx // 2
+    rows_s = pltpu.VMEM((length, LANES), BF16)
+    blocks_s = pltpu.VMEM((blocks, half, LANES), BF16)
+    return pl.pallas_call(
+        functools.partial(branch_back_kernel, tile, planes, seqs, chips),
+        out_shape=(
+            jax.ShapeDtypeStruct(shape, BF16),
+            jax.ShapeDtypeStruct((1, lanes), F32),
+            jax.ShapeDtypeStruct(weight.shape, BF16),
+            jax.ShapeDtypeStruct((rows, width), BF16),
+            jax.ShapeDtypeStruct((n_ctx,) + down_own.shape, BF16),
+        ),
+        in_specs=[SMEM, SMEM] + [ANY] * 7 + [VMEM] * 3,
+        out_specs=(VMEM, VMEM, VMEM, VMEM, ANY),
+        scratch_shapes=[
+            pltpu.VMEM(d_branch.shape, BF16),
+            pltpu.VMEM(weight.shape, BF16),
+            pltpu.VMEM(att.shape, BF16),
+            pltpu.VMEM(shape, BF16),
+            pltpu.VMEM(att_exact.shape, F32),
+            DMA((5,)),
+            pltpu.VMEM((n_ctx, seqs, 2, half, weight.shape[0]), BF16),
+            pltpu.VMEM((planes, n_ctx, 2, half, LANES), BF16),
+            DMA((planes - 1,)),
+            DMA((planes - 1,)),
+            DMA,
+            rows_s,
+            rows_s,
+            rows_s,
+            rows_s,
+            pltpu.VMEM((LANES, length), BF16),
+            blocks_s,
+            blocks_s,
+            blocks_s,
+            pltpu.VMEM((2, length, LANES), BF16),
+            pltpu.VMEM((2, length, LANES), BF16),
+            pltpu.VMEM((2, length), F32),
+            pltpu.VMEM((2, tile, length), BF16),
+            pltpu.VMEM((2, length, length), BF16),
+        ]
+        + scatter_scratch(chips, rows, width)
+        + gather_sems(chips),
+        compiler_params=params(10),
+        cost_estimate=SMALL,
+        name="branch_back",
+    )(places, inverse, d_branch, weight, att, qkv, att_exact, down_own, out_part, mixed, vec, lse)
 
 
 def attend_backward(order, qkv, grad, att, lse, tile):
     blocks, half, lanes = qkv.shape
     length = blocks * half
-    rows, short = pltpu.VMEM((length, LANES), BF16), length <= SHORT
+    rows = pltpu.VMEM((length, LANES), BF16)
     flipped = pltpu.VMEM((LANES, length), BF16)
     return pl.pallas_call(
-        functools.partial(backward_kernel if short else long_backward_kernel, tile),
+        functools.partial(long_backward_kernel, tile),
         out_shape=(
             jax.ShapeDtypeStruct((blocks, half, 3 * LANES), BF16),
             jax.ShapeDtypeStruct((1, 3 * LANES), F32),
         ),
         in_specs=[SMEM, VMEM, VMEM, VMEM, VMEM],
         out_specs=(VMEM, VMEM),
-        scratch_shapes=[rows, rows, rows, rows, flipped, rows, rows, rows]
-        + [pltpu.VMEM((2, length, LANES), BF16)] * 2
-        + [pltpu.VMEM((2, length), F32), pltpu.VMEM((2, tile, length), BF16), pltpu.VMEM((2, length, length), BF16)]
-        if short
-        else [rows, rows, rows, rows, flipped, rows] + [pltpu.VMEM((length, LANES), F32)] * 2,
+        scratch_shapes=[rows, rows, rows, rows, flipped, rows] + [pltpu.VMEM((length, LANES), F32)] * 2,
         compiler_params=params(),
         cost_estimate=SMALL,
         name="attend_backward",
@@ -1607,11 +1935,6 @@
             for p in range(pairs)
         ]
     )
-    next_rows = lax.ppermute(out_weight[:HD], "fsdp", [(j + 1, j) for j in range(planes - 1)])
-    out_own = lax.dynamic_slice(
-        jnp.concatenate([out_weight, next_rows]), ((first_own + c) * HD - f * quarter, 0), (HD, width)
-    )
-    out_own = jnp.where(c < count_own, out_own, jnp.zeros_like(out_own))
     down_own = lax.dynamic_slice(down_weight, (c * ff_piece, 0), (ff_piece, width))
 
 
@@ -1623,11 +1946,6 @@
     vector_list += [up_bias[k * quarter : (k + 1) * quarter] for k in range(ff // width)]
     packed = jnp.concatenate([jnp.pad(v, (0, short)) for v in vector_list])
     packed = jnp.pad(packed, (0, -packed.size % (16 * LANES))).reshape(-1, LANES)
-    vectors, og_all, h1, qkv_slice = first_norm_gather(tok, og, packed, qkv_own, n_ctx, planes, seqs)
-    h1 = h1.reshape(length, width)
-    qkv_slice = qkv_slice.reshape(width, 3 * pair_span)
-    h1, up_weight, down_own = lax.optimization_barrier((h1, up_weight, down_own))
-    down_slice = lax.all_gather(down_own, "fsdp", axis=0, tiled=True)
     up_own = jnp.concatenate(
         [
             lax.dynamic_slice(up_weight, (0, k * ff_quarter + c * ff_piece), (quarter, ff_piece))
@@ -1635,6 +1953,18 @@
         ],
         axis=1,
     )
+    tok_first, up_own = lax.optimization_barrier((tok, up_own))
+    vectors, og_all, h1, qkv_slice, next_rows = first_norm_gather(
+        tok_first, og, packed, qkv_own, out_weight, n_ctx, planes, seqs
+    )
+    out_own = lax.dynamic_slice(
+        jnp.concatenate([out_weight, next_rows]), ((first_own + c) * HD - f * quarter, 0), (HD, width)
+    )
+    out_own = jnp.where(c < count_own, out_own, jnp.zeros_like(out_own))
+    h1 = h1.reshape(length, width)
+    qkv_slice = qkv_slice.reshape(width, 3 * pair_span)
+    h1, up_own, down_own = lax.optimization_barrier((h1, up_own, down_own))
+    down_slice = lax.all_gather(down_own, "fsdp", axis=0, tiled=True)
     up_slice = lax.all_gather(up_own, "fsdp", axis=0, tiled=True)
     og_all = og_all.reshape(plane_rows, width)
     vectors = vectors.reshape(planes, -1)[:, : len(vector_list) * (quarter + short)]
@@ -1653,13 +1983,18 @@
 
     qkv_shift = jnp.concatenate(head_part(bias_q) + [jnp.zeros((pair_span,), F32)] + head_part(bias_v))
 
-    qkv = product(h1, qkv_slice, qkv_shift).reshape(blocks, half, 3 * pair_span)
-    att_heads, att_exact, lse = attend_forward(order, qkv, tile)
-    att, out_slice = to_tokens(att_heads.reshape(planes, n_ctx, local_rows, LANES), seqs, 6, out_own)
+    if length <= SHORT:
+        places, inverse = block_places(order, n_ctx)
+        qkv, att_exact, lse, att, out_slice = attend(
+            places, inverse, h1, qkv_slice, qkv_shift[None, :], out_own, n_ctx, planes, seqs, half, tile
+        )
+    else:
+        qkv = product(h1, qkv_slice, qkv_shift).reshape(blocks, half, 3 * pair_span)
+        att_heads, att_exact, lse = attend_forward(order, qkv, tile)
+        att, out_slice = to_tokens(att_heads.reshape(planes, n_ctx, local_rows, LANES), seqs, 6, out_own)
     out_slice = out_slice.reshape(span, width)
     att = att.reshape(plane_rows, span)
-    branch = product(att, out_slice).reshape(n_ctx, rows, width)
-    mixed, h2 = second_norm_gather(branch, tok, jnp.stack([gain2, bias2, bias_o]))
+    mixed, h2 = second_norm_gather(att, out_slice, tok, jnp.stack([gain2, bias2, bias_o]), n_ctx)
     h2 = h2.reshape(plane_rows, width)
     def reduce_own(part):
         return lax.psum_scatter(part, "fsdp", scatter_dimension=0, tiled=True)
@@ -1672,14 +2007,37 @@
     up_own_grad = reduce_own(up_part)
     out_part = out_part.reshape(n_ctx, rows, width)
     d_branch = d_branch.reshape(plane_rows, width)
-    d_att, out_w_part = out_back(att, d_branch, out_slice)
-    d_att_heads, down_parts = to_heads(d_att.reshape(n_ctx, seqs, local_rows, span), planes, 7, down_own_grad)
-    d_qkv, d_qkv_sum = attend_backward(
-        order, qkv, d_att_heads.reshape(blocks, half, LANES), att_exact, lse, tile
-    )
+    if length <= SHORT:
+        d_qkv, d_qkv_sum, out_w_part, block_out, down_parts = branch_back(
+            places,
+            inverse,
+            d_branch,
+            out_slice,
+            att,
+            qkv,
+            att_exact,
+            lse,
+            down_own_grad,
+            out_part,
+            mixed,
+            bias_d[None, :],
+            planes,
+            tile,
+        )
+    else:
+        d_att, out_w_part = out_back(att, d_branch, out_slice)
+        d_att_heads, down_parts = to_heads(
+            d_att.reshape(n_ctx, seqs, local_rows, span), planes, 7, down_own_grad
+        )
+        d_qkv, d_qkv_sum = attend_backward(
+            order, qkv, d_att_heads.reshape(blocks, half, LANES), att_exact, lse, tile
+        )
+        total = lax.psum_scatter(out_part.reshape(plane_rows, width), "ctx", scatter_dimension=0, tiled=True)
+        block_out = (mixed + total.astype(F32) + bias_d).astype(BF16)
     d_qkv, d_qkv_sum = d_qkv.reshape(length, 3 * pair_span), d_qkv_sum[0]
     down_parts, unused = lax.optimization_barrier((down_parts, d_qkv))
     down_grad = down_parts.reshape(ff_quarter, width).astype(F32)
+    up_own_grad, down_grad = lax.optimization_barrier((up_own_grad, down_grad))
 
     d_up_sum = d_up_sum.reshape(planes, ff_piece)
     up_spread = lax.dynamic_update_slice(jnp.zeros((planes, ff_quarter), F32), d_up_sum, (0, c * ff_piece))
@@ -1700,17 +2058,16 @@
     flat = jnp.pad(flat, ((0, 0), (0, -size % (8 * LANES)))).reshape(planes, -1, LANES)
 
     if length <= SHORT:
-        grad_tok, block_out, qkv_parts, out_parts, sums1, totals = finish(
+        grad_tok, qkv_parts, up_parts, out_parts, sums1, totals = finish(
             h1,
             d_qkv,
             qkv_slice,
-            out_part,
+            up_own_grad,
             out_w_part.reshape(planes, HD, width),
             flat,
             tok,
             d_mixed,
-            mixed,
-            jnp.stack([gain1, bias_d]),
+            gain1[None, :],
         )
     else:
         d_h1, qkv_part, unused = product_back(h1, d_qkv, qkv_slice)
@@ -1723,10 +2080,7 @@
             d_mixed,
             gain1[None, :],
         )
-        total = lax.psum_scatter(out_part.reshape(plane_rows, width), "ctx", scatter_dimension=0, tiled=True)
-        block_out = (mixed + total.astype(F32) + bias_d).astype(BF16)
-    qkv_parts, up_own_grad = lax.optimization_barrier((qkv_parts, up_own_grad))
-    up_parts = lax.all_gather(up_own_grad, "ctx", axis=0)
+        up_parts = lax.all_gather(up_own_grad, "ctx", axis=0)
     sums1 = sums1[:2, :quarter]
     totals = totals.reshape(-1)
     sums = totals[: 6 * quarter].reshape(6, quarter)

time: 517 us -> 491 us (0.950)
  Pallas kernels: 424 us -> 399 us
    pallas_call x7 -> x2, Pallas kernels: 136 us -> 113 us  [the longest x1 65.6 us: attend(): pl.pallas_call(functools.partial(attend_kernel, tile, planes, seqs), out_...]
    all_gather x1 -> x0, waiting for transfers between devices: 15.6 us -> none  [local(): up_parts = lax.all_gather(up_own_grad, 'ctx', axis=0)]
    all_gather x1, waiting for transfers between devices: 0.02 us -> 10.4 us  [local(): down_slice = lax.all_gather(down_own, 'fsdp', axis=0, tiled=True)]
    pallas_call x1, Pallas kernels: 69.3 us -> 59.5 us  [first_norm_gather(): pl.pallas_call(functools.partial(first_kernel, chips, planes, seqs, width...]
    pallas_call x1, Pallas kernels: 94.7 us -> 104 us  [finish(): pl.pallas_call(functools.partial(finish_kernel, chips, planes, seqs), out...]
    reduce_scatter x1, waiting for transfers between devices: 0.02 us -> 5.76 us  [reduce_own(): return lax.psum_scatter(part, 'fsdp', scatter_dimension=0, tiled=True)]
  transfers between devices with their start and end apart: 7 -> 5, of which waited for: 1 -> 3; matrix products, arithmetic and copies ran while one was open for 5% -> 5% of each run, Pallas kernels for 68% -> 49%
where the time goes in v6:
time: 491 us; the launch traced here: 485 us
  Pallas kernels  399 us (81%)
  local copies, waits for them, and re-layouts  28.4 us (6%)
  between operations  19.3 us (4%)
  waiting for transfers between devices  17.5 us (4%)
  other arithmetic  14.4 us (3%)
  starting transfers between devices  6.2 us (1%)
    pallas_call x1, Pallas kernels, finish(): pl.pallas_call(functools.partial(finish_kernel, chips, planes, seqs), out...  104 us
    pallas_call x1, Pallas kernels, attend(): pl.pallas_call(functools.partial(attend_kernel, tile, planes, seqs), out_...  65.6 us
    pallas_call x1, Pallas kernels, first_norm_gather(): pl.pallas_call(functools.partial(first_kernel, chips, planes, seqs, width...  59.5 us
    pallas_call x1, Pallas kernels, feed_back(): pl.pallas_call(functools.partial(third_kernel, chips), out_shape=(jax.Sha...  49.6 us
    pallas_call x1, Pallas kernels, branch_back(): pl.pallas_call(functools.partial(branch_back_kernel, tile, planes, seqs,...  46.9 us
    pallas_call x1, Pallas kernels, second_norm_gather(): pl.pallas_call(functools.partial(second_kernel, chips), out_shape=(jax.Sh...  42.7 us
    pallas_call x2, Pallas kernels, assemble(): pl.pallas_call(functools.partial(assemble_kernel, pieces), grid=(rows //...  15.6 us
    pallas_call x1, Pallas kernels, feed_up(): pl.pallas_call(up_kernel, grid=(rows // block,), out_shape=(jax.ShapeDtyp...  14.9 us
  transfers between devices with their start and end apart: 5, of which 3 were waited for; matrix products, arithmetic and copies ran while one was open for 5% of the time, Pallas kernels for 49%

profile of v6, /device:TPU:0, one launch (start us, length us, event | category | flops | bytes accessed | tf_op | source)
XLA Modules:
  0.0 484.8 jit_solution(7533691888233351788)
XLA Ops:
  7.3 1.9 copy.55
  9.1 1.6 constant_dynamic-slice_fusion.18
  10.7 1.2 pad_maximum_fusion
  12.1 0.8 copy.56
  12.9 1.9 constant_dynamic-slice_fusion.9
  15.3 0.9 pad_maximum_fusion.1.weight_ref
  16.4 2.0 constant_dynamic-slice_fusion.2
  18.4 3.6 concatenate.133.vec_ref
  21.9 59.5 %norm_gather.1 = (bf16[4,48,128]{2,1,0:T(8,128)(2,1)}, bf16[8,128,1600]{2,1,0:T(8,128)(2,1)}, bf16[4,8,64,1600]{3,2,1,0:T(8,128)(2,1)}, bf16[4,400,384]{2,1,0:T(8,128)(2,1)}, bf16[64,1600]{1,0:T(8,128)(2,1)}) custom-call(bf16[128,1600]{1,0:T(8,128)(2,1)} %bitcast.90, bf16[128,1600]{1,0:T(8,128)(2,1)} %bitcast.96, bf16[48,128]{1,0:T(8,128)(2,1)} %concatenate.133.vec_ref, ...), custom_call_target="tpu_custom_call" | custom-call | flops 1 | bytes 1 | tf_op jit(solution)/shard_map/norm_gather/pallas_call | solution.py:415
  81.5 0.7 all-gather.5.cloned.1.call-update
  84.2 0.8 reshape_reshape.3
  89.7 0.8 fusion.3.out_w_ref
  90.5 65.6 %attend.1 = (bf16[4,8,2,32,384]{4,3,2,1,0:T(8,128)(2,1)}, f32[2048,128]{1,0:T(8,128)}, f32[2,2048]{1,0:T(2,128)}, bf16[8,2,2,32,256]{4,3,2,1,0:T(8,128)(2,1)}, bf16[4,64,1600]{2,1,0:T(8,128)(2,1)}) custom-call(s32[3,64]{1,0:T(4,128)} %pad_add_fusion.order_ref, s32[64]{0:T(128)} %select_reduce_fusion.place_ref, bf16[2048,1600]{1,0:T(8,128)(2,1)} %bitcast.84, ...), custom_call_target="tpu_custom_call" | custom-call | flops 1 | bytes 1 | tf_op jit(solution)/shard_map/attend/pallas_call | solution.py:1327
  157.1 42.7 %scatter_norm_gather.1 = (f32[128,1600]{1,0:T(8,128)}, bf16[8,128,1600]{2,1,0:T(8,128)(2,1)}) custom-call(bf16[1024,256]{1,0:T(8,128)(2,1)} %bitcast.104, bf16[256,1600]{1,0:T(8,128)(2,1)} %bitcast.100, bf16[128,1600]{1,0:T(8,128)(2,1)} %bitcast.91, f32[3,1600]{1,0:T(4,128)} %pad_maximum_fusion.2.vec_ref), custom_call_target="tpu_custom_call" | custom-call | flops 1 | bytes 1 | tf_op jit(solution)/shard_map/scatter_norm_gather/pallas_call | solution.py:472
  200.7 14.9 %feed_up.1 = (bf16[1024,800]{1,0:T(8,128)(2,1)}, f32[1024,800]{1,0:T(8,128)}, bf16[800,1600]{1,0:T(8,128)(2,1)}) custom-call(bf16[1024,1600]{1,0:T(8,128)(2,1)} %bitcast.88, bf16[1024,1600]{1,0:T(8,128)(2,1)} %bitcast.86, bf16[1600,800]{1,0:T(8,128)(2,1)} %all-gather.3.cloned.1.call-done.weight_ref.up_w_hbm, f32[1,800]{1,0:T(1,128)} %broadcast_in_dim_reshape.3.shift_ref), custom_call_target="tpu_custom_call" | custom-call | flops 1 | bytes 1 | tf_op jit(solution)/shard_map/feed_up/pallas_call | solution.py:1845
  216.2 10.4 %all-gather.5.cloned.1.call-done.down_w_hbm = bf16[800,1600]{1,0:T(8,128)(2,1)} async-done(((bf16[200,1600]{1,0:T(8,128)(2,1)}), bf16[800,1600]{1,0:T(8,128)(2,1)}) %all-gather.5.cloned.1.call-update) | async-done | bytes 2560016 | tf_op jit(solution)/shard_map/all_gather | solution.py:1967
  226.6 49.6 %feed_back.1 = (f32[128,1600]{1,0:T(8,128)}, f32[4,1600]{1,0:T(4,128)}, bf16[8,128,1600]{2,1,0:T(8,128)(2,1)}, bf16[1024,1600]{1,0:T(8,128)(2,1)}, bf16[1600,800]{1,0:T(8,128)(2,1)}, /*index=5*/f32[1,800]{1,0:T(1,128)}) custom-call(bf16[1024,1600]{1,0:T(8,128)(2,1)} %bitcast.89, bf16[1024,1600]{1,0:T(8,128)(2,1)} %bitcast.87, ...), custom_call_target="tpu_custom_call" | custom-call | flops 1 | bytes 1 | tf_op jit(solution)/shard_map/feed_back/pallas_call | solution.py:580
  280.7 46.9 %branch_back.1 = (bf16[4,8,2,32,384]{4,3,2,1,0:T(8,128)(2,1)}, f32[1,384]{1,0:T(1,128)}, bf16[256,1600]{1,0:T(8,128)(2,1)}, bf16[128,1600]{1,0:T(8,128)(2,1)}, bf16[8,200,1600]{2,1,0:T(8,128)(2,1)}) custom-call(s32[3,64]{1,0:T(4,128)} %pad_add_fusion.order_ref, s32[64]{0:T(128)} %select_reduce_fusion.place_ref, bf16[1024,1600]{1,0:T(8,128)(2,1)} %bitcast.98, ...), custom_call_target="tpu_custom_call" | custom-call | flops 1 | bytes 1 | tf_op jit(solution)/shard_map/branch_back/pallas_call | solution.py:1609
  327.6 0.7 bitcast_dynamic-update-slice_fusion.3
  328.3 0.9 bitcast_dynamic-update-slice_fusion.2
  329.1 0.9 bitcast_dynamic-update-slice_fusion
  331.0 7.4 %bitcast_convert_fusion = f32[1600,1600]{1,0:T(8,128)} fusion(bf16[8,200,1600]{2,1,0:T(8,128)(2,1)} %get-tuple-element.81), kind=kLoop, calls=%fused_computation | loop fusion | flops 2560000 | bytes 15360000 | tf_op jit(solution)/shard_map/convert_element_type | solution.py:2039
  338.4 5.8 %reduce-scatter.5.cloned.1.call-done.up_ref = bf16[400,800]{1,0:T(8,128)(2,1)} async-done(((bf16[1600,800]{1,0:T(8,128)(2,1)}), bf16[400,800]{1,0:T(8,128)(2,1)}) %reduce-scatter.5.cloned.1.call-update) | async-done | bytes 640016 | tf_op jit(solution)/shard_map/reduce_scatter | solution.py:2000
  344.2 104.2 %finish.1 = (f32[128,1600]{1,0:T(8,128)}, bf16[8,2,400,384]{3,2,1,0:T(8,128)(2,1)}, bf16[8,400,800]{2,1,0:T(8,128)(2,1)}, bf16[8,64,1600]{2,1,0:T(8,128)(2,1)}, f32[8,512]{1,0:T(8,128)}, /*index=5*/f32[32,128]{1,0:T(8,128)}) custom-call(bf16[2048,1600]{1,0:T(8,128)(2,1)} %bitcast.85, bf16[2048,384]{1,0:T(8,128)(2,1)} %bitcast.106, ...), custom_call_target="tpu_custom_call" | custom-call | flops 1 | bytes 1 | tf_op jit(solution)/shard_map/finish/pallas_call | solution.py:953
  448.4 1.0 constant_dynamic-slice_fusion
  449.4 5.6 %collective-permute-start = (bf16[64,1600]{1,0:T(8,128)(2,1)S(1)}, bf16[64,1600]{1,0:T(8,128)(2,1)S(1)}, u32[]{:S(2)}, u32[]{:S(2)}) collective-permute-start(bf16[64,1600]{1,0:T(8,128)(2,1)S(1)} %constant_dynamic-slice_fusion), channel_id=1, source_target_pairs={{0,1},{1,2},{2,3},{4,5},{5,6},{6,7},{8,9},{9,10},{10,11},{12,13},{... | collective-permute-start | bytes 614408 | tf_op jit(solution)/shard_map/ppermute | solution.py:2104
  455.0 8.3 %assemble.3 = f32[400,6400]{1,0:T(8,128)} custom-call(bf16[8,400,800]{2,1,0:T(8,128)(2,1)} %get-tuple-element.93.part_ref), custom_call_target="tpu_custom_call" | custom-call | tf_op jit(solution)/shard_map/assemble/pallas_call | solution.py:1681
  463.3 7.3 %assemble.2 = f32[400,4800]{1,0:T(8,128)} custom-call(bf16[16,400,384]{2,1,0:T(8,128)(2,1)} %bitcast.93), custom_call_target="tpu_custom_call" | custom-call | tf_op jit(solution)/shard_map/assemble/pallas_call | solution.py:1681
  470.5 1.6 copy.64
  472.8 1.4 fusion.9
  474.2 1.2 copy.65
  476.0 1.8 fusion.1
  (111 shorter events, 11.9 us)
Async XLA Ops:
  7.2 4.8 copy-start.10
  7.2 4.9 %copy-start.3 = (bf16[64,2,1600]{2,1,0:T(2,128)(2,1)S(1)}, bf16[64,2,1600]{2,1,0:T(2,128)(2,1)}, u32[]{:S(2)}) copy-start(bf16[64,2,1600]{2,1,0:T(2,128)(2,1)} %param.26) | copy-start | bytes 1228804
  7.2 193.5 %all-gather.3.cloned.1.call-start = ((), (), s32[]{:S(2)}) async-start(), calls=%async_computation.2 | async-start | bytes 3584000 | tf_op jit(solution)/shard_map/all_gather | solution.py:1968
  12.9 3.3 copy-start.20
  12.9 3.3 copy-start.12
  12.9 3.4 copy-start.13
  12.9 3.4 copy-start.14
  12.9 3.4 copy-start.15
  12.9 3.4 copy-start.16
  12.9 3.4 copy-start.17
  12.9 3.4 copy-start.18
  12.9 3.4 copy-start.19
  16.4 65.9 %copy-start.9 = (s32[5]{0:T(128)S(1)}, s32[5]{0:T(128)}, u32[]{:S(2)}) copy-start(s32[5]{0:T(128)} %constant.127.clone) | copy-start | bytes 64
  18.4 68.5 %copy-start.8 = (s32[4]{0:T(128)S(1)}, s32[4]{0:T(128)}, u32[]{:S(2)}) copy-start(s32[4]{0:T(128)} %constant.128.clone) | copy-start | bytes 52
  18.4 69.8 %copy-start.21 = (s32[32]{0:T(128)S(1)}, s32[32]{0:T(128)}, u32[]{:S(2)}) copy-start(s32[32]{0:T(128)} %param.25) | copy-start | bytes 388
  18.4 71.4 %copy-start = (bf16[400,1600]{1,0:T(8,128)(2,1)S(1)}, bf16[400,1600]{1,0:T(8,128)(2,1)}, u32[]{:S(2)}) copy-start(bf16[400,1600]{1,0:T(8,128)(2,1)} %out_w_ref.1) | copy-start | bytes 3840004
  81.5 145.1 %all-gather.5.cloned.1.call-start = ((), (), s32[]{:S(2)}) async-start(), calls=%async_computation.3 | async-start | bytes 3328000 | tf_op jit(solution)/shard_map/all_gather | solution.py:1967
  82.2 198.5 %reduce-scatter.7.cloned.1.call-start = ((), (), s32[]{:S(2)}) async-start(), calls=%async_computation.5 | async-start | bytes 3328000
  156.5 59.2 %copy-start.5 = (f32[1,1600]{1,0:T(1,128)}, f32[1,1600]{1,0:T(1,128)S(1)}, u32[]{:S(2)}) copy-start(f32[1,1600]{1,0:T(1,128)S(1)} %stack_reshape_squeeze.9.vec_ref) | copy-start | bytes 19204
  215.7 128.5 %reduce-scatter.5.cloned.1.call-start = ((), (), s32[]{:S(2)}) async-start(), calls=%async_computation.4 | async-start | bytes 3584000 | tf_op jit(solution)/shard_map/reduce_scatter | solution.py:2000
  276.2 3.4 copy-start.6
  276.2 3.5 copy-start.11
  449.4 26.6 %collective-permute-start = (bf16[64,1600]{1,0:T(8,128)(2,1)S(1)}, bf16[64,1600]{1,0:T(8,128)(2,1)S(1)}, u32[]{:S(2)}, u32[]{:S(2)}) collective-permute-start(bf16[64,1600]{1,0:T(8,128)(2,1)S(1)} %constant_dynamic-slice_fusion), channel_id=1, source_target_pairs={{0,1},{1,2},{2,3},{4,5},{5,6},{6,7},{8,9},{9,10},{10,11},{12,13},{... | collective-permute-start | bytes 614408 | tf_op jit(solution)/shard_map/ppermute | solution.py:2104
  463.3 7.3 %copy-start.2 = (f32[128,1600]{1,0:T(8,128)S(1)}, f32[128,1600]{1,0:T(8,128)}, u32[]{:S(2)}) copy-start(f32[128,1600]{1,0:T(8,128)} %get-tuple-element.88) | copy-start | bytes 2457604
  463.3 8.8 %copy-start.7 = (f32[32,128]{1,0:T(8,128)S(1)}, f32[32,128]{1,0:T(8,128)}, u32[]{:S(2)}) copy-start(f32[32,128]{1,0:T(8,128)} %get-tuple-element.91) | copy-start | bytes 49156
  463.3 10.9 %copy-start.4 = (bf16[128,1600]{1,0:T(8,128)(2,1)S(1)}, bf16[128,1600]{1,0:T(8,128)(2,1)}, u32[]{:S(2)}) copy-start(bf16[128,1600]{1,0:T(8,128)(2,1)} %get-tuple-element.77) | copy-start | bytes 1228804
  470.5 5.5 %copy-start.1 = (bf16[8,64,1600]{2,1,0:T(8,128)(2,1)S(1)}, bf16[8,64,1600]{2,1,0:T(8,128)(2,1)}, u32[]{:S(2)}) copy-start(bf16[8,64,1600]{2,1,0:T(8,128)(2,1)} %get-tuple-element.92) | copy-start | bytes 4915204
Sparse Core Ops, SparseCore 0:
  81.6 88.7 all-gather.2
  172.5 54.0 all-gather.4
  229.5 51.1 reduce-scatter.6
  282.8 61.3 reduce-scatter.4

commit v7 on v6

--- a/solution.py
+++ b/solution.py
@@ -778,6 +778,7 @@
     chips,
     planes,
     seqs,
+    counts,
     h1_hbm,
     d_hbm,
     w_hbm,
@@ -791,6 +792,7 @@
     qkv_all,
     up_all,
     outw_all,
+    tail_ref,
     sums_ref,
     flat_out,
     h1_ref,
@@ -821,6 +823,8 @@
     z_recv,
     c_send,
     c_recv,
+    t_send,
+    t_recv,
     *scratch,
 ):
     n_ctx = 2 * chips
@@ -836,6 +840,7 @@
     for load in loads:
         load.start()
     greet(around, others)
+    up_started = plane_gather_start([up_ref], [up_all], up_sems, chips)
     outw_sent = [
         send(outw_ref.at[peer], outw_arrived.at[k], o_send.at[k], o_recv.at[k], "fsdp", peer)
         for k, peer in enumerate(others)
@@ -861,7 +866,12 @@
     part = made[0]
     half = part.shape[3]
 
+    calls = []
+
     def make(k, target):
+        calls.append(k)
+        if len(calls) == chips - 1:
+            plane_gather_middle(up_started, [up_all], up_sems, chips)
         blocks = []
         for j in range(planes):
             start = pl.multiple_of(j * n_ctx * half + target * 2 * half, 2 * half)
@@ -880,7 +890,6 @@
     ]
     rows_arrived[plane] = rows_own[plane]
 
-    up_started = plane_gather_start([up_ref], [up_all], up_sems, chips)
     total = outw_ref[plane].astype(F32)
     for k, copy in enumerate(outw_sent):
         copy.wait()
@@ -893,7 +902,6 @@
         terms = [q_arrived[seq * pairs + pair].astype(F32) for seq in range(seqs)]
         q_own[pair] = sum(terms[1:], terms[0]).astype(BF16)
     qkv_started = plane_gather_start([q_own], [qkv_all], qkv_sems, chips)
-    plane_gather_middle(up_started, [up_all], up_sems, chips)
     plane_gather_middle(outw_started, [outw_all], outw_sems, chips)
     plane_gather_middle(qkv_started, [qkv_all], qkv_sems, chips)
 
@@ -929,6 +937,22 @@
         sent.append(send(small_own, small_c.at[k], c_send.at[0, k], c_recv.at[0, k], "ctx", peer))
         sent.append(send(flat_own, flat_c.at[k], c_send.at[1, k], c_recv.at[1, k], "ctx", peer))
     plane_gather_end(outw_started, [outw_all], outw_sems, chips)
+    last_head = sum((plane == j).astype(jnp.int32) * (counts[j] - 1) for j in range(planes))
+
+    def tail_copy():
+        return pltpu.make_async_remote_copy(
+            src_ref=outw_all.at[last_head],
+            dst_ref=tail_ref,
+            send_sem=t_send,
+            recv_sem=t_recv,
+            device_id={"fsdp": lax.rem(plane + 1, planes)},
+            device_id_type=MESH,
+        )
+
+    @pl.when(plane < planes - 1)
+    def _():
+        tail_copy().start()
+
     plane_gather_end(qkv_started, [qkv_all], qkv_sems, chips)
     plane_gather_end(up_started, [up_all], up_sems, chips)
     for copy in sent:
@@ -936,11 +960,19 @@
     for k in range(n_ctx - 1):
         small_total = small_total + small_c[k]
         flat_total = flat_total + flat_c[k]
+    @pl.when(plane < planes - 1)
+    def _():
+        tail_copy().wait_send()
+
+    @pl.when(plane > 0)
+    def _():
+        tail_copy().wait_recv()
+
     sums_ref[...] = small_total
     flat_out[...] = flat_total
 
 
-def finish(h1, d_qkv, weight, up_own, outw_part, flat, tok, dmixed, vecs):
+def finish(h1, d_qkv, weight, up_own, outw_part, flat, tok, dmixed, vecs, counts):
     rows, width = tok.shape
     planes = outw_part.shape[0]
     n_ctx = lax.axis_size("ctx")
@@ -951,17 +983,18 @@
     size = (8, quarter + -quarter % LANES)
     piece = outw_part.shape[1:]
     return pl.pallas_call(
-        functools.partial(finish_kernel, chips, planes, seqs),
+        functools.partial(finish_kernel, chips, planes, seqs, counts),
         out_shape=(
             jax.ShapeDtypeStruct((rows, width), F32),
             jax.ShapeDtypeStruct((n_ctx, pairs, quarter, columns), BF16),
             jax.ShapeDtypeStruct((n_ctx,) + up_own.shape, BF16),
             jax.ShapeDtypeStruct((n_ctx,) + piece, BF16),
+            jax.ShapeDtypeStruct(piece, BF16),
             jax.ShapeDtypeStruct(size, F32),
             jax.ShapeDtypeStruct(flat.shape[1:], F32),
         ),
         in_specs=[ANY] * 4 + [VMEM] * 5,
-        out_specs=(VMEM, ANY, ANY, ANY, VMEM, VMEM),
+        out_specs=(VMEM, ANY, ANY, ANY, ANY, VMEM, VMEM),
         scratch_shapes=[
             pltpu.VMEM(h1.shape, BF16),
             pltpu.VMEM(d_qkv.shape, BF16),
@@ -991,6 +1024,8 @@
             DMA((2, planes - 1)),
             DMA((2, n_ctx - 1)),
             DMA((2, n_ctx - 1)),
+            DMA,
+            DMA,
         ]
         + made_scratch(chips, planes, half, width)
         + gather_sems(chips)
@@ -1676,11 +1711,12 @@
         out_ref[:, start : start + size] = part_ref[source, :, first : first + size].astype(F32)
 
 
-def assemble(parts, pieces, width, block):
+def assemble(parts, pieces, width):
     n_ctx, rows, columns = parts.shape
+    block = -(-rows // 32) * 16
     return pl.pallas_call(
         functools.partial(assemble_kernel, pieces),
-        grid=(rows // block,),
+        grid=(-(-rows // block),),
         out_shape=jax.ShapeDtypeStruct((rows, width), F32),
         in_specs=[pl.BlockSpec((n_ctx, block, columns), lambda i: (0, i, 0))],
         out_specs=pl.BlockSpec((block, width), lambda i: (i, 0)),
@@ -2058,7 +2094,7 @@
     flat = jnp.pad(flat, ((0, 0), (0, -size % (8 * LANES)))).reshape(planes, -1, LANES)
 
     if length <= SHORT:
-        grad_tok, qkv_parts, up_parts, out_parts, sums1, totals = finish(
+        grad_tok, qkv_parts, up_parts, out_parts, tail_rows, sums1, totals = finish(
             h1,
             d_qkv,
             qkv_slice,
@@ -2068,6 +2104,7 @@
             tok,
             d_mixed,
             gain1[None, :],
+            counts,
         )
     else:
         d_h1, qkv_part, unused = product_back(h1, d_qkv, qkv_slice)
@@ -2081,32 +2118,32 @@
             gain1[None, :],
         )
         up_parts = lax.all_gather(up_own_grad, "ctx", axis=0)
+        tail_rows = lax.dynamic_index_in_dim(out_parts, count_own - 1, 0, keepdims=False)
+        tail_rows = lax.ppermute(tail_rows, "fsdp", [(j, j + 1) for j in range(planes - 1)])
     sums1 = sums1[:2, :quarter]
     totals = totals.reshape(-1)
     sums = totals[: 6 * quarter].reshape(6, quarter)
     up_bias_grad = totals[6 * quarter : size]
 
-    block = quarter // 5
     up_pieces = [
         (j * ff_quarter + d * ff_piece, d, j * ff_piece, ff_piece) for j in range(planes) for d in range(n_ctx)
     ]
-    up_grad = assemble(up_parts, up_pieces, ff, block)
+    up_grad = assemble(up_parts, up_pieces, ff)
     qkv_pieces = [
         (k * width + (first[j] + d) * HD, d * pairs + j // 2, k * pair_span + j % 2 * HD, HD)
         for k in range(3)
         for j in range(planes)
         for d in range(counts[j])
     ]
-    qkv_grad = assemble(qkv_parts.reshape(n_ctx * pairs, quarter, 3 * pair_span), qkv_pieces, 3 * width, block)
+    qkv_grad = assemble(qkv_parts.reshape(n_ctx * pairs, quarter, 3 * pair_span), qkv_pieces, 3 * width)
     out_rows = out_parts.reshape(n_ctx * HD, width)
-    tail = (f + 1) * quarter - first_own * HD
-    tail_rows = lax.dynamic_slice(out_rows, (tail, 0), (HD, width))
-    tail_rows = lax.ppermute(tail_rows, "fsdp", [(j, j + 1) for j in range(planes - 1)])
     lead = first_own * HD - f * quarter
     shifted = lax.dynamic_slice(
         jnp.concatenate([jnp.zeros((HD, width), BF16), out_rows]), (HD - lead, 0), (quarter, width)
     )
-    from_tail = jnp.concatenate([tail_rows, jnp.zeros((quarter - HD, width), BF16)])
+    from_tail = lax.dynamic_slice(
+        jnp.concatenate([tail_rows, jnp.zeros((quarter, width), BF16)]), (HD - lead, 0), (quarter, width)
+    )
     row_ids = lax.broadcasted_iota(jnp.int32, (quarter, width), 0)
     out_grad_own = jnp.where(row_ids < lead, from_tail, shifted).astype(F32)
 

time: 491 us -> 477 us (0.971)
  Pallas kernels: 399 us -> 391 us
  starting transfers between devices: 6.2 us -> 0.62 us
    pallas_call x3, Pallas kernels: 120 us -> 111 us  [the longest x1 98.3 us: finish(): pl.pallas_call(functools.partial(finish_kernel, chips, planes, seqs, coun...]
    ppermute x1 -> x0, starting transfers between devices: 5.57 us -> none  [local(): lax.ppermute(tail_rows, 'fsdp', [(j, j + 1) for j in range(planes - 1)])]
  transfers between devices with their start and end apart: 5 -> 4, of which waited for: 3 -> 3; matrix products, arithmetic and copies ran while one was open for 5% -> 4% of each run, Pallas kernels for 49% -> 47%
where the time goes in v7:
time: 477 us; the launch traced here: 471 us
  Pallas kernels  391 us (82%)
  local copies, waits for them, and re-layouts  29 us (6%)
  between operations  19.3 us (4%)
  waiting for transfers between devices  17.1 us (4%)
  other arithmetic  14.4 us (3%)
    pallas_call x1, Pallas kernels, finish(): pl.pallas_call(functools.partial(finish_kernel, chips, planes, seqs, coun...  98.3 us
    pallas_call x1, Pallas kernels, attend(): pl.pallas_call(functools.partial(attend_kernel, tile, planes, seqs), out_...  65.7 us
    pallas_call x1, Pallas kernels, first_norm_gather(): pl.pallas_call(functools.partial(first_kernel, chips, planes, seqs, width...  59.5 us
    pallas_call x1, Pallas kernels, feed_back(): pl.pallas_call(functools.partial(third_kernel, chips), out_shape=(jax.Sha...  49.7 us
    pallas_call x1, Pallas kernels, branch_back(): pl.pallas_call(functools.partial(branch_back_kernel, tile, planes, seqs,...  47 us
    pallas_call x1, Pallas kernels, second_norm_gather(): pl.pallas_call(functools.partial(second_kernel, chips), out_shape=(jax.Sh...  42.8 us
    pallas_call x1, Pallas kernels, feed_up(): pl.pallas_call(up_kernel, grid=(rows // block,), out_shape=(jax.ShapeDtyp...  14.9 us
    pallas_call x2, Pallas kernels, assemble(): pl.pallas_call(functools.partial(assemble_kernel, pieces), grid=(-(-rows...  12.9 us
  transfers between devices with their start and end apart: 4, of which 3 were waited for; matrix products, arithmetic and copies ran while one was open for 4% of the time, Pallas kernels for 47%

profile of v7, /device:TPU:0, one launch (start us, length us, event | category | flops | bytes accessed | tf_op | source)
XLA Modules:
  0.0 471.2 jit_solution(1755398354213056376)
XLA Ops:
  7.3 1.9 copy.55
  9.1 1.6 constant_dynamic-slice_fusion.17
  10.7 1.2 pad_maximum_fusion
  12.1 0.8 copy.56
  12.9 1.9 constant_dynamic-slice_fusion.8
  15.3 0.9 pad_maximum_fusion.1.weight_ref
  16.4 2.0 constant_dynamic-slice_fusion.1
  18.4 3.6 concatenate.133.vec_ref
  22.0 59.5 %norm_gather.1 = (bf16[4,48,128]{2,1,0:T(8,128)(2,1)}, bf16[8,128,1600]{2,1,0:T(8,128)(2,1)}, bf16[4,8,64,1600]{3,2,1,0:T(8,128)(2,1)}, bf16[4,400,384]{2,1,0:T(8,128)(2,1)}, bf16[64,1600]{1,0:T(8,128)(2,1)}) custom-call(bf16[128,1600]{1,0:T(8,128)(2,1)} %bitcast.90, bf16[128,1600]{1,0:T(8,128)(2,1)} %bitcast.96, bf16[48,128]{1,0:T(8,128)(2,1)} %concatenate.133.vec_ref, ...), custom_call_target="tpu_custom_call" | custom-call | flops 1 | bytes 1 | tf_op jit(solution)/shard_map/norm_gather/pallas_call | solution.py:415
  81.5 0.7 all-gather.5.cloned.1.call-update
  84.2 0.8 reshape_reshape.3
  89.8 0.8 fusion.3.out_w_ref
  90.6 65.7 %attend.1 = (bf16[4,8,2,32,384]{4,3,2,1,0:T(8,128)(2,1)}, f32[2048,128]{1,0:T(8,128)}, f32[2,2048]{1,0:T(2,128)}, bf16[8,2,2,32,256]{4,3,2,1,0:T(8,128)(2,1)}, bf16[4,64,1600]{2,1,0:T(8,128)(2,1)}) custom-call(s32[3,64]{1,0:T(4,128)} %pad_add_fusion.order_ref, s32[64]{0:T(128)} %select_reduce_fusion.place_ref, bf16[2048,1600]{1,0:T(8,128)(2,1)} %bitcast.84, ...), custom_call_target="tpu_custom_call" | custom-call | flops 1 | bytes 1 | tf_op jit(solution)/shard_map/attend/pallas_call | solution.py:1362
  157.2 42.8 %scatter_norm_gather.1 = (f32[128,1600]{1,0:T(8,128)}, bf16[8,128,1600]{2,1,0:T(8,128)(2,1)}) custom-call(bf16[1024,256]{1,0:T(8,128)(2,1)} %bitcast.102, bf16[256,1600]{1,0:T(8,128)(2,1)} %bitcast.100, bf16[128,1600]{1,0:T(8,128)(2,1)} %bitcast.91, f32[3,1600]{1,0:T(4,128)} %pad_maximum_fusion.2.vec_ref), custom_call_target="tpu_custom_call" | custom-call | flops 1 | bytes 1 | tf_op jit(solution)/shard_map/scatter_norm_gather/pallas_call | solution.py:472
  200.8 14.9 %feed_up.1 = (bf16[1024,800]{1,0:T(8,128)(2,1)}, f32[1024,800]{1,0:T(8,128)}, bf16[800,1600]{1,0:T(8,128)(2,1)}) custom-call(bf16[1024,1600]{1,0:T(8,128)(2,1)} %bitcast.88, bf16[1024,1600]{1,0:T(8,128)(2,1)} %bitcast.86, bf16[1600,800]{1,0:T(8,128)(2,1)} %all-gather.3.cloned.1.call-done.weight_ref.up_w_hbm, f32[1,800]{1,0:T(1,128)} %broadcast_in_dim_reshape.3.shift_ref), custom_call_target="tpu_custom_call" | custom-call | flops 1 | bytes 1 | tf_op jit(solution)/shard_map/feed_up/pallas_call | solution.py:1881
  216.3 10.3 %all-gather.5.cloned.1.call-done.down_w_hbm = bf16[800,1600]{1,0:T(8,128)(2,1)} async-done(((bf16[200,1600]{1,0:T(8,128)(2,1)}), bf16[800,1600]{1,0:T(8,128)(2,1)}) %all-gather.5.cloned.1.call-update) | async-done | bytes 2560016 | tf_op jit(solution)/shard_map/all_gather | solution.py:2003
  226.6 49.7 %feed_back.1 = (f32[128,1600]{1,0:T(8,128)}, f32[4,1600]{1,0:T(4,128)}, bf16[8,128,1600]{2,1,0:T(8,128)(2,1)}, bf16[1024,1600]{1,0:T(8,128)(2,1)}, bf16[1600,800]{1,0:T(8,128)(2,1)}, /*index=5*/f32[1,800]{1,0:T(1,128)}) custom-call(bf16[1024,1600]{1,0:T(8,128)(2,1)} %bitcast.89, bf16[1024,1600]{1,0:T(8,128)(2,1)} %bitcast.87, ...), custom_call_target="tpu_custom_call" | custom-call | flops 1 | bytes 1 | tf_op jit(solution)/shard_map/feed_back/pallas_call | solution.py:580
  280.7 47.0 %branch_back.1 = (bf16[4,8,2,32,384]{4,3,2,1,0:T(8,128)(2,1)}, f32[1,384]{1,0:T(1,128)}, bf16[256,1600]{1,0:T(8,128)(2,1)}, bf16[128,1600]{1,0:T(8,128)(2,1)}, bf16[8,200,1600]{2,1,0:T(8,128)(2,1)}) custom-call(s32[3,64]{1,0:T(4,128)} %pad_add_fusion.order_ref, s32[64]{0:T(128)} %select_reduce_fusion.place_ref, bf16[1024,1600]{1,0:T(8,128)(2,1)} %bitcast.98, ...), custom_call_target="tpu_custom_call" | custom-call | flops 1 | bytes 1 | tf_op jit(solution)/shard_map/branch_back/pallas_call | solution.py:1644
  327.7 0.8 bitcast_dynamic-update-slice_fusion.3
  328.5 0.9 bitcast_dynamic-update-slice_fusion.2
  329.4 0.8 bitcast_dynamic-update-slice_fusion
  331.3 7.4 %bitcast_convert_fusion = f32[1600,1600]{1,0:T(8,128)} fusion(bf16[8,200,1600]{2,1,0:T(8,128)(2,1)} %get-tuple-element.82), kind=kLoop, calls=%fused_computation | loop fusion | flops 2560000 | bytes 15360000 | tf_op jit(solution)/shard_map/convert_element_type | solution.py:2075
  338.7 5.5 %reduce-scatter.5.cloned.1.call-done.up_ref = bf16[400,800]{1,0:T(8,128)(2,1)} async-done(((bf16[1600,800]{1,0:T(8,128)(2,1)}), bf16[400,800]{1,0:T(8,128)(2,1)}) %reduce-scatter.5.cloned.1.call-update) | async-done | bytes 640016 | tf_op jit(solution)/shard_map/reduce_scatter | solution.py:2036
  344.2 98.3 %finish.1 = (f32[128,1600]{1,0:T(8,128)}, bf16[8,2,400,384]{3,2,1,0:T(8,128)(2,1)}, bf16[8,400,800]{2,1,0:T(8,128)(2,1)}, bf16[8,64,1600]{2,1,0:T(8,128)(2,1)}, ...) custom-call(bf16[2048,1600]{1,0:T(8,128)(2,1)} %bitcast.85, bf16[2048,384]{1,0:T(8,128)(2,1)} %bitcast.105, ...), custom_call_target="tpu_custom_call" | custom-call | flops 1 | bytes 1 | tf_op jit(solution)/shard_map/finish/pallas_call | solution.py:985
  442.5 1.5 fusion.8
  444.0 1.4 slice.169
  445.4 7.2 %assemble.3 = f32[400,6400]{1,0:T(8,128)} custom-call(bf16[8,400,800]{2,1,0:T(8,128)(2,1)} %get-tuple-element.95.part_ref), custom_call_target="tpu_custom_call" | custom-call | tf_op jit(solution)/shard_map/assemble/pallas_call | solution.py:1717
  452.6 5.7 %assemble.2 = f32[400,4800]{1,0:T(8,128)} custom-call(bf16[16,400,384]{2,1,0:T(8,128)(2,1)} %bitcast.93), custom_call_target="tpu_custom_call" | custom-call | tf_op jit(solution)/shard_map/assemble/pallas_call | solution.py:1717
  458.3 1.6 copy.64
  459.8 1.4 fusion.9
  461.2 1.2 copy.65
  462.4 1.8 fusion.1
  (108 shorter events, 10.5 us)
Async XLA Ops:
  7.2 4.8 %copy-start.10 = (bf16[1600]{0:T(1024)(128)(2,1)S(1)}, bf16[1600]{0:T(1024)(128)(2,1)}, u32[]{:S(2)}) copy-start(bf16[1600]{0:T(1024)(128)(2,1)} %param.37) | copy-start | bytes 9604
  7.2 4.9 %copy-start.3 = (bf16[64,2,1600]{2,1,0:T(2,128)(2,1)S(1)}, bf16[64,2,1600]{2,1,0:T(2,128)(2,1)}, u32[]{:S(2)}) copy-start(bf16[64,2,1600]{2,1,0:T(2,128)(2,1)} %param.26) | copy-start | bytes 1228804
  7.2 193.6 %all-gather.3.cloned.1.call-start = ((), (), s32[]{:S(2)}) async-start(), calls=%async_computation.2 | async-start | bytes 3584000 | tf_op jit(solution)/shard_map/all_gather | solution.py:2004
  12.9 3.3 copy-start.20
  12.9 3.3 copy-start.12
  12.9 3.4 copy-start.13
  12.9 3.4 copy-start.14
  12.9 3.4 copy-start.15
  12.9 3.4 copy-start.16
  12.9 3.4 copy-start.17
  12.9 3.4 copy-start.18
  12.9 3.4 copy-start.19
  16.4 65.9 %copy-start.9 = (s32[5]{0:T(128)S(1)}, s32[5]{0:T(128)}, u32[]{:S(2)}) copy-start(s32[5]{0:T(128)} %constant.127.clone) | copy-start | bytes 64
  18.4 68.5 %copy-start.8 = (s32[4]{0:T(128)S(1)}, s32[4]{0:T(128)}, u32[]{:S(2)}) copy-start(s32[4]{0:T(128)} %constant.128.clone) | copy-start | bytes 52
  18.4 69.8 %copy-start.21 = (s32[32]{0:T(128)S(1)}, s32[32]{0:T(128)}, u32[]{:S(2)}) copy-start(s32[32]{0:T(128)} %param.25) | copy-start | bytes 388
  18.4 71.4 %copy-start = (bf16[400,1600]{1,0:T(8,128)(2,1)S(1)}, bf16[400,1600]{1,0:T(8,128)(2,1)}, u32[]{:S(2)}) copy-start(bf16[400,1600]{1,0:T(8,128)(2,1)} %out_w_ref.1) | copy-start | bytes 3840004
  81.5 145.1 %all-gather.5.cloned.1.call-start = ((), (), s32[]{:S(2)}) async-start(), calls=%async_computation.3 | async-start | bytes 3328000 | tf_op jit(solution)/shard_map/all_gather | solution.py:2003
  82.2 198.5 %reduce-scatter.7.cloned.1.call-start = ((), (), s32[]{:S(2)}) async-start(), calls=%async_computation.5 | async-start | bytes 3328000
  156.5 59.3 %copy-start.6 = (f32[1,1600]{1,0:T(1,128)}, f32[1,1600]{1,0:T(1,128)S(1)}, u32[]{:S(2)}) copy-start(f32[1,1600]{1,0:T(1,128)S(1)} %stack_reshape_squeeze.9.vec_ref) | copy-start | bytes 19204
  215.8 128.4 %reduce-scatter.5.cloned.1.call-start = ((), (), s32[]{:S(2)}) async-start(), calls=%async_computation.4 | async-start | bytes 3584000 | tf_op jit(solution)/shard_map/reduce_scatter | solution.py:2036
  276.3 3.4 copy-start.7
  276.3 3.5 copy-start.11
  452.6 5.7 %copy-start.2 = (f32[128,1600]{1,0:T(8,128)S(1)}, f32[128,1600]{1,0:T(8,128)}, u32[]{:S(2)}) copy-start(f32[128,1600]{1,0:T(8,128)} %get-tuple-element.89) | copy-start | bytes 2457604
  452.6 8.6 %copy-start.4 = (bf16[128,1600]{1,0:T(8,128)(2,1)S(1)}, bf16[128,1600]{1,0:T(8,128)(2,1)}, u32[]{:S(2)}) copy-start(bf16[128,1600]{1,0:T(8,128)(2,1)} %get-tuple-element.78) | copy-start | bytes 1228804
  458.3 4.1 copy-start.1
  458.3 4.1 copy-start.5
Sparse Core Ops, SparseCore 0:
  81.6 88.7 all-gather.2
  172.5 54.0 all-gather.4
  229.5 51.1 reduce-scatter.6
  282.8 61.3 reduce-scatter.4

commit v8 on v7

--- a/solution.py
+++ b/solution.py
@@ -488,6 +488,8 @@
 
 def third_kernel(
     chips,
+    planes,
+    packed,
     h_hbm,
     og_hbm,
     act_hbm,
@@ -536,13 +538,17 @@
     greet(to + [sibling])
     unit, inverse = normalize(mixed_ref[...])
     rows = mixed_ref.shape[0]
-    for load in loads[:4]:
-        load.wait()
+    waiting = loads[:4]
     part = made[0]
 
     def make(k, target):
         span = pl.ds(pl.multiple_of(target * 2 * rows, 2 * rows), 2 * rows)
-        d_up = (nt(ogs_ref[span, :], down_w_ref[...]) * slope_ref[span, :]).astype(BF16)
+        while len(waiting) > 2:
+            waiting.pop(0).wait()
+        d_act = nt(ogs_ref[span, :], down_w_ref[...])
+        while waiting:
+            waiting.pop(0).wait()
+        d_up = (d_act * slope_ref[span, :]).astype(BF16)
         d_up_ref[span, :] = d_up
         d_h = nt(d_up, up_w_ref[...]).astype(BF16)
         part[k, 0] = d_h[:rows]
@@ -553,7 +559,17 @@
             load.wait()
         d_up = d_up_ref[...]
         up_sum_ref[...] = jnp.sum(d_up.astype(F32), axis=0, keepdims=True)
-        up_grad_ref[...] = tn(d_up, h_ref[...]).T.astype(BF16)
+        up_grad = tn(d_up, h_ref[...]).T
+        if packed:
+            hidden = up_grad.shape[1]
+            lines = up_grad.shape[0] // planes // 2
+            for j in range(2 * planes):
+                rows_at, lanes_at = j // 2 * lines, j % 2 * hidden
+                up_grad_ref[rows_at : rows_at + lines, lanes_at : lanes_at + hidden] = up_grad[
+                    j * lines : (j + 1) * lines
+                ].astype(BF16)
+        else:
+            up_grad_ref[...] = up_grad.astype(BF16)
         out_ref[...] = nn(act_ref[...], down_w_ref[...]).astype(BF16)
         pltpu.make_async_copy(out_ref, out_hbm, out_sem).start()
 
@@ -572,19 +588,19 @@
     pltpu.make_async_copy(out_ref, out_hbm, out_sem).wait()
 
 
-def feed_back(values, out_grads, act, slope, up_weight, down_weight, mixed, og, vecs):
+def feed_back(values, out_grads, act, slope, up_weight, down_weight, mixed, og, vecs, planes, packed):
     rows, width = mixed.shape
     total_rows, hidden = act.shape
     n_ctx = total_rows // rows
     chips = n_ctx // 2
     return pl.pallas_call(
-        functools.partial(third_kernel, chips),
+        functools.partial(third_kernel, chips, planes, packed),
         out_shape=(
             jax.ShapeDtypeStruct((rows, width), F32),
             jax.ShapeDtypeStruct((4, width), F32),
             jax.ShapeDtypeStruct((n_ctx, rows, width), BF16),
             jax.ShapeDtypeStruct((total_rows, width), BF16),
-            jax.ShapeDtypeStruct((width, hidden), BF16),
+            jax.ShapeDtypeStruct((width // 2, 2 * hidden) if packed else (width, hidden), BF16),
             jax.ShapeDtypeStruct((1, hidden), F32),
         ),
         in_specs=[ANY] * 6 + [VMEM] * 3,
@@ -896,6 +912,7 @@
         total = total + outw_arrived[k].astype(F32)
     outw_own[...] = total.astype(BF16)
     outw_started = plane_gather_start([outw_own], [outw_all], outw_sems, chips)
+    plane_gather_end(up_started, [up_all], up_sems, chips)
     for copy in pushed:
         copy.wait()
     for pair in range(pairs):
@@ -954,7 +971,6 @@
         tail_copy().start()
 
     plane_gather_end(qkv_started, [qkv_all], qkv_sems, chips)
-    plane_gather_end(up_started, [up_all], up_sems, chips)
     for copy in sent:
         copy.wait()
     for k in range(n_ctx - 1):
@@ -1725,6 +1741,30 @@
     )(parts)
 
 
+def assemble_packed_kernel(pieces, part_ref, out_ref):
+    hidden = part_ref.shape[2] // 2
+    for side in range(2):
+
+        @pl.when(pl.program_id(0) == side)
+        def _(side=side):
+            for start, source, first, size in pieces:
+                first = first + side * hidden
+                out_ref[:, start : start + size] = part_ref[source, :, first : first + size].astype(F32)
+
+
+def assemble_packed(parts, pieces, width):
+    n_ctx, rows, columns = parts.shape
+    return pl.pallas_call(
+        functools.partial(assemble_packed_kernel, pieces),
+        grid=(2,),
+        out_shape=jax.ShapeDtypeStruct((2 * rows, width), F32),
+        in_specs=[pl.BlockSpec((n_ctx, rows, columns), lambda i: (0, 0, 0), pipeline_mode=pl.Buffered(1))],
+        out_specs=pl.BlockSpec((rows, width), lambda i: (i, 0)),
+        compiler_params=params(),
+        name="assemble_packed",
+    )(parts)
+
+
 def tn(left, right):
     return nn(left.T, right)
 
@@ -1941,6 +1981,7 @@
     ff_piece = ff_quarter // n_ctx
     ff_span = ff_piece * planes
     tile = 256
+    halved = quarter % 16 == 0
 
     device_ids = jnp.arange(devices, dtype=jnp.int32)
     device_of_block = jnp.sum(
@@ -2038,7 +2079,7 @@
     act, slope, down_part = feed_up(h2, og_all, up_slice, bias_up)
     down_own_grad = reduce_own(down_part)
     d_mixed, sums2, d_branch, out_part, up_part, d_up_sum = feed_back(
-        h2, og_all, act, slope, up_slice, down_slice, mixed, og, gain2[None, :]
+        h2, og_all, act, slope, up_slice, down_slice, mixed, og, gain2[None, :], planes, halved
     )
     up_own_grad = reduce_own(up_part)
     out_part = out_part.reshape(n_ctx, rows, width)
@@ -2128,24 +2169,19 @@
     up_pieces = [
         (j * ff_quarter + d * ff_piece, d, j * ff_piece, ff_piece) for j in range(planes) for d in range(n_ctx)
     ]
-    up_grad = assemble(up_parts, up_pieces, ff)
     qkv_pieces = [
         (k * width + (first[j] + d) * HD, d * pairs + j // 2, k * pair_span + j % 2 * HD, HD)
         for k in range(3)
         for j in range(planes)
         for d in range(counts[j])
     ]
+    up_grad = (assemble_packed if halved else assemble)(up_parts, up_pieces, ff)
     qkv_grad = assemble(qkv_parts.reshape(n_ctx * pairs, quarter, 3 * pair_span), qkv_pieces, 3 * width)
     out_rows = out_parts.reshape(n_ctx * HD, width)
     lead = first_own * HD - f * quarter
-    shifted = lax.dynamic_slice(
-        jnp.concatenate([jnp.zeros((HD, width), BF16), out_rows]), (HD - lead, 0), (quarter, width)
-    )
-    from_tail = lax.dynamic_slice(
-        jnp.concatenate([tail_rows, jnp.zeros((quarter, width), BF16)]), (HD - lead, 0), (quarter, width)
-    )
-    row_ids = lax.broadcasted_iota(jnp.int32, (quarter, width), 0)
-    out_grad_own = jnp.where(row_ids < lead, from_tail, shifted).astype(F32)
+    out_grad_own = lax.dynamic_slice(
+        jnp.concatenate([tail_rows, out_rows]), (HD - lead, 0), (quarter, width)
+    ).astype(F32)
 
     def back(values):
         return jnp.swapaxes(values.reshape(seqs, local_rows, width), 0, 1)

time: 477 us -> 474 us (level)
    pallas_call x2 -> x1, Pallas kernels: 12.9 us -> 5.68 us  [assemble(): pl.pallas_call(functools.partial(assemble_kernel, pieces), grid=(-(-rows...]
    pallas_call x1 -> x2, Pallas kernels: 49.7 us -> 56.6 us  [the longest x1 48.8 us: feed_back(): pl.pallas_call(functools.partial(third_kernel, chips, planes, packed), ou...]
    reduce_scatter x1 -> x0, waiting for transfers between devices: 5.53 us -> none  [reduce_own(): return lax.psum_scatter(part, 'fsdp', scatter_dimension=0, tiled=True)]
where the time goes in v8:
time: 474 us; the launch traced here: 468 us
  Pallas kernels  388 us (82%)
  local copies, waits for them, and re-layouts  29 us (6%)
  between operations  19.3 us (4%)
  waiting for transfers between devices  16.6 us (4%)
  other arithmetic  14.2 us (3%)
    pallas_call x1, Pallas kernels, finish(): pl.pallas_call(functools.partial(finish_kernel, chips, planes, seqs, coun...  96.3 us
    pallas_call x1, Pallas kernels, attend(): pl.pallas_call(functools.partial(attend_kernel, tile, planes, seqs), out_...  65.7 us
    pallas_call x1, Pallas kernels, first_norm_gather(): pl.pallas_call(functools.partial(first_kernel, chips, planes, seqs, width...  59.5 us
    pallas_call x1, Pallas kernels, feed_back(): pl.pallas_call(functools.partial(third_kernel, chips, planes, packed), ou...  48.8 us
    pallas_call x1, Pallas kernels, branch_back(): pl.pallas_call(functools.partial(branch_back_kernel, tile, planes, seqs,...  46.9 us
    pallas_call x1, Pallas kernels, second_norm_gather(): pl.pallas_call(functools.partial(second_kernel, chips), out_shape=(jax.Sh...  42.7 us
    pallas_call x1, Pallas kernels, feed_up(): pl.pallas_call(up_kernel, grid=(rows // block,), out_shape=(jax.ShapeDtyp...  14.9 us
    all_gather x1, waiting for transfers between devices, local(): down_slice = lax.all_gather(down_own, 'fsdp', axis=0, tiled=True)  10.3 us
  transfers between devices with their start and end apart: 4, of which 3 were waited for; matrix products, arithmetic and copies ran while one was open for 4% of the time, Pallas kernels for 47%

profile of v8, /device:TPU:0, one launch (start us, length us, event | category | flops | bytes accessed | tf_op | source)
XLA Modules:
  0.0 468.1 jit_solution(11140090058832125766)
XLA Ops:
  7.3 1.9 copy.55
  9.1 1.6 constant_dynamic-slice_fusion.17
  10.7 1.2 pad_maximum_fusion
  12.1 0.8 copy.56
  12.9 1.9 constant_dynamic-slice_fusion.8
  15.3 0.9 pad_maximum_fusion.1.weight_ref
  16.4 2.0 constant_dynamic-slice_fusion.1
  18.4 3.6 concatenate.130.vec_ref
  22.0 59.5 %norm_gather.1 = (bf16[4,48,128]{2,1,0:T(8,128)(2,1)}, bf16[8,128,1600]{2,1,0:T(8,128)(2,1)}, bf16[4,8,64,1600]{3,2,1,0:T(8,128)(2,1)}, bf16[4,400,384]{2,1,0:T(8,128)(2,1)}, bf16[64,1600]{1,0:T(8,128)(2,1)}) custom-call(bf16[128,1600]{1,0:T(8,128)(2,1)} %bitcast.90, bf16[128,1600]{1,0:T(8,128)(2,1)} %bitcast.96, bf16[48,128]{1,0:T(8,128)(2,1)} %concatenate.130.vec_ref, ...), custom_call_target="tpu_custom_call" | custom-call | flops 1 | bytes 1 | tf_op jit(solution)/shard_map/norm_gather/pallas_call | solution.py:415
  84.2 0.8 reshape_reshape.3
  89.8 0.8 fusion.3.out_w_ref
  90.6 65.7 %attend.1 = (bf16[4,8,2,32,384]{4,3,2,1,0:T(8,128)(2,1)}, f32[2048,128]{1,0:T(8,128)}, f32[2,2048]{1,0:T(2,128)}, bf16[8,2,2,32,256]{4,3,2,1,0:T(8,128)(2,1)}, bf16[4,64,1600]{2,1,0:T(8,128)(2,1)}) custom-call(s32[3,64]{1,0:T(4,128)} %pad_add_fusion.order_ref, s32[64]{0:T(128)} %select_reduce_fusion.place_ref, bf16[2048,1600]{1,0:T(8,128)(2,1)} %bitcast.84, ...), custom_call_target="tpu_custom_call" | custom-call | flops 1 | bytes 1 | tf_op jit(solution)/shard_map/attend/pallas_call | solution.py:1378
  157.1 42.7 %scatter_norm_gather.1 = (f32[128,1600]{1,0:T(8,128)}, bf16[8,128,1600]{2,1,0:T(8,128)(2,1)}) custom-call(bf16[1024,256]{1,0:T(8,128)(2,1)} %bitcast.102, bf16[256,1600]{1,0:T(8,128)(2,1)} %bitcast.100, bf16[128,1600]{1,0:T(8,128)(2,1)} %bitcast.91, f32[3,1600]{1,0:T(4,128)} %pad_maximum_fusion.2.vec_ref), custom_call_target="tpu_custom_call" | custom-call | flops 1 | bytes 1 | tf_op jit(solution)/shard_map/scatter_norm_gather/pallas_call | solution.py:472
  200.8 14.9 %feed_up.1 = (bf16[1024,800]{1,0:T(8,128)(2,1)}, f32[1024,800]{1,0:T(8,128)}, bf16[800,1600]{1,0:T(8,128)(2,1)}) custom-call(bf16[1024,1600]{1,0:T(8,128)(2,1)} %bitcast.88, bf16[1024,1600]{1,0:T(8,128)(2,1)} %bitcast.86, bf16[1600,800]{1,0:T(8,128)(2,1)} %all-gather.3.cloned.1.call-done.weight_ref.up_w_hbm, f32[1,800]{1,0:T(1,128)} %broadcast_in_dim_reshape.3.shift_ref), custom_call_target="tpu_custom_call" | custom-call | flops 1 | bytes 1 | tf_op jit(solution)/shard_map/feed_up/pallas_call | solution.py:1921
  216.3 10.3 %all-gather.5.cloned.1.call-done.down_w_hbm = bf16[800,1600]{1,0:T(8,128)(2,1)} async-done(((bf16[200,1600]{1,0:T(8,128)(2,1)}), bf16[800,1600]{1,0:T(8,128)(2,1)}) %all-gather.5.cloned.1.call-update) | async-done | bytes 2560016 | tf_op jit(solution)/shard_map/all_gather | solution.py:2044
  226.6 48.8 %feed_back.1 = (f32[128,1600]{1,0:T(8,128)}, f32[4,1600]{1,0:T(4,128)}, bf16[8,128,1600]{2,1,0:T(8,128)(2,1)}, bf16[1024,1600]{1,0:T(8,128)(2,1)}, bf16[800,1600]{1,0:T(8,128)(2,1)}, /*index=5*/f32[1,800]{1,0:T(1,128)}) custom-call(bf16[1024,1600]{1,0:T(8,128)(2,1)} %bitcast.89, bf16[1024,1600]{1,0:T(8,128)(2,1)} %bitcast.87, ...), custom_call_target="tpu_custom_call" | custom-call | flops 1 | bytes 1 | tf_op jit(solution)/shard_map/feed_back/pallas_call | solution.py:596
  279.2 1.4 reduce-scatter.7.cloned.1.call-done.down_ref
  280.7 46.9 %branch_back.1 = (bf16[4,8,2,32,384]{4,3,2,1,0:T(8,128)(2,1)}, f32[1,384]{1,0:T(1,128)}, bf16[256,1600]{1,0:T(8,128)(2,1)}, bf16[128,1600]{1,0:T(8,128)(2,1)}, bf16[8,200,1600]{2,1,0:T(8,128)(2,1)}) custom-call(s32[3,64]{1,0:T(4,128)} %pad_add_fusion.order_ref, s32[64]{0:T(128)} %select_reduce_fusion.place_ref, bf16[1024,1600]{1,0:T(8,128)(2,1)} %bitcast.98, ...), custom_call_target="tpu_custom_call" | custom-call | flops 1 | bytes 1 | tf_op jit(solution)/shard_map/branch_back/pallas_call | solution.py:1660
  327.6 0.8 bitcast_dynamic-update-slice_fusion.3
  328.4 0.9 bitcast_dynamic-update-slice_fusion.2
  329.3 0.8 bitcast_dynamic-update-slice_fusion
  331.2 7.3 %bitcast_convert_fusion = f32[1600,1600]{1,0:T(8,128)} fusion(bf16[8,200,1600]{2,1,0:T(8,128)(2,1)} %get-tuple-element.82), kind=kLoop, calls=%fused_computation | loop fusion | flops 2560000 | bytes 15360000 | tf_op jit(solution)/shard_map/convert_element_type | solution.py:2116
  338.5 4.1 reduce-scatter.9.cloned.1.call-done.up_ref
  342.6 96.3 %finish.1 = (f32[128,1600]{1,0:T(8,128)}, bf16[8,2,400,384]{3,2,1,0:T(8,128)(2,1)}, bf16[8,200,1600]{2,1,0:T(8,128)(2,1)}, bf16[8,64,1600]{2,1,0:T(8,128)(2,1)},...) custom-call(bf16[2048,1600]{1,0:T(8,128)(2,1)} %bitcast.85, bf16[2048,384]{1,0:T(8,128)(2,1)} %bitcast.105, ...), custom_call_target="tpu_custom_call" | custom-call | flops 1 | bytes 1 | tf_op jit(solution)/shard_map/finish/pallas_call | solution.py:1001
  438.9 1.5 fusion.8
  440.4 1.4 slice.169
  441.8 7.9 %assemble_packed.1 = f32[400,6400]{1,0:T(8,128)} custom-call(bf16[8,200,1600]{2,1,0:T(8,128)(2,1)} %get-tuple-element.95.part_ref), custom_call_target="tpu_custom_call" | custom-call | tf_op jit(solution)/shard_map/assemble_packed/pallas_call | solution.py:1757
  449.6 5.7 %assemble.1 = f32[400,4800]{1,0:T(8,128)} custom-call(bf16[16,400,384]{2,1,0:T(8,128)(2,1)} %bitcast.93), custom_call_target="tpu_custom_call" | custom-call | tf_op jit(solution)/shard_map/assemble/pallas_call | solution.py:1733
  455.3 1.6 copy.64
  456.9 1.4 fusion.9
  458.3 1.2 copy.65
  459.5 1.7 fusion.1
  (107 shorter events, 10.6 us)
Async XLA Ops:
  7.2 4.8 %copy-start.10 = (bf16[1600]{0:T(1024)(128)(2,1)S(1)}, bf16[1600]{0:T(1024)(128)(2,1)}, u32[]{:S(2)}) copy-start(bf16[1600]{0:T(1024)(128)(2,1)} %param.37) | copy-start | bytes 9604
  7.2 4.9 %copy-start.3 = (bf16[64,2,1600]{2,1,0:T(2,128)(2,1)S(1)}, bf16[64,2,1600]{2,1,0:T(2,128)(2,1)}, u32[]{:S(2)}) copy-start(bf16[64,2,1600]{2,1,0:T(2,128)(2,1)} %param.26) | copy-start | bytes 1228804
  7.2 193.6 %all-gather.3.cloned.1.call-start = ((), (), s32[]{:S(2)}) async-start(), calls=%async_computation.2 | async-start | bytes 3584000 | tf_op jit(solution)/shard_map/all_gather | solution.py:2045
  12.9 3.3 copy-start.20
  12.9 3.3 copy-start.12
  12.9 3.4 copy-start.13
  12.9 3.4 copy-start.14
  12.9 3.4 copy-start.15
  12.9 3.4 copy-start.16
  12.9 3.4 copy-start.17
  12.9 3.4 copy-start.18
  12.9 3.4 copy-start.19
  16.4 65.9 %copy-start.9 = (s32[5]{0:T(128)S(1)}, s32[5]{0:T(128)}, u32[]{:S(2)}) copy-start(s32[5]{0:T(128)} %constant.124.clone) | copy-start | bytes 64
  18.4 68.5 %copy-start.8 = (s32[4]{0:T(128)S(1)}, s32[4]{0:T(128)}, u32[]{:S(2)}) copy-start(s32[4]{0:T(128)} %constant.125.clone) | copy-start | bytes 52
  18.4 69.8 %copy-start.21 = (s32[32]{0:T(128)S(1)}, s32[32]{0:T(128)}, u32[]{:S(2)}) copy-start(s32[32]{0:T(128)} %param.25) | copy-start | bytes 388
  18.4 71.4 %copy-start = (bf16[400,1600]{1,0:T(8,128)(2,1)S(1)}, bf16[400,1600]{1,0:T(8,128)(2,1)}, u32[]{:S(2)}) copy-start(bf16[400,1600]{1,0:T(8,128)(2,1)} %out_w_ref.1) | copy-start | bytes 3840004
  81.5 145.1 %all-gather.5.cloned.1.call-start = ((), (), s32[]{:S(2)}) async-start(), calls=%async_computation.3 | async-start | bytes 3328000 | tf_op jit(solution)/shard_map/all_gather | solution.py:2044
  82.2 198.5 %reduce-scatter.7.cloned.1.call-start = ((), (), s32[]{:S(2)}) async-start(), calls=%async_computation.4 | async-start | bytes 3328000
  156.5 59.2 %copy-start.6 = (f32[1,1600]{1,0:T(1,128)}, f32[1,1600]{1,0:T(1,128)S(1)}, u32[]{:S(2)}) copy-start(f32[1,1600]{1,0:T(1,128)S(1)} %stack_reshape_squeeze.9.vec_ref) | copy-start | bytes 19204
  215.8 126.8 %reduce-scatter.9.cloned.1.call-start = ((), (), s32[]{:S(2)}) async-start(), calls=%async_computation.5 | async-start | bytes 3328000
  275.4 3.4 copy-start.7
  275.4 3.5 copy-start.11
  449.6 5.7 %copy-start.2 = (f32[128,1600]{1,0:T(8,128)S(1)}, f32[128,1600]{1,0:T(8,128)}, u32[]{:S(2)}) copy-start(f32[128,1600]{1,0:T(8,128)} %get-tuple-element.89) | copy-start | bytes 2457604
  449.6 8.6 %copy-start.4 = (bf16[128,1600]{1,0:T(8,128)(2,1)S(1)}, bf16[128,1600]{1,0:T(8,128)(2,1)}, u32[]{:S(2)}) copy-start(bf16[128,1600]{1,0:T(8,128)(2,1)} %get-tuple-element.78) | copy-start | bytes 1228804
  455.3 4.1 copy-start.1
  455.3 4.1 copy-start.5
Sparse Core Ops, SparseCore 0:
  81.6 88.7 all-gather.2
  172.5 54.0 all-gather.4
  229.5 51.1 reduce-scatter.6
  282.9 59.6 reduce-scatter.8

commit v9 on v8

--- a/solution.py
+++ b/solution.py
@@ -564,12 +564,12 @@
             hidden = up_grad.shape[1]
             lines = up_grad.shape[0] // planes // 2
             for j in range(2 * planes):
-                rows_at, lanes_at = j // 2 * lines, j % 2 * hidden
-                up_grad_ref[rows_at : rows_at + lines, lanes_at : lanes_at + hidden] = up_grad[
-                    j * lines : (j + 1) * lines
-                ].astype(BF16)
+                lanes_at = j % 2 * hidden
+                up_grad_ref[j // 2, :, lanes_at : lanes_at + hidden] = up_grad[j * lines : (j + 1) * lines].astype(BF16)
         else:
-            up_grad_ref[...] = up_grad.astype(BF16)
+            for j in range(planes):
+                lines = up_grad.shape[0] // planes
+                up_grad_ref[j] = up_grad[j * lines : (j + 1) * lines].astype(BF16)
         out_ref[...] = nn(act_ref[...], down_w_ref[...]).astype(BF16)
         pltpu.make_async_copy(out_ref, out_hbm, out_sem).start()
 
@@ -600,7 +600,7 @@
             jax.ShapeDtypeStruct((4, width), F32),
             jax.ShapeDtypeStruct((n_ctx, rows, width), BF16),
             jax.ShapeDtypeStruct((total_rows, width), BF16),
-            jax.ShapeDtypeStruct((width // 2, 2 * hidden) if packed else (width, hidden), BF16),
+            jax.ShapeDtypeStruct((planes,) + ((width // planes // 2, 2 * hidden) if packed else (width // planes, hidden)), BF16),
             jax.ShapeDtypeStruct((1, hidden), F32),
         ),
         in_specs=[ANY] * 6 + [VMEM] * 3,
@@ -2081,7 +2081,7 @@
     d_mixed, sums2, d_branch, out_part, up_part, d_up_sum = feed_back(
         h2, og_all, act, slope, up_slice, down_slice, mixed, og, gain2[None, :], planes, halved
     )
-    up_own_grad = reduce_own(up_part)
+    up_own_grad = lax.psum_scatter(up_part, "fsdp", scatter_dimension=0, tiled=False)
     out_part = out_part.reshape(n_ctx, rows, width)
     d_branch = d_branch.reshape(plane_rows, width)
     if length <= SHORT:

time: 474 us -> 474 us (level)
  no operation moved by 1% of the time
where the time goes in v9:
time: 474 us; the launch traced here: 468 us
  Pallas kernels  388 us (82%)
  local copies, waits for them, and re-layouts  29 us (6%)
  between operations  19.3 us (4%)
  waiting for transfers between devices  16.6 us (4%)
  other arithmetic  14.2 us (3%)
    pallas_call x1, Pallas kernels, finish(): pl.pallas_call(functools.partial(finish_kernel, chips, planes, seqs, coun...  96.3 us
    pallas_call x1, Pallas kernels, attend(): pl.pallas_call(functools.partial(attend_kernel, tile, planes, seqs), out_...  65.7 us
    pallas_call x1, Pallas kernels, first_norm_gather(): pl.pallas_call(functools.partial(first_kernel, chips, planes, seqs, width...  59.5 us
    pallas_call x1, Pallas kernels, feed_back(): pl.pallas_call(functools.partial(third_kernel, chips, planes, packed), ou...  48.8 us
    pallas_call x1, Pallas kernels, branch_back(): pl.pallas_call(functools.partial(branch_back_kernel, tile, planes, seqs,...  46.9 us
    pallas_call x1, Pallas kernels, second_norm_gather(): pl.pallas_call(functools.partial(second_kernel, chips), out_shape=(jax.Sh...  42.7 us
    pallas_call x1, Pallas kernels, feed_up(): pl.pallas_call(up_kernel, grid=(rows // block,), out_shape=(jax.ShapeDtyp...  14.9 us
    all_gather x1, waiting for transfers between devices, local(): down_slice = lax.all_gather(down_own, 'fsdp', axis=0, tiled=True)  10.3 us
  transfers between devices with their start and end apart: 4, of which 3 were waited for; matrix products, arithmetic and copies ran while one was open for 4% of the time, Pallas kernels for 47%

profile of v9, /device:TPU:0, one launch (start us, length us, event | category | flops | bytes accessed | tf_op | source)
XLA Modules:
  0.0 468.1 jit_solution(15739375718275044953)
XLA Ops:
  7.3 1.9 copy.55
  9.1 1.6 constant_dynamic-slice_fusion.17
  10.7 1.2 pad_maximum_fusion
  12.1 0.8 copy.56
  12.9 1.9 constant_dynamic-slice_fusion.8
  15.3 0.9 pad_maximum_fusion.1.weight_ref
  16.4 2.0 constant_dynamic-slice_fusion.1
  18.4 3.6 concatenate.130.vec_ref
  22.0 59.5 %norm_gather.1 = (bf16[4,48,128]{2,1,0:T(8,128)(2,1)}, bf16[8,128,1600]{2,1,0:T(8,128)(2,1)}, bf16[4,8,64,1600]{3,2,1,0:T(8,128)(2,1)}, bf16[4,400,384]{2,1,0:T(8,128)(2,1)}, bf16[64,1600]{1,0:T(8,128)(2,1)}) custom-call(bf16[128,1600]{1,0:T(8,128)(2,1)} %bitcast.91, bf16[128,1600]{1,0:T(8,128)(2,1)} %bitcast.97, bf16[48,128]{1,0:T(8,128)(2,1)} %concatenate.130.vec_ref, ...), custom_call_target="tpu_custom_call" | custom-call | flops 1 | bytes 1 | tf_op jit(solution)/shard_map/norm_gather/pallas_call | solution.py:415
  84.2 0.8 reshape_reshape.3
  89.8 0.8 fusion.3.out_w_ref
  90.6 65.7 %attend.1 = (bf16[4,8,2,32,384]{4,3,2,1,0:T(8,128)(2,1)}, f32[2048,128]{1,0:T(8,128)}, f32[2,2048]{1,0:T(2,128)}, bf16[8,2,2,32,256]{4,3,2,1,0:T(8,128)(2,1)}, bf16[4,64,1600]{2,1,0:T(8,128)(2,1)}) custom-call(s32[3,64]{1,0:T(4,128)} %pad_add_fusion.order_ref, s32[64]{0:T(128)} %select_reduce_fusion.place_ref, bf16[2048,1600]{1,0:T(8,128)(2,1)} %bitcast.85, ...), custom_call_target="tpu_custom_call" | custom-call | flops 1 | bytes 1 | tf_op jit(solution)/shard_map/attend/pallas_call | solution.py:1378
  157.1 42.7 %scatter_norm_gather.1 = (f32[128,1600]{1,0:T(8,128)}, bf16[8,128,1600]{2,1,0:T(8,128)(2,1)}) custom-call(bf16[1024,256]{1,0:T(8,128)(2,1)} %bitcast.103, bf16[256,1600]{1,0:T(8,128)(2,1)} %bitcast.101, bf16[128,1600]{1,0:T(8,128)(2,1)} %bitcast.92, f32[3,1600]{1,0:T(4,128)} %pad_maximum_fusion.2.vec_ref), custom_call_target="tpu_custom_call" | custom-call | flops 1 | bytes 1 | tf_op jit(solution)/shard_map/scatter_norm_gather/pallas_call | solution.py:472
  200.8 14.9 %feed_up.1 = (bf16[1024,800]{1,0:T(8,128)(2,1)}, f32[1024,800]{1,0:T(8,128)}, bf16[800,1600]{1,0:T(8,128)(2,1)}) custom-call(bf16[1024,1600]{1,0:T(8,128)(2,1)} %bitcast.89, bf16[1024,1600]{1,0:T(8,128)(2,1)} %bitcast.87, bf16[1600,800]{1,0:T(8,128)(2,1)} %all-gather.3.cloned.1.call-done.weight_ref.up_w_hbm, f32[1,800]{1,0:T(1,128)} %broadcast_in_dim_reshape.3.shift_ref), custom_call_target="tpu_custom_call" | custom-call | flops 1 | bytes 1 | tf_op jit(solution)/shard_map/feed_up/pallas_call | solution.py:1921
  216.3 10.3 %all-gather.5.cloned.1.call-done.down_w_hbm = bf16[800,1600]{1,0:T(8,128)(2,1)} async-done(((bf16[200,1600]{1,0:T(8,128)(2,1)}), bf16[800,1600]{1,0:T(8,128)(2,1)}) %all-gather.5.cloned.1.call-update) | async-done | bytes 2560016 | tf_op jit(solution)/shard_map/all_gather | solution.py:2044
  226.6 48.8 %feed_back.1 = (f32[128,1600]{1,0:T(8,128)}, f32[4,1600]{1,0:T(4,128)}, bf16[8,128,1600]{2,1,0:T(8,128)(2,1)}, bf16[1024,1600]{1,0:T(8,128)(2,1)}, bf16[4,200,1600]{2,1,0:T(8,128)(2,1)}, /*index=5*/f32[1,800]{1,0:T(1,128)}) custom-call(bf16[1024,1600]{1,0:T(8,128)(2,1)} %bitcast.90, bf16[1024,1600]{1,0:T(8,128)(2,1)} %bitcast.88, ...), custom_call_target="tpu_custom_call" | custom-call | flops 1 | bytes 1 | tf_op jit(solution)/shard_map/feed_back/pallas_call | solution.py:596
  279.2 1.4 reduce-scatter.7.cloned.1.call-done.down_ref
  280.7 46.9 %branch_back.1 = (bf16[4,8,2,32,384]{4,3,2,1,0:T(8,128)(2,1)}, f32[1,384]{1,0:T(1,128)}, bf16[256,1600]{1,0:T(8,128)(2,1)}, bf16[128,1600]{1,0:T(8,128)(2,1)}, bf16[8,200,1600]{2,1,0:T(8,128)(2,1)}) custom-call(s32[3,64]{1,0:T(4,128)} %pad_add_fusion.order_ref, s32[64]{0:T(128)} %select_reduce_fusion.place_ref, bf16[1024,1600]{1,0:T(8,128)(2,1)} %bitcast.99, ...), custom_call_target="tpu_custom_call" | custom-call | flops 1 | bytes 1 | tf_op jit(solution)/shard_map/branch_back/pallas_call | solution.py:1660
  327.6 0.8 bitcast_dynamic-update-slice_fusion.3
  328.4 0.9 bitcast_dynamic-update-slice_fusion.2
  329.3 0.8 bitcast_dynamic-update-slice_fusion
  331.2 7.3 %bitcast_convert_fusion = f32[1600,1600]{1,0:T(8,128)} fusion(bf16[8,200,1600]{2,1,0:T(8,128)(2,1)} %get-tuple-element.82), kind=kLoop, calls=%fused_computation | loop fusion | flops 2560000 | bytes 15360000 | tf_op jit(solution)/shard_map/convert_element_type | solution.py:2116
  338.5 4.1 reduce-scatter.9.cloned.1.call-done
  342.6 96.3 %finish.1 = (f32[128,1600]{1,0:T(8,128)}, bf16[8,2,400,384]{3,2,1,0:T(8,128)(2,1)}, bf16[8,200,1600]{2,1,0:T(8,128)(2,1)}, bf16[8,64,1600]{2,1,0:T(8,128)(2,1)},...) custom-call(bf16[2048,1600]{1,0:T(8,128)(2,1)} %bitcast.86, bf16[2048,384]{1,0:T(8,128)(2,1)} %bitcast.106, ...), custom_call_target="tpu_custom_call" | custom-call | flops 1 | bytes 1 | tf_op jit(solution)/shard_map/finish/pallas_call | solution.py:1001
  438.9 1.5 fusion.8
  440.4 1.4 slice.169
  441.8 7.9 %assemble_packed.1 = f32[400,6400]{1,0:T(8,128)} custom-call(bf16[8,200,1600]{2,1,0:T(8,128)(2,1)} %get-tuple-element.95.part_ref), custom_call_target="tpu_custom_call" | custom-call | tf_op jit(solution)/shard_map/assemble_packed/pallas_call | solution.py:1757
  449.6 5.7 %assemble.1 = f32[400,4800]{1,0:T(8,128)} custom-call(bf16[16,400,384]{2,1,0:T(8,128)(2,1)} %bitcast.94), custom_call_target="tpu_custom_call" | custom-call | tf_op jit(solution)/shard_map/assemble/pallas_call | solution.py:1733
  455.3 1.6 copy.64
  456.9 1.4 fusion.9
  458.3 1.2 copy.65
  459.5 1.7 fusion.1
  (107 shorter events, 10.6 us)
Async XLA Ops:
  7.2 4.8 %copy-start.10 = (bf16[1600]{0:T(1024)(128)(2,1)S(1)}, bf16[1600]{0:T(1024)(128)(2,1)}, u32[]{:S(2)}) copy-start(bf16[1600]{0:T(1024)(128)(2,1)} %param.37) | copy-start | bytes 9604
  7.2 4.9 %copy-start.3 = (bf16[64,2,1600]{2,1,0:T(2,128)(2,1)S(1)}, bf16[64,2,1600]{2,1,0:T(2,128)(2,1)}, u32[]{:S(2)}) copy-start(bf16[64,2,1600]{2,1,0:T(2,128)(2,1)} %param.26) | copy-start | bytes 1228804
  7.2 193.6 %all-gather.3.cloned.1.call-start = ((), (), s32[]{:S(2)}) async-start(), calls=%async_computation.2 | async-start | bytes 3584000 | tf_op jit(solution)/shard_map/all_gather | solution.py:2045
  12.9 3.3 copy-start.20
  12.9 3.3 copy-start.12
  12.9 3.4 copy-start.13
  12.9 3.4 copy-start.14
  12.9 3.4 copy-start.15
  12.9 3.4 copy-start.16
  12.9 3.4 copy-start.17
  12.9 3.4 copy-start.18
  12.9 3.4 copy-start.19
  16.4 65.9 %copy-start.9 = (s32[5]{0:T(128)S(1)}, s32[5]{0:T(128)}, u32[]{:S(2)}) copy-start(s32[5]{0:T(128)} %constant.124.clone) | copy-start | bytes 64
  18.4 68.5 %copy-start.8 = (s32[4]{0:T(128)S(1)}, s32[4]{0:T(128)}, u32[]{:S(2)}) copy-start(s32[4]{0:T(128)} %constant.125.clone) | copy-start | bytes 52
  18.4 69.8 %copy-start.21 = (s32[32]{0:T(128)S(1)}, s32[32]{0:T(128)}, u32[]{:S(2)}) copy-start(s32[32]{0:T(128)} %param.25) | copy-start | bytes 388
  18.4 71.4 %copy-start = (bf16[400,1600]{1,0:T(8,128)(2,1)S(1)}, bf16[400,1600]{1,0:T(8,128)(2,1)}, u32[]{:S(2)}) copy-start(bf16[400,1600]{1,0:T(8,128)(2,1)} %out_w_ref.1) | copy-start | bytes 3840004
  81.5 145.1 %all-gather.5.cloned.1.call-start = ((), (), s32[]{:S(2)}) async-start(), calls=%async_computation.3 | async-start | bytes 3328000 | tf_op jit(solution)/shard_map/all_gather | solution.py:2044
  82.2 198.5 %reduce-scatter.7.cloned.1.call-start = ((), (), s32[]{:S(2)}) async-start(), calls=%async_computation.4 | async-start | bytes 3328000
  156.5 59.2 %copy-start.6 = (f32[1,1600]{1,0:T(1,128)}, f32[1,1600]{1,0:T(1,128)S(1)}, u32[]{:S(2)}) copy-start(f32[1,1600]{1,0:T(1,128)S(1)} %stack_reshape_squeeze.9.vec_ref) | copy-start | bytes 19204
  215.8 126.8 %reduce-scatter.9.cloned.1.call-start = ((), (), s32[]{:S(2)}) async-start(), calls=%async_computation.5 | async-start | bytes 3328000
  275.4 3.4 copy-start.7
  275.4 3.5 copy-start.11
  449.6 5.7 %copy-start.2 = (f32[128,1600]{1,0:T(8,128)S(1)}, f32[128,1600]{1,0:T(8,128)}, u32[]{:S(2)}) copy-start(f32[128,1600]{1,0:T(8,128)} %get-tuple-element.89) | copy-start | bytes 2457604
  449.6 8.6 %copy-start.4 = (bf16[128,1600]{1,0:T(8,128)(2,1)S(1)}, bf16[128,1600]{1,0:T(8,128)(2,1)}, u32[]{:S(2)}) copy-start(bf16[128,1600]{1,0:T(8,128)(2,1)} %get-tuple-element.78) | copy-start | bytes 1228804
  455.3 4.1 copy-start.1
  455.3 4.1 copy-start.5
Sparse Core Ops, SparseCore 0:
  81.6 88.7 all-gather.2
  172.5 54.0 all-gather.4
  229.5 51.1 reduce-scatter.6
  282.9 59.6 reduce-scatter.8
